TPU v7x, 32 devices: a whole 2x2x4 slice. The times are simulated.
32 devices in a mesh: groups: 2 (over y), graph: 4 (over z), dp: 4 (over x, core).
Axes of the slice: x: 2, y: 2, z: 4, core: 2. Of those that a mesh axis runs over, the one named last changes fastest.
Arguments:
- edge_emb: bfloat16 [8, 4096, 512], P(('groups', 'dp'), 'graph'), parts along dimension 0, may hold values from -6 to 6
- cotangent: bfloat16 [8, 4096, 512], P(('groups', 'dp'), 'graph'), parts along dimension 0, may hold values from -6 to 6
- fetch_rows: int32 [8, 4, 4, 64], P(('groups', 'dp'), 'graph'), parts along dimension 0, may hold values from 0 to 1023, as said below
- store_rows: int32 [8, 4, 4, 64], P(('groups', 'dp'), 'graph'), parts along dimension 0, may hold values from 0 to 1023, as said below
- trip_src: int32 [8, 128, 128], P(('groups', 'dp'), 'graph'), parts along dimension 0, may hold values from 0 to 255
- trip_dst: int32 [8, 128, 128], P(('groups', 'dp'), 'graph'), parts along dimension 0, may hold values from 0 to 255
- trip_basis: bfloat16 [8, 16384, 128], P(('groups', 'dp'), 'graph'), parts along dimension 0, may hold values from -6 to 6
- block_count: int32 [8, 4], P(('groups', 'dp'), 'graph'), parts along dimension 0, may hold values from 1 to 32, as said below
- w_basis: bfloat16 [128, 512], replicated, may hold values from -0.5 to 0.5
- w_out: bfloat16 [512, 512], replicated, may hold values from -0.25 to 0.25
Outputs:
- updated: bfloat16 [8, 4096, 512], P(('groups', 'dp'), 'graph'), parts along dimension 0
- grad_edges: bfloat16 [8, 4096, 512], P(('groups', 'dp'), 'graph'), parts along dimension 0
- grad_out: float32 [1024, 512], P('groups'), parts along dimension 0
- grad_basis: float32 [256, 512], P('groups'), parts along dimension 0
There are 2 independent parts, one for each index of `groups`. A program takes and returns all parts, laid end to end along the dimension named above; an argument that names none is the same for every part. Nothing has to cross between parts.
Inputs may be any that keep to these rules, and one draw needn't show every extreme that they name: `fetch_rows`: within one device's list for one owner the 64 indices are distinct. `store_rows`: within one device's list for one owner the 64 indices are distinct. `block_count`: in each graph batch some device uses all 32 blocks.
All inputs are finite; a program needn't handle non-finite values.
Results may differ from a plain program's by a relative error of at most 0.01.
Values may be sent and summed in bfloat16 or wider, within the bound.
No kernel may reach another device: no remote copies, remote signals or barrier semaphores. Data moves between devices by JAX's collectives and lax.ppermute only.
A program may use at most 64 MiB of HBM per device.

v0:
```python
import math

import jax
import jax.numpy as jnp
from jax import lax
from jax.sharding import PartitionSpec as P


def silu_grad(value):
    sig = jax.nn.sigmoid(value)
    return sig * (1.0 + value * (1.0 - sig))


def one_hot(index, count):
    columns = jnp.arange(count, dtype=jnp.int32)[None, :]
    return (index[:, None] == columns).astype(jnp.bfloat16)


def pick_rows(table, index):
    return jnp.dot(one_hot(index, table.shape[0]), table, preferred_element_type=jnp.float32)


def spread_rows(values, index, count):
    table = one_hot(index, count)
    upper = values.astype(jnp.bfloat16)
    lower = (values - upper.astype(jnp.float32)).astype(jnp.bfloat16)
    dims = (((0,), (0,)), ((), ()))
    first = lax.dot_general(table, upper, dims, preferred_element_type=jnp.float32)
    second = lax.dot_general(table, lower, dims, preferred_element_type=jnp.float32)
    return first + second


def triplet_forward(fetched, src, dst, basis, live, w_basis):
    pre = jnp.dot(basis, w_basis, preferred_element_type=jnp.float32)
    filt = jax.nn.silu(pre)
    message = pick_rows(fetched, src) * filt * live[:, None]
    return spread_rows(message, dst, fetched.shape[0])


def triplet_backward(fetched, dpartial, src, dst, basis, live, w_basis):
    pre = jnp.dot(basis, w_basis, preferred_element_type=jnp.float32)
    filt = jax.nn.silu(pre)
    dmsg = pick_rows(dpartial, dst) * live[:, None]
    dfilt = dmsg * pick_rows(fetched, src)
    dpre = (dfilt * silu_grad(pre)).astype(jnp.bfloat16)
    dweight = lax.dot_general(
        basis, dpre, (((0,), (0,)), ((), ())), preferred_element_type=jnp.float32
    )
    dsource = spread_rows(dmsg * filt, src, fetched.shape[0])
    return (dweight, dsource)


def per_device(
    edge_emb,
    cotangent,
    fetch_rows,
    store_rows,
    trip_src,
    trip_dst,
    trip_basis,
    block_count,
    w_basis,
    w_out,
):
    edges = edge_emb[0]
    upstream = cotangent[0]
    ranks = lax.axis_size("graph")
    copies = lax.axis_size("dp")
    edge_dev = edges.shape[0]
    width = edges.shape[1]
    wanted = fetch_rows[0, 0]
    filled = store_rows[0, 0]
    per_owner = wanted.shape[1]
    slots = ranks * per_owner
    lent, kept = (
        lax.all_to_all(wanted, "graph", split_axis=0, concat_axis=0, tiled=True),
        lax.all_to_all(filled, "graph", split_axis=0, concat_axis=0, tiled=True),
    )
    lent_flat = lent.reshape(-1)
    kept_flat = kept.reshape(-1)
    lend_rows = pick_rows(edges, lent_flat).astype(jnp.bfloat16).reshape(ranks, per_owner, width)
    fetched = lax.all_to_all(lend_rows, "graph", split_axis=0, concat_axis=0, tiled=True).reshape(
        slots, width
    )
    blocks = trip_src.shape[1]
    block_rows = trip_src.shape[2]
    basis_width = trip_basis.shape[2]
    group = math.gcd(blocks, 16)
    span = group * block_rows
    src_flat = trip_src[0].reshape(-1)
    dst_flat = trip_dst[0].reshape(-1)
    basis_flat = trip_basis[0]
    count = block_count[0, 0]
    offsets = jnp.arange(span, dtype=jnp.int32)

    def one_group(index):
        start = index * span
        src = lax.dynamic_slice_in_dim(src_flat, start, span, 0)
        dst = lax.dynamic_slice_in_dim(dst_flat, start, span, 0)
        basis = lax.dynamic_slice_in_dim(basis_flat, start, span, 0)
        live = ((start + offsets) // block_rows < count).astype(jnp.float32)
        return (src, dst, basis, live)

    turns = blocks // group

    def forward_step(index, total):
        src, dst, basis, live = one_group(index)
        return total + triplet_forward(fetched, src, dst, basis, live, w_basis)

    partial_value = lax.fori_loop(0, turns, forward_step, jnp.zeros((slots, width), jnp.float32))
    home = lax.all_to_all(
        partial_value.reshape(ranks, per_owner, width),
        "graph",
        split_axis=0,
        concat_axis=0,
        tiled=True,
    )
    agg = spread_rows(home.reshape(-1, width), kept_flat, edge_dev)
    hidden = jax.nn.silu(agg).astype(jnp.bfloat16)
    updated = (
        edges.astype(jnp.float32) + jnp.dot(hidden, w_out, preferred_element_type=jnp.float32)
    ).astype(jnp.bfloat16)
    out_term = lax.dot_general(
        hidden, upstream, (((0,), (0,)), ((), ())), preferred_element_type=jnp.float32
    )
    out_scale = jnp.sqrt(jnp.float32(copies * ranks * edge_dev))
    basis_scale = jnp.sqrt(jnp.float32(copies * ranks * blocks * block_rows))
    grad_w_out = lax.psum(out_term, ("graph", "dp")) / out_scale
    dhidden = lax.dot_general(
        upstream, w_out, (((1,), (1,)), ((), ())), preferred_element_type=jnp.float32
    )
    dagg = (dhidden * silu_grad(agg)).astype(jnp.bfloat16)
    back_rows = pick_rows(dagg, kept_flat).astype(jnp.bfloat16).reshape(ranks, per_owner, width)
    dpartial = lax.all_to_all(back_rows, "graph", split_axis=0, concat_axis=0, tiled=True).reshape(
        slots, width
    )

    def backward_step(index, totals):
        src, dst, basis, live = one_group(index)
        dweight, dsource = triplet_backward(fetched, dpartial, src, dst, basis, live, w_basis)
        return (totals[0] + dweight, totals[1] + dsource)

    basis_term, dfetch = lax.fori_loop(
        0,
        turns,
        backward_step,
        (jnp.zeros((basis_width, width), jnp.float32), jnp.zeros((slots, width), jnp.float32)),
    )
    grad_w_basis = lax.psum(basis_term, ("graph", "dp")) / basis_scale
    returned = lax.all_to_all(
        dfetch.reshape(ranks, per_owner, width).astype(jnp.bfloat16),
        "graph",
        split_axis=0,
        concat_axis=0,
        tiled=True,
    ).astype(jnp.float32)
    summed = spread_rows(returned.reshape(-1, width), lent_flat, edge_dev)
    grad_edge = (upstream.astype(jnp.float32) + summed).astype(jnp.bfloat16)
    return (updated[None], grad_edge[None], grad_w_out, grad_w_basis)


def solution(mesh):
    placed = (
        P(("groups", "dp"), "graph", None),
        P(("groups", "dp"), "graph", None),
        P(("groups", "dp"), "graph", None, None),
        P(("groups", "dp"), "graph", None, None),
        P(("groups", "dp"), "graph", None),
        P(("groups", "dp"), "graph", None),
        P(("groups", "dp"), "graph", None),
        P(("groups", "dp"), "graph"),
        P(),
        P(),
    )
    return jax.shard_map(
        per_device,
        mesh=mesh,
        in_specs=placed,
        out_specs=(
            P(("groups", "dp"), "graph", None),
            P(("groups", "dp"), "graph", None),
            P("groups", None),
            P("groups", None),
        ),
        check_vma=False,
    )
```

profile of v0, /device:TPU:0, one launch (start us, length us, event | category | flops | bytes accessed | tf_op | source)
XLA Modules:
  0.0 237.9 jit_solution(5746693765359674473)
XLA Ops:
  7.2 11.9 %all_to_all.38 = s32[4,1,64]{2,1,0:T(1,128)S(1)} all-to-all(s32[4,1,64]{2,1,0:T(1,128)} %bitcast.64), channel_id=1, replica_groups=mesh['groups'=2,'graph'=4,'dp'=4] {'graph'}, dimensions={0} | all-to-all | bytes 2048 | tf_op jit(solution)/shard_map/all_to_all | solution.py:76
  20.5 2.4 %convolution_convert_fusion = bf16[256,512]{1,0:T(8,128)(2,1)} fusion(bf16[1,1024,512]{2,1,0:T(8,128)(2,1)} %param.14, s32[256]{0:T(256)S(1)} %eq.191), kind=kOutput, calls=%fused_computation.81 | convolution fusion | flops 268828672 | bytes 1311744 | tf_op jit(solution)/shard_map/dot_general | solution.py:20
  22.9 3.4 %all-to-all-start.2 = ((bf16[4,64,512]{2,1,0:T(8,128)(2,1)}), bf16[4,64,512]{2,1,0:T(8,128)(2,1)S(1)}, u32[]{:S(2)}, u32[]{:S(2)}) async-start(bf16[4,64,512]{2,1,0:T(8,128)(2,1)} %bitcast.5), calls=%async_computation.2 | async-start | bytes 524288 | tf_op jit(solution)/shard_map/all_to_all | solution.py:82
  26.3 7.9 %all-to-all-done.2 = bf16[4,64,512]{2,1,0:T(8,128)(2,1)S(1)} async-done(((bf16[4,64,512]{2,1,0:T(8,128)(2,1)}), bf16[4,64,512]{2,1,0:T(8,128)(2,1)S(1)}, u32[]{:S(2)}, u32[]{:S(2)}) %all-to-all-start.2) | async-done | bytes 262176 | tf_op jit(solution)/shard_map/all_to_all | solution.py:82
  34.2 3.2 %all-to-all-start = ((s32[4,1,64]{2,1,0:T(1,128)}), s32[4,1,64]{2,1,0:T(1,128)S(1)}, u32[]{:S(2)}, u32[]{:S(2)}) async-start(s32[4,1,64]{2,1,0:T(1,128)} %bitcast.1), calls=%async_computation | async-start | bytes 4096 | tf_op jit(solution)/shard_map/all_to_all | solution.py:77
  37.5 13.0 %while.34 = (s32[]{:T(128)}, f32[256,512]{1,0:T(8,128)}, s32[4096]{0:T(1024)S(1)}, s32[4096]{0:T(1024)S(1)}, bf16[256,512]{1,0:T(8,128)(2,1)S(1)}, /*index=5*/bf...) while((s32[]{:T(128)}, f32[256,512]{1,0:T(8,128)}, ...), condition=%wide.region_1.2_spmd.clone, body=%wide.region_0.1_spmd.clone.sunk | while | flops 1892585472 | bytes 24060104 | solution.py:110
  38.9 1.5 multiply_multiply_fusion.4
  41.5 1.9 fusion.109
  44.9 1.5 multiply_multiply_fusion.4
  47.5 3.0 %fusion.109 = f32[256,512]{1,0:T(8,128)} fusion(f32[256,512]{1,0:T(8,128)S(1)} %fusion.108, f32[2048,512]{1,0:T(8,128)S(1)} %multiply_multiply_fusion.4, s32[2048]{0:T(1024)S(1)} %dynamic_slice.83, f32[256,512]{1,0:T(8,128)} %get-tuple-element.727, pred[]{:T(512)S(6)} %compare.36), kind=kOutput, calls=%fused_computation.9.clone.1 | convolution fusion | flops 538836992 | bytes 5775361 | tf_op jit(solution)/shard_map/while/body/eval_jaxpr/dot_general | solution.py:28
  50.5 5.0 %all-to-all-start.3 = ((f32[4,64,512]{2,1,0:T(8,128)}), f32[4,64,512]{2,1,0:T(8,128)S(1)}, u32[]{:S(2)}, u32[]{:S(2)}) async-start(f32[4,64,512]{2,1,0:T(8,128)} %bitcast.9), calls=%async_computation.3 | async-start | bytes 1048576 | tf_op jit(solution)/shard_map/all_to_all | solution.py:111
  56.3 11.3 %all-to-all-done.3 = f32[4,64,512]{2,1,0:T(8,128)S(1)} async-done(((f32[4,64,512]{2,1,0:T(8,128)}), f32[4,64,512]{2,1,0:T(8,128)S(1)}, u32[]{:S(2)}, u32[]{:S(2)}) %all-to-all-start.3) | async-done | bytes 524320 | tf_op jit(solution)/shard_map/all_to_all | solution.py:111
  68.2 1.9 convolution_add_fusion
  70.1 3.7 %fusion.57 = bf16[256,512]{1,0:T(8,128)(2,1)} fusion(f32[1024,512]{1,0:T(8,128)} %convolution_add_fusion, bf16[512,512]{1,0:T(8,128)(2,1)S(1)} %copy-done, bf16[1,1024,512]{2,1,0:T(8,128)(2,1)S(1)} %copy-done.5, s32[256]{0:T(256)S(1)} %eq.187), kind=kOutput, calls=%fused_computation.80 | convolution fusion | flops 810418176 | bytes 3933184 | tf_op jit(solution)/shard_map/dot_general | solution.py:20
  73.8 3.6 %all-to-all-start.4 = ((bf16[4,64,512]{2,1,0:T(8,128)(2,1)}), bf16[4,64,512]{2,1,0:T(8,128)(2,1)S(1)}, u32[]{:S(2)}, u32[]{:S(2)}) async-start(bf16[4,64,512]{2,1,0:T(8,128)(2,1)} %bitcast.63), calls=%async_computation.4 | async-start | bytes 524288 | tf_op jit(solution)/shard_map/all_to_all | solution.py:134
  77.4 3.3 %fusion.58 = f32[512,512]{1,0:T(8,128)} fusion(bf16[1,1024,512]{2,1,0:T(8,128)(2,1)S(1)} %copy-done.5, f32[1024,512]{1,0:T(8,128)} %convolution_add_fusion), kind=kOutput, calls=%fused_computation.82 | convolution fusion | flops 539492352 | bytes 4194304 | tf_op jit(solution)/shard_map/dot_general | solution.py:123
  80.7 3.2 %all-to-all-done.4 = bf16[4,64,512]{2,1,0:T(8,128)(2,1)S(1)} async-done(((bf16[4,64,512]{2,1,0:T(8,128)(2,1)}), bf16[4,64,512]{2,1,0:T(8,128)(2,1)S(1)}, u32[]{:S(2)}, u32[]{:S(2)}) %all-to-all-start.4) | async-done | bytes 262176 | tf_op jit(solution)/shard_map/all_to_all | solution.py:134
  84.0 39.9 %while.35 = (s32[]{:T(128)}, f32[128,512]{1,0:T(8,128)}, f32[256,512]{1,0:T(8,128)S(1)}, bf16[4096,128]{1,0:T(8,128)(2,1)S(1)}, s32[4096]{0:T(1024)}, /*index=5*...) while((s32[]{:T(128)}, f32[128,512]{1,0:T(8,128)}, ...), condition=%wide.region_3.4_spmd.clone, body=%wide.region_2.3_spmd.clone.sunk | while | flops 2710081536 | bytes 71524632 | solution.py:143
  86.8 4.4 %multiply_multiply_fusion.5 = (f32[2048,512]{1,0:T(8,128)}, f32[2048,512]{1,0:T(8,128)}) fusion(f32[2048,512]{1,0:T(8,128)S(1)} %fusion.115, f32[2048]{0:T(1024)S(1)} %fusion.116, bf16[128,512]{1,0:T(8,128)(2,1)S(1)} %get-tuple-element.787, bf16[4096,128]{1,0:T(8,128)(2,1)S(1)} %get-tuple-element.781, s32[]{:T(128)S(6)} %select_n.75), kind=kOutput, calls=%fused_computation.33.clone.1 | convolution fusion | flops 274726912 | bytes 13246468 | tf_op jit(solution)/shard_map/while/body/eval_jaxpr/dot_general | solution.py:41
  91.2 6.7 %fusion.117 = f32[128,512]{1,0:T(8,128)} fusion(f32[2048,512]{1,0:T(8,128)} %get-tuple-element.712, f32[2048,512]{1,0:T(8,128)} %copy-done.1, bf16[256,512]{1,0:T(8,128)(2,1)} %get-tuple-element.786, f32[2048]{0:T(1024)S(1)} %fusion.116, s32[2048]{0:T(1024)S(1)} %dynamic_slice.87, bf16[4096,128]{1,0:T(8,128)(2,1)S(1)} %get-tuple-element.781, ...), kind=kOutput, calls=%fused_computation.44.clone.1 | convolution fusion | flops 817496064 | bytes 9715717 | tf_op jit(solution)/shard_map/while/body/eval_jaxpr/dot_general | solution.py:46
  97.9 4.7 %fusion.118 = f32[256,512]{1,0:T(8,128)S(1)} fusion(f32[2048,512]{1,0:T(8,128)} %get-tuple-element.713, s32[2048]{0:T(1024)S(1)} %dynamic_slice.87), kind=kOutput, calls=%fused_computation.36.clone.1 | convolution fusion | flops 541589504 | bytes 4726784 | tf_op jit(solution)/shard_map/while/body/eval_jaxpr/dot_general | solution.py:29
  102.7 1.2 fusion.119
  106.7 4.4 %multiply_multiply_fusion.5 = (f32[2048,512]{1,0:T(8,128)}, f32[2048,512]{1,0:T(8,128)}) fusion(f32[2048,512]{1,0:T(8,128)S(1)} %fusion.115, f32[2048]{0:T(1024)S(1)} %fusion.116, bf16[128,512]{1,0:T(8,128)(2,1)S(1)} %get-tuple-element.787, bf16[4096,128]{1,0:T(8,128)(2,1)S(1)} %get-tuple-element.781, s32[]{:T(128)S(6)} %select_n.75), kind=kOutput, calls=%fused_computation.33.clone.1 | convolution fusion | flops 274726912 | bytes 13246468 | tf_op jit(solution)/shard_map/while/body/eval_jaxpr/dot_general | solution.py:41
  111.2 6.7 %fusion.117 = f32[128,512]{1,0:T(8,128)} fusion(f32[2048,512]{1,0:T(8,128)} %get-tuple-element.712, f32[2048,512]{1,0:T(8,128)} %copy-done.1, bf16[256,512]{1,0:T(8,128)(2,1)} %get-tuple-element.786, f32[2048]{0:T(1024)S(1)} %fusion.116, s32[2048]{0:T(1024)S(1)} %dynamic_slice.87, bf16[4096,128]{1,0:T(8,128)(2,1)S(1)} %get-tuple-element.781, ...), kind=kOutput, calls=%fused_computation.44.clone.1 | convolution fusion | flops 817496064 | bytes 9715717 | tf_op jit(solution)/shard_map/while/body/eval_jaxpr/dot_general | solution.py:46
  117.9 4.7 %fusion.118 = f32[256,512]{1,0:T(8,128)S(1)} fusion(f32[2048,512]{1,0:T(8,128)} %get-tuple-element.713, s32[2048]{0:T(1024)S(1)} %dynamic_slice.87), kind=kOutput, calls=%fused_computation.36.clone.1 | convolution fusion | flops 541589504 | bytes 4726784 | tf_op jit(solution)/shard_map/while/body/eval_jaxpr/dot_general | solution.py:29
  122.6 1.2 fusion.119
  124.6 3.4 %all-to-all-start.5 = ((bf16[4,64,512]{2,1,0:T(8,128)(2,1)}), bf16[4,64,512]{2,1,0:T(8,128)(2,1)S(1)}, u32[]{:S(2)}, u32[]{:S(2)}) async-start(bf16[4,64,512]{2,1,0:T(8,128)(2,1)} %bitcast.15), calls=%async_computation.5 | async-start | bytes 524288 | tf_op jit(solution)/shard_map/all_to_all | solution.py:150
  128.8 3.4 %fusion.54 = bf16[1,1024,512]{2,1,0:T(8,128)(2,1)} fusion(bf16[512,512]{1,0:T(8,128)(2,1)S(1)} %copy-done, bf16[1,1024,512]{2,1,0:T(8,128)(2,1)S(1)} %copy-done.12, f32[1024,512]{1,0:T(8,128)} %convolution_add_fusion), kind=kOutput, calls=%fused_computation.77 | convolution fusion | flops 541065216 | bytes 4718592 | tf_op jit(solution)/shard_map/dot_general | solution.py:121
  132.1 2.7 %all-to-all-done.5 = bf16[4,64,512]{2,1,0:T(8,128)(2,1)S(1)} async-done(((bf16[4,64,512]{2,1,0:T(8,128)(2,1)}), bf16[4,64,512]{2,1,0:T(8,128)(2,1)S(1)}, u32[]{:S(2)}, u32[]{:S(2)}) %all-to-all-start.5) | async-done | bytes 262176 | tf_op jit(solution)/shard_map/all_to_all | solution.py:150
  135.4 1.6 fusion.55
  136.9 91.1 %all-reduce.3.cloned.1.call-done = (f32[512,512]{1,0:T(8,128)}, f32[128,512]{1,0:T(8,128)}) async-done(((f32[512,512]{1,0:T(8,128)}, f32[128,512]{1,0:T(8,128)}), (f32[512,512]{1,0:T(8,128)}, f32[128,512]{1,0:T(8,128)})) %all-reduce.3.cloned.1.call-update) | async-done | bytes 1310736 | tf_op jit(solution)/shard_map/psum | solution.py:128
  228.0 2.3 broadcast_multiply_fusion
  (64 shorter events, 16.2 us)
Async XLA Ops:
  7.2 62.9 %copy-start = (bf16[512,512]{1,0:T(8,128)(2,1)S(1)}, bf16[512,512]{1,0:T(8,128)(2,1)}, u32[]{:S(2)}) copy-start(bf16[512,512]{1,0:T(8,128)(2,1)} %param.23) | copy-start | bytes 1572868
  7.2 30.2 %copy-start.4 = (bf16[128,512]{1,0:T(8,128)(2,1)S(1)}, bf16[128,512]{1,0:T(8,128)(2,1)}, u32[]{:S(2)}) copy-start(bf16[128,512]{1,0:T(8,128)(2,1)} %param.22) | copy-start | bytes 393220
  7.2 30.2 %copy-start.3 = (bf16[1,4096,128]{2,1,0:T(8,128)(2,1)S(1)}, bf16[1,4096,128]{2,1,0:T(8,128)(2,1)}, u32[]{:S(2)}) copy-start(bf16[1,4096,128]{2,1,0:T(8,128)(2,1)} %param.20) | copy-start | bytes 3145732
  7.2 30.2 %copy-start.6 = (s32[1,32,128]{2,1,0:T(8,128)S(1)}, s32[1,32,128]{2,1,0:T(8,128)}, u32[]{:S(2)}) copy-start(s32[1,32,128]{2,1,0:T(8,128)} %param.19) | copy-start | bytes 49156
  7.2 30.2 %copy-start.7 = (s32[1,32,128]{2,1,0:T(8,128)S(1)}, s32[1,32,128]{2,1,0:T(8,128)}, u32[]{:S(2)}) copy-start(s32[1,32,128]{2,1,0:T(8,128)} %param.18) | copy-start | bytes 49156
  20.5 17.0 %copy-start.10 = (s32[256]{0:T(256)}, s32[256]{0:T(256)S(1)}, u32[]{:S(2)}) copy-start(s32[256]{0:T(256)S(1)} %eq.191) | copy-start | bytes 3076
  22.9 11.3 %all-to-all-start.2 = ((bf16[4,64,512]{2,1,0:T(8,128)(2,1)}), bf16[4,64,512]{2,1,0:T(8,128)(2,1)S(1)}, u32[]{:S(2)}, u32[]{:S(2)}) async-start(bf16[4,64,512]{2,1,0:T(8,128)(2,1)} %bitcast.5), calls=%async_computation.2 | async-start | bytes 524288 | tf_op jit(solution)/shard_map/all_to_all | solution.py:82
  34.2 16.3 %all-to-all-start = ((s32[4,1,64]{2,1,0:T(1,128)}), s32[4,1,64]{2,1,0:T(1,128)S(1)}, u32[]{:S(2)}, u32[]{:S(2)}) async-start(s32[4,1,64]{2,1,0:T(1,128)} %bitcast.1), calls=%async_computation | async-start | bytes 4096 | tf_op jit(solution)/shard_map/all_to_all | solution.py:77
  50.5 5.8 %copy-start.8 = (bf16[256,512]{1,0:T(8,128)(2,1)}, bf16[256,512]{1,0:T(8,128)(2,1)S(1)}, u32[]{:S(2)}) copy-start(bf16[256,512]{1,0:T(8,128)(2,1)S(1)} %get-tuple-element.809) | copy-start | bytes 786436
  50.5 17.1 %all-to-all-start.3 = ((f32[4,64,512]{2,1,0:T(8,128)}), f32[4,64,512]{2,1,0:T(8,128)S(1)}, u32[]{:S(2)}, u32[]{:S(2)}) async-start(f32[4,64,512]{2,1,0:T(8,128)} %bitcast.9), calls=%async_computation.3 | async-start | bytes 1048576 | tf_op jit(solution)/shard_map/all_to_all | solution.py:111
  68.2 1.9 copy-start.5
  73.8 10.2 %all-to-all-start.4 = ((bf16[4,64,512]{2,1,0:T(8,128)(2,1)}), bf16[4,64,512]{2,1,0:T(8,128)(2,1)S(1)}, u32[]{:S(2)}, u32[]{:S(2)}) async-start(bf16[4,64,512]{2,1,0:T(8,128)(2,1)} %bitcast.63), calls=%async_computation.4 | async-start | bytes 524288 | tf_op jit(solution)/shard_map/all_to_all | solution.py:134
  86.8 4.5 %copy-start.1 = (f32[2048,512]{1,0:T(8,128)}, f32[2048,512]{1,0:T(8,128)S(1)}, u32[]{:S(2)}) copy-start(f32[2048,512]{1,0:T(8,128)S(1)} %fusion.115) | copy-start | bytes 12582916 | tf_op jit(solution)/shard_map/while
  97.9 4.7 %copy-start.2 = (f32[2048,512]{1,0:T(8,128)S(1)}, f32[2048,512]{1,0:T(8,128)}, u32[]{:S(2)}) copy-start(f32[2048,512]{1,0:T(8,128)} %get-tuple-element.713) | copy-start | bytes 12582916 | tf_op jit(solution)/shard_map/while
  106.7 4.5 %copy-start.1 = (f32[2048,512]{1,0:T(8,128)}, f32[2048,512]{1,0:T(8,128)S(1)}, u32[]{:S(2)}) copy-start(f32[2048,512]{1,0:T(8,128)S(1)} %fusion.115) | copy-start | bytes 12582916 | tf_op jit(solution)/shard_map/while
  117.9 4.7 %copy-start.2 = (f32[2048,512]{1,0:T(8,128)S(1)}, f32[2048,512]{1,0:T(8,128)}, u32[]{:S(2)}) copy-start(f32[2048,512]{1,0:T(8,128)} %get-tuple-element.713) | copy-start | bytes 12582916 | tf_op jit(solution)/shard_map/while
  123.9 4.9 %copy-start.12 = (bf16[1,1024,512]{2,1,0:T(8,128)(2,1)S(1)}, bf16[1,1024,512]{2,1,0:T(8,128)(2,1)}, u32[]{:S(2)}) copy-start(bf16[1,1024,512]{2,1,0:T(8,128)(2,1)} %param.14) | copy-start | bytes 3145732
  124.6 10.2 %all-to-all-start.5 = ((bf16[4,64,512]{2,1,0:T(8,128)(2,1)}), bf16[4,64,512]{2,1,0:T(8,128)(2,1)S(1)}, u32[]{:S(2)}, u32[]{:S(2)}) async-start(bf16[4,64,512]{2,1,0:T(8,128)(2,1)} %bitcast.15), calls=%async_computation.5 | async-start | bytes 524288 | tf_op jit(solution)/shard_map/all_to_all | solution.py:150
  128.0 100.0 %all-reduce.3.cloned.1.call-start = ((), (), s32[]{:S(2)}) async-start(), calls=%async_computation.6 | async-start | bytes 2621440 | tf_op jit(solution)/shard_map/psum | solution.py:128
  128.8 6.0 %copy-start.11 = (s32[256]{0:T(256)S(1)}, s32[256]{0:T(256)}, u32[]{:S(2)}) copy-start(s32[256]{0:T(256)} %copy-done.10) | copy-start | bytes 3076
  228.0 2.3 copy-start.9
Sparse Core Ops, SparseCore 0:
  132.9 95.0 all-reduce.2
where the time goes:
time: 239 us; the launch traced here: 238 us
  waiting for transfers between devices  117 us (49%)
  matrix products  64.5 us (27%)
  starting transfers between devices  18.7 us (8%)
  between operations  14.2 us (6%)
  blocking collectives  11.9 us (5%)
  other arithmetic  7.75 us (3%)
  local copies, waits for them, and re-layouts  3.84 us (2%)
    psum x1, waiting for transfers between devices, per_device(): grad_w_out = lax.psum(out_term, ('graph', 'dp')) / out_scale  91.1 us
    dot_general x6, matrix products, spread_rows(): lax.dot_general(table, lower, dims, preferred_element_type=jnp.float32)  15.1 us
    dot_general x2, matrix products, triplet_backward(): lax.dot_general(basis, dpre, (((0,), (0,)), ((), ())), preferred_element_...  13.4 us
    all_to_all x1, blocking collectives, per_device(): lax.all_to_all(wanted, 'graph', split_axis=0, concat_axis=0, tiled=True)  11.9 us
    all_to_all x1, waiting for transfers between devices, per_device(): lax.all_to_all(partial_value.reshape(ranks, per_owner, width), 'graph', s...  11.3 us
    dot_general x6, matrix products, pick_rows(): jnp.dot(one_hot(index, table.shape[0]), table, preferred_element_type=jnp...  10.7 us
    dot_general x2, matrix products, triplet_backward(): pre = jnp.dot(basis, w_basis, preferred_element_type=jnp.float32)  8.72 us
    dot_general x6, matrix products, spread_rows(): lax.dot_general(table, upper, dims, preferred_element_type=jnp.float32)  8.43 us
  transfers between devices with their start and end apart: 6, of which 5 were waited for; matrix products, arithmetic and copies ran while one was open for 9% of the time, Pallas kernels for 0%

commit v1 on v0

v1 whole, which is shorter than its diff:
```python
import functools

import jax
import jax.numpy as jnp
from jax import lax
from jax.experimental import pallas as pl
from jax.experimental.pallas import tpu as pltpu
from jax.sharding import PartitionSpec as P

BF16 = jnp.bfloat16
F32 = jnp.float32
VMEM = pl.BlockSpec(memory_space=pltpu.VMEM)
SMEM = pl.BlockSpec(memory_space=pltpu.SMEM)
NN = (((1,), (0,)), ((), ()))
NT = (((1,), (1,)), ((), ()))


def dot(a, b, dims=NN):
    return lax.dot_general(a, b, dims, preferred_element_type=F32)


def silu_parts(value):
    sig = 0.5 * jnp.tanh(0.5 * value) + 0.5
    act = value * sig
    return act, sig + act * (1.0 - sig)


def call(body, outs, args, specs=None, flops=0, scratch=(), vmem=48):
    moved = sum(a.size * a.dtype.itemsize for a in args) + sum(
        o.size * o.dtype.itemsize for o in outs
    )
    return pl.pallas_call(
        body,
        out_shape=tuple(outs),
        in_specs=[VMEM] * len(args) if specs is None else specs,
        out_specs=tuple([VMEM] * len(outs)),
        scratch_shapes=list(scratch),
        cost_estimate=pl.CostEstimate(flops=flops, bytes_accessed=moved, transcendentals=0),
        compiler_params=pltpu.CompilerParams(vmem_limit_bytes=vmem << 20),
    )(*args)


def shape(dims, dtype=BF16):
    return jax.ShapeDtypeStruct(dims, dtype)


def prepare_kernel(per_owner, ranks, step, me, count, src, dst, basis, weight, filt, slope, s_hot, d_hot):
    slots = ranks * per_owner
    block = src.shape[1]
    weight_t = weight[...].T
    offset = me[0] * per_owner
    rows = lax.broadcasted_iota(jnp.int32, (slots, block), 0)

    def turn(i, carry):
        start = pl.multiple_of(i * step, step)
        pre = dot(weight_t, basis[pl.ds(start, step), :], NT)
        lane = lax.broadcasted_iota(jnp.int32, (1, step), 1) + start
        live = (lane < count[0, 0] * block).astype(F32)
        act, grad = silu_parts(pre)
        filt[:, pl.ds(start, step)] = (act * live).astype(BF16)
        slope[:, pl.ds(start, step)] = (grad * live).astype(BF16)
        for k in range(step // block):
            b = i * (step // block) + k
            at = pl.multiple_of(start + k * block, block)
            for index, hot in ((src, s_hot), (dst, d_hot)):
                slot = index[pl.ds(b, 1), :] - offset
                slot = jnp.where(slot < 0, slot + slots, slot)
                hot[:, pl.ds(at, block)] = jnp.where(rows == slot, 1.0, 0.0).astype(BF16)
        return carry

    lax.fori_loop(0, basis.shape[0] // step, turn, 0)


def lend_kernel(per_owner, ranks, me, *refs):
    lists, edges = refs[:ranks], refs[ranks]
    outs = refs[ranks + 1 : 2 * ranks + 1]
    lent_hot, kept_hot = refs[2 * ranks + 1], refs[2 * ranks + 2]
    edge_dev = edges.shape[0]
    columns = lax.broadcasted_iota(jnp.int32, (per_owner, edge_dev), 1).astype(F32)
    for s in range(ranks):
        row = lists[s][pl.ds(me[0], 1), :].astype(F32)
        column = jnp.broadcast_to(row, (8, row.shape[1])).T[:, :1]
        rows = pl.ds(s * per_owner, per_owner)
        lent_hot[rows, :] = jnp.where(columns == column[:per_owner], 1.0, 0.0).astype(BF16)
        kept_hot[rows, :] = jnp.where(
            columns == column[per_owner : 2 * per_owner], 1.0, 0.0
        ).astype(BF16)
    got = dot(lent_hot[...], edges[...]).astype(BF16)
    for s in range(ranks):
        outs[s][...] = got[s * per_owner : (s + 1) * per_owner]


def owner_kernel(kept_hot, upstream, w_out, same, dhidden):
    hot = kept_hot[...]
    same[...] = dot(hot, hot, NT).astype(BF16)
    picked = dot(hot, upstream[...]).astype(BF16)
    dhidden[...] = dot(picked, w_out[...], NT)


def gathered(pieces):
    return jnp.concatenate([p[...] for p in pieces], axis=0)


def forward_kernel(ranks, step, *refs):
    pieces, (filt, s_hot, d_hot) = refs[:ranks], refs[ranks : ranks + 3]
    outs, total = refs[ranks + 3 : 2 * ranks + 3], refs[2 * ranks + 3]
    table = gathered(pieces).T
    total[...] = jnp.zeros_like(total)

    def turn(i, carry):
        at = pl.ds(pl.multiple_of(i * step, step), step)
        rows = dot(table, s_hot[:, at]).astype(BF16)
        total[...] += dot(rows * filt[:, at], d_hot[:, at], NT)
        return carry

    lax.fori_loop(0, filt.shape[1] // step, turn, 0)
    result = total[...].astype(BF16).T
    per = result.shape[0] // ranks
    for s in range(ranks):
        outs[s][...] = result[s * per : (s + 1) * per]


def slope_kernel(ranks, step, *refs):
    pieces, (slope, s_hot, out) = refs[:ranks], refs[ranks:]
    table = gathered(pieces).T

    def turn(i, carry):
        at = pl.ds(pl.multiple_of(i * step, step), step)
        out[:, at] = dot(table, s_hot[:, at]).astype(BF16) * slope[:, at]
        return carry

    lax.fori_loop(0, slope.shape[1] // step, turn, 0)


def return_kernel(ranks, *refs):
    pieces, (same, dhidden) = refs[:ranks], refs[ranks : ranks + 2]
    outs = refs[ranks + 2 :]
    agg = dot(same[...], gathered(pieces))
    back = (dhidden[...] * silu_parts(agg)[1]).astype(BF16)
    per = back.shape[0] // ranks
    for s in range(ranks):
        outs[s][...] = back[s * per : (s + 1) * per]


def update_kernel(ranks, step, *refs):
    pieces = refs[:ranks]
    kept_hot, edges, upstream, w_out, updated, term, hot_t = refs[ranks:]
    home = gathered(pieces)
    hot_t[...] = kept_hot[...].T
    term[...] = jnp.zeros_like(term)
    for i in range(edges.shape[0] // step):
        at = pl.ds(i * step, step)
        agg = dot(hot_t[at, :], home)
        hidden = silu_parts(agg)[0].astype(BF16)
        fresh = edges[at, :].astype(F32) + dot(hidden, w_out[...])
        updated[at, :] = fresh.astype(BF16)
        term[...] += dot(hidden.T, upstream[at, :])


def backward_kernel(ranks, step, *refs):
    pieces, (filt, slope, s_hot, d_hot, basis) = refs[:ranks], refs[ranks : ranks + 5]
    outs = refs[ranks + 5 : 2 * ranks + 5]
    weight, total, dweight = refs[2 * ranks + 5 :]
    table = gathered(pieces).T
    total[...] = jnp.zeros_like(total)
    dweight[...] = jnp.zeros_like(dweight)

    def turn(i, carry):
        at = pl.ds(pl.multiple_of(i * step, step), step)
        rows = dot(table, d_hot[:, at]).astype(BF16)
        dweight[...] += dot(rows * slope[:, at], basis[at, :])
        total[...] += dot(rows * filt[:, at], s_hot[:, at], NT)
        return carry

    lax.fori_loop(0, filt.shape[1] // step, turn, 0)
    weight[...] = dweight[...].T
    result = total[...].astype(BF16).T
    per = result.shape[0] // ranks
    for s in range(ranks):
        outs[s][...] = result[s * per : (s + 1) * per]


def final_kernel(ranks, step, *refs):
    pieces, (lent_hot, upstream, out, hot_t) = refs[:ranks], refs[ranks:]
    back = gathered(pieces)
    hot_t[...] = lent_hot[...].T
    for i in range(upstream.shape[0] // step):
        at = pl.ds(i * step, step)
        out[at, :] = (upstream[at, :].astype(F32) + dot(hot_t[at, :], back)).astype(BF16)


def shift(value, axis, by):
    count = lax.axis_size(axis)
    return lax.ppermute(value, axis, [(k, (k + by) % count) for k in range(count)])


def spread(pieces, axis, sign):
    return [pieces[0]] + [shift(pieces[s], axis, sign * s) for s in range(1, len(pieces))]


def reduce_all(term):
    copies, ranks = lax.axis_size("dp"), lax.axis_size("graph")
    mine, me = lax.axis_index("dp"), lax.axis_index("graph")
    bits = copies.bit_length() - 1
    value = term
    for bit in range(bits):
        half = value.reshape(2, value.shape[0] // 2, value.shape[1])
        own = (mine >> bit) & 1
        away = lax.dynamic_index_in_dim(half, 1 - own, 0, keepdims=False).astype(BF16)
        got = lax.ppermute(away, "dp", [(k, k ^ (1 << bit)) for k in range(copies)])
        value = lax.dynamic_index_in_dim(half, own, 0, keepdims=False) + got.astype(F32)
    parts = value.reshape(ranks, value.shape[0] // ranks, value.shape[1])
    total = lax.dynamic_index_in_dim(parts, me, 0, keepdims=False)
    for s in range(1, ranks):
        away = lax.dynamic_index_in_dim(parts, (me + s) % ranks, 0, keepdims=False)
        total = total + shift(away.astype(BF16), "graph", s).astype(F32)
    piece = total.astype(BF16)
    ring = [piece] + [shift(piece, "graph", -s) for s in range(1, ranks)]
    twice = jnp.concatenate(ring + ring, axis=0)
    rows = piece.shape[0]
    value = lax.dynamic_slice_in_dim(twice, ((ranks - me) % ranks) * rows, ranks * rows, 0)
    for bit in reversed(range(bits)):
        got = lax.ppermute(value, "dp", [(k, k ^ (1 << bit)) for k in range(copies)])
        low = ((mine >> bit) & 1) == 0
        value = jnp.where(low, jnp.concatenate([value, got]), jnp.concatenate([got, value]))
    return value.astype(F32)


def per_device(
    edge_emb,
    cotangent,
    fetch_rows,
    store_rows,
    trip_src,
    trip_dst,
    trip_basis,
    block_count,
    w_basis,
    w_out,
):
    edges, upstream, basis = edge_emb[0], cotangent[0], trip_basis[0]
    ranks, copies = lax.axis_size("graph"), lax.axis_size("dp")
    me = lax.axis_index("graph").astype(jnp.int32).reshape(1)
    edge_dev, width = edges.shape
    per_owner = fetch_rows.shape[3]
    slots = ranks * per_owner
    blocks, block_rows = trip_src.shape[1:]
    triplets, basis_width = basis.shape
    piece = shape((per_owner, width))
    step = 512
    wide = 2 * triplets * slots * width

    both = jnp.concatenate([fetch_rows[0, 0], store_rows[0, 0]], axis=1)
    lists = [both] + [shift(both, "graph", s) for s in range(1, ranks)]

    filt, slope, s_hot, d_hot = call(
        functools.partial(prepare_kernel, per_owner, ranks, step),
        [shape((width, triplets))] * 2 + [shape((slots, triplets))] * 2,
        [me, block_count, trip_src[0], trip_dst[0], basis, w_basis],
        [SMEM, SMEM] + [VMEM] * 4,
        flops=6 * triplets * width * basis_width,
    )

    *lend, lent_hot, kept_hot = call(
        functools.partial(lend_kernel, per_owner, ranks),
        [piece] * ranks + [shape((slots, edge_dev))] * 2,
        [me] + lists + [edges],
        [SMEM] + [VMEM] * (ranks + 1),
        flops=2 * slots * edge_dev * width,
    )
    rows = spread(lend, "graph", -1)

    same, dhidden = call(
        owner_kernel,
        [shape((slots, slots)), shape((slots, width), F32)],
        [kept_hot, upstream, w_out],
        flops=4 * slots * edge_dev * width,
    )

    partial_rows = call(
        functools.partial(forward_kernel, ranks, step),
        [piece] * ranks,
        list(rows) + [filt, s_hot, d_hot],
        flops=2 * wide,
        scratch=[pltpu.VMEM((width, slots), F32)],
    )
    home = spread(partial_rows, "graph", 1)

    (weighted,) = call(
        functools.partial(slope_kernel, ranks, step),
        [shape((width, triplets))],
        list(rows) + [slope, s_hot],
        flops=wide,
    )

    back = call(
        functools.partial(return_kernel, ranks),
        [piece] * ranks,
        list(home) + [same, dhidden],
        flops=2 * slots * slots * width,
    )
    dpartial = spread(back, "graph", -1)

    updated, out_term = call(
        functools.partial(update_kernel, ranks, 256),
        [shape((edge_dev, width)), shape((width, width), F32)],
        list(home) + [kept_hot, edges, upstream, w_out],
        flops=2 * edge_dev * width * (2 * width + slots),
        scratch=[pltpu.VMEM((edge_dev, slots), BF16)],
    )
    out_scale = jnp.sqrt(F32(copies * ranks * edge_dev))
    grad_w_out = reduce_all(out_term) / out_scale

    *dfetch, basis_term = call(
        functools.partial(backward_kernel, ranks, step),
        [piece] * ranks + [shape((basis_width, width), F32)],
        list(dpartial) + [filt, weighted, s_hot, d_hot, basis],
        flops=2 * wide,
        scratch=[pltpu.VMEM((width, slots), F32), pltpu.VMEM((width, basis_width), F32)],
    )
    basis_scale = jnp.sqrt(F32(copies * ranks * blocks * block_rows))
    grad_w_basis = reduce_all(basis_term) / basis_scale
    returned = spread(dfetch, "graph", 1)

    (grad_edge,) = call(
        functools.partial(final_kernel, ranks, 256),
        [shape((edge_dev, width))],
        list(returned) + [lent_hot, upstream],
        flops=2 * slots * edge_dev * width,
        scratch=[pltpu.VMEM((edge_dev, slots), BF16)],
    )
    return (updated[None], grad_edge[None], grad_w_out, grad_w_basis)


def solution(mesh):
    placed = (
        P(("groups", "dp"), "graph", None),
        P(("groups", "dp"), "graph", None),
        P(("groups", "dp"), "graph", None, None),
        P(("groups", "dp"), "graph", None, None),
        P(("groups", "dp"), "graph", None),
        P(("groups", "dp"), "graph", None),
        P(("groups", "dp"), "graph", None),
        P(("groups", "dp"), "graph"),
        P(),
        P(),
    )
    return jax.shard_map(
        per_device,
        mesh=mesh,
        in_specs=placed,
        out_specs=(
            P(("groups", "dp"), "graph", None),
            P(("groups", "dp"), "graph", None),
            P("groups", None),
            P("groups", None),
        ),
        check_vma=False,
    )
```

time: 239 us -> 132 us (0.55)
  waiting for transfers between devices: 117 us -> 24.1 us
  matrix products: 64.5 us -> 0 us
  Pallas kernels: 0 us -> 41.1 us
  starting transfers between devices: 18.7 us -> 46.6 us
  between operations: 14.2 us -> 1.65 us
  blocking collectives: 11.9 us -> 0 us
  local copies, waits for them, and re-layouts: 3.84 us -> 15.2 us
  other arithmetic: 7.75 us -> 2.86 us
    psum x1 -> x0, waiting for transfers between devices: 91.1 us -> none  [per_device(): grad_w_out = lax.psum(out_term, ('graph', 'dp')) / out_scale]
    dot_general x26 -> x0, matrix products: 64.5 us -> none  [the longest x6 15.1 us: spread_rows(): lax.dot_general(table, lower, dims, preferred_element_type=jnp.float32)]
    ppermute x0 -> x35, starting transfers between devices: none -> 46.6 us  [the longest x27 41.9 us: shift(): lax.ppermute(value, axis, [(k, (k + by) % count) for k in range(count)])]
    pallas_call x0 -> x9, Pallas kernels: none -> 41.1 us  [call(): pl.pallas_call(body, out_shape=tuple(outs), in_specs=[VMEM] * len(args) i...]
    all_to_all x5 -> x0, waiting for transfers between devices: 25.1 us -> none  [the longest x1 11.3 us: per_device(): lax.all_to_all(partial_value.reshape(ranks, per_owner, width), 'graph', s...]
    ppermute x0 -> x35, waiting for transfers between devices: none -> 24.1 us  [the longest x27 16.2 us: shift(): lax.ppermute(value, axis, [(k, (k + by) % count) for k in range(count)])]
    all_to_all x5 -> x0, starting transfers between devices: 18.7 us -> none  [the longest x1 5.04 us: per_device(): lax.all_to_all(partial_value.reshape(ranks, per_owner, width), 'graph', s...]
    unnamed x22 -> x62, local copies, waits for them, and re-layouts: 0.06 us -> 14.3 us
  transfers between devices with their start and end apart: 6 -> 35, of which waited for: 5 -> 16; matrix products, arithmetic and copies ran while one was open for 9% -> 1% of each run, Pallas kernels for 0% -> 17%
where the time goes in v1:
time: 132 us
  starting transfers between devices  46.6 us (35%)
  Pallas kernels  41.1 us (31%)
  waiting for transfers between devices  24.1 us (18%)
  local copies, waits for them, and re-layouts  15.2 us (12%)
  other arithmetic  2.86 us (2%)
  between operations  1.65 us (1%)
    ppermute x27, starting transfers between devices, shift(): lax.ppermute(value, axis, [(k, (k + by) % count) for k in range(count)])  41.9 us
    pallas_call x9, Pallas kernels, call(): pl.pallas_call(body, out_shape=tuple(outs), in_specs=[VMEM] * len(args) i...  41.1 us
    ppermute x27, waiting for transfers between devices, shift(): lax.ppermute(value, axis, [(k, (k + by) % count) for k in range(count)])  16.2 us
    unnamed x62, local copies, waits for them, and re-layouts  14.3 us
    ppermute x4, waiting for transfers between devices, reduce_all(): got = lax.ppermute(away, 'dp', [(k, k ^ 1 << bit) for k in range(copies)])  4.79 us
    ppermute x4, waiting for transfers between devices, reduce_all(): got = lax.ppermute(value, 'dp', [(k, k ^ 1 << bit) for k in range(copies)])  3.15 us
  transfers between devices with their start and end apart: 35, of which 16 were waited for; matrix products, arithmetic and copies ran while one was open for 1% of the time, Pallas kernels for 17%

profile of v1, /device:TPU:0, one launch (start us, length us, event | category | flops | bytes accessed | tf_op | source)
XLA Modules:
  0.0 131.5 jit_solution(7043059218941569040)
XLA Ops:
  1.4 3.0 %collective-permute-start = (s32[4,128]{1,0:T(4,128)S(1)}, s32[4,128]{1,0:T(4,128)S(1)}, u32[]{:S(2)}, u32[]{:S(2)}) collective-permute-start(s32[4,128]{1,0:T(4,128)S(1)} %pad_add_fusion.refs_0_), channel_id=1, source_target_pairs={{0,4},{4,8},{8,12},{12,0},{1,5},{5,9},{9,13},{13,1},{2,6},{6,10},{... | collective-permute-start | bytes 6152 | tf_op jit(solution)/shard_map/ppermute | solution.py:194
  4.4 2.6 %collective-permute-start.1 = (s32[4,128]{1,0:T(4,128)S(1)}, s32[4,128]{1,0:T(4,128)S(1)}, u32[]{:S(2)}, u32[]{:S(2)}) collective-permute-start(s32[4,128]{1,0:T(4,128)S(1)} %pad_add_fusion.refs_0_), channel_id=1, source_target_pairs={{0,8},{4,12},{8,0},{12,4},{1,9},{5,13},{9,1},{13,5},{2,10},{6,14},... | collective-permute-start | bytes 6152 | tf_op jit(solution)/shard_map/ppermute | solution.py:194
  7.0 1.3 %collective-permute-start.2 = (s32[4,128]{1,0:T(4,128)S(1)}, s32[4,128]{1,0:T(4,128)S(1)}, u32[]{:S(2)}, u32[]{:S(2)}) collective-permute-start(s32[4,128]{1,0:T(4,128)S(1)} %pad_add_fusion.refs_0_), channel_id=1, source_target_pairs={{0,12},{4,0},{8,4},{12,8},{1,13},{5,1},{9,5},{13,9},{2,14},{6,2},{... | collective-permute-start | bytes 6152 | tf_op jit(solution)/shard_map/ppermute | solution.py:194
  9.0 1.6 %collective-permute-done.2.refs_3_ = s32[4,128]{1,0:T(4,128)S(1)} collective-permute-done((s32[4,128]{1,0:T(4,128)S(1)}, s32[4,128]{1,0:T(4,128)S(1)}, u32[]{:S(2)}, u32[]{:S(2)}) %collective-permute-start.2) | collective-permute-done | bytes 2080 | tf_op jit(solution)/shard_map/ppermute | solution.py:194
  14.2 3.1 %collective-permute-start.3 = (bf16[64,512]{1,0:T(8,128)(2,1)S(1)}, bf16[64,512]{1,0:T(8,128)(2,1)S(1)}, u32[]{:S(2)}, u32[]{:S(2)}) collective-permute-start(bf16[64,512]{1,0:T(8,128)(2,1)S(1)} %get-tuple-element.32), channel_id=1, source_target_pairs={{0,12},{4,0},{8,4},{12,8},{1,13},{5,1},{9,5},{13,9},{2,14},{6,2},{... | collective-permute-start | bytes 196616 | tf_op jit(solution)/shard_map/ppermute | solution.py:194
  21.5 9.3 %shard_map.130 = (bf16[512,4096]{1,0:T(8,128)(2,1)}, bf16[512,4096]{1,0:T(8,128)(2,1)}, bf16[256,4096]{1,0:T(8,128)(2,1)S(1)}, bf16[256,4096]{1,0:T(8,128)(2,1)S(1)}) custom-call(s32[1]{0:T(128)} %bitcast.me, s32[1,1]{1,0:T(1,128)S(6)} %copy.28.count, s32[32,128]{1,0:T(8,128)S(1)} %bitcast.76, s32[32,128]{1,0:T(8,128)S(1)} %bitcast.77, ...), custom_call_target="tpu_custom_call" | custom-call | flops 1610612736 | bytes 13795336 | tf_op jit(solution)/shard_map/pallas_call | solution.py:32
  30.8 7.4 %shard_map.131 = (bf16[64,512]{1,0:T(8,128)(2,1)S(1)}, bf16[64,512]{1,0:T(8,128)(2,1)}, bf16[64,512]{1,0:T(8,128)(2,1)}, bf16[64,512]{1,0:T(8,128)(2,1)}) custom-call(bf16[64,512]{1,0:T(8,128)(2,1)S(1)} %get-tuple-element.31.refs_0_, bf16[64,512]{1,0:T(8,128)(2,1)S(1)} %collective-permute-done.3.refs_1_, bf16[64,512]{1,0:T(8,128)(2,1)S(1)} %collective-permute-done.4.refs_2_, ...), custom_call_target="tpu_custom_call" | custom-call | flops 2147483648 | bytes 8912896 | tf_op jit(solution)/shard_map/pallas_call | solution.py:32
  38.2 2.9 %collective-permute-start.6 = (bf16[64,512]{1,0:T(8,128)(2,1)}, bf16[64,512]{1,0:T(8,128)(2,1)S(1)}, u32[]{:S(2)}, u32[]{:S(2)}) collective-permute-start(bf16[64,512]{1,0:T(8,128)(2,1)} %get-tuple-element.39), channel_id=1, source_target_pairs={{0,4},{4,8},{8,12},{12,0},{1,5},{5,9},{9,13},{13,1},{2,6},{6,10},{... | collective-permute-start | bytes 196616 | tf_op jit(solution)/shard_map/ppermute | solution.py:194
  42.0 1.5 %collective-permute-start.8 = (bf16[64,512]{1,0:T(8,128)(2,1)}, bf16[64,512]{1,0:T(8,128)(2,1)}, u32[]{:S(2)}, u32[]{:S(2)}) collective-permute-start(bf16[64,512]{1,0:T(8,128)(2,1)} %get-tuple-element.41), channel_id=1, source_target_pairs={{0,12},{4,0},{8,4},{12,8},{1,13},{5,1},{9,5},{13,9},{2,14},{6,2},{... | collective-permute-start | bytes 196616 | tf_op jit(solution)/shard_map/ppermute | solution.py:194
  48.6 1.4 %collective-permute-start.10 = (bf16[64,512]{1,0:T(8,128)(2,1)S(1)}, bf16[64,512]{1,0:T(8,128)(2,1)S(1)}, u32[]{:S(2)}, u32[]{:S(2)}) collective-permute-start(bf16[64,512]{1,0:T(8,128)(2,1)S(1)} %get-tuple-element.48), channel_id=1, source_target_pairs={{0,8},{4,12},{8,0},{12,4},{1,9},{5,13},{9,1},{13,5},{2,10},{6,14},... | collective-permute-start | bytes 196616 | tf_op jit(solution)/shard_map/ppermute | solution.py:194
  49.9 1.9 %collective-permute-start.11 = (bf16[64,512]{1,0:T(8,128)(2,1)S(1)}, bf16[64,512]{1,0:T(8,128)(2,1)S(1)}, u32[]{:S(2)}, u32[]{:S(2)}) collective-permute-start(bf16[64,512]{1,0:T(8,128)(2,1)S(1)} %get-tuple-element.49), channel_id=1, source_target_pairs={{0,4},{4,8},{8,12},{12,0},{1,5},{5,9},{9,13},{13,1},{2,6},{6,10},{... | collective-permute-start | bytes 196616 | tf_op jit(solution)/shard_map/ppermute | solution.py:194
  51.8 2.0 %collective-permute-start.9 = (bf16[64,512]{1,0:T(8,128)(2,1)S(1)}, bf16[64,512]{1,0:T(8,128)(2,1)S(1)}, u32[]{:S(2)}, u32[]{:S(2)}) collective-permute-start(bf16[64,512]{1,0:T(8,128)(2,1)S(1)} %get-tuple-element.47), channel_id=1, source_target_pairs={{0,12},{4,0},{8,4},{12,8},{1,13},{5,1},{9,5},{13,9},{2,14},{6,2},{... | collective-permute-start | bytes 196616 | tf_op jit(solution)/shard_map/ppermute | solution.py:194
  53.8 6.9 %shard_map.135.refs_5_ = bf16[512,4096]{1,0:T(8,128)(2,1)} custom-call(bf16[64,512]{1,0:T(8,128)(2,1)S(1)} %get-tuple-element.31.refs_0_, bf16[64,512]{1,0:T(8,128)(2,1)S(1)} %collective-permute-done.3.refs_1_, bf16[64,512]{1,0:T(8,128)(2,1)S(1)} %collective-permute-done.4.refs_2_, bf16[64,512]{1,0:T(8,128)(2,1)S(1)} %collective-permute-done.5.refs_3_, ...), custom_call_target="tpu_custom_call" | custom-call | flops 1073741824 | bytes 10747904 | tf_op jit(solution)/shard_map/pallas_call | solution.py:32
  60.7 9.3 %shard_map.136 = (bf16[64,512]{1,0:T(8,128)(2,1)S(1)}, bf16[64,512]{1,0:T(8,128)(2,1)S(1)}, bf16[64,512]{1,0:T(8,128)(2,1)S(1)}, bf16[64,512]{1,0:T(8,128)(2,1)S(1)}, f32[128,512]{1,0:T(8,128)S(1)}) custom-call(bf16[64,512]{1,0:T(8,128)(2,1)S(1)} %get-tuple-element.46.refs_0_, bf16[64,512]{1,0:T(8,128)(2,1)S(1)} %collective-permute-done.9.refs_1_, ...), custom_call_target="tpu_custom_call" | custom-call | flops 2147483648 | bytes 14417920 | tf_op jit(solution)/shard_map/pallas_call | solution.py:32
  73.9 1.6 %collective-permute-start.26 = (bf16[32,512]{1,0:T(8,128)(2,1)S(1)}, bf16[32,512]{1,0:T(8,128)(2,1)S(1)}, u32[]{:S(2)}, u32[]{:S(2)}) collective-permute-start(bf16[32,512]{1,0:T(8,128)(2,1)S(1)} %fusion.10), channel_id=1, source_target_pairs={{0,2},{1,3},{2,0},{3,1},{4,6},{5,7},{6,4},{7,5},{8,10},{9,11},{10,... | collective-permute-start | bytes 98312 | tf_op jit(solution)/shard_map/ppermute | solution.py:210
  78.8 3.8 %shard_map.132 = (bf16[1024,512]{1,0:T(8,128)(2,1)}, f32[512,512]{1,0:T(8,128)S(1)}) custom-call(bf16[64,512]{1,0:T(8,128)(2,1)S(1)} %get-tuple-element.38.refs_0_, bf16[64,512]{1,0:T(8,128)(2,1)S(1)} %collective-permute-done.6.refs_1_, bf16[64,512]{1,0:T(8,128)(2,1)} %collective-permute-done.7.refs_2_, bf16[64,512]{1,0:T(8,128)(2,1)} %collective-permute-done.8.refs_3_, ...), custom_call_target="tpu_custom_call" | custom-call | flops 1342177280 | bytes 5505024 | tf_op jit(solution)/shard_map/pallas_call | solution.py:32
  83.2 3.3 %collective-permute-start.29 = (bf16[8,512]{1,0:T(8,128)(2,1)S(1)}, bf16[8,512]{1,0:T(8,128)(2,1)S(1)}, u32[]{:S(2)}, u32[]{:S(2)}) collective-permute-start(bf16[8,512]{1,0:T(8,128)(2,1)S(1)} %get-tuple-element.66), channel_id=1, source_target_pairs={{0,12},{4,0},{8,4},{12,8},{1,13},{5,1},{9,5},{13,9},{2,14},{6,2},{... | collective-permute-start | bytes 24584 | tf_op jit(solution)/shard_map/ppermute | solution.py:194
  88.7 3.3 %collective-permute-start.30 = (bf16[8,512]{1,0:T(8,128)(2,1)S(1)}, bf16[8,512]{1,0:T(8,128)(2,1)S(1)}, u32[]{:S(2)}, u32[]{:S(2)}) collective-permute-start(bf16[8,512]{1,0:T(8,128)(2,1)S(1)} %get-tuple-element.59), channel_id=1, source_target_pairs={{0,12},{4,0},{8,4},{12,8},{1,13},{5,1},{9,5},{13,9},{2,14},{6,2},{... | collective-permute-start | bytes 24584 | tf_op jit(solution)/shard_map/ppermute | solution.py:194
  92.7 2.3 %collective-permute-start.31 = (bf16[8,512]{1,0:T(8,128)(2,1)S(1)}, bf16[8,512]{1,0:T(8,128)(2,1)S(1)}, u32[]{:S(2)}, u32[]{:S(2)}) collective-permute-start(bf16[8,512]{1,0:T(8,128)(2,1)S(1)} %get-tuple-element.59), channel_id=1, source_target_pairs={{0,8},{4,12},{8,0},{12,4},{1,9},{5,13},{9,1},{13,5},{2,10},{6,14},... | collective-permute-start | bytes 24584 | tf_op jit(solution)/shard_map/ppermute | solution.py:194
  95.0 1.4 %collective-permute-start.32 = (bf16[8,512]{1,0:T(8,128)(2,1)S(1)}, bf16[8,512]{1,0:T(8,128)(2,1)S(1)}, u32[]{:S(2)}, u32[]{:S(2)}) collective-permute-start(bf16[8,512]{1,0:T(8,128)(2,1)S(1)} %get-tuple-element.59), channel_id=1, source_target_pairs={{0,4},{4,8},{8,12},{12,0},{1,5},{5,9},{9,13},{13,1},{2,6},{6,10},{... | collective-permute-start | bytes 24584 | tf_op jit(solution)/shard_map/ppermute | solution.py:194
  96.4 2.5 %collective-permute-done.31 = bf16[8,512]{1,0:T(8,128)(2,1)S(1)} collective-permute-done((bf16[8,512]{1,0:T(8,128)(2,1)S(1)}, bf16[8,512]{1,0:T(8,128)(2,1)S(1)}, u32[]{:S(2)}, u32[]{:S(2)}) %collective-permute-start.31) | collective-permute-done | bytes 8224 | tf_op jit(solution)/shard_map/ppermute | solution.py:194
  100.5 3.6 %collective-permute-done.16 = bf16[128,512]{1,0:T(8,128)(2,1)S(1)} collective-permute-done((bf16[128,512]{1,0:T(8,128)(2,1)S(1)}, bf16[128,512]{1,0:T(8,128)(2,1)S(1)}, u32[]{:S(2)}, u32[]{:S(2)}) %collective-permute-start.16) | collective-permute-done | bytes 131104 | tf_op jit(solution)/shard_map/ppermute | solution.py:210
  104.1 2.1 %collective-permute-start.17 = (bf16[32,512]{1,0:T(8,128)(2,1)S(1)}, bf16[32,512]{1,0:T(8,128)(2,1)S(1)}, u32[]{:S(2)}, u32[]{:S(2)}) collective-permute-start(bf16[32,512]{1,0:T(8,128)(2,1)S(1)} %get-tuple-element.62), channel_id=1, source_target_pairs={{0,4},{4,8},{8,12},{12,0},{1,5},{5,9},{9,13},{13,1},{2,6},{6,10},{... | collective-permute-start | bytes 98312 | tf_op jit(solution)/shard_map/ppermute | solution.py:194
  107.0 1.6 %collective-permute-start.19 = (bf16[32,512]{1,0:T(8,128)(2,1)S(1)}, bf16[32,512]{1,0:T(8,128)(2,1)S(1)}, u32[]{:S(2)}, u32[]{:S(2)}) collective-permute-start(bf16[32,512]{1,0:T(8,128)(2,1)S(1)} %get-tuple-element.63), channel_id=1, source_target_pairs={{0,12},{4,0},{8,4},{12,8},{1,13},{5,1},{9,5},{13,9},{2,14},{6,2},{... | collective-permute-start | bytes 98312 | tf_op jit(solution)/shard_map/ppermute | solution.py:194
  108.7 1.3 %collective-permute-done.17 = bf16[32,512]{1,0:T(8,128)(2,1)S(1)} collective-permute-done((bf16[32,512]{1,0:T(8,128)(2,1)S(1)}, bf16[32,512]{1,0:T(8,128)(2,1)S(1)}, u32[]{:S(2)}, u32[]{:S(2)}) %collective-permute-start.17) | collective-permute-done | bytes 32800 | tf_op jit(solution)/shard_map/ppermute | solution.py:194
  111.3 3.4 %collective-permute-start.20 = (bf16[32,512]{1,0:T(8,128)(2,1)S(1)}, bf16[32,512]{1,0:T(8,128)(2,1)S(1)}, u32[]{:S(2)}, u32[]{:S(2)}) collective-permute-start(bf16[32,512]{1,0:T(8,128)(2,1)S(1)} %get-tuple-element.61), channel_id=1, source_target_pairs={{0,12},{4,0},{8,4},{12,8},{1,13},{5,1},{9,5},{13,9},{2,14},{6,2},{... | collective-permute-start | bytes 98312 | tf_op jit(solution)/shard_map/ppermute | solution.py:194
  114.7 1.6 %collective-permute-done.20 = bf16[32,512]{1,0:T(8,128)(2,1)S(1)} collective-permute-done((bf16[32,512]{1,0:T(8,128)(2,1)S(1)}, bf16[32,512]{1,0:T(8,128)(2,1)S(1)}, u32[]{:S(2)}, u32[]{:S(2)}) %collective-permute-start.20) | collective-permute-done | bytes 32800 | tf_op jit(solution)/shard_map/ppermute | solution.py:194
  116.8 2.8 %collective-permute-done.21 = bf16[32,512]{1,0:T(8,128)(2,1)S(1)} collective-permute-done((bf16[32,512]{1,0:T(8,128)(2,1)S(1)}, bf16[32,512]{1,0:T(8,128)(2,1)S(1)}, u32[]{:S(2)}, u32[]{:S(2)}) %collective-permute-start.21) | collective-permute-done | bytes 32800 | tf_op jit(solution)/shard_map/ppermute | solution.py:194
  119.5 2.8 %collective-permute-done.22 = bf16[32,512]{1,0:T(8,128)(2,1)S(1)} collective-permute-done((bf16[32,512]{1,0:T(8,128)(2,1)S(1)}, bf16[32,512]{1,0:T(8,128)(2,1)S(1)}, u32[]{:S(2)}, u32[]{:S(2)}) %collective-permute-start.22) | collective-permute-done | bytes 32800 | tf_op jit(solution)/shard_map/ppermute | solution.py:194
  123.0 1.5 %collective-permute-start.33 = (bf16[32,512]{1,0:T(8,128)(2,1)S(1)}, bf16[32,512]{1,0:T(8,128)(2,1)S(1)}, u32[]{:S(2)}, u32[]{:S(2)}) collective-permute-start(bf16[32,512]{1,0:T(8,128)(2,1)S(1)} %constant_dynamic-slice_fusion), channel_id=1, source_target_pairs={{0,2},{1,3},{2,0},{3,1},{4,6},{5,7},{6,4},{7,5},{8,10},{9,11},{10,... | collective-permute-start | bytes 98312 | tf_op jit(solution)/shard_map/ppermute | solution.py:223
  124.5 2.9 %collective-permute-done.23 = bf16[128,512]{1,0:T(8,128)(2,1)S(1)} collective-permute-done((bf16[128,512]{1,0:T(8,128)(2,1)S(1)}, bf16[128,512]{1,0:T(8,128)(2,1)S(1)}, u32[]{:S(2)}, u32[]{:S(2)}) %collective-permute-start.23) | collective-permute-done | bytes 131104 | tf_op jit(solution)/shard_map/ppermute | solution.py:223
  128.2 1.4 %shard_map.137 = bf16[1024,512]{1,0:T(8,128)(2,1)} custom-call(bf16[64,512]{1,0:T(8,128)(2,1)S(1)} %copy-done.15, bf16[64,512]{1,0:T(8,128)(2,1)S(1)} %collective-permute-done.12.refs_1_, bf16[64,512]{1,0:T(8,128)(2,1)S(1)} %collective-permute-done.13.refs_2_, bf16[64,512]{1,0:T(8,128)(2,1)S(1)} %collective-permute-done.14.refs_3_, ...), custom_call_target="tpu_custom_call" | custom-call | flops 268435456 | bytes 2883584 | tf_op jit(solution)/shard_map/pallas_call | solution.py:32
  (130 shorter events, 32.4 us)
Async XLA Ops:
  1.4 7.6 %collective-permute-start = (s32[4,128]{1,0:T(4,128)S(1)}, s32[4,128]{1,0:T(4,128)S(1)}, u32[]{:S(2)}, u32[]{:S(2)}) collective-permute-start(s32[4,128]{1,0:T(4,128)S(1)} %pad_add_fusion.refs_0_), channel_id=1, source_target_pairs={{0,4},{4,8},{8,12},{12,0},{1,5},{5,9},{9,13},{13,1},{2,6},{6,10},{... | collective-permute-start | bytes 6152 | tf_op jit(solution)/shard_map/ppermute | solution.py:194
  4.4 4.6 %collective-permute-start.1 = (s32[4,128]{1,0:T(4,128)S(1)}, s32[4,128]{1,0:T(4,128)S(1)}, u32[]{:S(2)}, u32[]{:S(2)}) collective-permute-start(s32[4,128]{1,0:T(4,128)S(1)} %pad_add_fusion.refs_0_), channel_id=1, source_target_pairs={{0,8},{4,12},{8,0},{12,4},{1,9},{5,13},{9,1},{13,5},{2,10},{6,14},... | collective-permute-start | bytes 6152 | tf_op jit(solution)/shard_map/ppermute | solution.py:194
  7.0 3.6 %collective-permute-start.2 = (s32[4,128]{1,0:T(4,128)S(1)}, s32[4,128]{1,0:T(4,128)S(1)}, u32[]{:S(2)}, u32[]{:S(2)}) collective-permute-start(s32[4,128]{1,0:T(4,128)S(1)} %pad_add_fusion.refs_0_), channel_id=1, source_target_pairs={{0,12},{4,0},{8,4},{12,8},{1,13},{5,1},{9,5},{13,9},{2,14},{6,2},{... | collective-permute-start | bytes 6152 | tf_op jit(solution)/shard_map/ppermute | solution.py:194
  14.2 16.6 %collective-permute-start.3 = (bf16[64,512]{1,0:T(8,128)(2,1)S(1)}, bf16[64,512]{1,0:T(8,128)(2,1)S(1)}, u32[]{:S(2)}, u32[]{:S(2)}) collective-permute-start(bf16[64,512]{1,0:T(8,128)(2,1)S(1)} %get-tuple-element.32), channel_id=1, source_target_pairs={{0,12},{4,0},{8,4},{12,8},{1,13},{5,1},{9,5},{13,9},{2,14},{6,2},{... | collective-permute-start | bytes 196616 | tf_op jit(solution)/shard_map/ppermute | solution.py:194
  17.3 13.4 %collective-permute-start.4 = (bf16[64,512]{1,0:T(8,128)(2,1)S(1)}, bf16[64,512]{1,0:T(8,128)(2,1)S(1)}, u32[]{:S(2)}, u32[]{:S(2)}) collective-permute-start(bf16[64,512]{1,0:T(8,128)(2,1)S(1)} %get-tuple-element.33), channel_id=1, source_target_pairs={{0,8},{4,12},{8,0},{12,4},{1,9},{5,13},{9,1},{13,5},{2,10},{6,14},... | collective-permute-start | bytes 196616 | tf_op jit(solution)/shard_map/ppermute | solution.py:194
  17.3 13.4 %collective-permute-start.5 = (bf16[64,512]{1,0:T(8,128)(2,1)S(1)}, bf16[64,512]{1,0:T(8,128)(2,1)S(1)}, u32[]{:S(2)}, u32[]{:S(2)}) collective-permute-start(bf16[64,512]{1,0:T(8,128)(2,1)S(1)} %get-tuple-element.34), channel_id=1, source_target_pairs={{0,4},{4,8},{8,12},{12,0},{1,5},{5,9},{9,13},{13,1},{2,6},{6,10},{... | collective-permute-start | bytes 196616 | tf_op jit(solution)/shard_map/ppermute | solution.py:194
  38.2 8.4 %collective-permute-start.6 = (bf16[64,512]{1,0:T(8,128)(2,1)}, bf16[64,512]{1,0:T(8,128)(2,1)S(1)}, u32[]{:S(2)}, u32[]{:S(2)}) collective-permute-start(bf16[64,512]{1,0:T(8,128)(2,1)} %get-tuple-element.39), channel_id=1, source_target_pairs={{0,4},{4,8},{8,12},{12,0},{1,5},{5,9},{9,13},{13,1},{2,6},{6,10},{... | collective-permute-start | bytes 196616 | tf_op jit(solution)/shard_map/ppermute | solution.py:194
  41.1 5.8 %collective-permute-start.7 = (bf16[64,512]{1,0:T(8,128)(2,1)}, bf16[64,512]{1,0:T(8,128)(2,1)}, u32[]{:S(2)}, u32[]{:S(2)}) collective-permute-start(bf16[64,512]{1,0:T(8,128)(2,1)} %get-tuple-element.40), channel_id=1, source_target_pairs={{0,8},{4,12},{8,0},{12,4},{1,9},{5,13},{9,1},{13,5},{2,10},{6,14},... | collective-permute-start | bytes 196616 | tf_op jit(solution)/shard_map/ppermute | solution.py:194
  42.0 5.3 %collective-permute-start.8 = (bf16[64,512]{1,0:T(8,128)(2,1)}, bf16[64,512]{1,0:T(8,128)(2,1)}, u32[]{:S(2)}, u32[]{:S(2)}) collective-permute-start(bf16[64,512]{1,0:T(8,128)(2,1)} %get-tuple-element.41), channel_id=1, source_target_pairs={{0,12},{4,0},{8,4},{12,8},{1,13},{5,1},{9,5},{13,9},{2,14},{6,2},{... | collective-permute-start | bytes 196616 | tf_op jit(solution)/shard_map/ppermute | solution.py:194
  48.6 12.1 %collective-permute-start.10 = (bf16[64,512]{1,0:T(8,128)(2,1)S(1)}, bf16[64,512]{1,0:T(8,128)(2,1)S(1)}, u32[]{:S(2)}, u32[]{:S(2)}) collective-permute-start(bf16[64,512]{1,0:T(8,128)(2,1)S(1)} %get-tuple-element.48), channel_id=1, source_target_pairs={{0,8},{4,12},{8,0},{12,4},{1,9},{5,13},{9,1},{13,5},{2,10},{6,14},... | collective-permute-start | bytes 196616 | tf_op jit(solution)/shard_map/ppermute | solution.py:194
  49.9 10.8 %collective-permute-start.11 = (bf16[64,512]{1,0:T(8,128)(2,1)S(1)}, bf16[64,512]{1,0:T(8,128)(2,1)S(1)}, u32[]{:S(2)}, u32[]{:S(2)}) collective-permute-start(bf16[64,512]{1,0:T(8,128)(2,1)S(1)} %get-tuple-element.49), channel_id=1, source_target_pairs={{0,4},{4,8},{8,12},{12,0},{1,5},{5,9},{9,13},{13,1},{2,6},{6,10},{... | collective-permute-start | bytes 196616 | tf_op jit(solution)/shard_map/ppermute | solution.py:194
  51.8 8.9 %collective-permute-start.9 = (bf16[64,512]{1,0:T(8,128)(2,1)S(1)}, bf16[64,512]{1,0:T(8,128)(2,1)S(1)}, u32[]{:S(2)}, u32[]{:S(2)}) collective-permute-start(bf16[64,512]{1,0:T(8,128)(2,1)S(1)} %get-tuple-element.47), channel_id=1, source_target_pairs={{0,12},{4,0},{8,4},{12,8},{1,13},{5,1},{9,5},{13,9},{2,14},{6,2},{... | collective-permute-start | bytes 196616 | tf_op jit(solution)/shard_map/ppermute | solution.py:194
  73.9 8.6 %collective-permute-start.26 = (bf16[32,512]{1,0:T(8,128)(2,1)S(1)}, bf16[32,512]{1,0:T(8,128)(2,1)S(1)}, u32[]{:S(2)}, u32[]{:S(2)}) collective-permute-start(bf16[32,512]{1,0:T(8,128)(2,1)S(1)} %fusion.10), channel_id=1, source_target_pairs={{0,2},{1,3},{2,0},{3,1},{4,6},{5,7},{6,4},{7,5},{8,10},{9,11},{10,... | collective-permute-start | bytes 98312 | tf_op jit(solution)/shard_map/ppermute | solution.py:210
  82.6 5.5 %collective-permute-start.27 = (bf16[8,512]{1,0:T(8,128)(2,1)S(1)}, bf16[8,512]{1,0:T(8,128)(2,1)S(1)}, u32[]{:S(2)}, u32[]{:S(2)}) collective-permute-start(bf16[8,512]{1,0:T(8,128)(2,1)S(1)} %get-tuple-element.65), channel_id=1, source_target_pairs={{0,4},{4,8},{8,12},{12,0},{1,5},{5,9},{9,13},{13,1},{2,6},{6,10},{... | collective-permute-start | bytes 24584 | tf_op jit(solution)/shard_map/ppermute | solution.py:194
  82.7 5.4 %collective-permute-start.28 = (bf16[8,512]{1,0:T(8,128)(2,1)S(1)}, bf16[8,512]{1,0:T(8,128)(2,1)S(1)}, u32[]{:S(2)}, u32[]{:S(2)}) collective-permute-start(bf16[8,512]{1,0:T(8,128)(2,1)S(1)} %get-tuple-element.67), channel_id=1, source_target_pairs={{0,8},{4,12},{8,0},{12,4},{1,9},{5,13},{9,1},{13,5},{2,10},{6,14},... | collective-permute-start | bytes 24584 | tf_op jit(solution)/shard_map/ppermute | solution.py:194
  83.2 5.4 %collective-permute-start.29 = (bf16[8,512]{1,0:T(8,128)(2,1)S(1)}, bf16[8,512]{1,0:T(8,128)(2,1)S(1)}, u32[]{:S(2)}, u32[]{:S(2)}) collective-permute-start(bf16[8,512]{1,0:T(8,128)(2,1)S(1)} %get-tuple-element.66), channel_id=1, source_target_pairs={{0,12},{4,0},{8,4},{12,8},{1,13},{5,1},{9,5},{13,9},{2,14},{6,2},{... | collective-permute-start | bytes 24584 | tf_op jit(solution)/shard_map/ppermute | solution.py:194
  87.2 11.7 %collective-permute-start.15 = (bf16[256,512]{1,0:T(8,128)(2,1)}, bf16[256,512]{1,0:T(8,128)(2,1)S(1)}, u32[]{:S(2)}, u32[]{:S(2)}) collective-permute-start(bf16[256,512]{1,0:T(8,128)(2,1)} %fusion), channel_id=1, source_target_pairs={{0,1},{1,0},{2,3},{3,2},{4,5},{5,4},{6,7},{7,6},{8,9},{9,8},{10,11... | collective-permute-start | bytes 786440 | tf_op jit(solution)/shard_map/ppermute | solution.py:210
  88.7 6.3 %collective-permute-start.30 = (bf16[8,512]{1,0:T(8,128)(2,1)S(1)}, bf16[8,512]{1,0:T(8,128)(2,1)S(1)}, u32[]{:S(2)}, u32[]{:S(2)}) collective-permute-start(bf16[8,512]{1,0:T(8,128)(2,1)S(1)} %get-tuple-element.59), channel_id=1, source_target_pairs={{0,12},{4,0},{8,4},{12,8},{1,13},{5,1},{9,5},{13,9},{2,14},{6,2},{... | collective-permute-start | bytes 24584 | tf_op jit(solution)/shard_map/ppermute | solution.py:194
  92.0 36.2 %collective-permute-start.12 = (bf16[64,512]{1,0:T(8,128)(2,1)S(1)}, bf16[64,512]{1,0:T(8,128)(2,1)S(1)}, u32[]{:S(2)}, u32[]{:S(2)}) collective-permute-start(bf16[64,512]{1,0:T(8,128)(2,1)S(1)} %copy-done.22), channel_id=1, source_target_pairs={{0,4},{4,8},{8,12},{12,0},{1,5},{5,9},{9,13},{13,1},{2,6},{6,10},{... | collective-permute-start | bytes 196616 | tf_op jit(solution)/shard_map/ppermute | solution.py:194
  92.0 36.1 %collective-permute-start.13 = (bf16[64,512]{1,0:T(8,128)(2,1)S(1)}, bf16[64,512]{1,0:T(8,128)(2,1)S(1)}, u32[]{:S(2)}, u32[]{:S(2)}) collective-permute-start(bf16[64,512]{1,0:T(8,128)(2,1)S(1)} %copy-done.20), channel_id=1, source_target_pairs={{0,8},{4,12},{8,0},{12,4},{1,9},{5,13},{9,1},{13,5},{2,10},{6,14},... | collective-permute-start | bytes 196616 | tf_op jit(solution)/shard_map/ppermute | solution.py:194
  92.7 6.2 %collective-permute-start.31 = (bf16[8,512]{1,0:T(8,128)(2,1)S(1)}, bf16[8,512]{1,0:T(8,128)(2,1)S(1)}, u32[]{:S(2)}, u32[]{:S(2)}) collective-permute-start(bf16[8,512]{1,0:T(8,128)(2,1)S(1)} %get-tuple-element.59), channel_id=1, source_target_pairs={{0,8},{4,12},{8,0},{12,4},{1,9},{5,13},{9,1},{13,5},{2,10},{6,14},... | collective-permute-start | bytes 24584 | tf_op jit(solution)/shard_map/ppermute | solution.py:194
  95.0 5.5 %collective-permute-start.32 = (bf16[8,512]{1,0:T(8,128)(2,1)S(1)}, bf16[8,512]{1,0:T(8,128)(2,1)S(1)}, u32[]{:S(2)}, u32[]{:S(2)}) collective-permute-start(bf16[8,512]{1,0:T(8,128)(2,1)S(1)} %get-tuple-element.59), channel_id=1, source_target_pairs={{0,4},{4,8},{8,12},{12,0},{1,5},{5,9},{9,13},{13,1},{2,6},{6,10},{... | collective-permute-start | bytes 24584 | tf_op jit(solution)/shard_map/ppermute | solution.py:194
  99.0 5.0 %collective-permute-start.16 = (bf16[128,512]{1,0:T(8,128)(2,1)S(1)}, bf16[128,512]{1,0:T(8,128)(2,1)S(1)}, u32[]{:S(2)}, u32[]{:S(2)}) collective-permute-start(bf16[128,512]{1,0:T(8,128)(2,1)S(1)} %fusion.1), channel_id=1, source_target_pairs={{0,2},{1,3},{2,0},{3,1},{4,6},{5,7},{6,4},{7,5},{8,10},{9,11},{10,... | collective-permute-start | bytes 393224 | tf_op jit(solution)/shard_map/ppermute | solution.py:210
  104.1 5.8 %collective-permute-start.17 = (bf16[32,512]{1,0:T(8,128)(2,1)S(1)}, bf16[32,512]{1,0:T(8,128)(2,1)S(1)}, u32[]{:S(2)}, u32[]{:S(2)}) collective-permute-start(bf16[32,512]{1,0:T(8,128)(2,1)S(1)} %get-tuple-element.62), channel_id=1, source_target_pairs={{0,4},{4,8},{8,12},{12,0},{1,5},{5,9},{9,13},{13,1},{2,6},{6,10},{... | collective-permute-start | bytes 98312 | tf_op jit(solution)/shard_map/ppermute | solution.py:194
  106.2 5.1 %collective-permute-start.18 = (bf16[32,512]{1,0:T(8,128)(2,1)S(1)}, bf16[32,512]{1,0:T(8,128)(2,1)S(1)}, u32[]{:S(2)}, u32[]{:S(2)}) collective-permute-start(bf16[32,512]{1,0:T(8,128)(2,1)S(1)} %get-tuple-element.64), channel_id=1, source_target_pairs={{0,8},{4,12},{8,0},{12,4},{1,9},{5,13},{9,1},{13,5},{2,10},{6,14},... | collective-permute-start | bytes 98312 | tf_op jit(solution)/shard_map/ppermute | solution.py:194
  107.0 4.3 %collective-permute-start.19 = (bf16[32,512]{1,0:T(8,128)(2,1)S(1)}, bf16[32,512]{1,0:T(8,128)(2,1)S(1)}, u32[]{:S(2)}, u32[]{:S(2)}) collective-permute-start(bf16[32,512]{1,0:T(8,128)(2,1)S(1)} %get-tuple-element.63), channel_id=1, source_target_pairs={{0,12},{4,0},{8,4},{12,8},{1,13},{5,1},{9,5},{13,9},{2,14},{6,2},{... | collective-permute-start | bytes 98312 | tf_op jit(solution)/shard_map/ppermute | solution.py:194
  110.0 18.2 %collective-permute-start.14 = (bf16[64,512]{1,0:T(8,128)(2,1)S(1)}, bf16[64,512]{1,0:T(8,128)(2,1)S(1)}, u32[]{:S(2)}, u32[]{:S(2)}) collective-permute-start(bf16[64,512]{1,0:T(8,128)(2,1)S(1)} %copy-done.18), channel_id=1, source_target_pairs={{0,12},{4,0},{8,4},{12,8},{1,13},{5,1},{9,5},{13,9},{2,14},{6,2},{... | collective-permute-start | bytes 196616 | tf_op jit(solution)/shard_map/ppermute | solution.py:194
  111.3 5.0 %collective-permute-start.20 = (bf16[32,512]{1,0:T(8,128)(2,1)S(1)}, bf16[32,512]{1,0:T(8,128)(2,1)S(1)}, u32[]{:S(2)}, u32[]{:S(2)}) collective-permute-start(bf16[32,512]{1,0:T(8,128)(2,1)S(1)} %get-tuple-element.61), channel_id=1, source_target_pairs={{0,12},{4,0},{8,4},{12,8},{1,13},{5,1},{9,5},{13,9},{2,14},{6,2},{... | collective-permute-start | bytes 98312 | tf_op jit(solution)/shard_map/ppermute | solution.py:194
  114.7 4.8 %collective-permute-start.21 = (bf16[32,512]{1,0:T(8,128)(2,1)S(1)}, bf16[32,512]{1,0:T(8,128)(2,1)S(1)}, u32[]{:S(2)}, u32[]{:S(2)}) collective-permute-start(bf16[32,512]{1,0:T(8,128)(2,1)S(1)} %get-tuple-element.61), channel_id=1, source_target_pairs={{0,8},{4,12},{8,0},{12,4},{1,9},{5,13},{9,1},{13,5},{2,10},{6,14},... | collective-permute-start | bytes 98312 | tf_op jit(solution)/shard_map/ppermute | solution.py:194
  116.3 6.0 %collective-permute-start.22 = (bf16[32,512]{1,0:T(8,128)(2,1)S(1)}, bf16[32,512]{1,0:T(8,128)(2,1)S(1)}, u32[]{:S(2)}, u32[]{:S(2)}) collective-permute-start(bf16[32,512]{1,0:T(8,128)(2,1)S(1)} %get-tuple-element.61), channel_id=1, source_target_pairs={{0,4},{4,8},{8,12},{12,0},{1,5},{5,9},{9,13},{13,1},{2,6},{6,10},{... | collective-permute-start | bytes 98312 | tf_op jit(solution)/shard_map/ppermute | solution.py:194
  122.4 5.0 %collective-permute-start.23 = (bf16[128,512]{1,0:T(8,128)(2,1)S(1)}, bf16[128,512]{1,0:T(8,128)(2,1)S(1)}, u32[]{:S(2)}, u32[]{:S(2)}) collective-permute-start(bf16[128,512]{1,0:T(8,128)(2,1)S(1)} %constant_dynamic-slice_fusion.1), channel_id=1, source_target_pairs={{0,2},{1,3},{2,0},{3,1},{4,6},{5,7},{6,4},{7,5},{8,10},{9,11},{10,... | collective-permute-start | bytes 393224 | tf_op jit(solution)/shard_map/ppermute | solution.py:223
  123.0 4.8 %collective-permute-start.33 = (bf16[32,512]{1,0:T(8,128)(2,1)S(1)}, bf16[32,512]{1,0:T(8,128)(2,1)S(1)}, u32[]{:S(2)}, u32[]{:S(2)}) collective-permute-start(bf16[32,512]{1,0:T(8,128)(2,1)S(1)} %constant_dynamic-slice_fusion), channel_id=1, source_target_pairs={{0,2},{1,3},{2,0},{3,1},{4,6},{5,7},{6,4},{7,5},{8,10},{9,11},{10,... | collective-permute-start | bytes 98312 | tf_op jit(solution)/shard_map/ppermute | solution.py:223
  (28 other events, 215.7 us)

commit v2 on v1

v2 whole, which is shorter than its diff:
```python
import functools

import jax
import jax.numpy as jnp
from jax import lax
from jax.experimental import pallas as pl
from jax.experimental.pallas import tpu as pltpu
from jax.sharding import PartitionSpec as P

BF16 = jnp.bfloat16
F32 = jnp.float32
VMEM = pl.BlockSpec(memory_space=pltpu.VMEM)
SMEM = pl.BlockSpec(memory_space=pltpu.SMEM)
ANY = pl.BlockSpec(memory_space=pl.ANY)
NN = (((1,), (0,)), ((), ()))
NT = (((1,), (1,)), ((), ()))


def dot(a, b, dims=NN):
    return lax.dot_general(a, b, dims, preferred_element_type=F32)


def silu_parts(value):
    sig = 0.5 * jnp.tanh(0.5 * value) + 0.5
    act = value * sig
    return act, sig + act * (1.0 - sig)


def call(body, outs, args, flops=0, scratch=(), vmem=20, smem=(), order=()):
    args = list(args) + list(order)
    moved = sum(a.size * a.dtype.itemsize for a in args) + sum(
        o.size * o.dtype.itemsize for o in outs
    )
    keep = len(args) - len(order)
    specs = [SMEM if i in smem else VMEM if i < keep else ANY for i in range(len(args))]

    def inner(*refs):
        body(*refs[:keep], *refs[len(args) :])

    return pl.pallas_call(
        inner if order else body,
        out_shape=tuple(outs),
        in_specs=specs,
        out_specs=tuple([VMEM] * len(outs)),
        scratch_shapes=list(scratch),
        cost_estimate=pl.CostEstimate(flops=flops, bytes_accessed=moved, transcendentals=0),
        compiler_params=pltpu.CompilerParams(vmem_limit_bytes=vmem << 20),
    )(*args)


def shape(dims, dtype=BF16):
    return jax.ShapeDtypeStruct(dims, dtype)


def prepare_kernel(step, count, src, dst, basis, weight, filt, s_hot, d_hot):
    blocks, block = src.shape
    slots = s_hot.shape[0]
    weight_t = weight[...].T
    rows = lax.broadcasted_iota(jnp.int32, (slots, block), 0)
    for i in range(basis.shape[0] // step):
        at = pl.ds(i * step, step)
        filt[:, at] = silu_parts(dot(weight_t, basis[at, :], NT))[0].astype(BF16)
    for b in range(blocks):
        at = pl.ds(b * block, block)
        s_hot[:, at] = jnp.where(rows == src[pl.ds(b, 1), :], 1.0, 0.0).astype(BF16)
        slot = jnp.where(b < count[0, 0], dst[pl.ds(b, 1), :], -1)
        d_hot[:, at] = jnp.where(rows == slot, 1.0, 0.0).astype(BF16)


def lend_kernel(lists, edges, out, lent_hot, kept_hot):
    ranks, per_owner = lists.shape[0], lists.shape[1] // 2
    edge_dev = edges.shape[0]
    columns = lax.broadcasted_iota(jnp.int32, (per_owner, edge_dev), 1).astype(F32)
    for s in range(ranks):
        row = lists[pl.ds(s, 1), :].astype(F32)
        column = jnp.broadcast_to(row, (8, row.shape[1])).T[:, :1]
        rows = pl.ds(s * per_owner, per_owner)
        lent_hot[rows, :] = jnp.where(columns == column[:per_owner], 1.0, 0.0).astype(BF16)
        kept_hot[rows, :] = jnp.where(columns == column[per_owner:], 1.0, 0.0).astype(BF16)
    out[...] = dot(lent_hot[...], edges[...]).astype(BF16)


def owner_kernel(kept_hot, upstream, w_out, same, dhidden):
    hot = kept_hot[...]
    same[...] = dot(hot, hot, NT).astype(BF16)
    picked = dot(hot, upstream[...]).astype(BF16)
    dhidden[...] = dot(picked, w_out[...], NT)


def forward_kernel(step, fetched, filt, s_hot, d_hot, out, message):
    table = fetched[...].T
    for i in range(filt.shape[1] // step):
        at = pl.ds(i * step, step)
        message[:, at] = dot(table, s_hot[:, at]).astype(BF16) * filt[:, at]
    out[...] = dot(d_hot[...], message[...], NT).astype(BF16)


def slope_kernel(step, fetched, s_hot, basis, weight, out):
    table = fetched[...].T
    weight_t = weight[...].T
    for i in range(out.shape[1] // step):
        at = pl.ds(i * step, step)
        slope = silu_parts(dot(weight_t, basis[at, :], NT))[1]
        out[:, at] = (dot(table, s_hot[:, at]) * slope).astype(BF16)


def return_kernel(home, same, dhidden, out):
    agg = dot(same[...], home[...])
    out[...] = (dhidden[...] * silu_parts(agg)[1]).astype(BF16)


def update_kernel(step, home, kept_hot, edges, upstream, w_out, updated, term, hot_t, hidden):
    hot_t[...] = kept_hot[...].T
    rows = edges.shape[0]
    for i in range(rows // step):
        at = pl.ds(i * step, step)
        fresh = silu_parts(dot(hot_t[at, :], home[...]))[0].astype(BF16)
        hidden[:, at] = fresh.T
        updated[at, :] = (edges[at, :].astype(F32) + dot(fresh, w_out[...])).astype(BF16)
    term[...] = dot(hidden[...], upstream[...])


def weight_kernel(step, rows_in, filt, weighted, d_hot, basis, weight, dmessage, dpre):
    table = rows_in[...].T
    for i in range(filt.shape[1] // step):
        at = pl.ds(i * step, step)
        rows = dot(table, d_hot[:, at]).astype(BF16)
        dpre[:, at] = rows * weighted[:, at]
        dmessage[:, at] = rows * filt[:, at]
    weight[...] = dot(dpre[...], basis[...]).T


def source_kernel(dmessage, s_hot, out):
    out[...] = dot(s_hot[...], dmessage[...], NT).astype(BF16)


def final_kernel(step, back, lent_hot, upstream, out, hot_t):
    hot_t[...] = lent_hot[...].T
    for i in range(upstream.shape[0] // step):
        at = pl.ds(i * step, step)
        out[at, :] = (upstream[at, :].astype(F32) + dot(hot_t[at, :], back[...])).astype(BF16)


def swap(value, axis, mask):
    return lax.ppermute(value, axis, [(k, k ^ mask) for k in range(lax.axis_size(axis))])


def exchange(value):
    return lax.all_to_all(value, "graph", split_axis=0, concat_axis=0, tiled=True)


def halve(value, mine, bit):
    half = value.reshape(2, value.shape[0] // 2, value.shape[1])
    own = (mine >> bit) & 1
    away = lax.dynamic_index_in_dim(half, 1 - own, 0, keepdims=False).astype(BF16)
    kept = lax.dynamic_index_in_dim(half, own, 0, keepdims=False)
    return kept + swap(away, "dp", 1 << bit).astype(F32)


def double(value, mine, bit):
    got = swap(value, "dp", 1 << bit)
    low = ((mine >> bit) & 1) == 0
    return jnp.where(low, jnp.concatenate([value, got]), jnp.concatenate([got, value]))


def reduce_large(term):
    copies, ranks = lax.axis_size("dp"), lax.axis_size("graph")
    mine, me = lax.axis_index("dp"), lax.axis_index("graph")
    bits = range(copies.bit_length() - 1)
    value = term
    for bit in bits:
        value = halve(value, mine, bit)
    parts = value.reshape(ranks, value.shape[0] // ranks, value.shape[1])
    total = lax.dynamic_index_in_dim(parts, me, 0, keepdims=False)
    for s in range(1, ranks):
        away = lax.dynamic_index_in_dim(parts, me ^ s, 0, keepdims=False)
        total = total + swap(away.astype(BF16), "graph", s).astype(F32)
    piece = total.astype(BF16)
    value = jnp.zeros((ranks,) + piece.shape, BF16)
    for s in range(ranks):
        got = swap(piece, "graph", s) if s else piece
        value = lax.dynamic_update_index_in_dim(value, got, me ^ s, 0)
    value = value.reshape(-1, piece.shape[1])
    for bit in reversed(bits):
        value = double(value, mine, bit)
    return value.astype(F32)


def reduce_small(term):
    copies, ranks = lax.axis_size("dp"), lax.axis_size("graph")
    mine = lax.axis_index("dp")
    value = halve(term, mine, 0)
    for bit in range(1, copies.bit_length() - 1):
        own = value.astype(BF16)
        value = own.astype(F32) + swap(own, "dp", 1 << bit).astype(F32)
    own = value.astype(BF16)
    level = [own.astype(F32)] + [swap(own, "graph", s).astype(F32) for s in range(1, ranks)]
    while len(level) > 1:
        level = [level[k] + level[k + 1] for k in range(0, len(level), 2)]
    return double(level[0].astype(BF16), mine, 0).astype(F32)


def per_device(
    edge_emb,
    cotangent,
    fetch_rows,
    store_rows,
    trip_src,
    trip_dst,
    trip_basis,
    block_count,
    w_basis,
    w_out,
):
    edges, upstream, basis = edge_emb[0], cotangent[0], trip_basis[0]
    ranks, copies = lax.axis_size("graph"), lax.axis_size("dp")
    edge_dev, width = edges.shape
    slots = ranks * fetch_rows.shape[3]
    blocks, block_rows = trip_src.shape[1:]
    triplets, basis_width = basis.shape
    table = shape((slots, width))
    plane = shape((width, triplets))
    hot = shape((slots, triplets))
    step = 512
    wide = 2 * triplets * slots * width
    narrow = 2 * triplets * basis_width * width

    lists = exchange(jnp.concatenate([fetch_rows[0, 0], store_rows[0, 0]], axis=1))
    filt, s_hot, d_hot = call(
        functools.partial(prepare_kernel, step),
        [plane, hot, hot],
        [block_count, trip_src[0], trip_dst[0], basis, w_basis],
        flops=8 * narrow,
        smem=(0,),
    )
    lend, lent_hot, kept_hot = call(
        lend_kernel,
        [table] + [shape((slots, edge_dev))] * 2,
        [lists, edges],
        flops=2 * slots * edge_dev * width,
    )
    fetched = exchange(lend)
    same, dhidden = call(
        owner_kernel,
        [shape((slots, slots)), shape((slots, width), F32)],
        [kept_hot, upstream, w_out],
        flops=4 * slots * edge_dev * width,
    )
    (partial_rows,) = call(
        functools.partial(forward_kernel, step),
        [table],
        [fetched, filt, s_hot, d_hot],
        flops=2 * wide,
        scratch=[pltpu.VMEM(plane.shape, BF16)],
    )
    home = exchange(partial_rows)
    (weighted,) = call(
        functools.partial(slope_kernel, step),
        [plane],
        [fetched, s_hot, basis, w_basis],
        flops=wide + 8 * narrow,
    )
    (back,) = call(
        return_kernel,
        [table],
        [home, same, dhidden],
        flops=2 * slots * slots * width,
        order=[weighted],
    )
    dpartial = exchange(back)
    updated, out_term = call(
        functools.partial(update_kernel, 256),
        [shape((edge_dev, width)), shape((width, width), F32)],
        [home, kept_hot, edges, upstream, w_out],
        flops=2 * edge_dev * width * (2 * width + slots),
        scratch=[pltpu.VMEM((edge_dev, slots), BF16), pltpu.VMEM((width, edge_dev), BF16)],
    )
    out_scale = jnp.sqrt(F32(copies * ranks * edge_dev))
    grad_w_out = reduce_large(out_term) / out_scale
    basis_term, dmessage = call(
        functools.partial(weight_kernel, step),
        [shape((basis_width, width), F32), plane],
        [dpartial, filt, weighted, d_hot, basis],
        flops=wide + narrow,
        scratch=[pltpu.VMEM(plane.shape, BF16)],
        order=[out_term],
    )
    basis_scale = jnp.sqrt(F32(copies * ranks * blocks * block_rows))
    grad_w_basis = reduce_small(basis_term) / basis_scale
    (dfetch,) = call(source_kernel, [table], [dmessage, s_hot], flops=wide)
    (grad_edge,) = call(
        functools.partial(final_kernel, 256),
        [shape((edge_dev, width))],
        [exchange(dfetch), lent_hot, upstream],
        flops=2 * slots * edge_dev * width,
        scratch=[pltpu.VMEM((edge_dev, slots), BF16)],
    )
    return (updated[None], grad_edge[None], grad_w_out, grad_w_basis)


def solution(mesh):
    placed = (
        P(("groups", "dp"), "graph", None),
        P(("groups", "dp"), "graph", None),
        P(("groups", "dp"), "graph", None, None),
        P(("groups", "dp"), "graph", None, None),
        P(("groups", "dp"), "graph", None),
        P(("groups", "dp"), "graph", None),
        P(("groups", "dp"), "graph", None),
        P(("groups", "dp"), "graph"),
        P(),
        P(),
    )
    return jax.shard_map(
        per_device,
        mesh=mesh,
        in_specs=placed,
        out_specs=(
            P(("groups", "dp"), "graph", None),
            P(("groups", "dp"), "graph", None),
            P("groups", None),
            P("groups", None),
        ),
        check_vma=False,
    )
```

time: 132 us -> 131 us (level)
  local copies, waits for them, and re-layouts: 15.2 us -> 35.4 us
  Pallas kernels: 41.1 us -> 22.7 us
  starting transfers between devices: 46.6 us -> 39.7 us
  other arithmetic: 2.86 us -> 6.53 us
    ppermute x35 -> x16, starting transfers between devices: 46.6 us -> 18.1 us  [swap(): lax.ppermute(value, axis, [(k, k ^ mask) for k in range(lax.axis_size(axi...]
    all_to_all x0 -> x5, starting transfers between devices: none -> 21.6 us  [exchange(): lax.all_to_all(value, 'graph', split_axis=0, concat_axis=0, tiled=True)]
    unnamed x62 -> x66, local copies, waits for them, and re-layouts: 14.3 us -> 33.6 us
    pallas_call x9 -> x10, Pallas kernels: 41.1 us -> 22.7 us  [call(): pl.pallas_call(inner if order else body, out_shape=tuple(outs), in_specs=...]
    ppermute x35 -> x16, waiting for transfers between devices: 24.1 us -> 9.97 us  [swap(): lax.ppermute(value, axis, [(k, k ^ mask) for k in range(lax.axis_size(axi...]
    all_to_all x0 -> x5, waiting for transfers between devices: none -> 14.1 us  [exchange(): lax.all_to_all(value, 'graph', split_axis=0, concat_axis=0, tiled=True)]
    add x3 -> x2, other arithmetic: 0.12 us -> 2.26 us  [halve(): return kept + swap(away, 'dp', 1 << bit).astype(F32)]
  transfers between devices with their start and end apart: 35 -> 21, of which waited for: 16 -> 10; matrix products, arithmetic and copies ran while one was open for 1% -> 4% of each run, Pallas kernels for 17% -> 12%
where the time goes in v2:
time: 131 us; the launch traced here: 130 us
  starting transfers between devices  39.7 us (30%)
  local copies, waits for them, and re-layouts  35.4 us (27%)
  waiting for transfers between devices  24.1 us (18%)
  Pallas kernels  22.7 us (17%)
  other arithmetic  6.53 us (5%)
  between operations  1.58 us (1%)
    unnamed x66, local copies, waits for them, and re-layouts  33.6 us
    pallas_call x10, Pallas kernels, call(): pl.pallas_call(inner if order else body, out_shape=tuple(outs), in_specs=...  22.7 us
    all_to_all x5, starting transfers between devices, exchange(): lax.all_to_all(value, 'graph', split_axis=0, concat_axis=0, tiled=True)  21.6 us
    ppermute x16, starting transfers between devices, swap(): lax.ppermute(value, axis, [(k, k ^ mask) for k in range(lax.axis_size(axi...  18.1 us
    all_to_all x5, waiting for transfers between devices, exchange(): lax.all_to_all(value, 'graph', split_axis=0, concat_axis=0, tiled=True)  14.1 us
    ppermute x16, waiting for transfers between devices, swap(): lax.ppermute(value, axis, [(k, k ^ mask) for k in range(lax.axis_size(axi...  9.97 us
  transfers between devices with their start and end apart: 21, of which 10 were waited for; matrix products, arithmetic and copies ran while one was open for 4% of the time, Pallas kernels for 12%

profile of v2, /device:TPU:0, one launch (start us, length us, event | category | flops | bytes accessed | tf_op | source)
XLA Modules:
  0.0 130.0 jit_solution(10348342534950013792)
XLA Ops:
  2.0 6.3 %all-to-all-start = ((s32[4,1,128]{2,1,0:T(1,128)}), s32[4,1,128]{2,1,0:T(1,128)S(1)}, u32[]{:S(2)}, u32[]{:S(2)}) async-start(s32[4,1,128]{2,1,0:T(1,128)} %bitcast.2), calls=%async_computation | async-start | bytes 4096 | tf_op jit(solution)/shard_map/all_to_all | solution.py:149
  9.0 4.8 %all-to-all-done = s32[4,1,128]{2,1,0:T(1,128)S(1)} async-done(((s32[4,1,128]{2,1,0:T(1,128)}), s32[4,1,128]{2,1,0:T(1,128)S(1)}, u32[]{:S(2)}, u32[]{:S(2)}) %all-to-all-start) | async-done | bytes 2080 | tf_op jit(solution)/shard_map/all_to_all | solution.py:149
  15.0 1.5 %shard_map.129 = (bf16[256,512]{1,0:T(8,128)(2,1)}, bf16[256,1024]{1,0:T(8,128)(2,1)S(1)}, bf16[256,1024]{1,0:T(8,128)(2,1)S(1)}) custom-call(s32[4,128]{1,0:T(4,128)S(1)} %bitcast.79, bf16[1024,512]{1,0:T(8,128)(2,1)S(1)} %bitcast.73), custom_call_target="tpu_custom_call" | custom-call | flops 268435456 | bytes 2361344 | tf_op jit(solution)/shard_map/pallas_call | solution.py:40
  18.1 3.4 %all-to-all-start.1 = ((bf16[4,64,512]{2,1,0:T(8,128)(2,1)}), bf16[4,64,512]{2,1,0:T(8,128)(2,1)S(1)}, u32[]{:S(2)}, u32[]{:S(2)}) async-start(bf16[4,64,512]{2,1,0:T(8,128)(2,1)} %bitcast.5), calls=%async_computation.1 | async-start | bytes 524288 | tf_op jit(solution)/shard_map/all_to_all | solution.py:149
  25.0 3.8 %shard_map.130 = (bf16[512,4096]{1,0:T(8,128)(2,1)S(1)}, bf16[256,4096]{1,0:T(8,128)(2,1)S(1)}, bf16[256,4096]{1,0:T(8,128)(2,1)S(1)}) custom-call(s32[1,1]{1,0:T(1,128)S(6)} %copy.18.count, s32[32,128]{1,0:T(8,128)S(1)} %bitcast.80, s32[32,128]{1,0:T(8,128)S(1)} %bitcast.81, bf16[4096,128]{1,0:T(8,128)(2,1)S(1)} %bitcast.66, bf16[128,512]{1,0:T(8,128)(2,1)S(1)} %copy-done.28), custom_call_target="tpu_custom_call" | custom-call | flops 4294967296 | bytes 9601028 | tf_op jit(solution)/shard_map/pallas_call | solution.py:40
  28.9 2.0 %copy-done = bf16[512,4096]{1,0:T(8,128)(2,1)} copy-done((bf16[512,4096]{1,0:T(8,128)(2,1)}, bf16[512,4096]{1,0:T(8,128)(2,1)S(1)}, u32[]{:S(2)}) %copy-start) | copy-done | bytes 4194328
  32.2 2.2 %copy-done.1 = bf16[512,4096]{1,0:T(8,128)(2,1)S(1)} copy-done((bf16[512,4096]{1,0:T(8,128)(2,1)S(1)}, bf16[512,4096]{1,0:T(8,128)(2,1)}, u32[]{:S(2)}) %copy-start.1) | copy-done | bytes 4194328
  34.4 1.6 %copy-done.6 = bf16[256,4096]{1,0:T(8,128)(2,1)S(1)} copy-done((bf16[256,4096]{1,0:T(8,128)(2,1)S(1)}, bf16[256,4096]{1,0:T(8,128)(2,1)}, u32[]{:S(2)}) %copy-start.6) | copy-done | bytes 2097176
  36.0 2.4 %shard_map.131 = bf16[256,512]{1,0:T(8,128)(2,1)S(1)} custom-call(bf16[256,512]{1,0:T(8,128)(2,1)S(1)} %bitcast.70, bf16[512,4096]{1,0:T(8,128)(2,1)S(1)} %copy-done.1, bf16[256,4096]{1,0:T(8,128)(2,1)S(1)} %get-tuple-element.18.s_hot, bf16[256,4096]{1,0:T(8,128)(2,1)S(1)} %copy-done.6), custom_call_target="tpu_custom_call" | custom-call | flops 2147483648 | bytes 8912896 | tf_op jit(solution)/shard_map/pallas_call | solution.py:40
  39.0 5.1 %all-to-all-start.2 = ((bf16[4,64,512]{2,1,0:T(8,128)(2,1)}), bf16[4,64,512]{2,1,0:T(8,128)(2,1)}, u32[]{:S(2)}, u32[]{:S(2)}) async-start(bf16[4,64,512]{2,1,0:T(8,128)(2,1)} %bitcast.72), calls=%async_computation.2 | async-start | bytes 524288 | tf_op jit(solution)/shard_map/all_to_all | solution.py:149
  47.9 3.1 %all-to-all-done.2 = bf16[4,64,512]{2,1,0:T(8,128)(2,1)} async-done(((bf16[4,64,512]{2,1,0:T(8,128)(2,1)}), bf16[4,64,512]{2,1,0:T(8,128)(2,1)}, u32[]{:S(2)}, u32[]{:S(2)}) %all-to-all-start.2) | async-done | bytes 262176 | tf_op jit(solution)/shard_map/all_to_all | solution.py:149
  54.4 3.4 %shard_map.132 = (bf16[1024,512]{1,0:T(8,128)(2,1)}, f32[512,512]{1,0:T(8,128)S(1)}) custom-call(bf16[256,512]{1,0:T(8,128)(2,1)} %bitcast.11.home.refs_0_, bf16[256,1024]{1,0:T(8,128)(2,1)S(1)} %copy-done.24, bf16[1024,512]{1,0:T(8,128)(2,1)S(1)} %bitcast.74, bf16[1024,512]{1,0:T(8,128)(2,1)S(1)} %bitcast.62, bf16[512,512]{1,0:T(8,128)(2,1)S(1)} %copy-done.19), custom_call_target="tpu_custom_call" | custom-call | flops 1342177280 | bytes 5505024 | tf_op jit(solution)/shard_map/pallas_call | solution.py:40
  58.8 3.5 %shard_map.134.refs_3_.refs_2_ = bf16[512,4096]{1,0:T(8,128)(2,1)S(1)} custom-call(bf16[256,512]{1,0:T(8,128)(2,1)S(1)} %bitcast.71, bf16[256,4096]{1,0:T(8,128)(2,1)S(1)} %get-tuple-element.18.s_hot, bf16[4096,128]{1,0:T(8,128)(2,1)S(1)} %bitcast.67, bf16[128,512]{1,0:T(8,128)(2,1)S(1)} %copy-done.29), custom_call_target="tpu_custom_call" | custom-call | flops 5368709120 | bytes 7733248 | tf_op jit(solution)/shard_map/pallas_call | solution.py:40
  63.6 2.0 %copy-done.3 = bf16[512,4096]{1,0:T(8,128)(2,1)} copy-done((bf16[512,4096]{1,0:T(8,128)(2,1)}, bf16[512,4096]{1,0:T(8,128)(2,1)S(1)}, u32[]{:S(2)}) %copy-start.3) | copy-done | bytes 4194328
  66.3 3.4 %all-to-all-start.3 = ((bf16[4,64,512]{2,1,0:T(8,128)(2,1)}), bf16[4,64,512]{2,1,0:T(8,128)(2,1)S(1)}, u32[]{:S(2)}, u32[]{:S(2)}) async-start(bf16[4,64,512]{2,1,0:T(8,128)(2,1)} %bitcast.76), calls=%async_computation.3 | async-start | bytes 524288 | tf_op jit(solution)/shard_map/all_to_all | solution.py:149
  71.8 1.5 %collective-permute-start.1 = (bf16[128,512]{1,0:T(8,128)(2,1)S(1)}, bf16[128,512]{1,0:T(8,128)(2,1)}, u32[]{:S(2)}, u32[]{:S(2)}) collective-permute-start(bf16[128,512]{1,0:T(8,128)(2,1)S(1)} %fusion.1), channel_id=1, source_target_pairs={{0,2},{1,3},{2,0},{3,1},{4,6},{5,7},{6,4},{7,5},{8,10},{9,11},{10,... | collective-permute-start | bytes 393224 | tf_op jit(solution)/shard_map/ppermute | solution.py:145
  73.2 6.3 %all-to-all-done.3 = bf16[4,64,512]{2,1,0:T(8,128)(2,1)S(1)} async-done(((bf16[4,64,512]{2,1,0:T(8,128)(2,1)}), bf16[4,64,512]{2,1,0:T(8,128)(2,1)S(1)}, u32[]{:S(2)}, u32[]{:S(2)}) %all-to-all-start.3) | async-done | bytes 262176 | tf_op jit(solution)/shard_map/all_to_all | solution.py:149
  79.5 2.2 %copy-done.2 = bf16[512,4096]{1,0:T(8,128)(2,1)S(1)} copy-done((bf16[512,4096]{1,0:T(8,128)(2,1)S(1)}, bf16[512,4096]{1,0:T(8,128)(2,1)}, u32[]{:S(2)}) %copy-start.2) | copy-done | bytes 4194328
  81.7 2.2 %copy-done.4 = bf16[512,4096]{1,0:T(8,128)(2,1)S(1)} copy-done((bf16[512,4096]{1,0:T(8,128)(2,1)S(1)}, bf16[512,4096]{1,0:T(8,128)(2,1)}, u32[]{:S(2)}) %copy-start.4) | copy-done | bytes 4194328
  83.9 1.6 %copy-done.7 = bf16[256,4096]{1,0:T(8,128)(2,1)S(1)} copy-done((bf16[256,4096]{1,0:T(8,128)(2,1)S(1)}, bf16[256,4096]{1,0:T(8,128)(2,1)}, u32[]{:S(2)}) %copy-start.7) | copy-done | bytes 2097176
  87.9 2.5 %shard_map.136 = (f32[128,512]{1,0:T(8,128)S(1)}, bf16[512,4096]{1,0:T(8,128)(2,1)S(1)}) custom-call(bf16[256,512]{1,0:T(8,128)(2,1)S(1)} %bitcast.69, bf16[512,4096]{1,0:T(8,128)(2,1)S(1)} %copy-done.2, bf16[512,4096]{1,0:T(8,128)(2,1)S(1)} %copy-done.4, bf16[256,4096]{1,0:T(8,128)(2,1)S(1)} %copy-done.7, bf16[4096,128]{1,0:T(8,128)(2,1)S(1)} %bitcast.68, ...), custom_call_target="tpu_custom_call" | custom-call | flops 1610612736 | bytes 17301504 | tf_op jit(solution)/shard_map/pallas_call | solution.py:40
  90.5 2.0 %shard_map.137 = bf16[256,512]{1,0:T(8,128)(2,1)} custom-call(bf16[512,4096]{1,0:T(8,128)(2,1)S(1)} %get-tuple-element.25.dmessage, bf16[256,4096]{1,0:T(8,128)(2,1)S(1)} %get-tuple-element.18.s_hot), custom_call_target="tpu_custom_call" | custom-call | flops 1073741824 | bytes 6553600 | tf_op jit(solution)/shard_map/pallas_call | solution.py:40
  92.4 3.4 %all-to-all-start.4 = ((bf16[4,64,512]{2,1,0:T(8,128)(2,1)}), bf16[4,64,512]{2,1,0:T(8,128)(2,1)S(1)}, u32[]{:S(2)}, u32[]{:S(2)}) async-start(bf16[4,64,512]{2,1,0:T(8,128)(2,1)} %bitcast.16), calls=%async_computation.4 | async-start | bytes 524288 | tf_op jit(solution)/shard_map/all_to_all | solution.py:149
  97.0 3.8 %collective-permute-start.4 = (bf16[32,512]{1,0:T(8,128)(2,1)S(1)}, bf16[32,512]{1,0:T(8,128)(2,1)S(1)}, u32[]{:S(2)}, u32[]{:S(2)}) collective-permute-start(bf16[32,512]{1,0:T(8,128)(2,1)S(1)} %get-tuple-element.31), channel_id=1, source_target_pairs={{0,12},{4,8},{8,4},{12,0},{1,13},{5,9},{9,5},{13,1},{2,14},{6,10},... | collective-permute-start | bytes 98312 | tf_op jit(solution)/shard_map/ppermute | solution.py:145
  102.4 2.4 %collective-permute-done.4 = bf16[32,512]{1,0:T(8,128)(2,1)S(1)} collective-permute-done((bf16[32,512]{1,0:T(8,128)(2,1)S(1)}, bf16[32,512]{1,0:T(8,128)(2,1)S(1)}, u32[]{:S(2)}, u32[]{:S(2)}) %collective-permute-start.4) | collective-permute-done | bytes 32800 | tf_op jit(solution)/shard_map/ppermute | solution.py:145
  104.9 1.8 %collective-permute-done.3 = bf16[32,512]{1,0:T(8,128)(2,1)S(1)} collective-permute-done((bf16[32,512]{1,0:T(8,128)(2,1)S(1)}, bf16[32,512]{1,0:T(8,128)(2,1)S(1)}, u32[]{:S(2)}, u32[]{:S(2)}) %collective-permute-start.3) | collective-permute-done | bytes 32800 | tf_op jit(solution)/shard_map/ppermute | solution.py:145
  107.0 1.8 %collective-permute-start.6 = (bf16[32,512]{1,0:T(8,128)(2,1)S(1)}, bf16[32,512]{1,0:T(8,128)(2,1)S(1)}, u32[]{:S(2)}, u32[]{:S(2)}) collective-permute-start(bf16[32,512]{1,0:T(8,128)(2,1)S(1)} %get-tuple-element.29), channel_id=1, source_target_pairs={{0,8},{4,12},{8,0},{12,4},{1,9},{5,13},{9,1},{13,5},{2,10},{6,14},... | collective-permute-start | bytes 98312 | tf_op jit(solution)/shard_map/ppermute | solution.py:145
  108.8 2.4 %collective-permute-start.7 = (bf16[32,512]{1,0:T(8,128)(2,1)S(1)}, bf16[32,512]{1,0:T(8,128)(2,1)S(1)}, u32[]{:S(2)}, u32[]{:S(2)}) collective-permute-start(bf16[32,512]{1,0:T(8,128)(2,1)S(1)} %get-tuple-element.29), channel_id=1, source_target_pairs={{0,12},{4,8},{8,4},{12,0},{1,13},{5,9},{9,5},{13,1},{2,14},{6,10},... | collective-permute-start | bytes 98312 | tf_op jit(solution)/shard_map/ppermute | solution.py:145
  112.1 1.5 %collective-permute-start.11 = (bf16[64,512]{1,0:T(8,128)(2,1)S(1)}, bf16[64,512]{1,0:T(8,128)(2,1)S(1)}, u32[]{:S(2)}, u32[]{:S(2)}) collective-permute-start(bf16[64,512]{1,0:T(8,128)(2,1)S(1)} %fusion.2), channel_id=1, source_target_pairs={{0,2},{1,3},{2,0},{3,1},{4,6},{5,7},{6,4},{7,5},{8,10},{9,11},{10,... | collective-permute-start | bytes 196616 | tf_op jit(solution)/shard_map/ppermute | solution.py:145
  116.7 1.7 %collective-permute-start.14 = (bf16[64,512]{1,0:T(8,128)(2,1)S(1)}, bf16[64,512]{1,0:T(8,128)(2,1)S(1)}, u32[]{:S(2)}, u32[]{:S(2)}) collective-permute-start(bf16[64,512]{1,0:T(8,128)(2,1)S(1)} %add_convert_fusion.1), channel_id=1, source_target_pairs={{0,12},{4,8},{8,4},{12,0},{1,13},{5,9},{9,5},{13,1},{2,14},{6,10},... | collective-permute-start | bytes 196616 | tf_op jit(solution)/shard_map/ppermute | solution.py:145
  118.5 2.7 %collective-permute-start.12 = (bf16[64,512]{1,0:T(8,128)(2,1)S(1)}, bf16[64,512]{1,0:T(8,128)(2,1)S(1)}, u32[]{:S(2)}, u32[]{:S(2)}) collective-permute-start(bf16[64,512]{1,0:T(8,128)(2,1)S(1)} %add_convert_fusion.1), channel_id=1, source_target_pairs={{0,4},{4,0},{8,12},{12,8},{1,5},{5,1},{9,13},{13,9},{2,6},{6,2},{1... | collective-permute-start | bytes 196616 | tf_op jit(solution)/shard_map/ppermute | solution.py:145
  121.3 1.5 %collective-permute-done.14 = bf16[64,512]{1,0:T(8,128)(2,1)S(1)} collective-permute-done((bf16[64,512]{1,0:T(8,128)(2,1)S(1)}, bf16[64,512]{1,0:T(8,128)(2,1)S(1)}, u32[]{:S(2)}, u32[]{:S(2)}) %collective-permute-start.14) | collective-permute-done | bytes 65568 | tf_op jit(solution)/shard_map/ppermute | solution.py:145
  (104 shorter events, 38.7 us)
Async XLA Ops:
  2.0 11.8 %all-to-all-start = ((s32[4,1,128]{2,1,0:T(1,128)}), s32[4,1,128]{2,1,0:T(1,128)S(1)}, u32[]{:S(2)}, u32[]{:S(2)}) async-start(s32[4,1,128]{2,1,0:T(1,128)} %bitcast.2), calls=%async_computation | async-start | bytes 4096 | tf_op jit(solution)/shard_map/all_to_all | solution.py:149
  18.1 14.1 %all-to-all-start.1 = ((bf16[4,64,512]{2,1,0:T(8,128)(2,1)}), bf16[4,64,512]{2,1,0:T(8,128)(2,1)S(1)}, u32[]{:S(2)}, u32[]{:S(2)}) async-start(bf16[4,64,512]{2,1,0:T(8,128)(2,1)} %bitcast.5), calls=%async_computation.1 | async-start | bytes 524288 | tf_op jit(solution)/shard_map/all_to_all | solution.py:149
  28.9 2.0 %copy-start = (bf16[512,4096]{1,0:T(8,128)(2,1)}, bf16[512,4096]{1,0:T(8,128)(2,1)S(1)}, u32[]{:S(2)}) copy-start(bf16[512,4096]{1,0:T(8,128)(2,1)S(1)} %get-tuple-element.17.filt.refs_1_) | copy-start | bytes 12582916
  32.2 2.2 %copy-start.1 = (bf16[512,4096]{1,0:T(8,128)(2,1)S(1)}, bf16[512,4096]{1,0:T(8,128)(2,1)}, u32[]{:S(2)}) copy-start(bf16[512,4096]{1,0:T(8,128)(2,1)} %copy-done) | copy-start | bytes 12582916
  34.4 1.6 %copy-start.6 = (bf16[256,4096]{1,0:T(8,128)(2,1)S(1)}, bf16[256,4096]{1,0:T(8,128)(2,1)}, u32[]{:S(2)}) copy-start(bf16[256,4096]{1,0:T(8,128)(2,1)} %copy-done.5) | copy-start | bytes 6291460
  36.0 8.1 %copy-start.8 = (bf16[1,1024,512]{2,1,0:T(8,128)(2,1)S(1)}, bf16[1,1024,512]{2,1,0:T(8,128)(2,1)}, u32[]{:S(2)}) copy-start(bf16[1,1024,512]{2,1,0:T(8,128)(2,1)} %param.11) | copy-start | bytes 3145732
  39.0 11.9 %all-to-all-start.2 = ((bf16[4,64,512]{2,1,0:T(8,128)(2,1)}), bf16[4,64,512]{2,1,0:T(8,128)(2,1)}, u32[]{:S(2)}, u32[]{:S(2)}) async-start(bf16[4,64,512]{2,1,0:T(8,128)(2,1)} %bitcast.72), calls=%async_computation.2 | async-start | bytes 524288 | tf_op jit(solution)/shard_map/all_to_all | solution.py:149
  51.0 7.9 %copy-start.12 = (bf16[1,4096,128]{2,1,0:T(8,128)(2,1)S(1)}, bf16[1,4096,128]{2,1,0:T(8,128)(2,1)}, u32[]{:S(2)}) copy-start(bf16[1,4096,128]{2,1,0:T(8,128)(2,1)} %param.16) | copy-start | bytes 3145732
  54.4 4.5 %copy-start.29 = (bf16[128,512]{1,0:T(8,128)(2,1)S(1)}, bf16[128,512]{1,0:T(8,128)(2,1)}, u32[]{:S(2)}) copy-start(bf16[128,512]{1,0:T(8,128)(2,1)} %weight.3) | copy-start | bytes 393220
  58.8 3.5 %copy-start.26 = (f32[256,512]{1,0:T(8,128)S(1)}, f32[256,512]{1,0:T(8,128)}, u32[]{:S(2)}) copy-start(f32[256,512]{1,0:T(8,128)} %copy-done.25) | copy-start | bytes 1572868
  58.8 10.9 %collective-permute-start = (bf16[256,512]{1,0:T(8,128)(2,1)}, bf16[256,512]{1,0:T(8,128)(2,1)}, u32[]{:S(2)}, u32[]{:S(2)}) collective-permute-start(bf16[256,512]{1,0:T(8,128)(2,1)} %fusion), channel_id=1, source_target_pairs={{0,1},{1,0},{2,3},{3,2},{4,5},{5,4},{6,7},{7,6},{8,9},{9,8},{10,11... | collective-permute-start | bytes 786440 | tf_op jit(solution)/shard_map/ppermute | solution.py:145
  63.6 2.0 %copy-start.3 = (bf16[512,4096]{1,0:T(8,128)(2,1)}, bf16[512,4096]{1,0:T(8,128)(2,1)S(1)}, u32[]{:S(2)}) copy-start(bf16[512,4096]{1,0:T(8,128)(2,1)S(1)} %shard_map.134.refs_3_.refs_2_) | copy-start | bytes 12582916
  66.3 13.2 %all-to-all-start.3 = ((bf16[4,64,512]{2,1,0:T(8,128)(2,1)}), bf16[4,64,512]{2,1,0:T(8,128)(2,1)S(1)}, u32[]{:S(2)}, u32[]{:S(2)}) async-start(bf16[4,64,512]{2,1,0:T(8,128)(2,1)} %bitcast.76), calls=%async_computation.3 | async-start | bytes 524288 | tf_op jit(solution)/shard_map/all_to_all | solution.py:149
  71.8 24.1 %collective-permute-start.1 = (bf16[128,512]{1,0:T(8,128)(2,1)S(1)}, bf16[128,512]{1,0:T(8,128)(2,1)}, u32[]{:S(2)}, u32[]{:S(2)}) collective-permute-start(bf16[128,512]{1,0:T(8,128)(2,1)S(1)} %fusion.1), channel_id=1, source_target_pairs={{0,2},{1,3},{2,0},{3,1},{4,6},{5,7},{6,4},{7,5},{8,10},{9,11},{10,... | collective-permute-start | bytes 393224 | tf_op jit(solution)/shard_map/ppermute | solution.py:145
  79.5 2.2 %copy-start.2 = (bf16[512,4096]{1,0:T(8,128)(2,1)S(1)}, bf16[512,4096]{1,0:T(8,128)(2,1)}, u32[]{:S(2)}) copy-start(bf16[512,4096]{1,0:T(8,128)(2,1)} %copy-done) | copy-start | bytes 12582916
  81.7 2.2 %copy-start.4 = (bf16[512,4096]{1,0:T(8,128)(2,1)S(1)}, bf16[512,4096]{1,0:T(8,128)(2,1)}, u32[]{:S(2)}) copy-start(bf16[512,4096]{1,0:T(8,128)(2,1)} %copy-done.3) | copy-start | bytes 12582916
  90.4 2.0 %copy-start.27 = (f32[128,512]{1,0:T(8,128)}, f32[128,512]{1,0:T(8,128)S(1)}, u32[]{:S(2)}) copy-start(f32[128,512]{1,0:T(8,128)S(1)} %get-tuple-element.27) | copy-start | bytes 786436
  92.4 33.9 %all-to-all-start.4 = ((bf16[4,64,512]{2,1,0:T(8,128)(2,1)}), bf16[4,64,512]{2,1,0:T(8,128)(2,1)S(1)}, u32[]{:S(2)}, u32[]{:S(2)}) async-start(bf16[4,64,512]{2,1,0:T(8,128)(2,1)} %bitcast.16), calls=%async_computation.4 | async-start | bytes 524288 | tf_op jit(solution)/shard_map/all_to_all | solution.py:149
  97.0 7.9 %collective-permute-start.4 = (bf16[32,512]{1,0:T(8,128)(2,1)S(1)}, bf16[32,512]{1,0:T(8,128)(2,1)S(1)}, u32[]{:S(2)}, u32[]{:S(2)}) collective-permute-start(bf16[32,512]{1,0:T(8,128)(2,1)S(1)} %get-tuple-element.31), channel_id=1, source_target_pairs={{0,12},{4,8},{8,4},{12,0},{1,13},{5,9},{9,5},{13,1},{2,14},{6,10},... | collective-permute-start | bytes 98312 | tf_op jit(solution)/shard_map/ppermute | solution.py:145
  100.8 5.9 %collective-permute-start.3 = (bf16[32,512]{1,0:T(8,128)(2,1)S(1)}, bf16[32,512]{1,0:T(8,128)(2,1)S(1)}, u32[]{:S(2)}, u32[]{:S(2)}) collective-permute-start(bf16[32,512]{1,0:T(8,128)(2,1)S(1)} %get-tuple-element.32), channel_id=1, source_target_pairs={{0,8},{4,12},{8,0},{12,4},{1,9},{5,13},{9,1},{13,5},{2,10},{6,14},... | collective-permute-start | bytes 98312 | tf_op jit(solution)/shard_map/ppermute | solution.py:145
  100.8 5.9 %collective-permute-start.2 = (bf16[32,512]{1,0:T(8,128)(2,1)S(1)}, bf16[32,512]{1,0:T(8,128)(2,1)S(1)}, u32[]{:S(2)}, u32[]{:S(2)}) collective-permute-start(bf16[32,512]{1,0:T(8,128)(2,1)S(1)} %get-tuple-element.30), channel_id=1, source_target_pairs={{0,4},{4,0},{8,12},{12,8},{1,5},{5,1},{9,13},{13,9},{2,6},{6,2},{1... | collective-permute-start | bytes 98312 | tf_op jit(solution)/shard_map/ppermute | solution.py:145
  102.4 8.8 %collective-permute-start.10 = (bf16[64,512]{1,0:T(8,128)(2,1)S(1)}, bf16[64,512]{1,0:T(8,128)(2,1)S(1)}, u32[]{:S(2)}, u32[]{:S(2)}) collective-permute-start(bf16[64,512]{1,0:T(8,128)(2,1)S(1)} %fusion.3), channel_id=1, source_target_pairs={{0,1},{1,0},{2,3},{3,2},{4,5},{5,4},{6,7},{7,6},{8,9},{9,8},{10,11... | collective-permute-start | bytes 196616 | tf_op jit(solution)/shard_map/ppermute | solution.py:145
  106.7 6.9 %collective-permute-start.5 = (bf16[32,512]{1,0:T(8,128)(2,1)S(1)}, bf16[32,512]{1,0:T(8,128)(2,1)S(1)}, u32[]{:S(2)}, u32[]{:S(2)}) collective-permute-start(bf16[32,512]{1,0:T(8,128)(2,1)S(1)} %get-tuple-element.29), channel_id=1, source_target_pairs={{0,4},{4,0},{8,12},{12,8},{1,5},{5,1},{9,13},{13,9},{2,6},{6,2},{1... | collective-permute-start | bytes 98312 | tf_op jit(solution)/shard_map/ppermute | solution.py:145
  107.0 6.7 %collective-permute-start.6 = (bf16[32,512]{1,0:T(8,128)(2,1)S(1)}, bf16[32,512]{1,0:T(8,128)(2,1)S(1)}, u32[]{:S(2)}, u32[]{:S(2)}) collective-permute-start(bf16[32,512]{1,0:T(8,128)(2,1)S(1)} %get-tuple-element.29), channel_id=1, source_target_pairs={{0,8},{4,12},{8,0},{12,4},{1,9},{5,13},{9,1},{13,5},{2,10},{6,14},... | collective-permute-start | bytes 98312 | tf_op jit(solution)/shard_map/ppermute | solution.py:145
  108.8 5.7 %collective-permute-start.7 = (bf16[32,512]{1,0:T(8,128)(2,1)S(1)}, bf16[32,512]{1,0:T(8,128)(2,1)S(1)}, u32[]{:S(2)}, u32[]{:S(2)}) collective-permute-start(bf16[32,512]{1,0:T(8,128)(2,1)S(1)} %get-tuple-element.29), channel_id=1, source_target_pairs={{0,12},{4,8},{8,4},{12,0},{1,13},{5,9},{9,5},{13,1},{2,14},{6,10},... | collective-permute-start | bytes 98312 | tf_op jit(solution)/shard_map/ppermute | solution.py:145
  112.1 4.6 %collective-permute-start.11 = (bf16[64,512]{1,0:T(8,128)(2,1)S(1)}, bf16[64,512]{1,0:T(8,128)(2,1)S(1)}, u32[]{:S(2)}, u32[]{:S(2)}) collective-permute-start(bf16[64,512]{1,0:T(8,128)(2,1)S(1)} %fusion.2), channel_id=1, source_target_pairs={{0,2},{1,3},{2,0},{3,1},{4,6},{5,7},{6,4},{7,5},{8,10},{9,11},{10,... | collective-permute-start | bytes 196616 | tf_op jit(solution)/shard_map/ppermute | solution.py:145
  114.5 6.7 %collective-permute-start.8 = (bf16[128,512]{1,0:T(8,128)(2,1)S(1)}, bf16[128,512]{1,0:T(8,128)(2,1)S(1)}, u32[]{:S(2)}, u32[]{:S(2)}) collective-permute-start(bf16[128,512]{1,0:T(8,128)(2,1)S(1)} %bitcast.87), channel_id=1, source_target_pairs={{0,2},{1,3},{2,0},{3,1},{4,6},{5,7},{6,4},{7,5},{8,10},{9,11},{10,... | collective-permute-start | bytes 393224 | tf_op jit(solution)/shard_map/ppermute | solution.py:145
  116.7 6.1 %collective-permute-start.14 = (bf16[64,512]{1,0:T(8,128)(2,1)S(1)}, bf16[64,512]{1,0:T(8,128)(2,1)S(1)}, u32[]{:S(2)}, u32[]{:S(2)}) collective-permute-start(bf16[64,512]{1,0:T(8,128)(2,1)S(1)} %add_convert_fusion.1), channel_id=1, source_target_pairs={{0,12},{4,8},{8,4},{12,0},{1,13},{5,9},{9,5},{13,1},{2,14},{6,10},... | collective-permute-start | bytes 196616 | tf_op jit(solution)/shard_map/ppermute | solution.py:145
  118.5 5.8 %collective-permute-start.13 = (bf16[64,512]{1,0:T(8,128)(2,1)S(1)}, bf16[64,512]{1,0:T(8,128)(2,1)S(1)}, u32[]{:S(2)}, u32[]{:S(2)}) collective-permute-start(bf16[64,512]{1,0:T(8,128)(2,1)S(1)} %add_convert_fusion.1), channel_id=1, source_target_pairs={{0,8},{4,12},{8,0},{12,4},{1,9},{5,13},{9,1},{13,5},{2,10},{6,14},... | collective-permute-start | bytes 196616 | tf_op jit(solution)/shard_map/ppermute | solution.py:145
  118.5 5.8 %collective-permute-start.12 = (bf16[64,512]{1,0:T(8,128)(2,1)S(1)}, bf16[64,512]{1,0:T(8,128)(2,1)S(1)}, u32[]{:S(2)}, u32[]{:S(2)}) collective-permute-start(bf16[64,512]{1,0:T(8,128)(2,1)S(1)} %add_convert_fusion.1), channel_id=1, source_target_pairs={{0,4},{4,0},{8,12},{12,8},{1,5},{5,1},{9,13},{13,9},{2,6},{6,2},{1... | collective-permute-start | bytes 196616 | tf_op jit(solution)/shard_map/ppermute | solution.py:145
  121.3 7.6 %collective-permute-start.9 = (bf16[256,512]{1,0:T(8,128)(2,1)S(1)}, bf16[256,512]{1,0:T(8,128)(2,1)S(1)}, u32[]{:S(2)}, u32[]{:S(2)}) collective-permute-start(bf16[256,512]{1,0:T(8,128)(2,1)S(1)} %maximum_select_fusion.1), channel_id=1, source_target_pairs={{0,1},{1,0},{2,3},{3,2},{4,5},{5,4},{6,7},{7,6},{8,9},{9,8},{10,11... | collective-permute-start | bytes 786440 | tf_op jit(solution)/shard_map/ppermute | solution.py:145
  124.3 1.3 %collective-permute-start.15 = (bf16[64,512]{1,0:T(8,128)(2,1)S(1)}, bf16[64,512]{1,0:T(8,128)(2,1)S(1)}, u32[]{:S(2)}, u32[]{:S(2)}) collective-permute-start(bf16[64,512]{1,0:T(8,128)(2,1)S(1)} %add_convert_fusion), channel_id=1, source_target_pairs={{0,1},{1,0},{2,3},{3,2},{4,5},{5,4},{6,7},{7,6},{8,9},{9,8},{10,11... | collective-permute-start | bytes 196616 | tf_op jit(solution)/shard_map/ppermute | solution.py:145
  (22 other events, 22.3 us)

commit v3 on v2

v3 whole, which is shorter than its diff:
```python
import functools

import jax
import jax.numpy as jnp
from jax import lax
from jax.experimental import pallas as pl
from jax.experimental.pallas import tpu as pltpu
from jax.sharding import PartitionSpec as P

BF16 = jnp.bfloat16
F32 = jnp.float32
VMEM = pl.BlockSpec(memory_space=pltpu.VMEM)
SMEM = pl.BlockSpec(memory_space=pltpu.SMEM)
ANY = pl.BlockSpec(memory_space=pl.ANY)
NN = (((1,), (0,)), ((), ()))
NT = (((1,), (1,)), ((), ()))


def dot(a, b, dims=NN):
    return lax.dot_general(a, b, dims, preferred_element_type=F32)


def silu_parts(value):
    sig = 0.5 * jnp.tanh(0.5 * value) + 0.5
    act = value * sig
    return act, sig + act * (1.0 - sig)


def call(body, outs, args, flops=0, scratch=(), smem=(), far=(), far_out=(), order=()):
    args = list(args) + list(order)
    moved = sum(a.size * a.dtype.itemsize for a in args) + sum(
        o.size * o.dtype.itemsize for o in outs
    )
    keep = len(args) - len(order)
    specs = [
        SMEM if i in smem else ANY if i in far or i >= keep else VMEM for i in range(len(args))
    ]

    def inner(*refs):
        body(*refs[:keep], *refs[len(args) :])

    return pl.pallas_call(
        inner if order else body,
        out_shape=tuple(outs),
        in_specs=specs,
        out_specs=tuple(ANY if i in far_out else VMEM for i in range(len(outs))),
        scratch_shapes=list(scratch),
        cost_estimate=pl.CostEstimate(flops=flops, bytes_accessed=moved, transcendentals=0),
        compiler_params=pltpu.CompilerParams(vmem_limit_bytes=58 << 20),
    )(*args)


def shape(dims, dtype=BF16):
    return jax.ShapeDtypeStruct(dims, dtype)


def held(array):
    return pltpu.VMEM(array.shape, array.dtype)


def lane_copies(source, target, sems, step):
    return [
        pltpu.make_async_copy(
            source.at[:, pl.ds(i * step, step)], target.at[:, pl.ds(i * step, step)], sems.at[i]
        )
        for i in range(target.shape[1] // step)
    ]


def started(copies):
    for copy in copies:
        copy.start()
    return copies


def hot_lanes(index, first, count, slots, dead=None):
    block = index.shape[1]
    rows = lax.broadcasted_iota(jnp.int32, (slots, block), 0)
    parts = []
    for b in range(first, first + count):
        slot = index[pl.ds(b, 1), :]
        if dead is not None:
            slot = jnp.where(b < dead, slot, -1)
        parts.append(jnp.where(rows == slot, 1.0, 0.0).astype(BF16))
    return jnp.concatenate(parts, axis=1)


def turned(index, per_owner, ranks, me):
    slot = index[...] - me * per_owner
    return jnp.where(slot < 0, slot + ranks * per_owner, slot)


def gathered(pieces):
    return jnp.concatenate([p[...] for p in pieces], axis=0)


def scattered(value, outs):
    per = outs[0].shape[0]
    for s, out in enumerate(outs):
        out[...] = value[s * per : (s + 1) * per]


def columns_of(lists, me, kept, per_owner):
    parts = []
    for ref in lists:
        row = ref[pl.ds(me, 1), :].astype(F32)
        column = jnp.broadcast_to(row, (8, row.shape[1])).T[:, :1]
        parts.append(column[per_owner : 2 * per_owner] if kept else column[:per_owner])
    return jnp.concatenate(parts, axis=0)


def hot_rows(column, edge_dev):
    edges = lax.broadcasted_iota(jnp.int32, (column.shape[0], edge_dev), 1).astype(F32)
    return jnp.where(column == edges, 1.0, 0.0).astype(BF16)


def prepare_kernel(step, basis, weight, filt, buffer, sems):
    weight_t = weight[...].T
    leave = lane_copies(buffer, filt, sems, step)
    for i, copy in enumerate(leave):
        at = pl.ds(i * step, step)
        buffer[:, at] = silu_parts(dot(weight_t, basis[at, :], NT))[0].astype(BF16)
        copy.start()
    for copy in leave:
        copy.wait()


def lend_kernel(ranks, me, *refs):
    lists, edges, outs = refs[:ranks], refs[ranks], refs[ranks + 1 :]
    column = columns_of(lists, me[0], False, outs[0].shape[0])
    scattered(dot(hot_rows(column, edges.shape[0]), edges[...]).astype(BF16), outs)


def owner_kernel(ranks, me, *refs):
    lists, (upstream, w_out, same, dhidden) = refs[:ranks], refs[ranks:]
    hot = hot_rows(columns_of(lists, me[0], True, same.shape[0] // ranks), upstream.shape[0])
    same[...] = dot(hot, hot, NT).astype(BF16)
    dhidden[...] = dot(dot(hot, upstream[...]).astype(BF16), w_out[...], NT)


def forward_kernel(ranks, step, me, count, *refs):
    pieces, (src, dst, filt) = refs[:ranks], refs[ranks : ranks + 3]
    outs = refs[ranks + 3 : 2 * ranks + 3]
    filt_v, message, total, sems = refs[2 * ranks + 3 :]
    arrive = started(lane_copies(filt, filt_v, sems, step))
    per_owner = outs[0].shape[0]
    slots, block = ranks * per_owner, src.shape[1]
    table = gathered(pieces).T
    src_t = turned(src, per_owner, ranks, me[0])
    dst_t = turned(dst, per_owner, ranks, me[0])
    each = step // block
    for i, copy in enumerate(arrive):
        at = pl.ds(i * step, step)
        rows = dot(table, hot_lanes(src_t, i * each, each, slots)).astype(BF16)
        copy.wait()
        message[:, at] = rows * filt_v[:, at]
    hot = hot_lanes(dst_t, 0, src.shape[0], slots, count[0, 0])
    total[...] = dot(hot, message[...], NT)
    scattered(total[...].astype(BF16), outs)


def slope_kernel(ranks, step, me, *refs):
    pieces, (src, basis, weight, out, buffer, sems) = refs[:ranks], refs[ranks:]
    per_owner = pieces[0].shape[0]
    slots, block = ranks * per_owner, src.shape[1]
    table = gathered(pieces).T
    weight_t = weight[...].T
    src_t = turned(src, per_owner, ranks, me[0])
    each = step // block
    leave = lane_copies(buffer, out, sems, step)
    for i, copy in enumerate(leave):
        at = pl.ds(i * step, step)
        slope = silu_parts(dot(weight_t, basis[at, :], NT))[1]
        rows = dot(table, hot_lanes(src_t, i * each, each, slots))
        buffer[:, at] = (rows * slope).astype(BF16)
        copy.start()
    for copy in leave:
        copy.wait()


def return_kernel(ranks, *refs):
    pieces, (same, dhidden), outs = refs[:ranks], refs[ranks : ranks + 2], refs[ranks + 2 :]
    agg = dot(same[...], gathered(pieces))
    scattered((dhidden[...] * silu_parts(agg)[1]).astype(BF16), outs)


def update_kernel(ranks, step, me, *refs):
    lists, pieces = refs[:ranks], refs[ranks : 2 * ranks]
    edges, upstream, w_out, updated, term, hot_t, hidden = refs[2 * ranks :]
    home = gathered(pieces)
    rows = edges.shape[0]
    hot_t[...] = hot_rows(columns_of(lists, me[0], True, pieces[0].shape[0]), rows).T
    for i in range(rows // step):
        at = pl.ds(i * step, step)
        fresh = silu_parts(dot(hot_t[at, :], home))[0].astype(BF16)
        hidden[:, at] = fresh.T
        updated[at, :] = (edges[at, :].astype(F32) + dot(fresh, w_out[...])).astype(BF16)
    term[...] = dot(hidden[...], upstream[...])


def weight_kernel(ranks, step, me, count, *refs):
    pieces, (dst, filt, weighted, basis) = refs[:ranks], refs[ranks : ranks + 4]
    weight, dmessage, filt_v, weighted_v, dpre, sems = refs[ranks + 4 :]
    arrive = started(lane_copies(weighted, weighted_v, sems.at[0], step))
    arrive_filt = started(lane_copies(filt, filt_v, sems.at[1], step))
    per_owner = pieces[0].shape[0]
    slots, block = ranks * per_owner, dst.shape[1]
    table = gathered(pieces).T
    dst_t = turned(dst, per_owner, ranks, me[0])
    each = step // block
    for i in range(len(arrive)):
        at = pl.ds(i * step, step)
        rows = dot(table, hot_lanes(dst_t, i * each, each, slots, count[0, 0])).astype(BF16)
        arrive[i].wait()
        dpre[:, at] = rows * weighted_v[:, at]
        arrive_filt[i].wait()
        dmessage[:, at] = rows * filt_v[:, at]
    weight[...] = dot(dpre[...], basis[...]).T


def source_kernel(ranks, me, src, dmessage, *outs):
    per_owner = outs[0].shape[0]
    src_t = turned(src, per_owner, ranks, me[0])
    hot = hot_lanes(src_t, 0, src.shape[0], ranks * per_owner)
    scattered(dot(hot, dmessage[...], NT).astype(BF16), outs)


def final_kernel(ranks, step, me, *refs):
    lists, pieces = refs[:ranks], refs[ranks : 2 * ranks]
    upstream, out, hot_t = refs[2 * ranks :]
    back = gathered(pieces)
    rows = upstream.shape[0]
    hot_t[...] = hot_rows(columns_of(lists, me[0], False, pieces[0].shape[0]), rows).T
    for i in range(rows // step):
        at = pl.ds(i * step, step)
        out[at, :] = (upstream[at, :].astype(F32) + dot(hot_t[at, :], back)).astype(BF16)


def swap(value, axis, mask):
    return lax.ppermute(value, axis, [(k, k ^ mask) for k in range(lax.axis_size(axis))])


def shift(value, axis, by):
    count = lax.axis_size(axis)
    return lax.ppermute(value, axis, [(k, (k + by) % count) for k in range(count)])


def exchange(pieces, sign):
    return [pieces[0]] + [shift(pieces[s], "graph", sign * s) for s in range(1, len(pieces))]


def halve(value, mine, bit):
    half = value.reshape(2, value.shape[0] // 2, value.shape[1])
    own = (mine >> bit) & 1
    away = lax.dynamic_index_in_dim(half, 1 - own, 0, keepdims=False).astype(BF16)
    kept = lax.dynamic_index_in_dim(half, own, 0, keepdims=False)
    return kept + swap(away, "dp", 1 << bit).astype(F32)


def double(value, mine, bit):
    got = swap(value, "dp", 1 << bit)
    low = ((mine >> bit) & 1) == 0
    return jnp.where(low, jnp.concatenate([value, got]), jnp.concatenate([got, value]))


def reduce_large(term):
    copies, ranks = lax.axis_size("dp"), lax.axis_size("graph")
    mine, me = lax.axis_index("dp"), lax.axis_index("graph")
    bits = range(copies.bit_length() - 1)
    value = term
    for bit in bits:
        value = halve(value, mine, bit)
    parts = value.reshape(ranks, value.shape[0] // ranks, value.shape[1])
    total = lax.dynamic_index_in_dim(parts, me, 0, keepdims=False)
    for s in range(1, ranks):
        away = lax.dynamic_index_in_dim(parts, me ^ s, 0, keepdims=False)
        total = total + swap(away.astype(BF16), "graph", s).astype(F32)
    piece = total.astype(BF16)
    value = jnp.zeros((ranks,) + piece.shape, BF16)
    for s in range(ranks):
        got = swap(piece, "graph", s) if s else piece
        value = lax.dynamic_update_index_in_dim(value, got, me ^ s, 0)
    value = value.reshape(-1, piece.shape[1])
    for bit in reversed(bits):
        value = double(value, mine, bit)
    return value.astype(F32)


def reduce_small(term):
    copies, ranks = lax.axis_size("dp"), lax.axis_size("graph")
    mine = lax.axis_index("dp")
    value = halve(term, mine, 0)
    for bit in range(1, copies.bit_length() - 1):
        own = value.astype(BF16)
        value = own.astype(F32) + swap(own, "dp", 1 << bit).astype(F32)
    own = value.astype(BF16)
    level = [own.astype(F32)] + [swap(own, "graph", s).astype(F32) for s in range(1, ranks)]
    while len(level) > 1:
        level = [level[k] + level[k + 1] for k in range(0, len(level), 2)]
    return double(level[0].astype(BF16), mine, 0).astype(F32)


def per_device(
    edge_emb,
    cotangent,
    fetch_rows,
    store_rows,
    trip_src,
    trip_dst,
    trip_basis,
    block_count,
    w_basis,
    w_out,
):
    edges, upstream, basis = edge_emb[0], cotangent[0], trip_basis[0]
    ranks, copies = lax.axis_size("graph"), lax.axis_size("dp")
    me = lax.axis_index("graph").astype(jnp.int32).reshape(1)
    edge_dev, width = edges.shape
    per_owner = fetch_rows.shape[3]
    slots = ranks * per_owner
    blocks, block_rows = trip_src.shape[1:]
    triplets, basis_width = basis.shape
    src, dst = trip_src[0], trip_dst[0]
    pieces = [shape((per_owner, width))] * ranks
    plane = shape((width, triplets))
    step = 512
    turns = triplets // step
    wide = 2 * triplets * slots * width
    narrow = 2 * triplets * basis_width * width

    both = jnp.concatenate([fetch_rows[0, 0], store_rows[0, 0]], axis=1)
    lists = exchange([both] * ranks, 1)
    (filt,) = call(
        functools.partial(prepare_kernel, step),
        [plane],
        [basis, w_basis],
        flops=8 * narrow,
        far_out=(0,),
        scratch=[held(plane), pltpu.SemaphoreType.DMA((turns,))],
    )
    lend = call(
        functools.partial(lend_kernel, ranks),
        pieces,
        [me] + lists + [edges],
        smem=(0,),
        flops=2 * slots * edge_dev * width,
    )
    fetched = exchange(lend, -1)
    same, dhidden = call(
        functools.partial(owner_kernel, ranks),
        [shape((slots, slots)), shape((slots, width), F32)],
        [me] + lists + [upstream, w_out],
        smem=(0,),
        flops=4 * slots * edge_dev * width,
    )
    partial_rows = call(
        functools.partial(forward_kernel, ranks, step),
        pieces,
        [me, block_count] + fetched + [src, dst, filt],
        smem=(0, 1),
        far=(ranks + 4,),
        flops=2 * wide,
        scratch=[
            held(plane),
            held(plane),
            pltpu.VMEM((slots, width), F32),
            pltpu.SemaphoreType.DMA((turns,)),
        ],
    )
    home = exchange(partial_rows, 1)
    (weighted,) = call(
        functools.partial(slope_kernel, ranks, step),
        [plane],
        [me] + fetched + [src, basis, w_basis],
        smem=(0,),
        far_out=(0,),
        flops=wide + 8 * narrow,
        scratch=[held(plane), pltpu.SemaphoreType.DMA((turns,))],
    )
    back = call(
        functools.partial(return_kernel, ranks),
        pieces,
        home + [same, dhidden],
        flops=2 * slots * slots * width,
        order=[weighted],
    )
    dpartial = exchange(back, -1)
    updated, out_term = call(
        functools.partial(update_kernel, ranks, 256),
        [shape((edge_dev, width)), shape((width, width), F32)],
        [me] + lists + home + [edges, upstream, w_out],
        smem=(0,),
        flops=2 * edge_dev * width * (2 * width + slots),
        scratch=[pltpu.VMEM((edge_dev, slots), BF16), pltpu.VMEM((width, edge_dev), BF16)],
    )
    out_scale = jnp.sqrt(F32(copies * ranks * edge_dev))
    grad_w_out = reduce_large(out_term) / out_scale
    basis_term, dmessage = call(
        functools.partial(weight_kernel, ranks, step),
        [shape((basis_width, width), F32), plane],
        [me, block_count] + dpartial + [dst, filt, weighted, basis],
        smem=(0, 1),
        far=(ranks + 3, ranks + 4),
        flops=wide + narrow,
        scratch=[held(plane)] * 3 + [pltpu.SemaphoreType.DMA((2, turns))],
        order=[out_term],
    )
    basis_scale = jnp.sqrt(F32(copies * ranks * blocks * block_rows))
    grad_w_basis = reduce_small(basis_term) / basis_scale
    dfetch = call(
        functools.partial(source_kernel, ranks),
        pieces,
        [me, src, dmessage],
        smem=(0,),
        flops=wide,
    )
    (grad_edge,) = call(
        functools.partial(final_kernel, ranks, 256),
        [shape((edge_dev, width))],
        [me] + lists + exchange(dfetch, 1) + [upstream],
        smem=(0,),
        flops=2 * slots * edge_dev * width,
        scratch=[pltpu.VMEM((edge_dev, slots), BF16)],
    )
    return (updated[None], grad_edge[None], grad_w_out, grad_w_basis)


def solution(mesh):
    placed = (
        P(("groups", "dp"), "graph", None),
        P(("groups", "dp"), "graph", None),
        P(("groups", "dp"), "graph", None, None),
        P(("groups", "dp"), "graph", None, None),
        P(("groups", "dp"), "graph", None),
        P(("groups", "dp"), "graph", None),
        P(("groups", "dp"), "graph", None),
        P(("groups", "dp"), "graph"),
        P(),
        P(),
    )
    return jax.shard_map(
        per_device,
        mesh=mesh,
        in_specs=placed,
        out_specs=(
            P(("groups", "dp"), "graph", None),
            P(("groups", "dp"), "graph", None),
            P("groups", None),
            P("groups", None),
        ),
        check_vma=False,
    )
```

time: 131 us -> 119 us (0.908)
  local copies, waits for them, and re-layouts: 35.4 us -> 4.21 us
  Pallas kernels: 22.7 us -> 48.5 us
  other arithmetic: 6.53 us -> 2.89 us
  waiting for transfers between devices: 24.1 us -> 22 us
    unnamed x66 -> x36, local copies, waits for them, and re-layouts: 33.6 us -> 3.05 us
    pallas_call x10, Pallas kernels: 22.7 us -> 48.5 us  [call(): pl.pallas_call(inner if order else body, out_shape=tuple(outs), in_specs=...]
    ppermute x0 -> x15, starting transfers between devices: none -> 22.4 us  [shift(): lax.ppermute(value, axis, [(k, (k + by) % count) for k in range(count)])]
    all_to_all x5 -> x0, starting transfers between devices: 21.6 us -> none  [exchange(): lax.all_to_all(value, 'graph', split_axis=0, concat_axis=0, tiled=True)]
    all_to_all x5 -> x0, waiting for transfers between devices: 14.1 us -> none  [exchange(): lax.all_to_all(value, 'graph', split_axis=0, concat_axis=0, tiled=True)]
    ppermute x0 -> x15, waiting for transfers between devices: none -> 10.5 us  [shift(): lax.ppermute(value, axis, [(k, (k + by) % count) for k in range(count)])]
    add x2, other arithmetic: 2.26 us -> 0.1 us  [halve(): return kept + swap(away, 'dp', 1 << bit).astype(F32)]
    ppermute x16, waiting for transfers between devices: 9.97 us -> 11.5 us  [swap(): lax.ppermute(value, axis, [(k, k ^ mask) for k in range(lax.axis_size(axi...]
  transfers between devices with their start and end apart: 21 -> 31, of which waited for: 10 -> 14; matrix products, arithmetic and copies ran while one was open for 4% -> 1% of each run, Pallas kernels for 12% -> 29%
where the time goes in v3:
time: 119 us; the launch traced here: 118 us
  Pallas kernels  48.5 us (41%)
  starting transfers between devices  39.1 us (33%)
  waiting for transfers between devices  22 us (18%)
  local copies, waits for them, and re-layouts  4.21 us (4%)
  other arithmetic  2.89 us (2%)
  between operations  1.49 us (1%)
    pallas_call x10, Pallas kernels, call(): pl.pallas_call(inner if order else body, out_shape=tuple(outs), in_specs=...  48.5 us
    ppermute x15, starting transfers between devices, shift(): lax.ppermute(value, axis, [(k, (k + by) % count) for k in range(count)])  22.4 us
    ppermute x16, starting transfers between devices, swap(): lax.ppermute(value, axis, [(k, k ^ mask) for k in range(lax.axis_size(axi...  16.7 us
    ppermute x16, waiting for transfers between devices, swap(): lax.ppermute(value, axis, [(k, k ^ mask) for k in range(lax.axis_size(axi...  11.5 us
    ppermute x15, waiting for transfers between devices, shift(): lax.ppermute(value, axis, [(k, (k + by) % count) for k in range(count)])  10.5 us
    unnamed x36, local copies, waits for them, and re-layouts  3.05 us
  transfers between devices with their start and end apart: 31, of which 14 were waited for; matrix products, arithmetic and copies ran while one was open for 1% of the time, Pallas kernels for 29%

profile of v3, /device:TPU:0, one launch (start us, length us, event | category | flops | bytes accessed | tf_op | source)
XLA Modules:
  0.0 118.1 jit_solution(8462948567692741952)
XLA Ops:
  1.4 3.0 %collective-permute-start = (s32[4,128]{1,0:T(4,128)S(1)}, s32[4,128]{1,0:T(4,128)S(1)}, u32[]{:S(2)}, u32[]{:S(2)}) collective-permute-start(s32[4,128]{1,0:T(4,128)S(1)} %pad_add_fusion.refs_0_), channel_id=1, source_target_pairs={{0,4},{4,8},{8,12},{12,0},{1,5},{5,9},{9,13},{13,1},{2,6},{6,10},{... | collective-permute-start | bytes 6152 | tf_op jit(solution)/shard_map/ppermute | solution.py:245
  4.4 2.6 %collective-permute-start.1 = (s32[4,128]{1,0:T(4,128)S(1)}, s32[4,128]{1,0:T(4,128)S(1)}, u32[]{:S(2)}, u32[]{:S(2)}) collective-permute-start(s32[4,128]{1,0:T(4,128)S(1)} %pad_add_fusion.refs_0_), channel_id=1, source_target_pairs={{0,8},{4,12},{8,0},{12,4},{1,9},{5,13},{9,1},{13,5},{2,10},{6,14},... | collective-permute-start | bytes 6152 | tf_op jit(solution)/shard_map/ppermute | solution.py:245
  8.9 1.7 %collective-permute-done.2.refs_3_ = s32[4,128]{1,0:T(4,128)S(1)} collective-permute-done((s32[4,128]{1,0:T(4,128)S(1)}, s32[4,128]{1,0:T(4,128)S(1)}, u32[]{:S(2)}, u32[]{:S(2)}) %collective-permute-start.2) | collective-permute-done | bytes 2080 | tf_op jit(solution)/shard_map/ppermute | solution.py:245
  11.1 2.5 %shard_map.129 = (bf16[64,512]{1,0:T(8,128)(2,1)}, bf16[64,512]{1,0:T(8,128)(2,1)}, bf16[64,512]{1,0:T(8,128)(2,1)}, bf16[64,512]{1,0:T(8,128)(2,1)}) custom-call(s32[1]{0:T(128)} %bitcast.me.refs_0_, s32[4,128]{1,0:T(4,128)} %copy-done.11, s32[4,128]{1,0:T(4,128)} %copy-done.12, s32[4,128]{1,0:T(4,128)} %copy-done.13, s32[4,128]{1,0:T(4,128)} %copy-done.14, ...), custom_call_target="tpu_custom_call" | custom-call | flops 268435456 | bytes 1318916 | tf_op jit(solution)/shard_map/pallas_call | solution.py:42
  13.7 3.1 %collective-permute-start.3 = (bf16[64,512]{1,0:T(8,128)(2,1)}, bf16[64,512]{1,0:T(8,128)(2,1)S(1)}, u32[]{:S(2)}, u32[]{:S(2)}) collective-permute-start(bf16[64,512]{1,0:T(8,128)(2,1)} %get-tuple-element.27), channel_id=1, source_target_pairs={{0,12},{4,0},{8,4},{12,8},{1,13},{5,1},{9,5},{13,9},{2,14},{6,2},{... | collective-permute-start | bytes 196616 | tf_op jit(solution)/shard_map/ppermute | solution.py:245
  17.4 4.1 %shard_map.130.refs_6_.refs_7_ = bf16[512,4096]{1,0:T(8,128)(2,1)} custom-call(bf16[4096,128]{1,0:T(8,128)(2,1)} %bitcast.62, bf16[128,512]{1,0:T(8,128)(2,1)} %refs_6_.1), custom_call_target="tpu_custom_call" | custom-call | flops 4294967296 | bytes 5373952 | tf_op jit(solution)/shard_map/pallas_call | solution.py:42
  23.7 6.4 %shard_map.131 = (bf16[64,512]{1,0:T(8,128)(2,1)}, bf16[64,512]{1,0:T(8,128)(2,1)}, bf16[64,512]{1,0:T(8,128)(2,1)}, bf16[64,512]{1,0:T(8,128)(2,1)}) custom-call(s32[1]{0:T(128)} %bitcast.me.refs_0_, s32[1,1]{1,0:T(1,128)S(6)} %copy.18.count.refs_1_, bf16[64,512]{1,0:T(8,128)(2,1)} %get-tuple-element.26.refs_0_, bf16[64,512]{1,0:T(8,128)(2,1)} %copy-done.15, ...), custom_call_target="tpu_custom_call" | custom-call | flops 2147483648 | bytes 4751368 | tf_op jit(solution)/shard_map/pallas_call | solution.py:42
  30.1 2.1 %collective-permute-start.6 = (bf16[64,512]{1,0:T(8,128)(2,1)}, bf16[64,512]{1,0:T(8,128)(2,1)S(1)}, u32[]{:S(2)}, u32[]{:S(2)}) collective-permute-start(bf16[64,512]{1,0:T(8,128)(2,1)} %get-tuple-element.31), channel_id=1, source_target_pairs={{0,4},{4,8},{8,12},{12,0},{1,5},{5,9},{9,13},{13,1},{2,6},{6,10},{... | collective-permute-start | bytes 196616 | tf_op jit(solution)/shard_map/ppermute | solution.py:245
  33.1 1.5 %collective-permute-start.8 = (bf16[64,512]{1,0:T(8,128)(2,1)}, bf16[64,512]{1,0:T(8,128)(2,1)S(1)}, u32[]{:S(2)}, u32[]{:S(2)}) collective-permute-start(bf16[64,512]{1,0:T(8,128)(2,1)} %get-tuple-element.33), channel_id=1, source_target_pairs={{0,12},{4,0},{8,4},{12,8},{1,13},{5,1},{9,5},{13,9},{2,14},{6,2},{... | collective-permute-start | bytes 196616 | tf_op jit(solution)/shard_map/ppermute | solution.py:245
  34.7 3.4 %shard_map.133 = (bf16[256,256]{1,0:T(8,128)(2,1)}, f32[256,512]{1,0:T(8,128)}) custom-call(s32[1]{0:T(128)} %bitcast.me.refs_0_, s32[4,128]{1,0:T(4,128)} %copy-done.11, s32[4,128]{1,0:T(4,128)} %copy-done.12, s32[4,128]{1,0:T(4,128)} %copy-done.13, s32[4,128]{1,0:T(4,128)} %copy-done.14, bf16[1024,512]{1,0:T(8,128)(2,1)} %bitcast.58, bf16[512,512]{1,0:T(8,128)(2,1)} %refs_5_.1), custom_call_target="tpu_custom_call" | custom-call | flops 536870912 | bytes 2236420 | tf_op jit(solution)/shard_map/pallas_call | solution.py:42
  38.9 5.0 %shard_map.132 = (bf16[1024,512]{1,0:T(8,128)(2,1)}, f32[512,512]{1,0:T(8,128)}) custom-call(s32[1]{0:T(128)} %bitcast.me.refs_0_, s32[4,128]{1,0:T(4,128)} %copy-done.11, s32[4,128]{1,0:T(4,128)} %copy-done.12, s32[4,128]{1,0:T(4,128)} %copy-done.13, s32[4,128]{1,0:T(4,128)} %copy-done.14, bf16[64,512]{1,0:T(8,128)(2,1)} %get-tuple-element.30.refs_4_.refs_0_, ...), custom_call_target="tpu_custom_call" | custom-call | flops 1342177280 | bytes 4988932 | tf_op jit(solution)/shard_map/pallas_call | solution.py:42
  45.1 5.8 %shard_map.134.refs_6_.refs_8_ = bf16[512,4096]{1,0:T(8,128)(2,1)} custom-call(s32[1]{0:T(128)} %bitcast.me.refs_0_, bf16[64,512]{1,0:T(8,128)(2,1)} %get-tuple-element.26.refs_0_, bf16[64,512]{1,0:T(8,128)(2,1)} %copy-done.15, bf16[64,512]{1,0:T(8,128)(2,1)} %copy-done.16, bf16[64,512]{1,0:T(8,128)(2,1)} %copy-done.17, s32[32,128]{1,0:T(8,128)} %bitcast.74, ...), custom_call_target="tpu_custom_call" | custom-call | flops 5368709120 | bytes 5652484 | tf_op jit(solution)/shard_map/pallas_call | solution.py:42
  50.8 2.3 %shard_map.135 = (bf16[64,512]{1,0:T(8,128)(2,1)}, bf16[64,512]{1,0:T(8,128)(2,1)}, bf16[64,512]{1,0:T(8,128)(2,1)}, bf16[64,512]{1,0:T(8,128)(2,1)}) custom-call(bf16[64,512]{1,0:T(8,128)(2,1)} %get-tuple-element.30.refs_4_.refs_0_, bf16[64,512]{1,0:T(8,128)(2,1)} %copy-done.2, bf16[64,512]{1,0:T(8,128)(2,1)} %copy-done.3, bf16[64,512]{1,0:T(8,128)(2,1)} %copy-done.4, ...), custom_call_target="tpu_custom_call" | custom-call | flops 67108864 | bytes 5373952 | tf_op jit(solution)/shard_map/pallas_call | solution.py:42
  53.1 2.6 %collective-permute-start.9 = (bf16[64,512]{1,0:T(8,128)(2,1)}, bf16[64,512]{1,0:T(8,128)(2,1)S(1)}, u32[]{:S(2)}, u32[]{:S(2)}) collective-permute-start(bf16[64,512]{1,0:T(8,128)(2,1)} %get-tuple-element.38), channel_id=1, source_target_pairs={{0,12},{4,0},{8,4},{12,8},{1,13},{5,1},{9,5},{13,9},{2,14},{6,2},{... | collective-permute-start | bytes 196616 | tf_op jit(solution)/shard_map/ppermute | solution.py:245
  56.6 1.6 %collective-permute-start.16 = (bf16[128,512]{1,0:T(8,128)(2,1)S(1)}, bf16[128,512]{1,0:T(8,128)(2,1)S(1)}, u32[]{:S(2)}, u32[]{:S(2)}) collective-permute-start(bf16[128,512]{1,0:T(8,128)(2,1)S(1)} %fusion.1), channel_id=1, source_target_pairs={{0,2},{1,3},{2,0},{3,1},{4,6},{5,7},{6,4},{7,5},{8,10},{9,11},{10,... | collective-permute-start | bytes 393224 | tf_op jit(solution)/shard_map/ppermute | solution.py:240
  58.5 4.4 %collective-permute-done.10.refs_4_ = bf16[64,512]{1,0:T(8,128)(2,1)S(1)} collective-permute-done((bf16[64,512]{1,0:T(8,128)(2,1)}, bf16[64,512]{1,0:T(8,128)(2,1)S(1)}, u32[]{:S(2)}, u32[]{:S(2)}) %collective-permute-start.10) | collective-permute-done | bytes 65568 | tf_op jit(solution)/shard_map/ppermute | solution.py:245
  63.6 11.9 %shard_map.136 = (f32[128,512]{1,0:T(8,128)}, bf16[512,4096]{1,0:T(8,128)(2,1)}) custom-call(s32[1]{0:T(128)} %bitcast.me.refs_0_, s32[1,1]{1,0:T(1,128)S(6)} %copy.18.count.refs_1_, bf16[64,512]{1,0:T(8,128)(2,1)} %get-tuple-element.37.refs_2_, bf16[64,512]{1,0:T(8,128)(2,1)} %copy-done.5, bf16[64,512]{1,0:T(8,128)(2,1)} %copy-done.6, ...), custom_call_target="tpu_custom_call" | custom-call | flops 1610612736 | bytes 15220744 | tf_op jit(solution)/shard_map/pallas_call | solution.py:42
  75.5 4.2 %shard_map.137 = (bf16[64,512]{1,0:T(8,128)(2,1)}, bf16[64,512]{1,0:T(8,128)(2,1)}, bf16[64,512]{1,0:T(8,128)(2,1)}, bf16[64,512]{1,0:T(8,128)(2,1)}) custom-call(s32[1]{0:T(128)} %bitcast.me.refs_0_, s32[32,128]{1,0:T(8,128)} %bitcast.75, bf16[512,4096]{1,0:T(8,128)(2,1)} %get-tuple-element.42.dmessage), custom_call_target="tpu_custom_call" | custom-call | flops 1073741824 | bytes 4472836 | tf_op jit(solution)/shard_map/pallas_call | solution.py:42
  80.0 1.9 %collective-permute-start.13 = (bf16[64,512]{1,0:T(8,128)(2,1)}, bf16[64,512]{1,0:T(8,128)(2,1)S(1)}, u32[]{:S(2)}, u32[]{:S(2)}) collective-permute-start(bf16[64,512]{1,0:T(8,128)(2,1)} %get-tuple-element.45), channel_id=1, source_target_pairs={{0,8},{4,12},{8,0},{12,4},{1,9},{5,13},{9,1},{13,5},{2,10},{6,14},... | collective-permute-start | bytes 196616 | tf_op jit(solution)/shard_map/ppermute | solution.py:245
  81.9 2.5 %collective-permute-start.19 = (bf16[32,512]{1,0:T(8,128)(2,1)S(1)}, bf16[32,512]{1,0:T(8,128)(2,1)S(1)}, u32[]{:S(2)}, u32[]{:S(2)}) collective-permute-start(bf16[32,512]{1,0:T(8,128)(2,1)S(1)} %get-tuple-element.51), channel_id=1, source_target_pairs={{0,12},{4,8},{8,4},{12,0},{1,13},{5,9},{9,5},{13,1},{2,14},{6,10},... | collective-permute-start | bytes 98312 | tf_op jit(solution)/shard_map/ppermute | solution.py:240
  86.4 1.6 %collective-permute-done.19 = bf16[32,512]{1,0:T(8,128)(2,1)S(1)} collective-permute-done((bf16[32,512]{1,0:T(8,128)(2,1)S(1)}, bf16[32,512]{1,0:T(8,128)(2,1)S(1)}, u32[]{:S(2)}, u32[]{:S(2)}) %collective-permute-start.19) | collective-permute-done | bytes 32800 | tf_op jit(solution)/shard_map/ppermute | solution.py:240
  88.0 2.4 %collective-permute-done.18 = bf16[32,512]{1,0:T(8,128)(2,1)S(1)} collective-permute-done((bf16[32,512]{1,0:T(8,128)(2,1)S(1)}, bf16[32,512]{1,0:T(8,128)(2,1)S(1)}, u32[]{:S(2)}, u32[]{:S(2)}) %collective-permute-start.18) | collective-permute-done | bytes 32800 | tf_op jit(solution)/shard_map/ppermute | solution.py:240
  90.7 1.6 %collective-permute-start.26 = (bf16[64,512]{1,0:T(8,128)(2,1)S(1)}, bf16[64,512]{1,0:T(8,128)(2,1)S(1)}, u32[]{:S(2)}, u32[]{:S(2)}) collective-permute-start(bf16[64,512]{1,0:T(8,128)(2,1)S(1)} %fusion.2), channel_id=1, source_target_pairs={{0,2},{1,3},{2,0},{3,1},{4,6},{5,7},{6,4},{7,5},{8,10},{9,11},{10,... | collective-permute-start | bytes 196616 | tf_op jit(solution)/shard_map/ppermute | solution.py:240
  92.3 2.2 %collective-permute-start.21 = (bf16[32,512]{1,0:T(8,128)(2,1)S(1)}, bf16[32,512]{1,0:T(8,128)(2,1)S(1)}, u32[]{:S(2)}, u32[]{:S(2)}) collective-permute-start(bf16[32,512]{1,0:T(8,128)(2,1)S(1)} %get-tuple-element.49), channel_id=1, source_target_pairs={{0,8},{4,12},{8,0},{12,4},{1,9},{5,13},{9,1},{13,5},{2,10},{6,14},... | collective-permute-start | bytes 98312 | tf_op jit(solution)/shard_map/ppermute | solution.py:240
  94.4 2.0 %collective-permute-start.22 = (bf16[32,512]{1,0:T(8,128)(2,1)S(1)}, bf16[32,512]{1,0:T(8,128)(2,1)S(1)}, u32[]{:S(2)}, u32[]{:S(2)}) collective-permute-start(bf16[32,512]{1,0:T(8,128)(2,1)S(1)} %get-tuple-element.49), channel_id=1, source_target_pairs={{0,12},{4,8},{8,4},{12,0},{1,13},{5,9},{9,5},{13,1},{2,14},{6,10},... | collective-permute-start | bytes 98312 | tf_op jit(solution)/shard_map/ppermute | solution.py:240
  97.2 2.9 %collective-permute-done.22 = bf16[32,512]{1,0:T(8,128)(2,1)S(1)} collective-permute-done((bf16[32,512]{1,0:T(8,128)(2,1)S(1)}, bf16[32,512]{1,0:T(8,128)(2,1)S(1)}, u32[]{:S(2)}, u32[]{:S(2)}) %collective-permute-start.22) | collective-permute-done | bytes 32800 | tf_op jit(solution)/shard_map/ppermute | solution.py:240
  101.6 2.0 %collective-permute-start.29 = (bf16[64,512]{1,0:T(8,128)(2,1)S(1)}, bf16[64,512]{1,0:T(8,128)(2,1)S(1)}, u32[]{:S(2)}, u32[]{:S(2)}) collective-permute-start(bf16[64,512]{1,0:T(8,128)(2,1)S(1)} %add_convert_fusion.1), channel_id=1, source_target_pairs={{0,12},{4,8},{8,4},{12,0},{1,13},{5,9},{9,5},{13,1},{2,14},{6,10},... | collective-permute-start | bytes 196616 | tf_op jit(solution)/shard_map/ppermute | solution.py:240
  103.6 1.5 %collective-permute-done.23 = bf16[128,512]{1,0:T(8,128)(2,1)S(1)} collective-permute-done((bf16[128,512]{1,0:T(8,128)(2,1)S(1)}, bf16[128,512]{1,0:T(8,128)(2,1)S(1)}, u32[]{:S(2)}, u32[]{:S(2)}) %collective-permute-start.23) | collective-permute-done | bytes 131104 | tf_op jit(solution)/shard_map/ppermute | solution.py:240
  106.2 2.0 %collective-permute-done.29 = bf16[64,512]{1,0:T(8,128)(2,1)S(1)} collective-permute-done((bf16[64,512]{1,0:T(8,128)(2,1)S(1)}, bf16[64,512]{1,0:T(8,128)(2,1)S(1)}, u32[]{:S(2)}, u32[]{:S(2)}) %collective-permute-start.29) | collective-permute-done | bytes 65568 | tf_op jit(solution)/shard_map/ppermute | solution.py:240
  108.2 1.5 %collective-permute-start.14 = (bf16[64,512]{1,0:T(8,128)(2,1)}, bf16[64,512]{1,0:T(8,128)(2,1)S(1)}, u32[]{:S(2)}, u32[]{:S(2)}) collective-permute-start(bf16[64,512]{1,0:T(8,128)(2,1)} %get-tuple-element.46), channel_id=1, source_target_pairs={{0,12},{4,0},{8,4},{12,8},{1,13},{5,1},{9,5},{13,9},{2,14},{6,2},{... | collective-permute-start | bytes 196616 | tf_op jit(solution)/shard_map/ppermute | solution.py:245
  110.3 2.3 %collective-permute-done.14.refs_7_ = bf16[64,512]{1,0:T(8,128)(2,1)S(1)} collective-permute-done((bf16[64,512]{1,0:T(8,128)(2,1)}, bf16[64,512]{1,0:T(8,128)(2,1)S(1)}, u32[]{:S(2)}, u32[]{:S(2)}) %collective-permute-start.14) | collective-permute-done | bytes 65568 | tf_op jit(solution)/shard_map/ppermute | solution.py:245
  113.2 3.0 %shard_map.138 = bf16[1024,512]{1,0:T(8,128)(2,1)} custom-call(s32[1]{0:T(128)} %bitcast.me.refs_0_, s32[4,128]{1,0:T(4,128)} %copy-done.11, s32[4,128]{1,0:T(4,128)} %copy-done.12, s32[4,128]{1,0:T(4,128)} %copy-done.13, s32[4,128]{1,0:T(4,128)} %copy-done.14, bf16[64,512]{1,0:T(8,128)(2,1)} %get-tuple-element.43.refs_4_, bf16[64,512]{1,0:T(8,128)(2,1)} %copy-done.8, ...), custom_call_target="tpu_custom_call" | custom-call | flops 268435456 | bytes 2367492 | tf_op jit(solution)/shard_map/pallas_call | solution.py:42
  (94 shorter events, 19.3 us)
Async XLA Ops:
  1.4 7.0 %collective-permute-start = (s32[4,128]{1,0:T(4,128)S(1)}, s32[4,128]{1,0:T(4,128)S(1)}, u32[]{:S(2)}, u32[]{:S(2)}) collective-permute-start(s32[4,128]{1,0:T(4,128)S(1)} %pad_add_fusion.refs_0_), channel_id=1, source_target_pairs={{0,4},{4,8},{8,12},{12,0},{1,5},{5,9},{9,13},{13,1},{2,6},{6,10},{... | collective-permute-start | bytes 6152 | tf_op jit(solution)/shard_map/ppermute | solution.py:245
  4.4 4.5 %collective-permute-start.1 = (s32[4,128]{1,0:T(4,128)S(1)}, s32[4,128]{1,0:T(4,128)S(1)}, u32[]{:S(2)}, u32[]{:S(2)}) collective-permute-start(s32[4,128]{1,0:T(4,128)S(1)} %pad_add_fusion.refs_0_), channel_id=1, source_target_pairs={{0,8},{4,12},{8,0},{12,4},{1,9},{5,13},{9,1},{13,5},{2,10},{6,14},... | collective-permute-start | bytes 6152 | tf_op jit(solution)/shard_map/ppermute | solution.py:245
  7.0 3.6 %collective-permute-start.2 = (s32[4,128]{1,0:T(4,128)S(1)}, s32[4,128]{1,0:T(4,128)S(1)}, u32[]{:S(2)}, u32[]{:S(2)}) collective-permute-start(s32[4,128]{1,0:T(4,128)S(1)} %pad_add_fusion.refs_0_), channel_id=1, source_target_pairs={{0,12},{4,0},{8,4},{12,8},{1,13},{5,1},{9,5},{13,9},{2,14},{6,2},{... | collective-permute-start | bytes 6152 | tf_op jit(solution)/shard_map/ppermute | solution.py:245
  13.7 8.5 %collective-permute-start.3 = (bf16[64,512]{1,0:T(8,128)(2,1)}, bf16[64,512]{1,0:T(8,128)(2,1)S(1)}, u32[]{:S(2)}, u32[]{:S(2)}) collective-permute-start(bf16[64,512]{1,0:T(8,128)(2,1)} %get-tuple-element.27), channel_id=1, source_target_pairs={{0,12},{4,0},{8,4},{12,8},{1,13},{5,1},{9,5},{13,9},{2,14},{6,2},{... | collective-permute-start | bytes 196616 | tf_op jit(solution)/shard_map/ppermute | solution.py:245
  16.8 5.4 %collective-permute-start.4 = (bf16[64,512]{1,0:T(8,128)(2,1)}, bf16[64,512]{1,0:T(8,128)(2,1)S(1)}, u32[]{:S(2)}, u32[]{:S(2)}) collective-permute-start(bf16[64,512]{1,0:T(8,128)(2,1)} %get-tuple-element.28), channel_id=1, source_target_pairs={{0,8},{4,12},{8,0},{12,4},{1,9},{5,13},{9,1},{13,5},{2,10},{6,14},... | collective-permute-start | bytes 196616 | tf_op jit(solution)/shard_map/ppermute | solution.py:245
  16.8 6.3 %collective-permute-start.5 = (bf16[64,512]{1,0:T(8,128)(2,1)}, bf16[64,512]{1,0:T(8,128)(2,1)S(1)}, u32[]{:S(2)}, u32[]{:S(2)}) collective-permute-start(bf16[64,512]{1,0:T(8,128)(2,1)} %get-tuple-element.29), channel_id=1, source_target_pairs={{0,4},{4,8},{8,12},{12,0},{1,5},{5,9},{9,13},{13,1},{2,6},{6,10},{... | collective-permute-start | bytes 196616 | tf_op jit(solution)/shard_map/ppermute | solution.py:245
  30.1 7.9 %collective-permute-start.6 = (bf16[64,512]{1,0:T(8,128)(2,1)}, bf16[64,512]{1,0:T(8,128)(2,1)S(1)}, u32[]{:S(2)}, u32[]{:S(2)}) collective-permute-start(bf16[64,512]{1,0:T(8,128)(2,1)} %get-tuple-element.31), channel_id=1, source_target_pairs={{0,4},{4,8},{8,12},{12,0},{1,5},{5,9},{9,13},{13,1},{2,6},{6,10},{... | collective-permute-start | bytes 196616 | tf_op jit(solution)/shard_map/ppermute | solution.py:245
  32.2 5.8 %collective-permute-start.7 = (bf16[64,512]{1,0:T(8,128)(2,1)}, bf16[64,512]{1,0:T(8,128)(2,1)S(1)}, u32[]{:S(2)}, u32[]{:S(2)}) collective-permute-start(bf16[64,512]{1,0:T(8,128)(2,1)} %get-tuple-element.32), channel_id=1, source_target_pairs={{0,8},{4,12},{8,0},{12,4},{1,9},{5,13},{9,1},{13,5},{2,10},{6,14},... | collective-permute-start | bytes 196616 | tf_op jit(solution)/shard_map/ppermute | solution.py:245
  33.1 5.2 %collective-permute-start.8 = (bf16[64,512]{1,0:T(8,128)(2,1)}, bf16[64,512]{1,0:T(8,128)(2,1)S(1)}, u32[]{:S(2)}, u32[]{:S(2)}) collective-permute-start(bf16[64,512]{1,0:T(8,128)(2,1)} %get-tuple-element.33), channel_id=1, source_target_pairs={{0,12},{4,0},{8,4},{12,8},{1,13},{5,1},{9,5},{13,9},{2,14},{6,2},{... | collective-permute-start | bytes 196616 | tf_op jit(solution)/shard_map/ppermute | solution.py:245
  45.0 11.5 %collective-permute-start.15 = (bf16[256,512]{1,0:T(8,128)(2,1)S(1)}, bf16[256,512]{1,0:T(8,128)(2,1)S(1)}, u32[]{:S(2)}, u32[]{:S(2)}) collective-permute-start(bf16[256,512]{1,0:T(8,128)(2,1)S(1)} %fusion), channel_id=1, source_target_pairs={{0,1},{1,0},{2,3},{3,2},{4,5},{5,4},{6,7},{7,6},{8,9},{9,8},{10,11... | collective-permute-start | bytes 786440 | tf_op jit(solution)/shard_map/ppermute | solution.py:240
  53.1 5.4 %collective-permute-start.9 = (bf16[64,512]{1,0:T(8,128)(2,1)}, bf16[64,512]{1,0:T(8,128)(2,1)S(1)}, u32[]{:S(2)}, u32[]{:S(2)}) collective-permute-start(bf16[64,512]{1,0:T(8,128)(2,1)} %get-tuple-element.38), channel_id=1, source_target_pairs={{0,12},{4,0},{8,4},{12,8},{1,13},{5,1},{9,5},{13,9},{2,14},{6,2},{... | collective-permute-start | bytes 196616 | tf_op jit(solution)/shard_map/ppermute | solution.py:245
  55.8 7.2 %collective-permute-start.10 = (bf16[64,512]{1,0:T(8,128)(2,1)}, bf16[64,512]{1,0:T(8,128)(2,1)S(1)}, u32[]{:S(2)}, u32[]{:S(2)}) collective-permute-start(bf16[64,512]{1,0:T(8,128)(2,1)} %get-tuple-element.39), channel_id=1, source_target_pairs={{0,8},{4,12},{8,0},{12,4},{1,9},{5,13},{9,1},{13,5},{2,10},{6,14},... | collective-permute-start | bytes 196616 | tf_op jit(solution)/shard_map/ppermute | solution.py:245
  55.8 7.2 %collective-permute-start.11 = (bf16[64,512]{1,0:T(8,128)(2,1)}, bf16[64,512]{1,0:T(8,128)(2,1)S(1)}, u32[]{:S(2)}, u32[]{:S(2)}) collective-permute-start(bf16[64,512]{1,0:T(8,128)(2,1)} %get-tuple-element.40), channel_id=1, source_target_pairs={{0,4},{4,8},{8,12},{12,0},{1,5},{5,9},{9,13},{13,1},{2,6},{6,10},{... | collective-permute-start | bytes 196616 | tf_op jit(solution)/shard_map/ppermute | solution.py:245
  56.6 25.3 %collective-permute-start.16 = (bf16[128,512]{1,0:T(8,128)(2,1)S(1)}, bf16[128,512]{1,0:T(8,128)(2,1)S(1)}, u32[]{:S(2)}, u32[]{:S(2)}) collective-permute-start(bf16[128,512]{1,0:T(8,128)(2,1)S(1)} %fusion.1), channel_id=1, source_target_pairs={{0,2},{1,3},{2,0},{3,1},{4,6},{5,7},{6,4},{7,5},{8,10},{9,11},{10,... | collective-permute-start | bytes 393224 | tf_op jit(solution)/shard_map/ppermute | solution.py:240
  75.5 10.9 %copy-start.1 = (f32[128,512]{1,0:T(8,128)S(1)}, f32[128,512]{1,0:T(8,128)}, u32[]{:S(2)}) copy-start(f32[128,512]{1,0:T(8,128)} %get-tuple-element.47) | copy-start | bytes 786436
  79.6 30.7 %collective-permute-start.12 = (bf16[64,512]{1,0:T(8,128)(2,1)}, bf16[64,512]{1,0:T(8,128)(2,1)S(1)}, u32[]{:S(2)}, u32[]{:S(2)}) collective-permute-start(bf16[64,512]{1,0:T(8,128)(2,1)} %get-tuple-element.44), channel_id=1, source_target_pairs={{0,4},{4,8},{8,12},{12,0},{1,5},{5,9},{9,13},{13,1},{2,6},{6,10},{... | collective-permute-start | bytes 196616 | tf_op jit(solution)/shard_map/ppermute | solution.py:245
  80.0 30.3 %collective-permute-start.13 = (bf16[64,512]{1,0:T(8,128)(2,1)}, bf16[64,512]{1,0:T(8,128)(2,1)S(1)}, u32[]{:S(2)}, u32[]{:S(2)}) collective-permute-start(bf16[64,512]{1,0:T(8,128)(2,1)} %get-tuple-element.45), channel_id=1, source_target_pairs={{0,8},{4,12},{8,0},{12,4},{1,9},{5,13},{9,1},{13,5},{2,10},{6,14},... | collective-permute-start | bytes 196616 | tf_op jit(solution)/shard_map/ppermute | solution.py:245
  81.9 6.0 %collective-permute-start.19 = (bf16[32,512]{1,0:T(8,128)(2,1)S(1)}, bf16[32,512]{1,0:T(8,128)(2,1)S(1)}, u32[]{:S(2)}, u32[]{:S(2)}) collective-permute-start(bf16[32,512]{1,0:T(8,128)(2,1)S(1)} %get-tuple-element.51), channel_id=1, source_target_pairs={{0,12},{4,8},{8,4},{12,0},{1,13},{5,9},{9,5},{13,1},{2,14},{6,10},... | collective-permute-start | bytes 98312 | tf_op jit(solution)/shard_map/ppermute | solution.py:240
  84.4 5.9 %collective-permute-start.18 = (bf16[32,512]{1,0:T(8,128)(2,1)S(1)}, bf16[32,512]{1,0:T(8,128)(2,1)S(1)}, u32[]{:S(2)}, u32[]{:S(2)}) collective-permute-start(bf16[32,512]{1,0:T(8,128)(2,1)S(1)} %get-tuple-element.52), channel_id=1, source_target_pairs={{0,8},{4,12},{8,0},{12,4},{1,9},{5,13},{9,1},{13,5},{2,10},{6,14},... | collective-permute-start | bytes 98312 | tf_op jit(solution)/shard_map/ppermute | solution.py:240
  85.6 4.7 %collective-permute-start.17 = (bf16[32,512]{1,0:T(8,128)(2,1)S(1)}, bf16[32,512]{1,0:T(8,128)(2,1)S(1)}, u32[]{:S(2)}, u32[]{:S(2)}) collective-permute-start(bf16[32,512]{1,0:T(8,128)(2,1)S(1)} %get-tuple-element.50), channel_id=1, source_target_pairs={{0,4},{4,0},{8,12},{12,8},{1,5},{5,1},{9,13},{13,9},{2,6},{6,2},{1... | collective-permute-start | bytes 98312 | tf_op jit(solution)/shard_map/ppermute | solution.py:240
  88.0 2.7 %collective-permute-start.25 = (bf16[64,512]{1,0:T(8,128)(2,1)S(1)}, bf16[64,512]{1,0:T(8,128)(2,1)S(1)}, u32[]{:S(2)}, u32[]{:S(2)}) collective-permute-start(bf16[64,512]{1,0:T(8,128)(2,1)S(1)} %fusion.3), channel_id=1, source_target_pairs={{0,1},{1,0},{2,3},{3,2},{4,5},{5,4},{6,7},{7,6},{8,9},{9,8},{10,11... | collective-permute-start | bytes 196616 | tf_op jit(solution)/shard_map/ppermute | solution.py:240
  90.4 4.0 %collective-permute-start.20 = (bf16[32,512]{1,0:T(8,128)(2,1)S(1)}, bf16[32,512]{1,0:T(8,128)(2,1)S(1)}, u32[]{:S(2)}, u32[]{:S(2)}) collective-permute-start(bf16[32,512]{1,0:T(8,128)(2,1)S(1)} %get-tuple-element.49), channel_id=1, source_target_pairs={{0,4},{4,0},{8,12},{12,8},{1,5},{5,1},{9,13},{13,9},{2,6},{6,2},{1... | collective-permute-start | bytes 98312 | tf_op jit(solution)/shard_map/ppermute | solution.py:240
  90.7 10.9 %collective-permute-start.26 = (bf16[64,512]{1,0:T(8,128)(2,1)S(1)}, bf16[64,512]{1,0:T(8,128)(2,1)S(1)}, u32[]{:S(2)}, u32[]{:S(2)}) collective-permute-start(bf16[64,512]{1,0:T(8,128)(2,1)S(1)} %fusion.2), channel_id=1, source_target_pairs={{0,2},{1,3},{2,0},{3,1},{4,6},{5,7},{6,4},{7,5},{8,10},{9,11},{10,... | collective-permute-start | bytes 196616 | tf_op jit(solution)/shard_map/ppermute | solution.py:240
  92.3 5.0 %collective-permute-start.21 = (bf16[32,512]{1,0:T(8,128)(2,1)S(1)}, bf16[32,512]{1,0:T(8,128)(2,1)S(1)}, u32[]{:S(2)}, u32[]{:S(2)}) collective-permute-start(bf16[32,512]{1,0:T(8,128)(2,1)S(1)} %get-tuple-element.49), channel_id=1, source_target_pairs={{0,8},{4,12},{8,0},{12,4},{1,9},{5,13},{9,1},{13,5},{2,10},{6,14},... | collective-permute-start | bytes 98312 | tf_op jit(solution)/shard_map/ppermute | solution.py:240
  94.4 5.7 %collective-permute-start.22 = (bf16[32,512]{1,0:T(8,128)(2,1)S(1)}, bf16[32,512]{1,0:T(8,128)(2,1)S(1)}, u32[]{:S(2)}, u32[]{:S(2)}) collective-permute-start(bf16[32,512]{1,0:T(8,128)(2,1)S(1)} %get-tuple-element.49), channel_id=1, source_target_pairs={{0,12},{4,8},{8,4},{12,0},{1,13},{5,9},{9,5},{13,1},{2,14},{6,10},... | collective-permute-start | bytes 98312 | tf_op jit(solution)/shard_map/ppermute | solution.py:240
  100.2 5.0 %collective-permute-start.23 = (bf16[128,512]{1,0:T(8,128)(2,1)S(1)}, bf16[128,512]{1,0:T(8,128)(2,1)S(1)}, u32[]{:S(2)}, u32[]{:S(2)}) collective-permute-start(bf16[128,512]{1,0:T(8,128)(2,1)S(1)} %bitcast.67), channel_id=1, source_target_pairs={{0,2},{1,3},{2,0},{3,1},{4,6},{5,7},{6,4},{7,5},{8,10},{9,11},{10,... | collective-permute-start | bytes 393224 | tf_op jit(solution)/shard_map/ppermute | solution.py:240
  101.6 6.5 %collective-permute-start.29 = (bf16[64,512]{1,0:T(8,128)(2,1)S(1)}, bf16[64,512]{1,0:T(8,128)(2,1)S(1)}, u32[]{:S(2)}, u32[]{:S(2)}) collective-permute-start(bf16[64,512]{1,0:T(8,128)(2,1)S(1)} %add_convert_fusion.1), channel_id=1, source_target_pairs={{0,12},{4,8},{8,4},{12,0},{1,13},{5,9},{9,5},{13,1},{2,14},{6,10},... | collective-permute-start | bytes 196616 | tf_op jit(solution)/shard_map/ppermute | solution.py:240
  103.6 6.1 %collective-permute-start.28 = (bf16[64,512]{1,0:T(8,128)(2,1)S(1)}, bf16[64,512]{1,0:T(8,128)(2,1)S(1)}, u32[]{:S(2)}, u32[]{:S(2)}) collective-permute-start(bf16[64,512]{1,0:T(8,128)(2,1)S(1)} %add_convert_fusion.1), channel_id=1, source_target_pairs={{0,8},{4,12},{8,0},{12,4},{1,9},{5,13},{9,1},{13,5},{2,10},{6,14},... | collective-permute-start | bytes 196616 | tf_op jit(solution)/shard_map/ppermute | solution.py:240
  105.1 4.9 %collective-permute-start.27 = (bf16[64,512]{1,0:T(8,128)(2,1)S(1)}, bf16[64,512]{1,0:T(8,128)(2,1)S(1)}, u32[]{:S(2)}, u32[]{:S(2)}) collective-permute-start(bf16[64,512]{1,0:T(8,128)(2,1)S(1)} %add_convert_fusion.1), channel_id=1, source_target_pairs={{0,4},{4,0},{8,12},{12,8},{1,5},{5,1},{9,13},{13,9},{2,6},{6,2},{1... | collective-permute-start | bytes 196616 | tf_op jit(solution)/shard_map/ppermute | solution.py:240
  108.2 4.5 %collective-permute-start.14 = (bf16[64,512]{1,0:T(8,128)(2,1)}, bf16[64,512]{1,0:T(8,128)(2,1)S(1)}, u32[]{:S(2)}, u32[]{:S(2)}) collective-permute-start(bf16[64,512]{1,0:T(8,128)(2,1)} %get-tuple-element.46), channel_id=1, source_target_pairs={{0,12},{4,0},{8,4},{12,8},{1,13},{5,1},{9,5},{13,9},{2,14},{6,2},{... | collective-permute-start | bytes 196616 | tf_op jit(solution)/shard_map/ppermute | solution.py:245
  109.7 7.3 %collective-permute-start.24 = (bf16[256,512]{1,0:T(8,128)(2,1)S(1)}, bf16[256,512]{1,0:T(8,128)(2,1)S(1)}, u32[]{:S(2)}, u32[]{:S(2)}) collective-permute-start(bf16[256,512]{1,0:T(8,128)(2,1)S(1)} %maximum_select_fusion.1), channel_id=1, source_target_pairs={{0,1},{1,0},{2,3},{3,2},{4,5},{5,4},{6,7},{7,6},{8,9},{9,8},{10,11... | collective-permute-start | bytes 786440 | tf_op jit(solution)/shard_map/ppermute | solution.py:240
  110.1 6.2 %collective-permute-start.30 = (bf16[64,512]{1,0:T(8,128)(2,1)S(1)}, bf16[64,512]{1,0:T(8,128)(2,1)S(1)}, u32[]{:S(2)}, u32[]{:S(2)}) collective-permute-start(bf16[64,512]{1,0:T(8,128)(2,1)S(1)} %add_convert_fusion), channel_id=1, source_target_pairs={{0,1},{1,0},{2,3},{3,2},{4,5},{5,4},{6,7},{7,6},{8,9},{9,8},{10,11... | collective-permute-start | bytes 196616 | tf_op jit(solution)/shard_map/ppermute | solution.py:240
  (17 other events, 34.6 us)

commit v4 on v3

v4 whole, which is shorter than its diff:
```python
import functools

import jax
import jax.numpy as jnp
from jax import lax
from jax.experimental import pallas as pl
from jax.experimental.pallas import tpu as pltpu
from jax.sharding import PartitionSpec as P

BF16 = jnp.bfloat16
F32 = jnp.float32
VMEM = pl.BlockSpec(memory_space=pltpu.VMEM)
SMEM = pl.BlockSpec(memory_space=pltpu.SMEM)
ANY = pl.BlockSpec(memory_space=pl.ANY)
NN = (((1,), (0,)), ((), ()))
NT = (((1,), (1,)), ((), ()))


def dot(a, b, dims=NN):
    return lax.dot_general(a, b, dims, preferred_element_type=F32)


def silu_parts(value):
    sig = 0.5 * jnp.tanh(0.5 * value) + 0.5
    act = value * sig
    return act, sig + act * (1.0 - sig)


def call(body, outs, args, flops=0, scratch=(), smem=(), far=(), far_out=(), order=()):
    args = list(args) + list(order)
    moved = sum(a.size * a.dtype.itemsize for a in args) + sum(
        o.size * o.dtype.itemsize for o in outs
    )
    keep = len(args) - len(order)
    specs = [
        SMEM if i in smem else ANY if i in far or i >= keep else VMEM for i in range(len(args))
    ]

    def inner(*refs):
        body(*refs[:keep], *refs[len(args) :])

    return pl.pallas_call(
        inner if order else body,
        out_shape=tuple(outs),
        in_specs=specs,
        out_specs=tuple(ANY if i in far_out else VMEM for i in range(len(outs))),
        scratch_shapes=list(scratch),
        cost_estimate=pl.CostEstimate(flops=flops, bytes_accessed=moved, transcendentals=0),
        compiler_params=pltpu.CompilerParams(vmem_limit_bytes=58 << 20),
    )(*args)


def shape(dims, dtype=BF16):
    return jax.ShapeDtypeStruct(dims, dtype)


def held(array):
    return pltpu.VMEM(array.shape, array.dtype)


def lane_copies(source, target, sems, step):
    return [
        pltpu.make_async_copy(
            source.at[:, pl.ds(i * step, step)], target.at[:, pl.ds(i * step, step)], sems.at[i]
        )
        for i in range(target.shape[1] // step)
    ]


def started(copies):
    for copy in copies:
        copy.start()
    return copies


def waited(copies):
    for copy in copies:
        copy.wait()


def loads(sources, targets, sems):
    return started(
        [pltpu.make_async_copy(a, b, sems.at[i]) for i, (a, b) in enumerate(zip(sources, targets))]
    )


def hot_lanes(index, first, count, slots, dead=None):
    block = index.shape[1]
    rows = lax.broadcasted_iota(jnp.int32, (slots, block), 0)
    parts = []
    for b in range(first, first + count):
        slot = index[pl.ds(b, 1), :]
        if dead is not None:
            slot = jnp.where(b < dead, slot, -1)
        parts.append(jnp.where(rows == slot, 1.0, 0.0).astype(BF16))
    return jnp.concatenate(parts, axis=1)


def turned(index, per_owner, ranks, me):
    slot = index[...] - me * per_owner
    return jnp.where(slot < 0, slot + ranks * per_owner, slot)


def gathered(pieces):
    return jnp.concatenate([p[...] for p in pieces], axis=0)


def scattered(value, outs):
    per = outs[0].shape[0]
    for s, out in enumerate(outs):
        out[...] = value[s * per : (s + 1) * per]


def columns_of(lists, me, kept, per_owner):
    parts = []
    for ref in lists:
        row = ref[pl.ds(me, 1), :].astype(F32)
        column = jnp.broadcast_to(row, (8, row.shape[1])).T[:, :1]
        parts.append(column[per_owner : 2 * per_owner] if kept else column[:per_owner])
    return jnp.concatenate(parts, axis=0)


def hot_rows(column, edge_dev):
    edges = lax.broadcasted_iota(jnp.int32, (column.shape[0], edge_dev), 1).astype(F32)
    return jnp.where(column == edges, 1.0, 0.0).astype(BF16)


def prepare_kernel(step, part, basis, weight, filt, slope, basis_v, filt_v, slope_v, in_sems, sems):
    rows = basis_v.shape[0]
    arrive = loads([basis.at[pl.ds(part * rows, rows), :]], [basis_v], in_sems)
    weight_t = weight[...].T
    waited(arrive)
    leave = lane_copies(filt_v, filt, sems.at[0], step), lane_copies(slope_v, slope, sems.at[1], step)
    for i in range(len(leave[0])):
        at = pl.ds(i * step, step)
        act, grad = silu_parts(dot(weight_t, basis_v[at, :], NT))
        filt_v[:, at] = act.astype(BF16)
        leave[0][i].start()
        slope_v[:, at] = grad.astype(BF16)
        leave[1][i].start()
    waited(leave[0] + leave[1])


def lend_kernel(ranks, me, *refs):
    lists, edges, outs = refs[:ranks], refs[ranks], refs[ranks + 1 : 2 * ranks + 1]
    edges_v, sems = refs[2 * ranks + 1 :]
    arrive = loads([edges], [edges_v], sems)
    hot = hot_rows(columns_of(lists, me[0], False, outs[0].shape[0]), edges.shape[0])
    waited(arrive)
    scattered(dot(hot, edges_v[...]).astype(BF16), outs)


def owner_kernel(ranks, me, *refs):
    lists, (upstream, w_out, same, dhidden) = refs[:ranks], refs[ranks : ranks + 4]
    upstream_v, w_out_v, sems = refs[ranks + 4 :]
    arrive = loads([upstream, w_out], [upstream_v, w_out_v], sems)
    hot = hot_rows(columns_of(lists, me[0], True, same.shape[0] // ranks), upstream.shape[0])
    same[...] = dot(hot, hot, NT).astype(BF16)
    waited(arrive)
    dhidden[...] = dot(dot(hot, upstream_v[...]).astype(BF16), w_out_v[...], NT)


def forward_kernel(ranks, step, me, count, *refs):
    pieces, (src, dst), filt = refs[:ranks], refs[ranks : ranks + 2], refs[ranks + 2 : ranks + 4]
    outs = refs[ranks + 4 : 2 * ranks + 4]
    filt_v, message, hot, sems = refs[2 * ranks + 4 :]
    half = filt[0].shape[1]
    arrive = loads(filt, [filt_v.at[:, pl.ds(i * half, half)] for i in range(2)], sems)
    per_owner = outs[0].shape[0]
    slots, block = ranks * per_owner, src.shape[1]
    table = gathered(pieces).T
    src_t = turned(src, per_owner, ranks, me[0])
    dst_t = turned(dst, per_owner, ranks, me[0])
    each = step // block
    spans = [pl.ds(i * step, step) for i in range(2 * half // step)]
    for i, at in enumerate(spans):
        message[:, at] = dot(table, hot_lanes(src_t, i * each, each, slots)).astype(BF16)
    for i, at in enumerate(spans):
        hot[:, at] = hot_lanes(dst_t, i * each, each, slots, count[0, 0])
    waited(arrive)
    for at in spans:
        message[:, at] = message[:, at] * filt_v[:, at]
    scattered(dot(hot[...], message[...], NT).astype(BF16), outs)


def return_kernel(ranks, *refs):
    pieces, (same, dhidden), outs = refs[:ranks], refs[ranks : ranks + 2], refs[ranks + 2 :]
    agg = dot(same[...], gathered(pieces))
    scattered((dhidden[...] * silu_parts(agg)[1]).astype(BF16), outs)


def update_kernel(ranks, step, me, *refs):
    lists, pieces = refs[:ranks], refs[ranks : 2 * ranks]
    edges, upstream, w_out, updated, term = refs[2 * ranks : 2 * ranks + 5]
    edges_v, upstream_v, w_out_v, updated_v, hidden, sems, out_sems = refs[2 * ranks + 5 :]
    arrive = loads([w_out, edges, upstream], [w_out_v, edges_v, upstream_v], sems)
    home = gathered(pieces)
    rows = edges.shape[0]
    hot_t = hot_rows(columns_of(lists, me[0], True, pieces[0].shape[0]), rows).T
    turns = rows // step
    spans = [pl.ds(i * step, step) for i in range(turns)]
    leave = [
        pltpu.make_async_copy(updated_v.at[at, :], updated.at[at, :], out_sems.at[i])
        for i, at in enumerate(spans)
    ]
    fresh = [
        silu_parts(dot(hot_t[i * step : (i + 1) * step], home))[0].astype(BF16) for i in range(turns)
    ]
    waited(arrive)
    for i, at in enumerate(spans):
        total = edges_v[at, :].astype(F32) + dot(fresh[i], w_out_v[...])
        updated_v[at, :] = total.astype(BF16)
        leave[i].start()
        hidden[:, at] = fresh[i].T
    term[...] = dot(hidden[...], upstream_v[...]).astype(BF16)
    waited(leave)


def backward_kernel(ranks, step, me, count, *refs):
    fetched, pieces = refs[:ranks], refs[ranks : 2 * ranks]
    src, dst, basis = refs[2 * ranks : 2 * ranks + 3]
    filt, slope = refs[2 * ranks + 3 : 2 * ranks + 5], refs[2 * ranks + 5 : 2 * ranks + 7]
    weight, outs = refs[2 * ranks + 7], refs[2 * ranks + 8 : 3 * ranks + 8]
    basis_v, filt_v, slope_v, message, dpre, hot, sems = refs[3 * ranks + 8 :]
    half = filt[0].shape[1]
    halves = [pl.ds(i * half, half) for i in range(2)]
    first = loads(slope, [slope_v.at[:, at] for at in halves], sems.at[0])
    second = loads([basis], [basis_v], sems.at[1])
    third = loads(filt, [filt_v.at[:, at] for at in halves], sems.at[2])
    per_owner = outs[0].shape[0]
    slots, block = ranks * per_owner, src.shape[1]
    src_t = turned(src, per_owner, ranks, me[0])
    dst_t = turned(dst, per_owner, ranks, me[0])
    near, back = gathered(fetched).T, gathered(pieces).T
    each = step // block
    spans = [pl.ds(i * step, step) for i in range(2 * half // step)]
    for i, at in enumerate(spans):
        hot[:, at] = hot_lanes(src_t, i * each, each, slots)
        rows = dot(back, hot_lanes(dst_t, i * each, each, slots, count[0, 0])).astype(BF16)
        message[:, at] = rows
        dpre[:, at] = rows * dot(near, hot[:, at]).astype(BF16)
    waited(first + second)
    for at in spans:
        dpre[:, at] = dpre[:, at] * slope_v[:, at]
    weight[...] = dot(dpre[...], basis_v[...]).T
    waited(third)
    for at in spans:
        message[:, at] = message[:, at] * filt_v[:, at]
    scattered(dot(hot[...], message[...], NT).astype(BF16), outs)


def final_kernel(ranks, step, me, *refs):
    lists, pieces = refs[:ranks], refs[ranks : 2 * ranks]
    upstream, out, upstream_v, out_v, sems, out_sems = refs[2 * ranks :]
    arrive = loads([upstream], [upstream_v], sems)
    back = gathered(pieces)
    rows = upstream.shape[0]
    hot_t = hot_rows(columns_of(lists, me[0], False, pieces[0].shape[0]), rows).T
    waited(arrive)
    leave = []
    for i in range(rows // step):
        at = pl.ds(i * step, step)
        total = upstream_v[at, :].astype(F32) + dot(hot_t[i * step : (i + 1) * step], back)
        out_v[at, :] = total.astype(BF16)
        leave.append(pltpu.make_async_copy(out_v.at[at, :], out.at[at, :], out_sems.at[i]))
        leave[i].start()
    waited(leave)


def swap(value, axis, mask):
    return lax.ppermute(value, axis, [(k, k ^ mask) for k in range(lax.axis_size(axis))])


def shift(value, axis, by):
    count = lax.axis_size(axis)
    return lax.ppermute(value, axis, [(k, (k + by) % count) for k in range(count)])


def exchange(pieces, sign):
    return [pieces[0]] + [shift(pieces[s], "graph", sign * s) for s in range(1, len(pieces))]


def halve(value, axis, bit):
    half = value.reshape(2, value.shape[0] // 2, value.shape[1])
    own = (lax.axis_index(axis) >> bit) & 1
    away = lax.dynamic_index_in_dim(half, 1 - own, 0, keepdims=False).astype(BF16)
    kept = lax.dynamic_index_in_dim(half, own, 0, keepdims=False)
    return kept.astype(F32) + swap(away, axis, 1 << bit).astype(F32)


def double(value, got, axis, bit):
    low = ((lax.axis_index(axis) >> bit) & 1) == 0
    return jnp.where(low, jnp.concatenate([value, got]), jnp.concatenate([got, value]))


def bits_of(axis):
    return range(lax.axis_size(axis).bit_length() - 1)


def reduce_out(term):
    for bit in bits_of("dp"):
        term = halve(term, "dp", bit)
    for bit in reversed(bits_of("graph")):
        term = halve(term, "graph", bit)
    return term.astype(BF16)


def reduce_both(out, basis):
    for bit in bits_of("dp"):
        basis = halve(basis, "dp", bit)
    basis = basis.astype(BF16)
    rows = basis.shape[0]
    for bit in bits_of("graph"):
        got = swap(jnp.concatenate([basis, out]), "graph", 1 << bit)
        basis = (basis.astype(F32) + got[:rows].astype(F32)).astype(BF16)
        out = double(out, got[rows:], "graph", bit)
    for bit in reversed(bits_of("dp")):
        rows = basis.shape[0]
        got = swap(jnp.concatenate([basis, out]), "dp", 1 << bit)
        basis = double(basis, got[:rows], "dp", bit)
        out = double(out, got[rows:], "dp", bit)
    return out.astype(F32), basis.astype(F32)


def per_device(
    edge_emb,
    cotangent,
    fetch_rows,
    store_rows,
    trip_src,
    trip_dst,
    trip_basis,
    block_count,
    w_basis,
    w_out,
):
    edges, upstream, basis = edge_emb[0], cotangent[0], trip_basis[0]
    ranks, copies = lax.axis_size("graph"), lax.axis_size("dp")
    me = lax.axis_index("graph").astype(jnp.int32).reshape(1)
    edge_dev, width = edges.shape
    per_owner = fetch_rows.shape[3]
    slots = ranks * per_owner
    blocks, block_rows = trip_src.shape[1:]
    triplets, basis_width = basis.shape
    src, dst = trip_src[0], trip_dst[0]
    pieces = [shape((per_owner, width))] * ranks
    half = shape((width, triplets // 2))
    plane, hot = shape((width, triplets)), shape((slots, triplets))
    step = 512
    wide = 2 * triplets * slots * width
    narrow = 2 * triplets * basis_width * width
    dma = pltpu.SemaphoreType.DMA

    both = jnp.concatenate([fetch_rows[0, 0], store_rows[0, 0]], axis=1)
    lists = exchange([both] * ranks, 1)

    def prepare(part):
        rows = triplets // 2
        return call(
            functools.partial(prepare_kernel, step, part),
            [half, half],
            [basis, w_basis],
            flops=4 * narrow,
            far=(0,),
            far_out=(0, 1),
            scratch=[pltpu.VMEM((rows, basis_width), BF16), held(half), held(half)]
            + [dma((1,)), dma((2, rows // step))],
        )

    early = prepare(0)
    lend = call(
        functools.partial(lend_kernel, ranks),
        pieces,
        [me] + lists + [edges],
        smem=(0,),
        far=(ranks + 1,),
        flops=2 * slots * edge_dev * width,
        scratch=[held(edges), dma((1,))],
        order=[early[0]],
    )
    fetched = exchange(lend, -1)
    late = prepare(1)
    filt, slope = [early[0], late[0]], [early[1], late[1]]
    partial_rows = call(
        functools.partial(forward_kernel, ranks, step),
        pieces,
        [me, block_count] + fetched + [src, dst] + filt,
        smem=(0, 1),
        far=(ranks + 4, ranks + 5),
        flops=2 * wide,
        scratch=[held(plane), held(plane), held(hot), dma((2,))],
    )
    home = exchange(partial_rows, 1)
    same, dhidden = call(
        functools.partial(owner_kernel, ranks),
        [shape((slots, slots)), shape((slots, width), F32)],
        [me] + lists + [upstream, w_out],
        smem=(0,),
        far=(ranks + 1, ranks + 2),
        flops=4 * slots * edge_dev * width,
        scratch=[held(upstream), held(w_out), dma((2,))],
        order=[partial_rows[0]],
    )
    back = call(
        functools.partial(return_kernel, ranks),
        pieces,
        home + [same, dhidden],
        flops=2 * slots * slots * width,
    )
    dpartial = exchange(back, -1)
    updated, out_term = call(
        functools.partial(update_kernel, ranks, 256),
        [shape((edge_dev, width)), shape((width, width))],
        [me] + lists + home + [edges, upstream, w_out],
        smem=(0,),
        far=(2 * ranks + 1, 2 * ranks + 2, 2 * ranks + 3),
        far_out=(0,),
        flops=2 * edge_dev * width * (2 * width + slots),
        scratch=[held(edges), held(upstream), held(w_out), held(edges)]
        + [pltpu.VMEM((width, edge_dev), BF16), dma((3,)), dma((edge_dev // 256,))],
        order=[back[0]],
    )
    out_part = reduce_out(out_term)
    basis_term, *dfetch = call(
        functools.partial(backward_kernel, ranks, step),
        [shape((basis_width, width), F32)] + pieces,
        [me, block_count] + fetched + dpartial + [src, dst, basis] + filt + slope,
        smem=(0, 1),
        far=tuple(range(2 * ranks + 4, 2 * ranks + 9)),
        flops=3 * wide + narrow,
        scratch=[held(basis)] + [held(plane)] * 4 + [held(hot), dma((3, 2))],
        order=[out_term],
    )
    grad_w_out, grad_w_basis = reduce_both(out_part, basis_term)
    (grad_edge,) = call(
        functools.partial(final_kernel, ranks, 256),
        [shape((edge_dev, width))],
        [me] + lists + exchange(dfetch, 1) + [upstream],
        smem=(0,),
        far=(2 * ranks + 1,),
        far_out=(0,),
        flops=2 * slots * edge_dev * width,
        scratch=[held(upstream), held(upstream), dma((1,)), dma((edge_dev // 256,))],
    )
    out_scale = jnp.sqrt(F32(copies * ranks * edge_dev))
    basis_scale = jnp.sqrt(F32(copies * ranks * blocks * block_rows))
    return (updated[None], grad_edge[None], grad_w_out / out_scale, grad_w_basis / basis_scale)


def solution(mesh):
    placed = (
        P(("groups", "dp"), "graph", None),
        P(("groups", "dp"), "graph", None),
        P(("groups", "dp"), "graph", None, None),
        P(("groups", "dp"), "graph", None, None),
        P(("groups", "dp"), "graph", None),
        P(("groups", "dp"), "graph", None),
        P(("groups", "dp"), "graph", None),
        P(("groups", "dp"), "graph"),
        P(),
        P(),
    )
    return jax.shard_map(
        per_device,
        mesh=mesh,
        in_specs=placed,
        out_specs=(
            P(("groups", "dp"), "graph", None),
            P(("groups", "dp"), "graph", None),
            P("groups", None),
            P("groups", None),
        ),
        check_vma=False,
    )
```

time: 119 us -> 114 us (0.958)
  Pallas kernels: 48.5 us -> 43 us
  starting transfers between devices: 39.1 us -> 34.2 us
  waiting for transfers between devices: 22 us -> 25.6 us
    ppermute x16 -> x10, waiting for transfers between devices: 11.5 us -> 19.9 us  [swap(): lax.ppermute(value, axis, [(k, k ^ mask) for k in range(lax.axis_size(axi...]
    pallas_call x10 -> x9, Pallas kernels: 48.5 us -> 43 us  [call(): pl.pallas_call(inner if order else body, out_shape=tuple(outs), in_specs=...]
    ppermute x15, waiting for transfers between devices: 10.5 us -> 5.69 us  [shift(): lax.ppermute(value, axis, [(k, (k + by) % count) for k in range(count)])]
    ppermute x16 -> x10, starting transfers between devices: 16.7 us -> 13.1 us  [swap(): lax.ppermute(value, axis, [(k, k ^ mask) for k in range(lax.axis_size(axi...]
    ppermute x15, starting transfers between devices: 22.4 us -> 21.1 us  [shift(): lax.ppermute(value, axis, [(k, (k + by) % count) for k in range(count)])]
    unnamed x36 -> x40, local copies, waits for them, and re-layouts: 3.05 us -> 3.14 us
  transfers between devices with their start and end apart: 31 -> 25, of which waited for: 14 -> 9; matrix products, arithmetic and copies ran while one was open for 1% -> 3% of each run, Pallas kernels for 29% -> 28%
where the time goes in v4:
time: 114 us
  Pallas kernels  43 us (38%)
  starting transfers between devices  34.2 us (30%)
  waiting for transfers between devices  25.6 us (22%)
  local copies, waits for them, and re-layouts  5.15 us (5%)
  other arithmetic  3.89 us (3%)
  between operations  1.77 us (2%)
    pallas_call x9, Pallas kernels, call(): pl.pallas_call(inner if order else body, out_shape=tuple(outs), in_specs=...  43 us
    ppermute x15, starting transfers between devices, shift(): lax.ppermute(value, axis, [(k, (k + by) % count) for k in range(count)])  21.1 us
    ppermute x10, waiting for transfers between devices, swap(): lax.ppermute(value, axis, [(k, k ^ mask) for k in range(lax.axis_size(axi...  19.9 us
    ppermute x10, starting transfers between devices, swap(): lax.ppermute(value, axis, [(k, k ^ mask) for k in range(lax.axis_size(axi...  13.1 us
    ppermute x15, waiting for transfers between devices, shift(): lax.ppermute(value, axis, [(k, (k + by) % count) for k in range(count)])  5.69 us
    unnamed x40, local copies, waits for them, and re-layouts  3.14 us
  transfers between devices with their start and end apart: 25, of which 9 were waited for; matrix products, arithmetic and copies ran while one was open for 3% of the time, Pallas kernels for 28%

profile of v4, /device:TPU:0, one launch (start us, length us, event | category | flops | bytes accessed | tf_op | source)
XLA Modules:
  0.0 113.6 jit_solution(18381669126153449829)
XLA Ops:
  1.4 3.0 %collective-permute-start = (s32[4,128]{1,0:T(4,128)S(1)}, s32[4,128]{1,0:T(4,128)S(1)}, u32[]{:S(2)}, u32[]{:S(2)}) collective-permute-start(s32[4,128]{1,0:T(4,128)S(1)} %pad_add_fusion.refs_1_.refs_0_), channel_id=1, source_target_pairs={{0,4},{4,8},{8,12},{12,0},{1,5},{5,9},{9,13},{13,1},{2,6},{6,10},{... | collective-permute-start | bytes 6152 | tf_op jit(solution)/shard_map/ppermute | solution.py:276
  4.4 2.6 %collective-permute-start.1 = (s32[4,128]{1,0:T(4,128)S(1)}, s32[4,128]{1,0:T(4,128)S(1)}, u32[]{:S(2)}, u32[]{:S(2)}) collective-permute-start(s32[4,128]{1,0:T(4,128)S(1)} %pad_add_fusion.refs_1_.refs_0_), channel_id=1, source_target_pairs={{0,8},{4,12},{8,0},{12,4},{1,9},{5,13},{9,1},{13,5},{2,10},{6,14},... | collective-permute-start | bytes 6152 | tf_op jit(solution)/shard_map/ppermute | solution.py:276
  7.0 1.3 %collective-permute-start.2 = (s32[4,128]{1,0:T(4,128)S(1)}, s32[4,128]{1,0:T(4,128)S(1)}, u32[]{:S(2)}, u32[]{:S(2)}) collective-permute-start(s32[4,128]{1,0:T(4,128)S(1)} %pad_add_fusion.refs_1_.refs_0_), channel_id=1, source_target_pairs={{0,12},{4,0},{8,4},{12,8},{1,13},{5,1},{9,5},{13,9},{2,14},{6,2},{... | collective-permute-start | bytes 6152 | tf_op jit(solution)/shard_map/ppermute | solution.py:276
  8.4 4.6 %shard_map.129 = (bf16[512,2048]{1,0:T(8,128)(2,1)}, bf16[512,2048]{1,0:T(8,128)(2,1)}) custom-call(bf16[4096,128]{1,0:T(8,128)(2,1)} %bitcast.65, bf16[128,512]{1,0:T(8,128)(2,1)} %weight.3), custom_call_target="tpu_custom_call" | custom-call | flops 2147483648 | bytes 5373952 | tf_op jit(solution)/shard_map/pallas_call | solution.py:42
  13.7 3.0 %shard_map.130 = (bf16[64,512]{1,0:T(8,128)(2,1)}, bf16[64,512]{1,0:T(8,128)(2,1)}, bf16[64,512]{1,0:T(8,128)(2,1)}, bf16[64,512]{1,0:T(8,128)(2,1)}) custom-call(s32[1]{0:T(128)} %bitcast.refs_0_.me, s32[4,128]{1,0:T(4,128)} %copy-done.7, s32[4,128]{1,0:T(4,128)} %copy-done.8, s32[4,128]{1,0:T(4,128)} %copy-done.9, s32[4,128]{1,0:T(4,128)} %copy-done.10, ...), custom_call_target="tpu_custom_call" | custom-call | flops 268435456 | bytes 3416068 | tf_op jit(solution)/shard_map/pallas_call | solution.py:42
  17.4 1.5 %collective-permute-start.4 = (bf16[64,512]{1,0:T(8,128)(2,1)}, bf16[64,512]{1,0:T(8,128)(2,1)S(1)}, u32[]{:S(2)}, u32[]{:S(2)}) collective-permute-start(bf16[64,512]{1,0:T(8,128)(2,1)} %get-tuple-element.32), channel_id=1, source_target_pairs={{0,8},{4,12},{8,0},{12,4},{1,9},{5,13},{9,1},{13,5},{2,10},{6,14},... | collective-permute-start | bytes 196616 | tf_op jit(solution)/shard_map/ppermute | solution.py:276
  18.9 4.7 %shard_map.131 = (bf16[512,2048]{1,0:T(8,128)(2,1)}, bf16[512,2048]{1,0:T(8,128)(2,1)}) custom-call(bf16[4096,128]{1,0:T(8,128)(2,1)} %bitcast.66, bf16[128,512]{1,0:T(8,128)(2,1)} %weight.3), custom_call_target="tpu_custom_call" | custom-call | flops 2147483648 | bytes 5373952 | tf_op jit(solution)/shard_map/pallas_call | solution.py:42
  25.8 5.5 %shard_map.132 = (bf16[64,512]{1,0:T(8,128)(2,1)}, bf16[64,512]{1,0:T(8,128)(2,1)}, bf16[64,512]{1,0:T(8,128)(2,1)}, bf16[64,512]{1,0:T(8,128)(2,1)}) custom-call(s32[1]{0:T(128)} %bitcast.refs_0_.me, s32[1,1]{1,0:T(1,128)S(6)} %copy.14.count.refs_1_, bf16[64,512]{1,0:T(8,128)(2,1)} %get-tuple-element.30.refs_0_.refs_2_, bf16[64,512]{1,0:T(8,128)(2,1)} %copy-done.11, ...), custom_call_target="tpu_custom_call" | custom-call | flops 2147483648 | bytes 4751368 | tf_op jit(solution)/shard_map/pallas_call | solution.py:42
  32.5 2.4 %collective-permute-start.7 = (bf16[64,512]{1,0:T(8,128)(2,1)}, bf16[64,512]{1,0:T(8,128)(2,1)S(1)}, u32[]{:S(2)}, u32[]{:S(2)}) collective-permute-start(bf16[64,512]{1,0:T(8,128)(2,1)} %get-tuple-element.37), channel_id=1, source_target_pairs={{0,8},{4,12},{8,0},{12,4},{1,9},{5,13},{9,1},{13,5},{2,10},{6,14},... | collective-permute-start | bytes 196616 | tf_op jit(solution)/shard_map/ppermute | solution.py:276
  34.9 1.4 %collective-permute-start.8 = (bf16[64,512]{1,0:T(8,128)(2,1)}, bf16[64,512]{1,0:T(8,128)(2,1)S(1)}, u32[]{:S(2)}, u32[]{:S(2)}) collective-permute-start(bf16[64,512]{1,0:T(8,128)(2,1)} %get-tuple-element.38), channel_id=1, source_target_pairs={{0,12},{4,0},{8,4},{12,8},{1,13},{5,1},{9,5},{13,9},{2,14},{6,2},{... | collective-permute-start | bytes 196616 | tf_op jit(solution)/shard_map/ppermute | solution.py:276
  36.2 3.8 %shard_map.133 = (bf16[256,256]{1,0:T(8,128)(2,1)}, f32[256,512]{1,0:T(8,128)}) custom-call(s32[1]{0:T(128)} %bitcast.refs_0_.me, s32[4,128]{1,0:T(4,128)} %copy-done.7, s32[4,128]{1,0:T(4,128)} %copy-done.8, s32[4,128]{1,0:T(4,128)} %copy-done.9, s32[4,128]{1,0:T(4,128)} %copy-done.10, bf16[1024,512]{1,0:T(8,128)(2,1)} %bitcast.49, ...), custom_call_target="tpu_custom_call" | custom-call | flops 536870912 | bytes 2301956 | tf_op jit(solution)/shard_map/pallas_call | solution.py:42
  40.7 2.2 %shard_map.134 = (bf16[64,512]{1,0:T(8,128)(2,1)}, bf16[64,512]{1,0:T(8,128)(2,1)}, bf16[64,512]{1,0:T(8,128)(2,1)}, bf16[64,512]{1,0:T(8,128)(2,1)}) custom-call(bf16[64,512]{1,0:T(8,128)(2,1)} %get-tuple-element.35.refs_7_.refs_0_.refs_5_, bf16[64,512]{1,0:T(8,128)(2,1)} %copy-done.1, bf16[64,512]{1,0:T(8,128)(2,1)} %copy-done.2, ...), custom_call_target="tpu_custom_call" | custom-call | flops 67108864 | bytes 1179648 | tf_op jit(solution)/shard_map/pallas_call | solution.py:42
  43.0 2.4 %collective-permute-start.9 = (bf16[64,512]{1,0:T(8,128)(2,1)}, bf16[64,512]{1,0:T(8,128)(2,1)S(1)}, u32[]{:S(2)}, u32[]{:S(2)}) collective-permute-start(bf16[64,512]{1,0:T(8,128)(2,1)} %get-tuple-element.43), channel_id=1, source_target_pairs={{0,12},{4,0},{8,4},{12,8},{1,13},{5,1},{9,5},{13,9},{2,14},{6,2},{... | collective-permute-start | bytes 196616 | tf_op jit(solution)/shard_map/ppermute | solution.py:276
  46.0 4.9 %shard_map.135 = (bf16[1024,512]{1,0:T(8,128)(2,1)}, bf16[512,512]{1,0:T(8,128)(2,1)}) custom-call(s32[1]{0:T(128)} %bitcast.refs_0_.me, s32[4,128]{1,0:T(4,128)} %copy-done.7, s32[4,128]{1,0:T(4,128)} %copy-done.8, s32[4,128]{1,0:T(4,128)} %copy-done.9, s32[4,128]{1,0:T(4,128)} %copy-done.10, bf16[64,512]{1,0:T(8,128)(2,1)} %get-tuple-element.35.refs_7_.refs_0_.refs_5_, ...), custom_call_target="tpu_custom_call" | custom-call | flops 1342177280 | bytes 4530180 | tf_op jit(solution)/shard_map/pallas_call | solution.py:42
  52.7 10.7 %shard_map.136 = (f32[128,512]{1,0:T(8,128)}, bf16[64,512]{1,0:T(8,128)(2,1)}, bf16[64,512]{1,0:T(8,128)(2,1)}, bf16[64,512]{1,0:T(8,128)(2,1)}, bf16[64,512]{1,0:T(8,128)(2,1)}) custom-call(s32[1]{0:T(128)} %bitcast.refs_0_.me, s32[1,1]{1,0:T(1,128)S(6)} %copy.14.count.refs_1_, bf16[64,512]{1,0:T(8,128)(2,1)} %get-tuple-element.30.refs_0_.refs_2_, ...), custom_call_target="tpu_custom_call" | custom-call | flops 3758096384 | bytes 11042824 | tf_op jit(solution)/shard_map/pallas_call | solution.py:42
  65.0 1.6 %collective-permute-start.16 = (bf16[128,512]{1,0:T(8,128)(2,1)S(1)}, bf16[128,512]{1,0:T(8,128)(2,1)S(1)}, u32[]{:S(2)}, u32[]{:S(2)}) collective-permute-start(bf16[128,512]{1,0:T(8,128)(2,1)S(1)} %fusion), channel_id=1, source_target_pairs={{0,2},{1,3},{2,0},{3,1},{4,6},{5,7},{6,4},{7,5},{8,10},{9,11},{10,... | collective-permute-start | bytes 393224 | tf_op jit(solution)/shard_map/ppermute | solution.py:271
  67.5 3.0 %collective-permute-done.16 = bf16[128,512]{1,0:T(8,128)(2,1)S(1)} collective-permute-done((bf16[128,512]{1,0:T(8,128)(2,1)S(1)}, bf16[128,512]{1,0:T(8,128)(2,1)S(1)}, u32[]{:S(2)}, u32[]{:S(2)}) %collective-permute-start.16) | collective-permute-done | bytes 131104 | tf_op jit(solution)/shard_map/ppermute | solution.py:271
  70.6 2.4 %collective-permute-start.17 = (bf16[64,512]{1,0:T(8,128)(2,1)S(1)}, bf16[64,512]{1,0:T(8,128)(2,1)S(1)}, u32[]{:S(2)}, u32[]{:S(2)}) collective-permute-start(bf16[64,512]{1,0:T(8,128)(2,1)S(1)} %fusion.2), channel_id=1, source_target_pairs={{0,8},{4,12},{8,0},{12,4},{1,9},{5,13},{9,1},{13,5},{2,10},{6,14},... | collective-permute-start | bytes 196616 | tf_op jit(solution)/shard_map/ppermute | solution.py:271
  73.0 1.5 %collective-permute-start.20 = (bf16[32,512]{1,0:T(8,128)(2,1)S(1)}, bf16[32,512]{1,0:T(8,128)(2,1)S(1)}, u32[]{:S(2)}, u32[]{:S(2)}) collective-permute-start(bf16[32,512]{1,0:T(8,128)(2,1)S(1)} %fusion.7), channel_id=1, source_target_pairs={{0,2},{1,3},{2,0},{3,1},{4,6},{5,7},{6,4},{7,5},{8,10},{9,11},{10,... | collective-permute-start | bytes 98312 | tf_op jit(solution)/shard_map/ppermute | solution.py:271
  74.5 2.1 %collective-permute-done.17 = bf16[64,512]{1,0:T(8,128)(2,1)S(1)} collective-permute-done((bf16[64,512]{1,0:T(8,128)(2,1)S(1)}, bf16[64,512]{1,0:T(8,128)(2,1)S(1)}, u32[]{:S(2)}, u32[]{:S(2)}) %collective-permute-start.17) | collective-permute-done | bytes 65568 | tf_op jit(solution)/shard_map/ppermute | solution.py:271
  76.6 2.2 %collective-permute-start.18 = (bf16[32,512]{1,0:T(8,128)(2,1)S(1)}, bf16[32,512]{1,0:T(8,128)(2,1)S(1)}, u32[]{:S(2)}, u32[]{:S(2)}) collective-permute-start(bf16[32,512]{1,0:T(8,128)(2,1)S(1)} %fusion.6), channel_id=1, source_target_pairs={{0,4},{4,0},{8,12},{12,8},{1,5},{5,1},{9,13},{13,9},{2,6},{6,2},{1... | collective-permute-start | bytes 98312 | tf_op jit(solution)/shard_map/ppermute | solution.py:271
  78.8 1.9 %collective-permute-done.18 = bf16[32,512]{1,0:T(8,128)(2,1)S(1)} collective-permute-done((bf16[32,512]{1,0:T(8,128)(2,1)S(1)}, bf16[32,512]{1,0:T(8,128)(2,1)S(1)}, u32[]{:S(2)}, u32[]{:S(2)}) %collective-permute-start.18) | collective-permute-done | bytes 32800 | tf_op jit(solution)/shard_map/ppermute | solution.py:271
  80.8 2.4 %collective-permute-start.21 = (bf16[64,512]{1,0:T(8,128)(2,1)S(1)}, bf16[64,512]{1,0:T(8,128)(2,1)S(1)}, u32[]{:S(2)}, u32[]{:S(2)}) collective-permute-start(bf16[64,512]{1,0:T(8,128)(2,1)S(1)} %pad_maximum_fusion.4), channel_id=1, source_target_pairs={{0,4},{4,0},{8,12},{12,8},{1,5},{5,1},{9,13},{13,9},{2,6},{6,2},{1... | collective-permute-start | bytes 196616 | tf_op jit(solution)/shard_map/ppermute | solution.py:271
  83.2 3.3 %collective-permute-done.21 = bf16[64,512]{1,0:T(8,128)(2,1)S(1)} collective-permute-done((bf16[64,512]{1,0:T(8,128)(2,1)S(1)}, bf16[64,512]{1,0:T(8,128)(2,1)S(1)}, u32[]{:S(2)}, u32[]{:S(2)}) %collective-permute-start.21) | collective-permute-done | bytes 65568 | tf_op jit(solution)/shard_map/ppermute | solution.py:271
  87.4 5.8 %collective-permute-done.22 = bf16[96,512]{1,0:T(8,128)(2,1)S(1)} collective-permute-done((bf16[96,512]{1,0:T(8,128)(2,1)S(1)}, bf16[96,512]{1,0:T(8,128)(2,1)S(1)}, u32[]{:S(2)}, u32[]{:S(2)}) %collective-permute-start.22) | collective-permute-done | bytes 98336 | tf_op jit(solution)/shard_map/ppermute | solution.py:271
  93.2 1.5 %collective-permute-start.23 = (bf16[160,512]{1,0:T(8,128)(2,1)S(1)}, bf16[160,512]{1,0:T(8,128)(2,1)S(1)}, u32[]{:S(2)}, u32[]{:S(2)}) collective-permute-start(bf16[160,512]{1,0:T(8,128)(2,1)S(1)} %pad_maximum_fusion.1), channel_id=1, source_target_pairs={{0,2},{1,3},{2,0},{3,1},{4,6},{5,7},{6,4},{7,5},{8,10},{9,11},{10,... | collective-permute-start | bytes 491528 | tf_op jit(solution)/shard_map/ppermute | solution.py:271
  94.8 3.8 %collective-permute-done.23 = bf16[160,512]{1,0:T(8,128)(2,1)S(1)} collective-permute-done((bf16[160,512]{1,0:T(8,128)(2,1)S(1)}, bf16[160,512]{1,0:T(8,128)(2,1)S(1)}, u32[]{:S(2)}, u32[]{:S(2)}) %collective-permute-start.23) | collective-permute-done | bytes 163872 | tf_op jit(solution)/shard_map/ppermute | solution.py:271
  98.9 2.2 %collective-permute-start.13 = (bf16[64,512]{1,0:T(8,128)(2,1)S(1)}, bf16[64,512]{1,0:T(8,128)(2,1)S(1)}, u32[]{:S(2)}, u32[]{:S(2)}) collective-permute-start(bf16[64,512]{1,0:T(8,128)(2,1)S(1)} %copy-done.15), channel_id=1, source_target_pairs={{0,8},{4,12},{8,0},{12,4},{1,9},{5,13},{9,1},{13,5},{2,10},{6,14},... | collective-permute-start | bytes 196616 | tf_op jit(solution)/shard_map/ppermute | solution.py:276
  101.2 1.6 %collective-permute-start.14 = (bf16[64,512]{1,0:T(8,128)(2,1)S(1)}, bf16[64,512]{1,0:T(8,128)(2,1)S(1)}, u32[]{:S(2)}, u32[]{:S(2)}) collective-permute-start(bf16[64,512]{1,0:T(8,128)(2,1)S(1)} %copy-done.14), channel_id=1, source_target_pairs={{0,12},{4,0},{8,4},{12,8},{1,13},{5,1},{9,5},{13,9},{2,14},{6,2},{... | collective-permute-start | bytes 196616 | tf_op jit(solution)/shard_map/ppermute | solution.py:276
  102.8 2.9 %collective-permute-done.12.refs_5_ = bf16[64,512]{1,0:T(8,128)(2,1)S(1)} collective-permute-done((bf16[64,512]{1,0:T(8,128)(2,1)S(1)}, bf16[64,512]{1,0:T(8,128)(2,1)S(1)}, u32[]{:S(2)}, u32[]{:S(2)}) %collective-permute-start.12) | collective-permute-done | bytes 65568 | tf_op jit(solution)/shard_map/ppermute | solution.py:276
  105.7 1.9 %collective-permute-done.13.refs_6_ = bf16[64,512]{1,0:T(8,128)(2,1)S(1)} collective-permute-done((bf16[64,512]{1,0:T(8,128)(2,1)S(1)}, bf16[64,512]{1,0:T(8,128)(2,1)S(1)}, u32[]{:S(2)}, u32[]{:S(2)}) %collective-permute-start.13) | collective-permute-done | bytes 65568 | tf_op jit(solution)/shard_map/ppermute | solution.py:276
  108.2 3.4 %shard_map.137 = bf16[1024,512]{1,0:T(8,128)(2,1)} custom-call(s32[1]{0:T(128)} %bitcast.refs_0_.me, s32[4,128]{1,0:T(4,128)} %copy-done.7, s32[4,128]{1,0:T(4,128)} %copy-done.8, s32[4,128]{1,0:T(4,128)} %copy-done.9, s32[4,128]{1,0:T(4,128)} %copy-done.10, bf16[64,512]{1,0:T(8,128)(2,1)} %get-tuple-element.49.refs_4_, bf16[64,512]{1,0:T(8,128)(2,1)} %copy-done.4, ...), custom_call_target="tpu_custom_call" | custom-call | flops 268435456 | bytes 2367492 | tf_op jit(solution)/shard_map/pallas_call | solution.py:42
  (98 shorter events, 14.2 us)
Async XLA Ops:
  1.4 11.6 %copy-start.7 = (s32[4,128]{1,0:T(4,128)}, s32[4,128]{1,0:T(4,128)S(1)}, u32[]{:S(2)}) copy-start(s32[4,128]{1,0:T(4,128)S(1)} %pad_add_fusion.refs_1_.refs_0_) | copy-start | bytes 6148
  1.4 11.6 %collective-permute-start = (s32[4,128]{1,0:T(4,128)S(1)}, s32[4,128]{1,0:T(4,128)S(1)}, u32[]{:S(2)}, u32[]{:S(2)}) collective-permute-start(s32[4,128]{1,0:T(4,128)S(1)} %pad_add_fusion.refs_1_.refs_0_), channel_id=1, source_target_pairs={{0,4},{4,8},{8,12},{12,0},{1,5},{5,9},{9,13},{13,1},{2,6},{6,10},{... | collective-permute-start | bytes 6152 | tf_op jit(solution)/shard_map/ppermute | solution.py:276
  4.4 8.6 %collective-permute-start.1 = (s32[4,128]{1,0:T(4,128)S(1)}, s32[4,128]{1,0:T(4,128)S(1)}, u32[]{:S(2)}, u32[]{:S(2)}) collective-permute-start(s32[4,128]{1,0:T(4,128)S(1)} %pad_add_fusion.refs_1_.refs_0_), channel_id=1, source_target_pairs={{0,8},{4,12},{8,0},{12,4},{1,9},{5,13},{9,1},{13,5},{2,10},{6,14},... | collective-permute-start | bytes 6152 | tf_op jit(solution)/shard_map/ppermute | solution.py:276
  7.0 6.1 %collective-permute-start.2 = (s32[4,128]{1,0:T(4,128)S(1)}, s32[4,128]{1,0:T(4,128)S(1)}, u32[]{:S(2)}, u32[]{:S(2)}) collective-permute-start(s32[4,128]{1,0:T(4,128)S(1)} %pad_add_fusion.refs_1_.refs_0_), channel_id=1, source_target_pairs={{0,12},{4,0},{8,4},{12,8},{1,13},{5,1},{9,5},{13,9},{2,14},{6,2},{... | collective-permute-start | bytes 6152 | tf_op jit(solution)/shard_map/ppermute | solution.py:276
  16.7 7.6 %collective-permute-start.3 = (bf16[64,512]{1,0:T(8,128)(2,1)}, bf16[64,512]{1,0:T(8,128)(2,1)S(1)}, u32[]{:S(2)}, u32[]{:S(2)}) collective-permute-start(bf16[64,512]{1,0:T(8,128)(2,1)} %get-tuple-element.31), channel_id=1, source_target_pairs={{0,12},{4,0},{8,4},{12,8},{1,13},{5,1},{9,5},{13,9},{2,14},{6,2},{... | collective-permute-start | bytes 196616 | tf_op jit(solution)/shard_map/ppermute | solution.py:276
  17.4 6.9 %collective-permute-start.4 = (bf16[64,512]{1,0:T(8,128)(2,1)}, bf16[64,512]{1,0:T(8,128)(2,1)S(1)}, u32[]{:S(2)}, u32[]{:S(2)}) collective-permute-start(bf16[64,512]{1,0:T(8,128)(2,1)} %get-tuple-element.32), channel_id=1, source_target_pairs={{0,8},{4,12},{8,0},{12,4},{1,9},{5,13},{9,1},{13,5},{2,10},{6,14},... | collective-permute-start | bytes 196616 | tf_op jit(solution)/shard_map/ppermute | solution.py:276
  18.9 6.3 %collective-permute-start.5 = (bf16[64,512]{1,0:T(8,128)(2,1)}, bf16[64,512]{1,0:T(8,128)(2,1)S(1)}, u32[]{:S(2)}, u32[]{:S(2)}) collective-permute-start(bf16[64,512]{1,0:T(8,128)(2,1)} %get-tuple-element.33), channel_id=1, source_target_pairs={{0,4},{4,8},{8,12},{12,0},{1,5},{5,9},{9,13},{13,1},{2,6},{6,10},{... | collective-permute-start | bytes 196616 | tf_op jit(solution)/shard_map/ppermute | solution.py:276
  24.3 0.9 copy-start.11
  31.3 8.7 %collective-permute-start.6 = (bf16[64,512]{1,0:T(8,128)(2,1)}, bf16[64,512]{1,0:T(8,128)(2,1)S(1)}, u32[]{:S(2)}, u32[]{:S(2)}) collective-permute-start(bf16[64,512]{1,0:T(8,128)(2,1)} %get-tuple-element.36), channel_id=1, source_target_pairs={{0,4},{4,8},{8,12},{12,0},{1,5},{5,9},{9,13},{13,1},{2,6},{6,10},{... | collective-permute-start | bytes 196616 | tf_op jit(solution)/shard_map/ppermute | solution.py:276
  32.5 7.5 %collective-permute-start.7 = (bf16[64,512]{1,0:T(8,128)(2,1)}, bf16[64,512]{1,0:T(8,128)(2,1)S(1)}, u32[]{:S(2)}, u32[]{:S(2)}) collective-permute-start(bf16[64,512]{1,0:T(8,128)(2,1)} %get-tuple-element.37), channel_id=1, source_target_pairs={{0,8},{4,12},{8,0},{12,4},{1,9},{5,13},{9,1},{13,5},{2,10},{6,14},... | collective-permute-start | bytes 196616 | tf_op jit(solution)/shard_map/ppermute | solution.py:276
  34.9 5.2 %collective-permute-start.8 = (bf16[64,512]{1,0:T(8,128)(2,1)}, bf16[64,512]{1,0:T(8,128)(2,1)S(1)}, u32[]{:S(2)}, u32[]{:S(2)}) collective-permute-start(bf16[64,512]{1,0:T(8,128)(2,1)} %get-tuple-element.38), channel_id=1, source_target_pairs={{0,12},{4,0},{8,4},{12,8},{1,13},{5,1},{9,5},{13,9},{2,14},{6,2},{... | collective-permute-start | bytes 196616 | tf_op jit(solution)/shard_map/ppermute | solution.py:276
  43.0 9.0 %collective-permute-start.9 = (bf16[64,512]{1,0:T(8,128)(2,1)}, bf16[64,512]{1,0:T(8,128)(2,1)S(1)}, u32[]{:S(2)}, u32[]{:S(2)}) collective-permute-start(bf16[64,512]{1,0:T(8,128)(2,1)} %get-tuple-element.43), channel_id=1, source_target_pairs={{0,12},{4,0},{8,4},{12,8},{1,13},{5,1},{9,5},{13,9},{2,14},{6,2},{... | collective-permute-start | bytes 196616 | tf_op jit(solution)/shard_map/ppermute | solution.py:276
  45.4 6.7 %collective-permute-start.10 = (bf16[64,512]{1,0:T(8,128)(2,1)}, bf16[64,512]{1,0:T(8,128)(2,1)S(1)}, u32[]{:S(2)}, u32[]{:S(2)}) collective-permute-start(bf16[64,512]{1,0:T(8,128)(2,1)} %get-tuple-element.44), channel_id=1, source_target_pairs={{0,8},{4,12},{8,0},{12,4},{1,9},{5,13},{9,1},{13,5},{2,10},{6,14},... | collective-permute-start | bytes 196616 | tf_op jit(solution)/shard_map/ppermute | solution.py:276
  45.4 6.7 %collective-permute-start.11 = (bf16[64,512]{1,0:T(8,128)(2,1)}, bf16[64,512]{1,0:T(8,128)(2,1)S(1)}, u32[]{:S(2)}, u32[]{:S(2)}) collective-permute-start(bf16[64,512]{1,0:T(8,128)(2,1)} %get-tuple-element.45), channel_id=1, source_target_pairs={{0,4},{4,8},{8,12},{12,0},{1,5},{5,9},{9,13},{13,1},{2,6},{6,10},{... | collective-permute-start | bytes 196616 | tf_op jit(solution)/shard_map/ppermute | solution.py:276
  51.9 13.0 %collective-permute-start.15 = (bf16[256,512]{1,0:T(8,128)(2,1)S(1)}, bf16[256,512]{1,0:T(8,128)(2,1)S(1)}, u32[]{:S(2)}, u32[]{:S(2)}) collective-permute-start(bf16[256,512]{1,0:T(8,128)(2,1)S(1)} %dynamic-slice_bitcast_fusion), channel_id=1, source_target_pairs={{0,1},{1,0},{2,3},{3,2},{4,5},{5,4},{6,7},{7,6},{8,9},{9,8},{10,11... | collective-permute-start | bytes 786440 | tf_op jit(solution)/shard_map/ppermute | solution.py:271
  52.7 12.2 %copy-start = (bf16[512,512]{1,0:T(8,128)(2,1)S(1)}, bf16[512,512]{1,0:T(8,128)(2,1)}, u32[]{:S(2)}) copy-start(bf16[512,512]{1,0:T(8,128)(2,1)} %get-tuple-element.48.refs_17_) | copy-start | bytes 1572868
  64.4 2.2 %collective-permute-start.19 = (bf16[64,512]{1,0:T(8,128)(2,1)S(1)}, bf16[64,512]{1,0:T(8,128)(2,1)S(1)}, u32[]{:S(2)}, u32[]{:S(2)}) collective-permute-start(bf16[64,512]{1,0:T(8,128)(2,1)S(1)} %fusion.3), channel_id=1, source_target_pairs={{0,1},{1,0},{2,3},{3,2},{4,5},{5,4},{6,7},{7,6},{8,9},{9,8},{10,11... | collective-permute-start | bytes 196616 | tf_op jit(solution)/shard_map/ppermute | solution.py:271
  65.0 5.5 %collective-permute-start.16 = (bf16[128,512]{1,0:T(8,128)(2,1)S(1)}, bf16[128,512]{1,0:T(8,128)(2,1)S(1)}, u32[]{:S(2)}, u32[]{:S(2)}) collective-permute-start(bf16[128,512]{1,0:T(8,128)(2,1)S(1)} %fusion), channel_id=1, source_target_pairs={{0,2},{1,3},{2,0},{3,1},{4,6},{5,7},{6,4},{7,5},{8,10},{9,11},{10,... | collective-permute-start | bytes 393224 | tf_op jit(solution)/shard_map/ppermute | solution.py:271
  70.6 28.3 %copy-start.16 = (bf16[64,512]{1,0:T(8,128)(2,1)S(1)}, bf16[64,512]{1,0:T(8,128)(2,1)}, u32[]{:S(2)}) copy-start(bf16[64,512]{1,0:T(8,128)(2,1)} %get-tuple-element.50) | copy-start | bytes 196612
  70.6 28.3 %copy-start.15 = (bf16[64,512]{1,0:T(8,128)(2,1)S(1)}, bf16[64,512]{1,0:T(8,128)(2,1)}, u32[]{:S(2)}) copy-start(bf16[64,512]{1,0:T(8,128)(2,1)} %get-tuple-element.51) | copy-start | bytes 196612
  70.6 30.6 %copy-start.14 = (bf16[64,512]{1,0:T(8,128)(2,1)S(1)}, bf16[64,512]{1,0:T(8,128)(2,1)}, u32[]{:S(2)}) copy-start(bf16[64,512]{1,0:T(8,128)(2,1)} %get-tuple-element.52) | copy-start | bytes 196612
  70.6 5.9 %collective-permute-start.17 = (bf16[64,512]{1,0:T(8,128)(2,1)S(1)}, bf16[64,512]{1,0:T(8,128)(2,1)S(1)}, u32[]{:S(2)}, u32[]{:S(2)}) collective-permute-start(bf16[64,512]{1,0:T(8,128)(2,1)S(1)} %fusion.2), channel_id=1, source_target_pairs={{0,8},{4,12},{8,0},{12,4},{1,9},{5,13},{9,1},{13,5},{2,10},{6,14},... | collective-permute-start | bytes 196616 | tf_op jit(solution)/shard_map/ppermute | solution.py:271
  73.0 5.8 %collective-permute-start.20 = (bf16[32,512]{1,0:T(8,128)(2,1)S(1)}, bf16[32,512]{1,0:T(8,128)(2,1)S(1)}, u32[]{:S(2)}, u32[]{:S(2)}) collective-permute-start(bf16[32,512]{1,0:T(8,128)(2,1)S(1)} %fusion.7), channel_id=1, source_target_pairs={{0,2},{1,3},{2,0},{3,1},{4,6},{5,7},{6,4},{7,5},{8,10},{9,11},{10,... | collective-permute-start | bytes 98312 | tf_op jit(solution)/shard_map/ppermute | solution.py:271
  76.6 4.2 %collective-permute-start.18 = (bf16[32,512]{1,0:T(8,128)(2,1)S(1)}, bf16[32,512]{1,0:T(8,128)(2,1)S(1)}, u32[]{:S(2)}, u32[]{:S(2)}) collective-permute-start(bf16[32,512]{1,0:T(8,128)(2,1)S(1)} %fusion.6), channel_id=1, source_target_pairs={{0,4},{4,0},{8,12},{12,8},{1,5},{5,1},{9,13},{13,9},{2,6},{6,2},{1... | collective-permute-start | bytes 98312 | tf_op jit(solution)/shard_map/ppermute | solution.py:271
  80.8 5.7 %collective-permute-start.21 = (bf16[64,512]{1,0:T(8,128)(2,1)S(1)}, bf16[64,512]{1,0:T(8,128)(2,1)S(1)}, u32[]{:S(2)}, u32[]{:S(2)}) collective-permute-start(bf16[64,512]{1,0:T(8,128)(2,1)S(1)} %pad_maximum_fusion.4), channel_id=1, source_target_pairs={{0,4},{4,0},{8,12},{12,8},{1,5},{5,1},{9,13},{13,9},{2,6},{6,2},{1... | collective-permute-start | bytes 196616 | tf_op jit(solution)/shard_map/ppermute | solution.py:271
  86.5 6.6 %collective-permute-start.22 = (bf16[96,512]{1,0:T(8,128)(2,1)S(1)}, bf16[96,512]{1,0:T(8,128)(2,1)S(1)}, u32[]{:S(2)}, u32[]{:S(2)}) collective-permute-start(bf16[96,512]{1,0:T(8,128)(2,1)S(1)} %pad_maximum_fusion.2), channel_id=1, source_target_pairs={{0,8},{4,12},{8,0},{12,4},{1,9},{5,13},{9,1},{13,5},{2,10},{6,14},... | collective-permute-start | bytes 294920 | tf_op jit(solution)/shard_map/ppermute | solution.py:271
  93.2 5.4 %collective-permute-start.23 = (bf16[160,512]{1,0:T(8,128)(2,1)S(1)}, bf16[160,512]{1,0:T(8,128)(2,1)S(1)}, u32[]{:S(2)}, u32[]{:S(2)}) collective-permute-start(bf16[160,512]{1,0:T(8,128)(2,1)S(1)} %pad_maximum_fusion.1), channel_id=1, source_target_pairs={{0,2},{1,3},{2,0},{3,1},{4,6},{5,7},{6,4},{7,5},{8,10},{9,11},{10,... | collective-permute-start | bytes 491528 | tf_op jit(solution)/shard_map/ppermute | solution.py:271
  98.8 12.9 %collective-permute-start.24 = (bf16[320,512]{1,0:T(8,128)(2,1)S(1)}, bf16[320,512]{1,0:T(8,128)(2,1)S(1)}, u32[]{:S(2)}, u32[]{:S(2)}) collective-permute-start(bf16[320,512]{1,0:T(8,128)(2,1)S(1)} %pad_maximum_fusion), channel_id=1, source_target_pairs={{0,1},{1,0},{2,3},{3,2},{4,5},{5,4},{6,7},{7,6},{8,9},{9,8},{10,11... | collective-permute-start | bytes 983048 | tf_op jit(solution)/shard_map/ppermute | solution.py:271
  98.8 6.9 %collective-permute-start.12 = (bf16[64,512]{1,0:T(8,128)(2,1)S(1)}, bf16[64,512]{1,0:T(8,128)(2,1)S(1)}, u32[]{:S(2)}, u32[]{:S(2)}) collective-permute-start(bf16[64,512]{1,0:T(8,128)(2,1)S(1)} %copy-done.16), channel_id=1, source_target_pairs={{0,4},{4,8},{8,12},{12,0},{1,5},{5,9},{9,13},{13,1},{2,6},{6,10},{... | collective-permute-start | bytes 196616 | tf_op jit(solution)/shard_map/ppermute | solution.py:276
  98.9 8.7 %collective-permute-start.13 = (bf16[64,512]{1,0:T(8,128)(2,1)S(1)}, bf16[64,512]{1,0:T(8,128)(2,1)S(1)}, u32[]{:S(2)}, u32[]{:S(2)}) collective-permute-start(bf16[64,512]{1,0:T(8,128)(2,1)S(1)} %copy-done.15), channel_id=1, source_target_pairs={{0,8},{4,12},{8,0},{12,4},{1,9},{5,13},{9,1},{13,5},{2,10},{6,14},... | collective-permute-start | bytes 196616 | tf_op jit(solution)/shard_map/ppermute | solution.py:276
  101.2 6.4 %collective-permute-start.14 = (bf16[64,512]{1,0:T(8,128)(2,1)S(1)}, bf16[64,512]{1,0:T(8,128)(2,1)S(1)}, u32[]{:S(2)}, u32[]{:S(2)}) collective-permute-start(bf16[64,512]{1,0:T(8,128)(2,1)S(1)} %copy-done.14), channel_id=1, source_target_pairs={{0,12},{4,0},{8,4},{12,8},{1,13},{5,1},{9,5},{13,9},{2,14},{6,2},{... | collective-permute-start | bytes 196616 | tf_op jit(solution)/shard_map/ppermute | solution.py:276
  105.7 1.9 %copy-start.4 = (bf16[64,512]{1,0:T(8,128)(2,1)}, bf16[64,512]{1,0:T(8,128)(2,1)S(1)}, u32[]{:S(2)}) copy-start(bf16[64,512]{1,0:T(8,128)(2,1)S(1)} %collective-permute-done.12.refs_5_) | copy-start | bytes 196612
  (13 other events, 8.3 us)

commit v5 on v4

--- a/solution.py
+++ b/solution.py
@@ -20,10 +20,11 @@
     return lax.dot_general(a, b, dims, preferred_element_type=F32)
 
 
-def silu_parts(value):
-    sig = 0.5 * jnp.tanh(0.5 * value) + 0.5
-    act = value * sig
-    return act, sig + act * (1.0 - sig)
+def silu_parts(half):
+    tanh = jnp.tanh(half)
+    upper = 1.0 + tanh
+    act = half * upper
+    return act, upper + act * (1.0 - tanh)
 
 
 def call(body, outs, args, flops=0, scratch=(), smem=(), far=(), far_out=(), order=()):
@@ -56,15 +57,6 @@
 
 def held(array):
     return pltpu.VMEM(array.shape, array.dtype)
-
-
-def lane_copies(source, target, sems, step):
-    return [
-        pltpu.make_async_copy(
-            source.at[:, pl.ds(i * step, step)], target.at[:, pl.ds(i * step, step)], sems.at[i]
-        )
-        for i in range(target.shape[1] // step)
-    ]
 
 
 def started(copies):
@@ -125,22 +117,6 @@
     return jnp.where(column == edges, 1.0, 0.0).astype(BF16)
 
 
-def prepare_kernel(step, part, basis, weight, filt, slope, basis_v, filt_v, slope_v, in_sems, sems):
-    rows = basis_v.shape[0]
-    arrive = loads([basis.at[pl.ds(part * rows, rows), :]], [basis_v], in_sems)
-    weight_t = weight[...].T
-    waited(arrive)
-    leave = lane_copies(filt_v, filt, sems.at[0], step), lane_copies(slope_v, slope, sems.at[1], step)
-    for i in range(len(leave[0])):
-        at = pl.ds(i * step, step)
-        act, grad = silu_parts(dot(weight_t, basis_v[at, :], NT))
-        filt_v[:, at] = act.astype(BF16)
-        leave[0][i].start()
-        slope_v[:, at] = grad.astype(BF16)
-        leave[1][i].start()
-    waited(leave[0] + leave[1])
-
-
 def lend_kernel(ranks, me, *refs):
     lists, edges, outs = refs[:ranks], refs[ranks], refs[ranks + 1 : 2 * ranks + 1]
     edges_v, sems = refs[2 * ranks + 1 :]
@@ -160,39 +136,38 @@
     dhidden[...] = dot(dot(hot, upstream_v[...]).astype(BF16), w_out_v[...], NT)
 
 
-def forward_kernel(ranks, step, me, count, *refs):
-    pieces, (src, dst), filt = refs[:ranks], refs[ranks : ranks + 2], refs[ranks + 2 : ranks + 4]
+def forward_kernel(ranks, step, place, count, *refs):
+    pieces, (src, dst, weight, basis) = refs[:ranks], refs[ranks : ranks + 4]
     outs = refs[ranks + 4 : 2 * ranks + 4]
-    filt_v, message, hot, sems = refs[2 * ranks + 4 :]
-    half = filt[0].shape[1]
-    arrive = loads(filt, [filt_v.at[:, pl.ds(i * half, half)] for i in range(2)], sems)
+    basis_v, message, hot, near_hot, sems = refs[2 * ranks + 4 :]
+    arrive = loads([basis], [basis_v], sems)
     per_owner = outs[0].shape[0]
     slots, block = ranks * per_owner, src.shape[1]
-    table = gathered(pieces).T
-    src_t = turned(src, per_owner, ranks, me[0])
-    dst_t = turned(dst, per_owner, ranks, me[0])
+    table, weight_t = gathered(pieces).T, (0.5 * weight[...]).T
+    src_t = turned(src, per_owner, ranks, place[0])
+    dst_t = turned(dst, per_owner, ranks, place[0])
     each = step // block
-    spans = [pl.ds(i * step, step) for i in range(2 * half // step)]
+    spans = [pl.ds(i * step, step) for i in range(basis.shape[0] // step)]
     for i, at in enumerate(spans):
-        message[:, at] = dot(table, hot_lanes(src_t, i * each, each, slots)).astype(BF16)
-    for i, at in enumerate(spans):
+        near_hot[:, at] = hot_lanes(src_t, i * each, each, slots)
         hot[:, at] = hot_lanes(dst_t, i * each, each, slots, count[0, 0])
     waited(arrive)
     for at in spans:
-        message[:, at] = message[:, at] * filt_v[:, at]
+        act = silu_parts(dot(weight_t, basis_v[at, :], NT))[0]
+        message[:, at] = (dot(table, near_hot[:, at]) * act).astype(BF16)
     scattered(dot(hot[...], message[...], NT).astype(BF16), outs)
 
 
 def return_kernel(ranks, *refs):
     pieces, (same, dhidden), outs = refs[:ranks], refs[ranks : ranks + 2], refs[ranks + 2 :]
     agg = dot(same[...], gathered(pieces))
-    scattered((dhidden[...] * silu_parts(agg)[1]).astype(BF16), outs)
+    scattered((dhidden[...] * (0.5 * silu_parts(0.5 * agg)[1])).astype(BF16), outs)
 
 
 def update_kernel(ranks, step, me, *refs):
     lists, pieces = refs[:ranks], refs[ranks : 2 * ranks]
-    edges, upstream, w_out, updated, term = refs[2 * ranks : 2 * ranks + 5]
-    edges_v, upstream_v, w_out_v, updated_v, hidden, sems, out_sems = refs[2 * ranks + 5 :]
+    edges, upstream, w_out, updated, kept, away = refs[2 * ranks : 2 * ranks + 6]
+    edges_v, upstream_v, w_out_v, updated_v, hidden, sems, out_sems = refs[2 * ranks + 6 :]
     arrive = loads([w_out, edges, upstream], [w_out_v, edges_v, upstream_v], sems)
     home = gathered(pieces)
     rows = edges.shape[0]
@@ -204,7 +179,8 @@
         for i, at in enumerate(spans)
     ]
     fresh = [
-        silu_parts(dot(hot_t[i * step : (i + 1) * step], home))[0].astype(BF16) for i in range(turns)
+        silu_parts(0.5 * dot(hot_t[i * step : (i + 1) * step], home))[0].astype(BF16)
+        for i in range(turns)
     ]
     waited(arrive)
     for i, at in enumerate(spans):
@@ -212,40 +188,41 @@
         updated_v[at, :] = total.astype(BF16)
         leave[i].start()
         hidden[:, at] = fresh[i].T
-    term[...] = dot(hidden[...], upstream_v[...]).astype(BF16)
+    half = kept.shape[0]
+    own = pl.multiple_of(me[1] * half, half)
+    other = pl.multiple_of((1 - me[1]) * half, half)
+    away[...] = dot(hidden[pl.ds(other, half), :], upstream_v[...]).astype(BF16)
+    kept[...] = dot(hidden[pl.ds(own, half), :], upstream_v[...])
     waited(leave)
 
 
-def backward_kernel(ranks, step, me, count, *refs):
+def backward_kernel(ranks, step, place, count, *refs):
     fetched, pieces = refs[:ranks], refs[ranks : 2 * ranks]
-    src, dst, basis = refs[2 * ranks : 2 * ranks + 3]
-    filt, slope = refs[2 * ranks + 3 : 2 * ranks + 5], refs[2 * ranks + 5 : 2 * ranks + 7]
-    weight, outs = refs[2 * ranks + 7], refs[2 * ranks + 8 : 3 * ranks + 8]
-    basis_v, filt_v, slope_v, message, dpre, hot, sems = refs[3 * ranks + 8 :]
-    half = filt[0].shape[1]
-    halves = [pl.ds(i * half, half) for i in range(2)]
-    first = loads(slope, [slope_v.at[:, at] for at in halves], sems.at[0])
-    second = loads([basis], [basis_v], sems.at[1])
-    third = loads(filt, [filt_v.at[:, at] for at in halves], sems.at[2])
+    src, dst, weight, basis, kept, away = refs[2 * ranks : 2 * ranks + 6]
+    outs = refs[2 * ranks + 6 : 3 * ranks + 6]
+    basis_v, message, dpre, hot, back_hot, total, sems = refs[3 * ranks + 6 :]
+    arrive = loads([basis], [basis_v], sems)
     per_owner = outs[0].shape[0]
     slots, block = ranks * per_owner, src.shape[1]
-    src_t = turned(src, per_owner, ranks, me[0])
-    dst_t = turned(dst, per_owner, ranks, me[0])
+    src_t = turned(src, per_owner, ranks, place[0])
+    dst_t = turned(dst, per_owner, ranks, place[0])
     near, back = gathered(fetched).T, gathered(pieces).T
+    weight_t = (0.5 * weight[...]).T
     each = step // block
-    spans = [pl.ds(i * step, step) for i in range(2 * half // step)]
+    spans = [pl.ds(i * step, step) for i in range(basis.shape[0] // step)]
     for i, at in enumerate(spans):
         hot[:, at] = hot_lanes(src_t, i * each, each, slots)
-        rows = dot(back, hot_lanes(dst_t, i * each, each, slots, count[0, 0])).astype(BF16)
-        message[:, at] = rows
-        dpre[:, at] = rows * dot(near, hot[:, at]).astype(BF16)
-    waited(first + second)
+        back_hot[:, at] = hot_lanes(dst_t, i * each, each, slots, count[0, 0])
+    waited(arrive)
     for at in spans:
-        dpre[:, at] = dpre[:, at] * slope_v[:, at]
-    weight[...] = dot(dpre[...], basis_v[...]).T
-    waited(third)
-    for at in spans:
-        message[:, at] = message[:, at] * filt_v[:, at]
+        act, slope = silu_parts(dot(weight_t, basis_v[at, :], NT))
+        rows = dot(back, back_hot[:, at]).astype(BF16)
+        message[:, at] = rows * act.astype(BF16)
+        dpre[:, at] = rows * dot(near, hot[:, at]).astype(BF16) * slope.astype(BF16)
+    total[...] = dot(dpre[...], basis_v[...]).T
+    half = kept.shape[0]
+    kept[...] = total[pl.ds(pl.multiple_of(place[1] * half, half), half), :]
+    away[...] = total[pl.ds(pl.multiple_of((1 - place[1]) * half, half), half), :].astype(BF16)
     scattered(dot(hot[...], message[...], NT).astype(BF16), outs)
 
 
@@ -297,29 +274,27 @@
     return range(lax.axis_size(axis).bit_length() - 1)
 
 
-def reduce_out(term):
-    for bit in bits_of("dp"):
-        term = halve(term, "dp", bit)
-    for bit in reversed(bits_of("graph")):
-        term = halve(term, "graph", bit)
-    return term.astype(BF16)
-
-
-def reduce_both(out, basis):
-    for bit in bits_of("dp"):
-        basis = halve(basis, "dp", bit)
-    basis = basis.astype(BF16)
+def joined(kept, away):
+    return kept + swap(away, "dp", 1).astype(F32)
+
+
+def summed(value, axis, bit):
+    own = value.astype(BF16)
+    return own.astype(F32) + swap(own, axis, 1 << bit).astype(F32)
+
+
+def finish(out, basis):
+    out, basis = out.astype(BF16), basis.astype(BF16)
     rows = basis.shape[0]
     for bit in bits_of("graph"):
-        got = swap(jnp.concatenate([basis, out]), "graph", 1 << bit)
+        own = jnp.concatenate([basis, out])
+        got = swap(own, "graph", 1 << bit)
         basis = (basis.astype(F32) + got[:rows].astype(F32)).astype(BF16)
-        out = double(out, got[rows:], "graph", bit)
-    for bit in reversed(bits_of("dp")):
-        rows = basis.shape[0]
-        got = swap(jnp.concatenate([basis, out]), "dp", 1 << bit)
-        basis = double(basis, got[:rows], "dp", bit)
-        out = double(out, got[rows:], "dp", bit)
-    return out.astype(F32), basis.astype(F32)
+        out = (out.astype(F32) + got[rows:].astype(F32)).astype(BF16)
+    for bit in reversed(bits_of("dp")[1:]):
+        out = double(out, swap(out, "dp", 1 << bit), "dp", bit)
+    got = swap(jnp.concatenate([basis, out]), "dp", 1)
+    return double(out, got[rows:], "dp", 0).astype(F32), double(basis, got[:rows], "dp", 0).astype(F32)
 
 
 def per_device(
@@ -336,7 +311,7 @@
 ):
     edges, upstream, basis = edge_emb[0], cotangent[0], trip_basis[0]
     ranks, copies = lax.axis_size("graph"), lax.axis_size("dp")
-    me = lax.axis_index("graph").astype(jnp.int32).reshape(1)
+    place = jnp.stack([lax.axis_index("graph"), lax.axis_index("dp") & 1]).astype(jnp.int32)
     edge_dev, width = edges.shape
     per_owner = fetch_rows.shape[3]
     slots = ranks * per_owner
@@ -344,63 +319,45 @@
     triplets, basis_width = basis.shape
     src, dst = trip_src[0], trip_dst[0]
     pieces = [shape((per_owner, width))] * ranks
-    half = shape((width, triplets // 2))
     plane, hot = shape((width, triplets)), shape((slots, triplets))
-    step = 512
+    step = 256
     wide = 2 * triplets * slots * width
     narrow = 2 * triplets * basis_width * width
     dma = pltpu.SemaphoreType.DMA
 
     both = jnp.concatenate([fetch_rows[0, 0], store_rows[0, 0]], axis=1)
     lists = exchange([both] * ranks, 1)
-
-    def prepare(part):
-        rows = triplets // 2
-        return call(
-            functools.partial(prepare_kernel, step, part),
-            [half, half],
-            [basis, w_basis],
-            flops=4 * narrow,
-            far=(0,),
-            far_out=(0, 1),
-            scratch=[pltpu.VMEM((rows, basis_width), BF16), held(half), held(half)]
-            + [dma((1,)), dma((2, rows // step))],
-        )
-
-    early = prepare(0)
     lend = call(
         functools.partial(lend_kernel, ranks),
         pieces,
-        [me] + lists + [edges],
+        [place] + lists + [edges],
         smem=(0,),
         far=(ranks + 1,),
         flops=2 * slots * edge_dev * width,
         scratch=[held(edges), dma((1,))],
-        order=[early[0]],
     )
     fetched = exchange(lend, -1)
-    late = prepare(1)
-    filt, slope = [early[0], late[0]], [early[1], late[1]]
-    partial_rows = call(
-        functools.partial(forward_kernel, ranks, step),
-        pieces,
-        [me, block_count] + fetched + [src, dst] + filt,
-        smem=(0, 1),
-        far=(ranks + 4, ranks + 5),
-        flops=2 * wide,
-        scratch=[held(plane), held(plane), held(hot), dma((2,))],
-    )
-    home = exchange(partial_rows, 1)
     same, dhidden = call(
         functools.partial(owner_kernel, ranks),
         [shape((slots, slots)), shape((slots, width), F32)],
-        [me] + lists + [upstream, w_out],
+        [place] + lists + [upstream, w_out],
         smem=(0,),
         far=(ranks + 1, ranks + 2),
         flops=4 * slots * edge_dev * width,
         scratch=[held(upstream), held(w_out), dma((2,))],
-        order=[partial_rows[0]],
-    )
+        order=[lend[0]],
+    )
+    partial_rows = call(
+        functools.partial(forward_kernel, ranks, step),
+        pieces,
+        [place, block_count] + fetched + [src, dst, w_basis, basis],
+        smem=(0, 1),
+        far=(ranks + 5,),
+        flops=2 * wide + narrow,
+        scratch=[held(basis), held(plane), held(hot), held(hot), dma((1,))],
+        order=[same],
+    )
+    home = exchange(partial_rows, 1)
     back = call(
         functools.partial(return_kernel, ranks),
         pieces,
@@ -408,10 +365,10 @@
         flops=2 * slots * slots * width,
     )
     dpartial = exchange(back, -1)
-    updated, out_term = call(
+    updated, out_kept, out_away = call(
         functools.partial(update_kernel, ranks, 256),
-        [shape((edge_dev, width)), shape((width, width))],
-        [me] + lists + home + [edges, upstream, w_out],
+        [shape((edge_dev, width)), shape((width // 2, width), F32), shape((width // 2, width))],
+        [place] + lists + home + [edges, upstream, w_out],
         smem=(0,),
         far=(2 * ranks + 1, 2 * ranks + 2, 2 * ranks + 3),
         far_out=(0,),
@@ -420,22 +377,30 @@
         + [pltpu.VMEM((width, edge_dev), BF16), dma((3,)), dma((edge_dev // 256,))],
         order=[back[0]],
     )
-    out_part = reduce_out(out_term)
-    basis_term, *dfetch = call(
+    out_part = joined(out_kept, out_away)
+    basis_half = basis_width // 2
+    basis_kept, basis_away, *dfetch = call(
         functools.partial(backward_kernel, ranks, step),
-        [shape((basis_width, width), F32)] + pieces,
-        [me, block_count] + fetched + dpartial + [src, dst, basis] + filt + slope,
+        [shape((basis_half, width), F32), shape((basis_half, width))] + pieces,
+        [place, block_count] + fetched + dpartial + [src, dst, w_basis, basis],
         smem=(0, 1),
-        far=tuple(range(2 * ranks + 4, 2 * ranks + 9)),
-        flops=3 * wide + narrow,
-        scratch=[held(basis)] + [held(plane)] * 4 + [held(hot), dma((3, 2))],
-        order=[out_term],
-    )
-    grad_w_out, grad_w_basis = reduce_both(out_part, basis_term)
+        far=(2 * ranks + 5,),
+        flops=3 * wide + 2 * narrow,
+        scratch=[held(basis), held(plane), held(plane), held(hot), held(hot)]
+        + [pltpu.VMEM((basis_width, width), F32), dma((1,))],
+        order=[out_part],
+    )
+    returned = exchange(dfetch, 1)
+    basis_part = joined(basis_kept, basis_away)
+    for bit in bits_of("dp")[1:]:
+        out_part = halve(out_part, "dp", bit)
+        basis_part = summed(basis_part, "dp", bit)
+    out_part, basis_part, returned = lax.optimization_barrier((out_part, basis_part, returned))
+    grad_w_out, grad_w_basis = finish(out_part, basis_part)
     (grad_edge,) = call(
         functools.partial(final_kernel, ranks, 256),
         [shape((edge_dev, width))],
-        [me] + lists + exchange(dfetch, 1) + [upstream],
+        [place] + lists + returned + [upstream],
         smem=(0,),
         far=(2 * ranks + 1,),
         far_out=(0,),
@@ -443,7 +408,7 @@
         scratch=[held(upstream), held(upstream), dma((1,)), dma((edge_dev // 256,))],
     )
     out_scale = jnp.sqrt(F32(copies * ranks * edge_dev))
-    basis_scale = jnp.sqrt(F32(copies * ranks * blocks * block_rows))
+    basis_scale = 2.0 * jnp.sqrt(F32(copies * ranks * blocks * block_rows))
     return (updated[None], grad_edge[None], grad_w_out / out_scale, grad_w_basis / basis_scale)
 
 

time: 114 us -> 108 us (0.947)
  Pallas kernels: 43 us -> 33.5 us
  waiting for transfers between devices: 25.6 us -> 34.7 us
  starting transfers between devices: 34.2 us -> 26.8 us
  other arithmetic: 3.89 us -> 6.32 us
    pallas_call x9 -> x7, Pallas kernels: 43 us -> 33.5 us  [call(): pl.pallas_call(inner if order else body, out_shape=tuple(outs), in_specs=...]
    ppermute x10 -> x8, starting transfers between devices: 13.1 us -> 4.62 us  [swap(): lax.ppermute(value, axis, [(k, k ^ mask) for k in range(lax.axis_size(axi...]
    ppermute x15, waiting for transfers between devices: 5.69 us -> 11.1 us  [shift(): lax.ppermute(value, axis, [(k, (k + by) % count) for k in range(count)])]
    ppermute x10 -> x8, waiting for transfers between devices: 19.9 us -> 23.6 us  [swap(): lax.ppermute(value, axis, [(k, k ^ mask) for k in range(lax.axis_size(axi...]
    add x0 -> x2, other arithmetic: none -> 1.93 us  [the longest x1 1.91 us: joined(): return kept + swap(away, 'dp', 1).astype(F32)]
    unnamed x40 -> x42, local copies, waits for them, and re-layouts: 3.14 us -> 4.39 us
  transfers between devices with their start and end apart: 25 -> 23, of which waited for: 9 -> 10; matrix products, arithmetic and copies ran while one was open for 3% -> 3% of each run, Pallas kernels for 28% -> 7%
where the time goes in v5:
time: 108 us; the launch traced here: 107 us
  waiting for transfers between devices  34.7 us (32%)
  Pallas kernels  33.5 us (31%)
  starting transfers between devices  26.8 us (25%)
  other arithmetic  6.32 us (6%)
  local copies, waits for them, and re-layouts  4.44 us (4%)
  between operations  1.61 us (1%)
    pallas_call x7, Pallas kernels, call(): pl.pallas_call(inner if order else body, out_shape=tuple(outs), in_specs=...  33.5 us
    ppermute x8, waiting for transfers between devices, swap(): lax.ppermute(value, axis, [(k, k ^ mask) for k in range(lax.axis_size(axi...  23.6 us
    ppermute x15, starting transfers between devices, shift(): lax.ppermute(value, axis, [(k, (k + by) % count) for k in range(count)])  22.2 us
    ppermute x15, waiting for transfers between devices, shift(): lax.ppermute(value, axis, [(k, (k + by) % count) for k in range(count)])  11.1 us
    ppermute x8, starting transfers between devices, swap(): lax.ppermute(value, axis, [(k, k ^ mask) for k in range(lax.axis_size(axi...  4.62 us
    unnamed x42, local copies, waits for them, and re-layouts  4.39 us
  transfers between devices with their start and end apart: 23, of which 10 were waited for; matrix products, arithmetic and copies ran while one was open for 3% of the time, Pallas kernels for 7%

profile of v5, /device:TPU:0, one launch (start us, length us, event | category | flops | bytes accessed | tf_op | source)
XLA Modules:
  0.0 107.4 jit_solution(12384727892584517896)
XLA Ops:
  1.3 0.8 pad_add_fusion.refs_0_.refs_1_
  2.1 5.0 %collective-permute-start.2 = (s32[4,128]{1,0:T(4,128)S(1)}, s32[4,128]{1,0:T(4,128)S(1)}, u32[]{:S(2)}, u32[]{:S(2)}) collective-permute-start(s32[4,128]{1,0:T(4,128)S(1)} %pad_add_fusion.refs_0_.refs_1_), channel_id=1, source_target_pairs={{0,12},{4,0},{8,4},{12,8},{1,13},{5,1},{9,5},{13,9},{2,14},{6,2},{... | collective-permute-start | bytes 6152 | tf_op jit(solution)/shard_map/ppermute | solution.py:253
  7.1 1.0 collective-permute-start
  8.7 2.9 %collective-permute-done.1.refs_2_.refs_3_ = s32[4,128]{1,0:T(4,128)S(1)} collective-permute-done((s32[4,128]{1,0:T(4,128)S(1)}, s32[4,128]{1,0:T(4,128)S(1)}, u32[]{:S(2)}, u32[]{:S(2)}) %collective-permute-start.1) | collective-permute-done | bytes 2080 | tf_op jit(solution)/shard_map/ppermute | solution.py:253
  11.6 0.9 collective-permute-done.refs_1_.refs_2_
  13.1 3.1 %shard_map.129 = (bf16[64,512]{1,0:T(8,128)(2,1)}, bf16[64,512]{1,0:T(8,128)(2,1)}, bf16[64,512]{1,0:T(8,128)(2,1)}, bf16[64,512]{1,0:T(8,128)(2,1)}) custom-call(s32[2]{0:T(128)} %pad_add_fusion.1.me.refs_0_, s32[4,128]{1,0:T(4,128)} %copy-done.7, s32[4,128]{1,0:T(4,128)} %copy-done.10, s32[4,128]{1,0:T(4,128)} %copy-done.9, s32[4,128]{1,0:T(4,128)} %copy-done.8, ...), custom_call_target="tpu_custom_call" | custom-call | flops 268435456 | bytes 1318920 | tf_op jit(solution)/shard_map/pallas_call | solution.py:43
  17.5 1.9 %collective-permute-start.5 = (bf16[64,512]{1,0:T(8,128)(2,1)}, bf16[64,512]{1,0:T(8,128)(2,1)S(1)}, u32[]{:S(2)}, u32[]{:S(2)}) collective-permute-start(bf16[64,512]{1,0:T(8,128)(2,1)} %get-tuple-element.36), channel_id=1, source_target_pairs={{0,4},{4,8},{8,12},{12,0},{1,5},{5,9},{9,13},{13,1},{2,6},{6,10},{... | collective-permute-start | bytes 196616 | tf_op jit(solution)/shard_map/ppermute | solution.py:253
  20.1 3.9 %shard_map.130 = (bf16[256,256]{1,0:T(8,128)(2,1)}, f32[256,512]{1,0:T(8,128)}) custom-call(s32[2]{0:T(128)} %pad_add_fusion.1.me.refs_0_, s32[4,128]{1,0:T(4,128)} %copy-done.7, s32[4,128]{1,0:T(4,128)} %copy-done.10, s32[4,128]{1,0:T(4,128)} %copy-done.9, s32[4,128]{1,0:T(4,128)} %copy-done.8, bf16[1024,512]{1,0:T(8,128)(2,1)} %bitcast.20, ...), custom_call_target="tpu_custom_call" | custom-call | flops 536870912 | bytes 2301960 | tf_op jit(solution)/shard_map/pallas_call | solution.py:43
  24.7 6.4 %shard_map.131 = (bf16[64,512]{1,0:T(8,128)(2,1)}, bf16[64,512]{1,0:T(8,128)(2,1)}, bf16[64,512]{1,0:T(8,128)(2,1)}, bf16[64,512]{1,0:T(8,128)(2,1)}) custom-call(s32[2]{0:T(128)} %pad_add_fusion.1.me.refs_0_, s32[1,1]{1,0:T(1,128)S(6)} %copy.14.refs_1_, bf16[64,512]{1,0:T(8,128)(2,1)} %get-tuple-element.33.refs_7_.refs_2_, bf16[64,512]{1,0:T(8,128)(2,1)} %copy-done.12, ...), custom_call_target="tpu_custom_call" | custom-call | flops 2684354560 | bytes 1867788 | tf_op jit(solution)/shard_map/pallas_call | solution.py:43
  31.1 1.0 collective-permute-start.6
  32.0 1.5 %collective-permute-start.7 = (bf16[64,512]{1,0:T(8,128)(2,1)}, bf16[64,512]{1,0:T(8,128)(2,1)S(1)}, u32[]{:S(2)}, u32[]{:S(2)}) collective-permute-start(bf16[64,512]{1,0:T(8,128)(2,1)} %get-tuple-element.40), channel_id=1, source_target_pairs={{0,8},{4,12},{8,0},{12,4},{1,9},{5,13},{9,1},{13,5},{2,10},{6,14},... | collective-permute-start | bytes 196616 | tf_op jit(solution)/shard_map/ppermute | solution.py:253
  33.6 2.3 %collective-permute-start.8 = (bf16[64,512]{1,0:T(8,128)(2,1)}, bf16[64,512]{1,0:T(8,128)(2,1)S(1)}, u32[]{:S(2)}, u32[]{:S(2)}) collective-permute-start(bf16[64,512]{1,0:T(8,128)(2,1)} %get-tuple-element.41), channel_id=1, source_target_pairs={{0,12},{4,0},{8,4},{12,8},{1,13},{5,1},{9,5},{13,9},{2,14},{6,2},{... | collective-permute-start | bytes 196616 | tf_op jit(solution)/shard_map/ppermute | solution.py:253
  35.9 1.6 %collective-permute-done.6.refs_1_.refs_6_ = bf16[64,512]{1,0:T(8,128)(2,1)S(1)} collective-permute-done((bf16[64,512]{1,0:T(8,128)(2,1)}, bf16[64,512]{1,0:T(8,128)(2,1)S(1)}, u32[]{:S(2)}, u32[]{:S(2)}) %collective-permute-start.6) | collective-permute-done | bytes 65568 | tf_op jit(solution)/shard_map/ppermute | solution.py:253
  37.5 1.3 %collective-permute-done.7.refs_2_.refs_7_ = bf16[64,512]{1,0:T(8,128)(2,1)S(1)} collective-permute-done((bf16[64,512]{1,0:T(8,128)(2,1)}, bf16[64,512]{1,0:T(8,128)(2,1)S(1)}, u32[]{:S(2)}, u32[]{:S(2)}) %collective-permute-start.7) | collective-permute-done | bytes 65568 | tf_op jit(solution)/shard_map/ppermute | solution.py:253
  39.5 2.2 %shard_map.132 = (bf16[64,512]{1,0:T(8,128)(2,1)}, bf16[64,512]{1,0:T(8,128)(2,1)}, bf16[64,512]{1,0:T(8,128)(2,1)}, bf16[64,512]{1,0:T(8,128)(2,1)}) custom-call(bf16[64,512]{1,0:T(8,128)(2,1)} %get-tuple-element.38.refs_0_.refs_5_, bf16[64,512]{1,0:T(8,128)(2,1)} %copy-done.1, bf16[64,512]{1,0:T(8,128)(2,1)} %copy-done.2, bf16[64,512]{1,0:T(8,128)(2,1)} %copy-done.3, ...), custom_call_target="tpu_custom_call" | custom-call | flops 67108864 | bytes 1179648 | tf_op jit(solution)/shard_map/pallas_call | solution.py:43
  41.7 5.1 %shard_map.133 = (bf16[1024,512]{1,0:T(8,128)(2,1)}, f32[256,512]{1,0:T(8,128)}, bf16[256,512]{1,0:T(8,128)(2,1)}) custom-call(s32[2]{0:T(128)} %pad_add_fusion.1.me.refs_0_, s32[4,128]{1,0:T(4,128)} %copy-done.7, s32[4,128]{1,0:T(4,128)} %copy-done.10, s32[4,128]{1,0:T(4,128)} %copy-done.9, s32[4,128]{1,0:T(4,128)} %copy-done.8, ...), custom_call_target="tpu_custom_call" | custom-call | flops 1342177280 | bytes 4792328 | tf_op jit(solution)/shard_map/pallas_call | solution.py:43
  46.9 3.3 %collective-permute-start.11 = (bf16[64,512]{1,0:T(8,128)(2,1)S(1)}, bf16[64,512]{1,0:T(8,128)(2,1)S(1)}, u32[]{:S(2)}, u32[]{:S(2)}) collective-permute-start(bf16[64,512]{1,0:T(8,128)(2,1)S(1)} %copy-done.19), channel_id=1, source_target_pairs={{0,12},{4,0},{8,4},{12,8},{1,13},{5,1},{9,5},{13,9},{2,14},{6,2},{... | collective-permute-start | bytes 196616 | tf_op jit(solution)/shard_map/ppermute | solution.py:253
  50.9 1.9 %convert_add_fusion.refs_14_ = f32[256,512]{1,0:T(8,128)} fusion(f32[256,512]{1,0:T(8,128)} %get-tuple-element.45, bf16[256,512]{1,0:T(8,128)(2,1)S(1)} %collective-permute-done.9), kind=kLoop, calls=%fused_computation.2 | loop fusion | flops 262144 | bytes 1310720 | tf_op jit(solution)/shard_map/add | solution.py:278
  52.8 4.3 %collective-permute-done.12.refs_8_ = bf16[64,512]{1,0:T(8,128)(2,1)S(1)} collective-permute-done((bf16[64,512]{1,0:T(8,128)(2,1)S(1)}, bf16[64,512]{1,0:T(8,128)(2,1)S(1)}, u32[]{:S(2)}, u32[]{:S(2)}) %collective-permute-start.12) | collective-permute-done | bytes 65568 | tf_op jit(solution)/shard_map/ppermute | solution.py:253
  58.4 9.3 %shard_map.134 = (f32[64,512]{1,0:T(8,128)}, bf16[64,512]{1,0:T(8,128)(2,1)}, bf16[64,512]{1,0:T(8,128)(2,1)}, bf16[64,512]{1,0:T(8,128)(2,1)}, bf16[64,512]{1,0:T(8,128)(2,1)}, /*index=5*/bf16[64,512]{1,0:T(8,128)(2,1)}) custom-call(s32[2]{0:T(128)} %pad_add_fusion.1.me.refs_0_, s32[1,1]{1,0:T(1,128)S(6)} %copy.14.refs_1_, ...), custom_call_target="tpu_custom_call" | custom-call | flops 4294967296 | bytes 2719756 | tf_op jit(solution)/shard_map/pallas_call | solution.py:43
  67.9 2.3 %collective-permute-start.17 = (bf16[64,512]{1,0:T(8,128)(2,1)}, bf16[64,512]{1,0:T(8,128)(2,1)S(1)}, u32[]{:S(2)}, u32[]{:S(2)}) collective-permute-start(bf16[64,512]{1,0:T(8,128)(2,1)} %get-tuple-element.54), channel_id=1, source_target_pairs={{0,8},{4,12},{8,0},{12,4},{1,9},{5,13},{9,1},{13,5},{2,10},{6,14},... | collective-permute-start | bytes 196616 | tf_op jit(solution)/shard_map/ppermute | solution.py:253
  70.2 1.8 %collective-permute-start.18 = (bf16[64,512]{1,0:T(8,128)(2,1)}, bf16[64,512]{1,0:T(8,128)(2,1)S(1)}, u32[]{:S(2)}, u32[]{:S(2)}) collective-permute-start(bf16[64,512]{1,0:T(8,128)(2,1)} %get-tuple-element.55), channel_id=1, source_target_pairs={{0,12},{4,0},{8,4},{12,8},{1,13},{5,1},{9,5},{13,9},{2,14},{6,2},{... | collective-permute-start | bytes 196616 | tf_op jit(solution)/shard_map/ppermute | solution.py:253
  72.0 0.9 add_convert_fusion.4
  72.9 1.6 %collective-permute-start.15 = (bf16[64,512]{1,0:T(8,128)(2,1)S(1)}, bf16[64,512]{1,0:T(8,128)(2,1)S(1)}, u32[]{:S(2)}, u32[]{:S(2)}) collective-permute-start(bf16[64,512]{1,0:T(8,128)(2,1)S(1)} %add_convert_fusion.4), channel_id=1, source_target_pairs={{0,2},{1,3},{2,0},{3,1},{4,6},{5,7},{6,4},{7,5},{8,10},{9,11},{10,... | collective-permute-start | bytes 196616 | tf_op jit(solution)/shard_map/ppermute | solution.py:248
  75.1 2.8 %collective-permute-done.15 = bf16[64,512]{1,0:T(8,128)(2,1)S(1)} collective-permute-done((bf16[64,512]{1,0:T(8,128)(2,1)S(1)}, bf16[64,512]{1,0:T(8,128)(2,1)S(1)}, u32[]{:S(2)}, u32[]{:S(2)}) %collective-permute-start.15) | collective-permute-done | bytes 65568 | tf_op jit(solution)/shard_map/ppermute | solution.py:248
  78.0 2.0 %collective-permute-done.10 = bf16[128,512]{1,0:T(8,128)(2,1)S(1)} collective-permute-done((bf16[128,512]{1,0:T(8,128)(2,1)S(1)}, bf16[128,512]{1,0:T(8,128)(2,1)S(1)}, u32[]{:S(2)}, u32[]{:S(2)}) %collective-permute-start.10) | collective-permute-done | bytes 131104 | tf_op jit(solution)/shard_map/ppermute | solution.py:248
  81.0 5.6 %collective-permute-done.19 = bf16[192,512]{1,0:T(8,128)(2,1)S(1)} collective-permute-done((bf16[192,512]{1,0:T(8,128)(2,1)S(1)}, bf16[192,512]{1,0:T(8,128)(2,1)S(1)}, u32[]{:S(2)}, u32[]{:S(2)}) %collective-permute-start.19) | collective-permute-done | bytes 196640 | tf_op jit(solution)/shard_map/ppermute | solution.py:248
  86.7 1.8 %collective-permute-start.20 = (bf16[192,512]{1,0:T(8,128)(2,1)S(1)}, bf16[192,512]{1,0:T(8,128)(2,1)S(1)}, u32[]{:S(2)}, u32[]{:S(2)}) collective-permute-start(bf16[192,512]{1,0:T(8,128)(2,1)S(1)} %pad_maximum_fusion.2), channel_id=1, source_target_pairs={{0,8},{4,12},{8,0},{12,4},{1,9},{5,13},{9,1},{13,5},{2,10},{6,14},... | collective-permute-start | bytes 589832 | tf_op jit(solution)/shard_map/ppermute | solution.py:248
  88.5 8.3 %collective-permute-done.20 = bf16[192,512]{1,0:T(8,128)(2,1)S(1)} collective-permute-done((bf16[192,512]{1,0:T(8,128)(2,1)S(1)}, bf16[192,512]{1,0:T(8,128)(2,1)S(1)}, u32[]{:S(2)}, u32[]{:S(2)}) %collective-permute-start.20) | collective-permute-done | bytes 196640 | tf_op jit(solution)/shard_map/ppermute | solution.py:248
  97.0 4.8 %collective-permute-done.21 = bf16[128,512]{1,0:T(8,128)(2,1)S(1)} collective-permute-done((bf16[128,512]{1,0:T(8,128)(2,1)S(1)}, bf16[128,512]{1,0:T(8,128)(2,1)S(1)}, u32[]{:S(2)}, u32[]{:S(2)}) %collective-permute-start.21) | collective-permute-done | bytes 131104 | tf_op jit(solution)/shard_map/ppermute | solution.py:248
  102.0 3.4 %shard_map.135 = bf16[1024,512]{1,0:T(8,128)(2,1)} custom-call(s32[2]{0:T(128)} %pad_add_fusion.1.me.refs_0_, s32[4,128]{1,0:T(4,128)} %copy-done.7, s32[4,128]{1,0:T(4,128)} %copy-done.10, s32[4,128]{1,0:T(4,128)} %copy-done.9, s32[4,128]{1,0:T(4,128)} %copy-done.8, bf16[64,512]{1,0:T(8,128)(2,1)} %get-tuple-element.56.refs_4_, bf16[64,512]{1,0:T(8,128)(2,1)} %copy-done.4, ...), custom_call_target="tpu_custom_call" | custom-call | flops 268435456 | bytes 2367496 | tf_op jit(solution)/shard_map/pallas_call | solution.py:43
  106.3 1.1 %convert_multiply_fusion = f32[512,512]{1,0:T(8,128)} fusion(bf16[256,512]{1,0:T(8,128)(2,1)S(1)} %slice.28, bf16[256,512]{1,0:T(8,128)(2,1)S(1)} %maximum_select_fusion.1, pred[]{:T(512)S(6)} %eq.7), kind=kLoop, calls=%fused_computation | loop fusion | flops 2883584 | bytes 1572865 | tf_op jit(solution)/shard_map/div | solution.py:412
  (82 shorter events, 9.3 us)
Async XLA Ops:
  2.1 6.1 %copy-start.7 = (s32[4,128]{1,0:T(4,128)}, s32[4,128]{1,0:T(4,128)S(1)}, u32[]{:S(2)}) copy-start(s32[4,128]{1,0:T(4,128)S(1)} %pad_add_fusion.refs_0_.refs_1_) | copy-start | bytes 6148
  2.1 6.7 %collective-permute-start.2 = (s32[4,128]{1,0:T(4,128)S(1)}, s32[4,128]{1,0:T(4,128)S(1)}, u32[]{:S(2)}, u32[]{:S(2)}) collective-permute-start(s32[4,128]{1,0:T(4,128)S(1)} %pad_add_fusion.refs_0_.refs_1_), channel_id=1, source_target_pairs={{0,12},{4,0},{8,4},{12,8},{1,13},{5,1},{9,5},{13,9},{2,14},{6,2},{... | collective-permute-start | bytes 6152 | tf_op jit(solution)/shard_map/ppermute | solution.py:253
  7.1 4.5 %collective-permute-start.1 = (s32[4,128]{1,0:T(4,128)S(1)}, s32[4,128]{1,0:T(4,128)S(1)}, u32[]{:S(2)}, u32[]{:S(2)}) collective-permute-start(s32[4,128]{1,0:T(4,128)S(1)} %pad_add_fusion.refs_0_.refs_1_), channel_id=1, source_target_pairs={{0,8},{4,12},{8,0},{12,4},{1,9},{5,13},{9,1},{13,5},{2,10},{6,14},... | collective-permute-start | bytes 6152 | tf_op jit(solution)/shard_map/ppermute | solution.py:253
  7.1 5.4 %collective-permute-start = (s32[4,128]{1,0:T(4,128)S(1)}, s32[4,128]{1,0:T(4,128)S(1)}, u32[]{:S(2)}, u32[]{:S(2)}) collective-permute-start(s32[4,128]{1,0:T(4,128)S(1)} %pad_add_fusion.refs_0_.refs_1_), channel_id=1, source_target_pairs={{0,4},{4,8},{8,12},{12,0},{1,5},{5,9},{9,13},{13,1},{2,6},{6,10},{... | collective-permute-start | bytes 6152 | tf_op jit(solution)/shard_map/ppermute | solution.py:253
  8.7 3.8 %copy-start.8 = (s32[4,128]{1,0:T(4,128)}, s32[4,128]{1,0:T(4,128)S(1)}, u32[]{:S(2)}) copy-start(s32[4,128]{1,0:T(4,128)S(1)} %collective-permute-done.2.refs_3_.refs_4_) | copy-start | bytes 6148
  11.6 0.9 copy-start.9
  16.2 7.8 %collective-permute-start.3 = (bf16[64,512]{1,0:T(8,128)(2,1)}, bf16[64,512]{1,0:T(8,128)(2,1)S(1)}, u32[]{:S(2)}, u32[]{:S(2)}) collective-permute-start(bf16[64,512]{1,0:T(8,128)(2,1)} %get-tuple-element.34), channel_id=1, source_target_pairs={{0,12},{4,0},{8,4},{12,8},{1,13},{5,1},{9,5},{13,9},{2,14},{6,2},{... | collective-permute-start | bytes 196616 | tf_op jit(solution)/shard_map/ppermute | solution.py:253
  16.8 7.2 %collective-permute-start.4 = (bf16[64,512]{1,0:T(8,128)(2,1)}, bf16[64,512]{1,0:T(8,128)(2,1)S(1)}, u32[]{:S(2)}, u32[]{:S(2)}) collective-permute-start(bf16[64,512]{1,0:T(8,128)(2,1)} %get-tuple-element.35), channel_id=1, source_target_pairs={{0,8},{4,12},{8,0},{12,4},{1,9},{5,13},{9,1},{13,5},{2,10},{6,14},... | collective-permute-start | bytes 196616 | tf_op jit(solution)/shard_map/ppermute | solution.py:253
  17.5 6.6 %collective-permute-start.5 = (bf16[64,512]{1,0:T(8,128)(2,1)}, bf16[64,512]{1,0:T(8,128)(2,1)S(1)}, u32[]{:S(2)}, u32[]{:S(2)}) collective-permute-start(bf16[64,512]{1,0:T(8,128)(2,1)} %get-tuple-element.36), channel_id=1, source_target_pairs={{0,4},{4,8},{8,12},{12,0},{1,5},{5,9},{9,13},{13,1},{2,6},{6,10},{... | collective-permute-start | bytes 196616 | tf_op jit(solution)/shard_map/ppermute | solution.py:253
  31.1 6.4 %collective-permute-start.6 = (bf16[64,512]{1,0:T(8,128)(2,1)}, bf16[64,512]{1,0:T(8,128)(2,1)S(1)}, u32[]{:S(2)}, u32[]{:S(2)}) collective-permute-start(bf16[64,512]{1,0:T(8,128)(2,1)} %get-tuple-element.39), channel_id=1, source_target_pairs={{0,4},{4,8},{8,12},{12,0},{1,5},{5,9},{9,13},{13,1},{2,6},{6,10},{... | collective-permute-start | bytes 196616 | tf_op jit(solution)/shard_map/ppermute | solution.py:253
  32.0 6.8 %collective-permute-start.7 = (bf16[64,512]{1,0:T(8,128)(2,1)}, bf16[64,512]{1,0:T(8,128)(2,1)S(1)}, u32[]{:S(2)}, u32[]{:S(2)}) collective-permute-start(bf16[64,512]{1,0:T(8,128)(2,1)} %get-tuple-element.40), channel_id=1, source_target_pairs={{0,8},{4,12},{8,0},{12,4},{1,9},{5,13},{9,1},{13,5},{2,10},{6,14},... | collective-permute-start | bytes 196616 | tf_op jit(solution)/shard_map/ppermute | solution.py:253
  33.6 5.2 %collective-permute-start.8 = (bf16[64,512]{1,0:T(8,128)(2,1)}, bf16[64,512]{1,0:T(8,128)(2,1)S(1)}, u32[]{:S(2)}, u32[]{:S(2)}) collective-permute-start(bf16[64,512]{1,0:T(8,128)(2,1)} %get-tuple-element.41), channel_id=1, source_target_pairs={{0,12},{4,0},{8,4},{12,8},{1,13},{5,1},{9,5},{13,9},{2,14},{6,2},{... | collective-permute-start | bytes 196616 | tf_op jit(solution)/shard_map/ppermute | solution.py:253
  37.5 1.3 %copy-start.1 = (bf16[64,512]{1,0:T(8,128)(2,1)}, bf16[64,512]{1,0:T(8,128)(2,1)S(1)}, u32[]{:S(2)}) copy-start(bf16[64,512]{1,0:T(8,128)(2,1)S(1)} %collective-permute-done.6.refs_1_.refs_6_) | copy-start | bytes 196612
  41.7 5.2 %copy-start.19 = (bf16[64,512]{1,0:T(8,128)(2,1)S(1)}, bf16[64,512]{1,0:T(8,128)(2,1)}, u32[]{:S(2)}) copy-start(bf16[64,512]{1,0:T(8,128)(2,1)} %get-tuple-element.47) | copy-start | bytes 196612
  41.7 8.6 %copy-start.17 = (bf16[64,512]{1,0:T(8,128)(2,1)S(1)}, bf16[64,512]{1,0:T(8,128)(2,1)}, u32[]{:S(2)}) copy-start(bf16[64,512]{1,0:T(8,128)(2,1)} %get-tuple-element.48) | copy-start | bytes 196612
  41.7 8.6 %copy-start.15 = (bf16[64,512]{1,0:T(8,128)(2,1)S(1)}, bf16[64,512]{1,0:T(8,128)(2,1)}, u32[]{:S(2)}) copy-start(bf16[64,512]{1,0:T(8,128)(2,1)} %get-tuple-element.49) | copy-start | bytes 196612
  46.8 4.1 %collective-permute-start.9 = (bf16[256,512]{1,0:T(8,128)(2,1)}, bf16[256,512]{1,0:T(8,128)(2,1)S(1)}, u32[]{:S(2)}, u32[]{:S(2)}) collective-permute-start(bf16[256,512]{1,0:T(8,128)(2,1)} %get-tuple-element.46), channel_id=1, source_target_pairs={{0,1},{1,0},{2,3},{3,2},{4,5},{5,4},{6,7},{7,6},{8,9},{9,8},{10,11... | collective-permute-start | bytes 786440 | tf_op jit(solution)/shard_map/ppermute | solution.py:248
  46.9 5.9 %collective-permute-start.11 = (bf16[64,512]{1,0:T(8,128)(2,1)S(1)}, bf16[64,512]{1,0:T(8,128)(2,1)S(1)}, u32[]{:S(2)}, u32[]{:S(2)}) collective-permute-start(bf16[64,512]{1,0:T(8,128)(2,1)S(1)} %copy-done.19), channel_id=1, source_target_pairs={{0,12},{4,0},{8,4},{12,8},{1,13},{5,1},{9,5},{13,9},{2,14},{6,2},{... | collective-permute-start | bytes 196616 | tf_op jit(solution)/shard_map/ppermute | solution.py:253
  50.2 6.9 %collective-permute-start.12 = (bf16[64,512]{1,0:T(8,128)(2,1)S(1)}, bf16[64,512]{1,0:T(8,128)(2,1)S(1)}, u32[]{:S(2)}, u32[]{:S(2)}) collective-permute-start(bf16[64,512]{1,0:T(8,128)(2,1)S(1)} %copy-done.17), channel_id=1, source_target_pairs={{0,8},{4,12},{8,0},{12,4},{1,9},{5,13},{9,1},{13,5},{2,10},{6,14},... | collective-permute-start | bytes 196616 | tf_op jit(solution)/shard_map/ppermute | solution.py:253
  50.3 6.9 %collective-permute-start.13 = (bf16[64,512]{1,0:T(8,128)(2,1)S(1)}, bf16[64,512]{1,0:T(8,128)(2,1)S(1)}, u32[]{:S(2)}, u32[]{:S(2)}) collective-permute-start(bf16[64,512]{1,0:T(8,128)(2,1)S(1)} %copy-done.15), channel_id=1, source_target_pairs={{0,4},{4,8},{8,12},{12,0},{1,5},{5,9},{9,13},{13,1},{2,6},{6,10},{... | collective-permute-start | bytes 196616 | tf_op jit(solution)/shard_map/ppermute | solution.py:253
  52.8 21.7 %copy-start = (f32[256,512]{1,0:T(8,128)S(1)}, f32[256,512]{1,0:T(8,128)}, u32[]{:S(2)}) copy-start(f32[256,512]{1,0:T(8,128)} %convert_add_fusion.refs_14_) | copy-start | bytes 1572868
  52.8 4.3 %copy-start.16 = (bf16[64,512]{1,0:T(8,128)(2,1)}, bf16[64,512]{1,0:T(8,128)(2,1)S(1)}, u32[]{:S(2)}) copy-start(bf16[64,512]{1,0:T(8,128)(2,1)S(1)} %collective-permute-done.11.refs_7_) | copy-start | bytes 196612
  67.7 4.3 %collective-permute-start.14 = (bf16[64,512]{1,0:T(8,128)(2,1)}, bf16[64,512]{1,0:T(8,128)(2,1)S(1)}, u32[]{:S(2)}, u32[]{:S(2)}) collective-permute-start(bf16[64,512]{1,0:T(8,128)(2,1)} %get-tuple-element.51), channel_id=1, source_target_pairs={{0,1},{1,0},{2,3},{3,2},{4,5},{5,4},{6,7},{7,6},{8,9},{9,8},{10,11... | collective-permute-start | bytes 196616 | tf_op jit(solution)/shard_map/ppermute | solution.py:248
  67.8 12.2 %collective-permute-start.16 = (bf16[64,512]{1,0:T(8,128)(2,1)}, bf16[64,512]{1,0:T(8,128)(2,1)S(1)}, u32[]{:S(2)}, u32[]{:S(2)}) collective-permute-start(bf16[64,512]{1,0:T(8,128)(2,1)} %get-tuple-element.53), channel_id=1, source_target_pairs={{0,4},{4,8},{8,12},{12,0},{1,5},{5,9},{9,13},{13,1},{2,6},{6,10},{... | collective-permute-start | bytes 196616 | tf_op jit(solution)/shard_map/ppermute | solution.py:253
  67.9 12.2 %collective-permute-start.17 = (bf16[64,512]{1,0:T(8,128)(2,1)}, bf16[64,512]{1,0:T(8,128)(2,1)S(1)}, u32[]{:S(2)}, u32[]{:S(2)}) collective-permute-start(bf16[64,512]{1,0:T(8,128)(2,1)} %get-tuple-element.54), channel_id=1, source_target_pairs={{0,8},{4,12},{8,0},{12,4},{1,9},{5,13},{9,1},{13,5},{2,10},{6,14},... | collective-permute-start | bytes 196616 | tf_op jit(solution)/shard_map/ppermute | solution.py:253
  70.2 9.9 %collective-permute-start.18 = (bf16[64,512]{1,0:T(8,128)(2,1)}, bf16[64,512]{1,0:T(8,128)(2,1)S(1)}, u32[]{:S(2)}, u32[]{:S(2)}) collective-permute-start(bf16[64,512]{1,0:T(8,128)(2,1)} %get-tuple-element.55), channel_id=1, source_target_pairs={{0,12},{4,0},{8,4},{12,8},{1,13},{5,1},{9,5},{13,9},{2,14},{6,2},{... | collective-permute-start | bytes 196616 | tf_op jit(solution)/shard_map/ppermute | solution.py:253
  72.9 5.0 %collective-permute-start.15 = (bf16[64,512]{1,0:T(8,128)(2,1)S(1)}, bf16[64,512]{1,0:T(8,128)(2,1)S(1)}, u32[]{:S(2)}, u32[]{:S(2)}) collective-permute-start(bf16[64,512]{1,0:T(8,128)(2,1)S(1)} %add_convert_fusion.4), channel_id=1, source_target_pairs={{0,2},{1,3},{2,0},{3,1},{4,6},{5,7},{6,4},{7,5},{8,10},{9,11},{10,... | collective-permute-start | bytes 196616 | tf_op jit(solution)/shard_map/ppermute | solution.py:248
  74.5 5.5 %collective-permute-start.10 = (bf16[128,512]{1,0:T(8,128)(2,1)S(1)}, bf16[128,512]{1,0:T(8,128)(2,1)S(1)}, u32[]{:S(2)}, u32[]{:S(2)}) collective-permute-start(bf16[128,512]{1,0:T(8,128)(2,1)S(1)} %fusion), channel_id=1, source_target_pairs={{0,2},{1,3},{2,0},{3,1},{4,6},{5,7},{6,4},{7,5},{8,10},{9,11},{10,... | collective-permute-start | bytes 393224 | tf_op jit(solution)/shard_map/ppermute | solution.py:248
  80.7 5.9 %collective-permute-start.19 = (bf16[192,512]{1,0:T(8,128)(2,1)S(1)}, bf16[192,512]{1,0:T(8,128)(2,1)S(1)}, u32[]{:S(2)}, u32[]{:S(2)}) collective-permute-start(bf16[192,512]{1,0:T(8,128)(2,1)S(1)} %pad_maximum_fusion.1), channel_id=1, source_target_pairs={{0,4},{4,0},{8,12},{12,8},{1,5},{5,1},{9,13},{13,9},{2,6},{6,2},{1... | collective-permute-start | bytes 589832 | tf_op jit(solution)/shard_map/ppermute | solution.py:248
  86.7 10.1 %collective-permute-start.20 = (bf16[192,512]{1,0:T(8,128)(2,1)S(1)}, bf16[192,512]{1,0:T(8,128)(2,1)S(1)}, u32[]{:S(2)}, u32[]{:S(2)}) collective-permute-start(bf16[192,512]{1,0:T(8,128)(2,1)S(1)} %pad_maximum_fusion.2), channel_id=1, source_target_pairs={{0,8},{4,12},{8,0},{12,4},{1,9},{5,13},{9,1},{13,5},{2,10},{6,14},... | collective-permute-start | bytes 589832 | tf_op jit(solution)/shard_map/ppermute | solution.py:248
  96.8 5.0 %collective-permute-start.21 = (bf16[128,512]{1,0:T(8,128)(2,1)S(1)}, bf16[128,512]{1,0:T(8,128)(2,1)S(1)}, u32[]{:S(2)}, u32[]{:S(2)}) collective-permute-start(bf16[128,512]{1,0:T(8,128)(2,1)S(1)} %add_convert_fusion), channel_id=1, source_target_pairs={{0,2},{1,3},{2,0},{3,1},{4,6},{5,7},{6,4},{7,5},{8,10},{9,11},{10,... | collective-permute-start | bytes 393224 | tf_op jit(solution)/shard_map/ppermute | solution.py:248
  102.0 3.5 %collective-permute-start.22 = (bf16[320,512]{1,0:T(8,128)(2,1)S(1)}, bf16[320,512]{1,0:T(8,128)(2,1)S(1)}, u32[]{:S(2)}, u32[]{:S(2)}) collective-permute-start(bf16[320,512]{1,0:T(8,128)(2,1)S(1)} %pad_maximum_fusion), channel_id=1, source_target_pairs={{0,1},{1,0},{2,3},{3,2},{4,5},{5,4},{6,7},{7,6},{8,9},{9,8},{10,11... | collective-permute-start | bytes 983048 | tf_op jit(solution)/shard_map/ppermute | solution.py:248
  (12 other events, 7.5 us)

commit v6 on v5

--- a/solution.py
+++ b/solution.py
@@ -12,6 +12,7 @@
 VMEM = pl.BlockSpec(memory_space=pltpu.VMEM)
 SMEM = pl.BlockSpec(memory_space=pltpu.SMEM)
 ANY = pl.BlockSpec(memory_space=pl.ANY)
+HBM = pl.BlockSpec(memory_space=pltpu.HBM)
 NN = (((1,), (0,)), ((), ()))
 NT = (((1,), (1,)), ((), ()))
 
@@ -27,14 +28,15 @@
     return act, upper + act * (1.0 - tanh)
 
 
-def call(body, outs, args, flops=0, scratch=(), smem=(), far=(), far_out=(), order=()):
+def call(body, outs, args, flops=0, scratch=(), smem=(), far=(), far_out=(), order=(), vmem=16):
     args = list(args) + list(order)
     moved = sum(a.size * a.dtype.itemsize for a in args) + sum(
         o.size * o.dtype.itemsize for o in outs
     )
     keep = len(args) - len(order)
     specs = [
-        SMEM if i in smem else ANY if i in far or i >= keep else VMEM for i in range(len(args))
+        SMEM if i in smem else ANY if i >= keep else HBM if i in far else VMEM
+        for i in range(len(args))
     ]
 
     def inner(*refs):
@@ -44,10 +46,10 @@
         inner if order else body,
         out_shape=tuple(outs),
         in_specs=specs,
-        out_specs=tuple(ANY if i in far_out else VMEM for i in range(len(outs))),
+        out_specs=tuple(HBM if i in far_out else VMEM for i in range(len(outs))),
         scratch_shapes=list(scratch),
         cost_estimate=pl.CostEstimate(flops=flops, bytes_accessed=moved, transcendentals=0),
-        compiler_params=pltpu.CompilerParams(vmem_limit_bytes=58 << 20),
+        compiler_params=pltpu.CompilerParams(vmem_limit_bytes=vmem << 20),
     )(*args)
 
 
@@ -164,10 +166,15 @@
     scattered((dhidden[...] * (0.5 * silu_parts(0.5 * agg)[1])).astype(BF16), outs)
 
 
+def reverse(value, count):
+    bits = count.bit_length() - 1
+    return sum(((value >> b) & 1) << (bits - 1 - b) for b in range(bits))
+
+
 def update_kernel(ranks, step, me, *refs):
     lists, pieces = refs[:ranks], refs[ranks : 2 * ranks]
-    edges, upstream, w_out, updated, kept, away = refs[2 * ranks : 2 * ranks + 6]
-    edges_v, upstream_v, w_out_v, updated_v, hidden, sems, out_sems = refs[2 * ranks + 6 :]
+    edges, upstream, w_out, updated, term = refs[2 * ranks : 2 * ranks + 5]
+    edges_v, upstream_v, w_out_v, updated_v, hidden, sems, out_sems = refs[2 * ranks + 5 :]
     arrive = loads([w_out, edges, upstream], [w_out_v, edges_v, upstream_v], sems)
     home = gathered(pieces)
     rows = edges.shape[0]
@@ -188,11 +195,10 @@
         updated_v[at, :] = total.astype(BF16)
         leave[i].start()
         hidden[:, at] = fresh[i].T
-    half = kept.shape[0]
-    own = pl.multiple_of(me[1] * half, half)
-    other = pl.multiple_of((1 - me[1]) * half, half)
-    away[...] = dot(hidden[pl.ds(other, half), :], upstream_v[...]).astype(BF16)
-    kept[...] = dot(hidden[pl.ds(own, half), :], upstream_v[...])
+    copies, part = term.shape[0], term.shape[1]
+    total = dot(hidden[...], upstream_v[...]).astype(BF16)
+    for k in range(copies):
+        term[reverse(k, copies)] = total[k * part : (k + 1) * part]
     waited(leave)
 
 
@@ -278,23 +284,10 @@
     return kept + swap(away, "dp", 1).astype(F32)
 
 
-def summed(value, axis, bit):
-    own = value.astype(BF16)
-    return own.astype(F32) + swap(own, axis, 1 << bit).astype(F32)
-
-
-def finish(out, basis):
-    out, basis = out.astype(BF16), basis.astype(BF16)
+def doubled(out, basis, axis, bit):
     rows = basis.shape[0]
-    for bit in bits_of("graph"):
-        own = jnp.concatenate([basis, out])
-        got = swap(own, "graph", 1 << bit)
-        basis = (basis.astype(F32) + got[:rows].astype(F32)).astype(BF16)
-        out = (out.astype(F32) + got[rows:].astype(F32)).astype(BF16)
-    for bit in reversed(bits_of("dp")[1:]):
-        out = double(out, swap(out, "dp", 1 << bit), "dp", bit)
-    got = swap(jnp.concatenate([basis, out]), "dp", 1)
-    return double(out, got[rows:], "dp", 0).astype(F32), double(basis, got[:rows], "dp", 0).astype(F32)
+    got = swap(jnp.concatenate([basis, out]), axis, 1 << bit)
+    return got[:rows], double(out, got[rows:], axis, bit)
 
 
 def per_device(
@@ -356,6 +349,7 @@
         flops=2 * wide + narrow,
         scratch=[held(basis), held(plane), held(hot), held(hot), dma((1,))],
         order=[same],
+        vmem=30,
     )
     home = exchange(partial_rows, 1)
     back = call(
@@ -365,9 +359,9 @@
         flops=2 * slots * slots * width,
     )
     dpartial = exchange(back, -1)
-    updated, out_kept, out_away = call(
+    updated, out_term = call(
         functools.partial(update_kernel, ranks, 256),
-        [shape((edge_dev, width)), shape((width // 2, width), F32), shape((width // 2, width))],
+        [shape((edge_dev, width)), shape((copies, width // copies, width))],
         [place] + lists + home + [edges, upstream, w_out],
         smem=(0,),
         far=(2 * ranks + 1, 2 * ranks + 2, 2 * ranks + 3),
@@ -377,7 +371,7 @@
         + [pltpu.VMEM((width, edge_dev), BF16), dma((3,)), dma((edge_dev // 256,))],
         order=[back[0]],
     )
-    out_part = joined(out_kept, out_away)
+    out_parts = lax.all_to_all(out_term, "dp", split_axis=0, concat_axis=0, tiled=True)
     basis_half = basis_width // 2
     basis_kept, basis_away, *dfetch = call(
         functools.partial(backward_kernel, ranks, step),
@@ -388,15 +382,21 @@
         flops=3 * wide + 2 * narrow,
         scratch=[held(basis), held(plane), held(plane), held(hot), held(hot)]
         + [pltpu.VMEM((basis_width, width), F32), dma((1,))],
-        order=[out_part],
+        order=[out_term],
+        vmem=36,
     )
     returned = exchange(dfetch, 1)
     basis_part = joined(basis_kept, basis_away)
     for bit in bits_of("dp")[1:]:
-        out_part = halve(out_part, "dp", bit)
-        basis_part = summed(basis_part, "dp", bit)
-    out_part, basis_part, returned = lax.optimization_barrier((out_part, basis_part, returned))
-    grad_w_out, grad_w_basis = finish(out_part, basis_part)
+        basis_part = halve(basis_part, "dp", bit)
+    out_part = jnp.sum(out_parts.astype(F32), axis=0)
+    for bit in reversed(bits_of("graph")):
+        out_part = halve(out_part, "graph", bit)
+    out, total = out_part.astype(BF16), basis_part.astype(BF16)
+    out, total, returned = lax.optimization_barrier((out, total, returned))
+    for bit in bits_of("graph"):
+        got, out = doubled(out, total, "graph", bit)
+        total = (total.astype(F32) + got.astype(F32)).astype(BF16)
     (grad_edge,) = call(
         functools.partial(final_kernel, ranks, 256),
         [shape((edge_dev, width))],
@@ -407,9 +407,13 @@
         flops=2 * slots * edge_dev * width,
         scratch=[held(upstream), held(upstream), dma((1,)), dma((edge_dev // 256,))],
     )
+    out, total, grad_edge = lax.optimization_barrier((out, total, grad_edge))
+    for bit in reversed(bits_of("dp")):
+        got, out = doubled(out, total, "dp", bit)
+        total = double(total, got, "dp", bit)
     out_scale = jnp.sqrt(F32(copies * ranks * edge_dev))
     basis_scale = 2.0 * jnp.sqrt(F32(copies * ranks * blocks * block_rows))
-    return (updated[None], grad_edge[None], grad_w_out / out_scale, grad_w_basis / basis_scale)
+    return (updated[None], grad_edge[None], out.astype(F32) / out_scale, total.astype(F32) / basis_scale)
 
 
 def solution(mesh):

time: 108 us -> 93.1 us (0.86)
  Pallas kernels: 33.5 us -> 23.1 us
  waiting for transfers between devices: 34.7 us -> 28.5 us
  starting transfers between devices: 26.8 us -> 32.4 us
  other arithmetic: 6.32 us -> 4.1 us
  local copies, waits for them, and re-layouts: 4.44 us -> 3.06 us
    pallas_call x7, Pallas kernels: 33.5 us -> 23.1 us  [call(): pl.pallas_call(inner if order else body, out_shape=tuple(outs), in_specs=...]
    all_to_all x0 -> x1, starting transfers between devices: none -> 4.33 us  [per_device(): lax.all_to_all(out_term, 'dp', split_axis=0, concat_axis=0, tiled=True)]
    ppermute x15, waiting for transfers between devices: 11.1 us -> 7.3 us  [shift(): lax.ppermute(value, axis, [(k, (k + by) % count) for k in range(count)])]
    ppermute x8, waiting for transfers between devices: 23.6 us -> 21.2 us  [swap(): lax.ppermute(value, axis, [(k, k ^ mask) for k in range(lax.axis_size(axi...]
    add x1, other arithmetic: 1.91 us -> 0.02 us  [joined(): return kept + swap(away, 'dp', 1).astype(F32)]
    unnamed x42 -> x20, local copies, waits for them, and re-layouts: 4.39 us -> 2.97 us
    reduce_sum x0 -> x1, other arithmetic: none -> 1.15 us  [per_device(): out_part = jnp.sum(out_parts.astype(F32), axis=0)]
  transfers between devices with their start and end apart: 23 -> 24, of which waited for: 10 -> 12; matrix products, arithmetic and copies ran while one was open for 3% -> 1% of each run, Pallas kernels for 7% -> 18%
where the time goes in v6:
time: 93.1 us; the launch traced here: 92.8 us
  starting transfers between devices  32.4 us (35%)
  waiting for transfers between devices  28.5 us (31%)
  Pallas kernels  23.1 us (25%)
  other arithmetic  4.1 us (4%)
  local copies, waits for them, and re-layouts  3.06 us (3%)
  between operations  1.66 us (2%)
    pallas_call x7, Pallas kernels, call(): pl.pallas_call(inner if order else body, out_shape=tuple(outs), in_specs=...  23.1 us
    ppermute x15, starting transfers between devices, shift(): lax.ppermute(value, axis, [(k, (k + by) % count) for k in range(count)])  23.1 us
    ppermute x8, waiting for transfers between devices, swap(): lax.ppermute(value, axis, [(k, k ^ mask) for k in range(lax.axis_size(axi...  21.2 us
    ppermute x15, waiting for transfers between devices, shift(): lax.ppermute(value, axis, [(k, (k + by) % count) for k in range(count)])  7.3 us
    ppermute x8, starting transfers between devices, swap(): lax.ppermute(value, axis, [(k, k ^ mask) for k in range(lax.axis_size(axi...  5.01 us
    all_to_all x1, starting transfers between devices, per_device(): lax.all_to_all(out_term, 'dp', split_axis=0, concat_axis=0, tiled=True)  4.33 us
    unnamed x20, local copies, waits for them, and re-layouts  2.97 us
  transfers between devices with their start and end apart: 24, of which 12 were waited for; matrix products, arithmetic and copies ran while one was open for 1% of the time, Pallas kernels for 18%

profile of v6, /device:TPU:0, one launch (start us, length us, event | category | flops | bytes accessed | tf_op | source)
XLA Modules:
  0.0 92.8 jit_solution(3055107240001041907)
XLA Ops:
  2.1 5.0 %collective-permute-start.2 = (s32[4,128]{1,0:T(4,128)S(1)}, s32[4,128]{1,0:T(4,128)S(1)}, u32[]{:S(2)}, u32[]{:S(2)}) collective-permute-start(s32[4,128]{1,0:T(4,128)S(1)} %pad_add_fusion.refs_0_.refs_1_), channel_id=1, source_target_pairs={{0,12},{4,0},{8,4},{12,8},{1,13},{5,1},{9,5},{13,9},{2,14},{6,2},{... | collective-permute-start | bytes 6152 | tf_op jit(solution)/shard_map/ppermute | solution.py:259
  7.1 1.0 %collective-permute-start = (s32[4,128]{1,0:T(4,128)S(1)}, s32[4,128]{1,0:T(4,128)S(1)}, u32[]{:S(2)}, u32[]{:S(2)}) collective-permute-start(s32[4,128]{1,0:T(4,128)S(1)} %pad_add_fusion.refs_0_.refs_1_), channel_id=1, source_target_pairs={{0,4},{4,8},{8,12},{12,0},{1,5},{5,9},{9,13},{13,1},{2,6},{6,10},{... | collective-permute-start | bytes 6152 | tf_op jit(solution)/shard_map/ppermute | solution.py:259
  8.4 3.2 %collective-permute-done.1.refs_2_.refs_3_ = s32[4,128]{1,0:T(4,128)S(1)} collective-permute-done((s32[4,128]{1,0:T(4,128)S(1)}, s32[4,128]{1,0:T(4,128)S(1)}, u32[]{:S(2)}, u32[]{:S(2)}) %collective-permute-start.1) | collective-permute-done | bytes 2080 | tf_op jit(solution)/shard_map/ppermute | solution.py:259
  11.6 0.9 collective-permute-done.refs_1_.refs_2_
  12.5 1.2 %copy-done = bf16[1,1024,512]{2,1,0:T(8,128)(2,1)S(1)} copy-done((bf16[1,1024,512]{2,1,0:T(8,128)(2,1)S(1)}, bf16[1,1024,512]{2,1,0:T(8,128)(2,1)}, u32[]{:S(2)}) %copy-start) | copy-done | bytes 1048600
  13.7 1.2 %shard_map.129 = (bf16[64,512]{1,0:T(8,128)(2,1)S(1)}, bf16[64,512]{1,0:T(8,128)(2,1)S(1)}, bf16[64,512]{1,0:T(8,128)(2,1)S(1)}, bf16[64,512]{1,0:T(8,128)(2,1)S(1)}) custom-call(s32[2]{0:T(128)S(1)} %pad_add_fusion.1.me.refs_0_, s32[4,128]{1,0:T(4,128)S(1)} %pad_add_fusion.refs_0_.refs_1_, s32[4,128]{1,0:T(4,128)S(1)} %collective-permute-done.refs_1_.refs_2_, ...), custom_call_target="tpu_custom_call" | custom-call | flops 268435456 | bytes 1318920 | tf_op jit(solution)/shard_map/pallas_call | solution.py:45
  16.3 1.9 %collective-permute-start.5 = (bf16[64,512]{1,0:T(8,128)(2,1)S(1)}, bf16[64,512]{1,0:T(8,128)(2,1)S(1)}, u32[]{:S(2)}, u32[]{:S(2)}) collective-permute-start(bf16[64,512]{1,0:T(8,128)(2,1)S(1)} %get-tuple-element.38), channel_id=1, source_target_pairs={{0,4},{4,8},{8,12},{12,0},{1,5},{5,9},{9,13},{13,1},{2,6},{6,10},{... | collective-permute-start | bytes 196616 | tf_op jit(solution)/shard_map/ppermute | solution.py:259
  18.9 1.0 %copy-done.4 = bf16[512,512]{1,0:T(8,128)(2,1)S(1)} copy-done((bf16[512,512]{1,0:T(8,128)(2,1)S(1)}, bf16[512,512]{1,0:T(8,128)(2,1)}, u32[]{:S(2)}) %copy-start.4) | copy-done | bytes 524312
  19.9 2.4 %shard_map.130 = (bf16[256,256]{1,0:T(8,128)(2,1)S(1)}, f32[256,512]{1,0:T(8,128)S(1)}) custom-call(s32[2]{0:T(128)S(1)} %pad_add_fusion.1.me.refs_0_, s32[4,128]{1,0:T(4,128)S(1)} %pad_add_fusion.refs_0_.refs_1_, s32[4,128]{1,0:T(4,128)S(1)} %collective-permute-done.refs_1_.refs_2_, s32[4,128]{1,0:T(4,128)S(1)} %collective-permute-done.1.refs_2_.refs_3_, ...), custom_call_target="tpu_custom_call" | custom-call | flops 536870912 | bytes 2301960 | tf_op jit(solution)/shard_map/pallas_call | solution.py:45
  22.5 5.2 %shard_map.131 = (bf16[64,512]{1,0:T(8,128)(2,1)S(1)}, bf16[64,512]{1,0:T(8,128)(2,1)S(1)}, bf16[64,512]{1,0:T(8,128)(2,1)S(1)}, bf16[64,512]{1,0:T(8,128)(2,1)S(1)}) custom-call(s32[2]{0:T(128)S(1)} %pad_add_fusion.1.me.refs_0_, s32[1,1]{1,0:T(1,128)S(6)} %copy.14.refs_1_, bf16[64,512]{1,0:T(8,128)(2,1)S(1)} %get-tuple-element.35.refs_7_.refs_2_, ...), custom_call_target="tpu_custom_call" | custom-call | flops 2684354560 | bytes 1867788 | tf_op jit(solution)/shard_map/pallas_call | solution.py:45
  28.6 1.5 %collective-permute-start.7 = (bf16[64,512]{1,0:T(8,128)(2,1)S(1)}, bf16[64,512]{1,0:T(8,128)(2,1)S(1)}, u32[]{:S(2)}, u32[]{:S(2)}) collective-permute-start(bf16[64,512]{1,0:T(8,128)(2,1)S(1)} %get-tuple-element.42), channel_id=1, source_target_pairs={{0,8},{4,12},{8,0},{12,4},{1,9},{5,13},{9,1},{13,5},{2,10},{6,14},... | collective-permute-start | bytes 196616 | tf_op jit(solution)/shard_map/ppermute | solution.py:259
  30.1 2.3 %collective-permute-start.8 = (bf16[64,512]{1,0:T(8,128)(2,1)S(1)}, bf16[64,512]{1,0:T(8,128)(2,1)S(1)}, u32[]{:S(2)}, u32[]{:S(2)}) collective-permute-start(bf16[64,512]{1,0:T(8,128)(2,1)S(1)} %get-tuple-element.43), channel_id=1, source_target_pairs={{0,12},{4,0},{8,4},{12,8},{1,13},{5,1},{9,5},{13,9},{2,14},{6,2},{... | collective-permute-start | bytes 196616 | tf_op jit(solution)/shard_map/ppermute | solution.py:259
  32.4 1.6 %collective-permute-done.6.refs_1_.refs_6_ = bf16[64,512]{1,0:T(8,128)(2,1)S(1)} collective-permute-done((bf16[64,512]{1,0:T(8,128)(2,1)S(1)}, bf16[64,512]{1,0:T(8,128)(2,1)S(1)}, u32[]{:S(2)}, u32[]{:S(2)}) %collective-permute-start.6) | collective-permute-done | bytes 65568 | tf_op jit(solution)/shard_map/ppermute | solution.py:259
  34.0 1.3 %collective-permute-done.7.refs_2_.refs_7_ = bf16[64,512]{1,0:T(8,128)(2,1)S(1)} collective-permute-done((bf16[64,512]{1,0:T(8,128)(2,1)S(1)}, bf16[64,512]{1,0:T(8,128)(2,1)S(1)}, u32[]{:S(2)}, u32[]{:S(2)}) %collective-permute-start.7) | collective-permute-done | bytes 65568 | tf_op jit(solution)/shard_map/ppermute | solution.py:259
  35.6 3.3 %collective-permute-start.11 = (bf16[64,512]{1,0:T(8,128)(2,1)S(1)}, bf16[64,512]{1,0:T(8,128)(2,1)S(1)}, u32[]{:S(2)}, u32[]{:S(2)}) collective-permute-start(bf16[64,512]{1,0:T(8,128)(2,1)S(1)} %get-tuple-element.48), channel_id=1, source_target_pairs={{0,12},{4,0},{8,4},{12,8},{1,13},{5,1},{9,5},{13,9},{2,14},{6,2},{... | collective-permute-start | bytes 196616 | tf_op jit(solution)/shard_map/ppermute | solution.py:259
  39.5 3.8 %shard_map.133 = (bf16[1024,512]{1,0:T(8,128)(2,1)}, bf16[4,128,512]{2,1,0:T(8,128)(2,1)}) custom-call(s32[2]{0:T(128)S(1)} %pad_add_fusion.1.me.refs_0_, s32[4,128]{1,0:T(4,128)S(1)} %pad_add_fusion.refs_0_.refs_1_, s32[4,128]{1,0:T(4,128)S(1)} %collective-permute-done.refs_1_.refs_2_, s32[4,128]{1,0:T(4,128)S(1)} %collective-permute-done.1.refs_2_.refs_3_, ...), custom_call_target="tpu_custom_call" | custom-call | flops 1342177280 | bytes 4530184 | tf_op jit(solution)/shard_map/pallas_call | solution.py:45
  43.3 4.3 %all-to-all-start = ((bf16[4,128,512]{2,1,0:T(8,128)(2,1)}), bf16[4,128,512]{2,1,0:T(8,128)(2,1)}, u32[]{:S(2)}, u32[]{:S(2)}) async-start(bf16[4,128,512]{2,1,0:T(8,128)(2,1)} %get-tuple-element.47.refs_14_), calls=%async_computation | async-start | bytes 1048576 | tf_op jit(solution)/shard_map/all_to_all | solution.py:374
  47.7 7.9 %shard_map.134 = (f32[64,512]{1,0:T(8,128)S(1)}, bf16[64,512]{1,0:T(8,128)(2,1)S(1)}, bf16[64,512]{1,0:T(8,128)(2,1)S(1)}, bf16[64,512]{1,0:T(8,128)(2,1)S(1)}, ...) custom-call(s32[2]{0:T(128)S(1)} %pad_add_fusion.1.me.refs_0_, s32[1,1]{1,0:T(1,128)S(6)} %copy.14.refs_1_, ...), custom_call_target="tpu_custom_call" | custom-call | flops 4294967296 | bytes 2719756 | tf_op jit(solution)/shard_map/pallas_call | solution.py:45
  55.9 2.9 %collective-permute-start.16 = (bf16[64,512]{1,0:T(8,128)(2,1)S(1)}, bf16[64,512]{1,0:T(8,128)(2,1)S(1)}, u32[]{:S(2)}, u32[]{:S(2)}) collective-permute-start(bf16[64,512]{1,0:T(8,128)(2,1)S(1)} %get-tuple-element.54), channel_id=1, source_target_pairs={{0,4},{4,8},{8,12},{12,0},{1,5},{5,9},{9,13},{13,1},{2,6},{6,10},{... | collective-permute-start | bytes 196616 | tf_op jit(solution)/shard_map/ppermute | solution.py:259
  58.8 0.9 collective-permute-start.17
  59.7 1.5 %collective-permute-start.18 = (bf16[64,512]{1,0:T(8,128)(2,1)S(1)}, bf16[64,512]{1,0:T(8,128)(2,1)S(1)}, u32[]{:S(2)}, u32[]{:S(2)}) collective-permute-start(bf16[64,512]{1,0:T(8,128)(2,1)S(1)} %get-tuple-element.56), channel_id=1, source_target_pairs={{0,12},{4,0},{8,4},{12,8},{1,13},{5,1},{9,5},{13,9},{2,14},{6,2},{... | collective-permute-start | bytes 196616 | tf_op jit(solution)/shard_map/ppermute | solution.py:259
  61.2 1.2 %convert_reduce_fusion = f32[128,512]{1,0:T(8,128)S(1)} fusion(bf16[4,128,512]{2,1,0:T(8,128)(2,1)} %all-to-all-done), kind=kLoop, calls=%fused_computation.1 | loop fusion | flops 458752 | bytes 786432 | tf_op jit(solution)/shard_map/reduce_sum | solution.py:392
  63.1 1.7 %collective-permute-start.15 = (bf16[32,512]{1,0:T(8,128)(2,1)S(1)}, bf16[32,512]{1,0:T(8,128)(2,1)S(1)}, u32[]{:S(2)}, u32[]{:S(2)}) collective-permute-start(bf16[32,512]{1,0:T(8,128)(2,1)S(1)} %fusion.5), channel_id=1, source_target_pairs={{0,2},{1,3},{2,0},{3,1},{4,6},{5,7},{6,4},{7,5},{8,10},{9,11},{10,... | collective-permute-start | bytes 98312 | tf_op jit(solution)/shard_map/ppermute | solution.py:254
  64.8 4.3 %collective-permute-done.9 = bf16[64,512]{1,0:T(8,128)(2,1)S(1)} collective-permute-done((bf16[64,512]{1,0:T(8,128)(2,1)S(1)}, bf16[64,512]{1,0:T(8,128)(2,1)S(1)}, u32[]{:S(2)}, u32[]{:S(2)}) %collective-permute-start.9) | collective-permute-done | bytes 65568 | tf_op jit(solution)/shard_map/ppermute | solution.py:254
  69.2 3.9 %collective-permute-done.10 = bf16[32,512]{1,0:T(8,128)(2,1)S(1)} collective-permute-done((bf16[32,512]{1,0:T(8,128)(2,1)S(1)}, bf16[32,512]{1,0:T(8,128)(2,1)S(1)}, u32[]{:S(2)}, u32[]{:S(2)}) %collective-permute-start.10) | collective-permute-done | bytes 32800 | tf_op jit(solution)/shard_map/ppermute | solution.py:254
  73.2 4.2 %collective-permute-done.19 = bf16[64,512]{1,0:T(8,128)(2,1)S(1)} collective-permute-done((bf16[64,512]{1,0:T(8,128)(2,1)S(1)}, bf16[64,512]{1,0:T(8,128)(2,1)S(1)}, u32[]{:S(2)}, u32[]{:S(2)}) %collective-permute-start.19) | collective-permute-done | bytes 65568 | tf_op jit(solution)/shard_map/ppermute | solution.py:254
  77.8 2.2 %shard_map.135 = bf16[1024,512]{1,0:T(8,128)(2,1)} custom-call(s32[2]{0:T(128)S(1)} %pad_add_fusion.1.me.refs_0_, s32[4,128]{1,0:T(4,128)S(1)} %pad_add_fusion.refs_0_.refs_1_, s32[4,128]{1,0:T(4,128)S(1)} %collective-permute-done.refs_1_.refs_2_, s32[4,128]{1,0:T(4,128)S(1)} %collective-permute-done.1.refs_2_.refs_3_, ...), custom_call_target="tpu_custom_call" | custom-call | flops 268435456 | bytes 2367496 | tf_op jit(solution)/shard_map/pallas_call | solution.py:45
  80.0 3.6 %collective-permute-done.20 = bf16[96,512]{1,0:T(8,128)(2,1)S(1)} collective-permute-done((bf16[96,512]{1,0:T(8,128)(2,1)S(1)}, bf16[96,512]{1,0:T(8,128)(2,1)S(1)}, u32[]{:S(2)}, u32[]{:S(2)}) %collective-permute-start.20) | collective-permute-done | bytes 98336 | tf_op jit(solution)/shard_map/ppermute | solution.py:254
  83.7 1.8 %collective-permute-start.21 = (bf16[160,512]{1,0:T(8,128)(2,1)S(1)}, bf16[160,512]{1,0:T(8,128)(2,1)S(1)}, u32[]{:S(2)}, u32[]{:S(2)}) collective-permute-start(bf16[160,512]{1,0:T(8,128)(2,1)S(1)} %pad_maximum_fusion.1), channel_id=1, source_target_pairs={{0,2},{1,3},{2,0},{3,1},{4,6},{5,7},{6,4},{7,5},{8,10},{9,11},{10,... | collective-permute-start | bytes 491528 | tf_op jit(solution)/shard_map/ppermute | solution.py:254
  85.5 3.6 %collective-permute-done.21 = bf16[160,512]{1,0:T(8,128)(2,1)S(1)} collective-permute-done((bf16[160,512]{1,0:T(8,128)(2,1)S(1)}, bf16[160,512]{1,0:T(8,128)(2,1)S(1)}, u32[]{:S(2)}, u32[]{:S(2)}) %collective-permute-start.21) | collective-permute-done | bytes 163872 | tf_op jit(solution)/shard_map/ppermute | solution.py:254
  89.3 1.6 %collective-permute-done.22 = bf16[320,512]{1,0:T(8,128)(2,1)S(1)} collective-permute-done((bf16[320,512]{1,0:T(8,128)(2,1)S(1)}, bf16[320,512]{1,0:T(8,128)(2,1)S(1)}, u32[]{:S(2)}, u32[]{:S(2)}) %collective-permute-start.22) | collective-permute-done | bytes 327712 | tf_op jit(solution)/shard_map/ppermute | solution.py:254
  91.6 1.1 %convert_multiply_fusion = f32[512,512]{1,0:T(8,128)} fusion(bf16[256,512]{1,0:T(8,128)(2,1)S(1)} %slice.38, bf16[256,512]{1,0:T(8,128)(2,1)S(1)} %maximum_select_fusion.1, pred[]{:T(512)S(6)} %eq.16), kind=kLoop, calls=%fused_computation | loop fusion | flops 2883584 | bytes 1572865 | tf_op jit(solution)/shard_map/div | solution.py:416
  (71 shorter events, 7.6 us)
Async XLA Ops:
  2.1 6.4 %collective-permute-start.2 = (s32[4,128]{1,0:T(4,128)S(1)}, s32[4,128]{1,0:T(4,128)S(1)}, u32[]{:S(2)}, u32[]{:S(2)}) collective-permute-start(s32[4,128]{1,0:T(4,128)S(1)} %pad_add_fusion.refs_0_.refs_1_), channel_id=1, source_target_pairs={{0,12},{4,0},{8,4},{12,8},{1,13},{5,1},{9,5},{13,9},{2,14},{6,2},{... | collective-permute-start | bytes 6152 | tf_op jit(solution)/shard_map/ppermute | solution.py:259
  7.1 4.5 %collective-permute-start.1 = (s32[4,128]{1,0:T(4,128)S(1)}, s32[4,128]{1,0:T(4,128)S(1)}, u32[]{:S(2)}, u32[]{:S(2)}) collective-permute-start(s32[4,128]{1,0:T(4,128)S(1)} %pad_add_fusion.refs_0_.refs_1_), channel_id=1, source_target_pairs={{0,8},{4,12},{8,0},{12,4},{1,9},{5,13},{9,1},{13,5},{2,10},{6,14},... | collective-permute-start | bytes 6152 | tf_op jit(solution)/shard_map/ppermute | solution.py:259
  7.1 5.4 %collective-permute-start = (s32[4,128]{1,0:T(4,128)S(1)}, s32[4,128]{1,0:T(4,128)S(1)}, u32[]{:S(2)}, u32[]{:S(2)}) collective-permute-start(s32[4,128]{1,0:T(4,128)S(1)} %pad_add_fusion.refs_0_.refs_1_), channel_id=1, source_target_pairs={{0,4},{4,8},{8,12},{12,0},{1,5},{5,9},{9,13},{13,1},{2,6},{6,10},{... | collective-permute-start | bytes 6152 | tf_op jit(solution)/shard_map/ppermute | solution.py:259
  12.5 1.2 %copy-start = (bf16[1,1024,512]{2,1,0:T(8,128)(2,1)S(1)}, bf16[1,1024,512]{2,1,0:T(8,128)(2,1)}, u32[]{:S(2)}) copy-start(bf16[1,1024,512]{2,1,0:T(8,128)(2,1)} %param.10) | copy-start | bytes 3145732
  13.7 5.1 %copy-start.2 = (bf16[1,1024,512]{2,1,0:T(8,128)(2,1)S(1)}, bf16[1,1024,512]{2,1,0:T(8,128)(2,1)}, u32[]{:S(2)}) copy-start(bf16[1,1024,512]{2,1,0:T(8,128)(2,1)} %param.11) | copy-start | bytes 3145732
  15.0 7.5 %copy-start.3 = (bf16[1,4096,128]{2,1,0:T(8,128)(2,1)S(1)}, bf16[1,4096,128]{2,1,0:T(8,128)(2,1)}, u32[]{:S(2)}) copy-start(bf16[1,4096,128]{2,1,0:T(8,128)(2,1)} %param.16) | copy-start | bytes 3145732
  15.0 7.3 %collective-permute-start.3 = (bf16[64,512]{1,0:T(8,128)(2,1)S(1)}, bf16[64,512]{1,0:T(8,128)(2,1)S(1)}, u32[]{:S(2)}, u32[]{:S(2)}) collective-permute-start(bf16[64,512]{1,0:T(8,128)(2,1)S(1)} %get-tuple-element.36), channel_id=1, source_target_pairs={{0,12},{4,0},{8,4},{12,8},{1,13},{5,1},{9,5},{13,9},{2,14},{6,2},{... | collective-permute-start | bytes 196616 | tf_op jit(solution)/shard_map/ppermute | solution.py:259
  15.6 6.7 %collective-permute-start.4 = (bf16[64,512]{1,0:T(8,128)(2,1)S(1)}, bf16[64,512]{1,0:T(8,128)(2,1)S(1)}, u32[]{:S(2)}, u32[]{:S(2)}) collective-permute-start(bf16[64,512]{1,0:T(8,128)(2,1)S(1)} %get-tuple-element.37), channel_id=1, source_target_pairs={{0,8},{4,12},{8,0},{12,4},{1,9},{5,13},{9,1},{13,5},{2,10},{6,14},... | collective-permute-start | bytes 196616 | tf_op jit(solution)/shard_map/ppermute | solution.py:259
  16.3 6.2 %collective-permute-start.5 = (bf16[64,512]{1,0:T(8,128)(2,1)S(1)}, bf16[64,512]{1,0:T(8,128)(2,1)S(1)}, u32[]{:S(2)}, u32[]{:S(2)}) collective-permute-start(bf16[64,512]{1,0:T(8,128)(2,1)S(1)} %get-tuple-element.38), channel_id=1, source_target_pairs={{0,4},{4,8},{8,12},{12,0},{1,5},{5,9},{9,13},{13,1},{2,6},{6,10},{... | collective-permute-start | bytes 196616 | tf_op jit(solution)/shard_map/ppermute | solution.py:259
  19.9 2.5 %copy-start.6 = (bf16[128,512]{1,0:T(8,128)(2,1)S(1)}, bf16[128,512]{1,0:T(8,128)(2,1)}, u32[]{:S(2)}) copy-start(bf16[128,512]{1,0:T(8,128)(2,1)} %refs_12_.1) | copy-start | bytes 393220
  19.9 2.5 %copy-start.7 = (s32[1,32,128]{2,1,0:T(8,128)S(1)}, s32[1,32,128]{2,1,0:T(8,128)}, u32[]{:S(2)}) copy-start(s32[1,32,128]{2,1,0:T(8,128)} %param.14) | copy-start | bytes 49156
  19.9 2.5 %copy-start.8 = (s32[1,32,128]{2,1,0:T(8,128)S(1)}, s32[1,32,128]{2,1,0:T(8,128)}, u32[]{:S(2)}) copy-start(s32[1,32,128]{2,1,0:T(8,128)} %param.15) | copy-start | bytes 49156
  22.5 17.0 %copy-start.1 = (bf16[1,1024,512]{2,1,0:T(8,128)(2,1)S(1)}, bf16[1,1024,512]{2,1,0:T(8,128)(2,1)}, u32[]{:S(2)}) copy-start(bf16[1,1024,512]{2,1,0:T(8,128)(2,1)} %param.10) | copy-start | bytes 3145732
  27.7 11.8 %copy-start.5 = (bf16[512,512]{1,0:T(8,128)(2,1)S(1)}, bf16[512,512]{1,0:T(8,128)(2,1)}, u32[]{:S(2)}) copy-start(bf16[512,512]{1,0:T(8,128)(2,1)} %refs_11_.1) | copy-start | bytes 1572868
  27.7 6.2 %collective-permute-start.6 = (bf16[64,512]{1,0:T(8,128)(2,1)S(1)}, bf16[64,512]{1,0:T(8,128)(2,1)S(1)}, u32[]{:S(2)}, u32[]{:S(2)}) collective-permute-start(bf16[64,512]{1,0:T(8,128)(2,1)S(1)} %get-tuple-element.41), channel_id=1, source_target_pairs={{0,4},{4,8},{8,12},{12,0},{1,5},{5,9},{9,13},{13,1},{2,6},{6,10},{... | collective-permute-start | bytes 196616 | tf_op jit(solution)/shard_map/ppermute | solution.py:259
  28.6 6.7 %collective-permute-start.7 = (bf16[64,512]{1,0:T(8,128)(2,1)S(1)}, bf16[64,512]{1,0:T(8,128)(2,1)S(1)}, u32[]{:S(2)}, u32[]{:S(2)}) collective-permute-start(bf16[64,512]{1,0:T(8,128)(2,1)S(1)} %get-tuple-element.42), channel_id=1, source_target_pairs={{0,8},{4,12},{8,0},{12,4},{1,9},{5,13},{9,1},{13,5},{2,10},{6,14},... | collective-permute-start | bytes 196616 | tf_op jit(solution)/shard_map/ppermute | solution.py:259
  30.1 5.1 %collective-permute-start.8 = (bf16[64,512]{1,0:T(8,128)(2,1)S(1)}, bf16[64,512]{1,0:T(8,128)(2,1)S(1)}, u32[]{:S(2)}, u32[]{:S(2)}) collective-permute-start(bf16[64,512]{1,0:T(8,128)(2,1)S(1)} %get-tuple-element.43), channel_id=1, source_target_pairs={{0,12},{4,0},{8,4},{12,8},{1,13},{5,1},{9,5},{13,9},{2,14},{6,2},{... | collective-permute-start | bytes 196616 | tf_op jit(solution)/shard_map/ppermute | solution.py:259
  35.6 12.1 %collective-permute-start.11 = (bf16[64,512]{1,0:T(8,128)(2,1)S(1)}, bf16[64,512]{1,0:T(8,128)(2,1)S(1)}, u32[]{:S(2)}, u32[]{:S(2)}) collective-permute-start(bf16[64,512]{1,0:T(8,128)(2,1)S(1)} %get-tuple-element.48), channel_id=1, source_target_pairs={{0,12},{4,0},{8,4},{12,8},{1,13},{5,1},{9,5},{13,9},{2,14},{6,2},{... | collective-permute-start | bytes 196616 | tf_op jit(solution)/shard_map/ppermute | solution.py:259
  38.9 8.8 %collective-permute-start.12 = (bf16[64,512]{1,0:T(8,128)(2,1)S(1)}, bf16[64,512]{1,0:T(8,128)(2,1)S(1)}, u32[]{:S(2)}, u32[]{:S(2)}) collective-permute-start(bf16[64,512]{1,0:T(8,128)(2,1)S(1)} %get-tuple-element.49), channel_id=1, source_target_pairs={{0,8},{4,12},{8,0},{12,4},{1,9},{5,13},{9,1},{13,5},{2,10},{6,14},... | collective-permute-start | bytes 196616 | tf_op jit(solution)/shard_map/ppermute | solution.py:259
  38.9 8.8 %collective-permute-start.13 = (bf16[64,512]{1,0:T(8,128)(2,1)S(1)}, bf16[64,512]{1,0:T(8,128)(2,1)S(1)}, u32[]{:S(2)}, u32[]{:S(2)}) collective-permute-start(bf16[64,512]{1,0:T(8,128)(2,1)S(1)} %get-tuple-element.50), channel_id=1, source_target_pairs={{0,4},{4,8},{8,12},{12,0},{1,5},{5,9},{9,13},{13,1},{2,6},{6,10},{... | collective-permute-start | bytes 196616 | tf_op jit(solution)/shard_map/ppermute | solution.py:259
  43.3 17.9 %all-to-all-start = ((bf16[4,128,512]{2,1,0:T(8,128)(2,1)}), bf16[4,128,512]{2,1,0:T(8,128)(2,1)}, u32[]{:S(2)}, u32[]{:S(2)}) async-start(bf16[4,128,512]{2,1,0:T(8,128)(2,1)} %get-tuple-element.47.refs_14_), calls=%async_computation | async-start | bytes 1048576 | tf_op jit(solution)/shard_map/all_to_all | solution.py:374
  55.6 5.6 %collective-permute-start.14 = (bf16[64,512]{1,0:T(8,128)(2,1)S(1)}, bf16[64,512]{1,0:T(8,128)(2,1)S(1)}, u32[]{:S(2)}, u32[]{:S(2)}) collective-permute-start(bf16[64,512]{1,0:T(8,128)(2,1)S(1)} %get-tuple-element.52), channel_id=1, source_target_pairs={{0,1},{1,0},{2,3},{3,2},{4,5},{5,4},{6,7},{7,6},{8,9},{9,8},{10,11... | collective-permute-start | bytes 196616 | tf_op jit(solution)/shard_map/ppermute | solution.py:254
  55.9 17.1 %collective-permute-start.16 = (bf16[64,512]{1,0:T(8,128)(2,1)S(1)}, bf16[64,512]{1,0:T(8,128)(2,1)S(1)}, u32[]{:S(2)}, u32[]{:S(2)}) collective-permute-start(bf16[64,512]{1,0:T(8,128)(2,1)S(1)} %get-tuple-element.54), channel_id=1, source_target_pairs={{0,4},{4,8},{8,12},{12,0},{1,5},{5,9},{9,13},{13,1},{2,6},{6,10},{... | collective-permute-start | bytes 196616 | tf_op jit(solution)/shard_map/ppermute | solution.py:259
  58.8 14.3 %collective-permute-start.17 = (bf16[64,512]{1,0:T(8,128)(2,1)S(1)}, bf16[64,512]{1,0:T(8,128)(2,1)S(1)}, u32[]{:S(2)}, u32[]{:S(2)}) collective-permute-start(bf16[64,512]{1,0:T(8,128)(2,1)S(1)} %get-tuple-element.55), channel_id=1, source_target_pairs={{0,8},{4,12},{8,0},{12,4},{1,9},{5,13},{9,1},{13,5},{2,10},{6,14},... | collective-permute-start | bytes 196616 | tf_op jit(solution)/shard_map/ppermute | solution.py:259
  59.7 13.4 %collective-permute-start.18 = (bf16[64,512]{1,0:T(8,128)(2,1)S(1)}, bf16[64,512]{1,0:T(8,128)(2,1)S(1)}, u32[]{:S(2)}, u32[]{:S(2)}) collective-permute-start(bf16[64,512]{1,0:T(8,128)(2,1)S(1)} %get-tuple-element.56), channel_id=1, source_target_pairs={{0,12},{4,0},{8,4},{12,8},{1,13},{5,1},{9,5},{13,9},{2,14},{6,2},{... | collective-permute-start | bytes 196616 | tf_op jit(solution)/shard_map/ppermute | solution.py:259
  62.4 6.6 %collective-permute-start.9 = (bf16[64,512]{1,0:T(8,128)(2,1)S(1)}, bf16[64,512]{1,0:T(8,128)(2,1)S(1)}, u32[]{:S(2)}, u32[]{:S(2)}) collective-permute-start(bf16[64,512]{1,0:T(8,128)(2,1)S(1)} %fusion.1), channel_id=1, source_target_pairs={{0,8},{4,12},{8,0},{12,4},{1,9},{5,13},{9,1},{13,5},{2,10},{6,14},... | collective-permute-start | bytes 196616 | tf_op jit(solution)/shard_map/ppermute | solution.py:254
  63.1 6.1 %collective-permute-start.15 = (bf16[32,512]{1,0:T(8,128)(2,1)S(1)}, bf16[32,512]{1,0:T(8,128)(2,1)S(1)}, u32[]{:S(2)}, u32[]{:S(2)}) collective-permute-start(bf16[32,512]{1,0:T(8,128)(2,1)S(1)} %fusion.5), channel_id=1, source_target_pairs={{0,2},{1,3},{2,0},{3,1},{4,6},{5,7},{6,4},{7,5},{8,10},{9,11},{10,... | collective-permute-start | bytes 98312 | tf_op jit(solution)/shard_map/ppermute | solution.py:254
  69.1 4.0 %collective-permute-start.10 = (bf16[32,512]{1,0:T(8,128)(2,1)S(1)}, bf16[32,512]{1,0:T(8,128)(2,1)S(1)}, u32[]{:S(2)}, u32[]{:S(2)}) collective-permute-start(bf16[32,512]{1,0:T(8,128)(2,1)S(1)} %fusion.4), channel_id=1, source_target_pairs={{0,4},{4,0},{8,12},{12,8},{1,5},{5,1},{9,13},{13,9},{2,6},{6,2},{1... | collective-permute-start | bytes 98312 | tf_op jit(solution)/shard_map/ppermute | solution.py:254
  73.1 4.3 %collective-permute-start.19 = (bf16[64,512]{1,0:T(8,128)(2,1)S(1)}, bf16[64,512]{1,0:T(8,128)(2,1)S(1)}, u32[]{:S(2)}, u32[]{:S(2)}) collective-permute-start(bf16[64,512]{1,0:T(8,128)(2,1)S(1)} %pad_maximum_fusion.4), channel_id=1, source_target_pairs={{0,4},{4,0},{8,12},{12,8},{1,5},{5,1},{9,13},{13,9},{2,6},{6,2},{1... | collective-permute-start | bytes 196616 | tf_op jit(solution)/shard_map/ppermute | solution.py:254
  77.5 6.1 %collective-permute-start.20 = (bf16[96,512]{1,0:T(8,128)(2,1)S(1)}, bf16[96,512]{1,0:T(8,128)(2,1)S(1)}, u32[]{:S(2)}, u32[]{:S(2)}) collective-permute-start(bf16[96,512]{1,0:T(8,128)(2,1)S(1)} %pad_maximum_fusion.2), channel_id=1, source_target_pairs={{0,8},{4,12},{8,0},{12,4},{1,9},{5,13},{9,1},{13,5},{2,10},{6,14},... | collective-permute-start | bytes 294920 | tf_op jit(solution)/shard_map/ppermute | solution.py:254
  83.7 5.4 %collective-permute-start.21 = (bf16[160,512]{1,0:T(8,128)(2,1)S(1)}, bf16[160,512]{1,0:T(8,128)(2,1)S(1)}, u32[]{:S(2)}, u32[]{:S(2)}) collective-permute-start(bf16[160,512]{1,0:T(8,128)(2,1)S(1)} %pad_maximum_fusion.1), channel_id=1, source_target_pairs={{0,2},{1,3},{2,0},{3,1},{4,6},{5,7},{6,4},{7,5},{8,10},{9,11},{10,... | collective-permute-start | bytes 491528 | tf_op jit(solution)/shard_map/ppermute | solution.py:254
  89.2 1.7 %collective-permute-start.22 = (bf16[320,512]{1,0:T(8,128)(2,1)S(1)}, bf16[320,512]{1,0:T(8,128)(2,1)S(1)}, u32[]{:S(2)}, u32[]{:S(2)}) collective-permute-start(bf16[320,512]{1,0:T(8,128)(2,1)S(1)} %pad_maximum_fusion), channel_id=1, source_target_pairs={{0,1},{1,0},{2,3},{3,2},{4,5},{5,4},{6,7},{7,6},{8,9},{9,8},{10,11... | collective-permute-start | bytes 983048 | tf_op jit(solution)/shard_map/ppermute | solution.py:254
  (2 other events, 1.7 us)

commit v7 on v6

--- a/solution.py
+++ b/solution.py
@@ -28,8 +28,11 @@
     return act, upper + act * (1.0 - tanh)
 
 
-def call(body, outs, args, flops=0, scratch=(), smem=(), far=(), far_out=(), order=(), vmem=16):
-    args = list(args) + list(order)
+def call(body, outs, args, flops=0, scratch=(), smem=(), far=(), far_out=(), order=(), vmem=16, pin=False):
+    args = [
+        pltpu.with_memory_space_constraint(a, pltpu.HBM) if pin and i in far else a
+        for i, a in enumerate(args)
+    ] + list(order)
     moved = sum(a.size * a.dtype.itemsize for a in args) + sum(
         o.size * o.dtype.itemsize for o in outs
     )
@@ -117,6 +120,11 @@
 def hot_rows(column, edge_dev):
     edges = lax.broadcasted_iota(jnp.int32, (column.shape[0], edge_dev), 1).astype(F32)
     return jnp.where(column == edges, 1.0, 0.0).astype(BF16)
+
+
+def pair_kernel(fetch, store, out, fetch_v, store_v, sems):
+    waited(loads([fetch, store], [fetch_v, store_v], sems))
+    out[...] = jnp.concatenate([fetch_v[...], store_v[...]], axis=1)
 
 
 def lend_kernel(ranks, me, *refs):
@@ -195,10 +203,15 @@
         updated_v[at, :] = total.astype(BF16)
         leave[i].start()
         hidden[:, at] = fresh[i].T
-    copies, part = term.shape[0], term.shape[1]
     total = dot(hidden[...], upstream_v[...]).astype(BF16)
-    for k in range(copies):
-        term[reverse(k, copies)] = total[k * part : (k + 1) * part]
+    if len(term.shape) == 2:
+        term[...] = total
+    else:
+        parts, part = term.shape[0], term.shape[1]
+        copies = parts // ranks
+        for k in range(parts):
+            block = reverse(k % copies, copies) * ranks + k // copies
+            term[k] = total[block * part : (block + 1) * part]
     waited(leave)
 
 
@@ -318,7 +331,14 @@
     narrow = 2 * triplets * basis_width * width
     dma = pltpu.SemaphoreType.DMA
 
-    both = jnp.concatenate([fetch_rows[0, 0], store_rows[0, 0]], axis=1)
+    (both,) = call(
+        pair_kernel,
+        [shape((ranks, 2 * per_owner), jnp.int32)],
+        [fetch_rows[0, 0], store_rows[0, 0]],
+        far=(0, 1),
+        scratch=[pltpu.VMEM((ranks, per_owner), jnp.int32)] * 2 + [dma((2,))],
+        pin=True,
+    )
     lists = exchange([both] * ranks, 1)
     lend = call(
         functools.partial(lend_kernel, ranks),
@@ -328,6 +348,7 @@
         far=(ranks + 1,),
         flops=2 * slots * edge_dev * width,
         scratch=[held(edges), dma((1,))],
+        pin=True,
     )
     fetched = exchange(lend, -1)
     same, dhidden = call(
@@ -339,6 +360,7 @@
         flops=4 * slots * edge_dev * width,
         scratch=[held(upstream), held(w_out), dma((2,))],
         order=[lend[0]],
+        pin=True,
     )
     partial_rows = call(
         functools.partial(forward_kernel, ranks, step),
@@ -350,6 +372,7 @@
         scratch=[held(basis), held(plane), held(hot), held(hot), dma((1,))],
         order=[same],
         vmem=30,
+        pin=True,
     )
     home = exchange(partial_rows, 1)
     back = call(
@@ -359,9 +382,12 @@
         flops=2 * slots * slots * width,
     )
     dpartial = exchange(back, -1)
+    parts = ranks * copies
+    part = width // parts
+    term_dims = (width, width) if part % 16 else (parts, part, width)
     updated, out_term = call(
         functools.partial(update_kernel, ranks, 256),
-        [shape((edge_dev, width)), shape((copies, width // copies, width))],
+        [shape((edge_dev, width)), shape(term_dims)],
         [place] + lists + home + [edges, upstream, w_out],
         smem=(0,),
         far=(2 * ranks + 1, 2 * ranks + 2, 2 * ranks + 3),
@@ -371,7 +397,12 @@
         + [pltpu.VMEM((width, edge_dev), BF16), dma((3,)), dma((edge_dev // 256,))],
         order=[back[0]],
     )
-    out_parts = lax.all_to_all(out_term, "dp", split_axis=0, concat_axis=0, tiled=True)
+    sent = out_term
+    if part % 16:
+        blocks_of = [reverse(k % copies, copies) * ranks + k // copies for k in range(parts)]
+        split = out_term.reshape(parts, part, width)
+        sent = jnp.stack([split[block] for block in blocks_of])
+    out_parts = lax.all_to_all(sent, ("graph", "dp"), split_axis=0, concat_axis=0, tiled=True)
     basis_half = basis_width // 2
     basis_kept, basis_away, *dfetch = call(
         functools.partial(backward_kernel, ranks, step),
@@ -384,17 +415,19 @@
         + [pltpu.VMEM((basis_width, width), F32), dma((1,))],
         order=[out_term],
         vmem=36,
+        pin=True,
     )
     returned = exchange(dfetch, 1)
     basis_part = joined(basis_kept, basis_away)
     for bit in bits_of("dp")[1:]:
         basis_part = halve(basis_part, "dp", bit)
     out_part = jnp.sum(out_parts.astype(F32), axis=0)
-    for bit in reversed(bits_of("graph")):
-        out_part = halve(out_part, "graph", bit)
     out, total = out_part.astype(BF16), basis_part.astype(BF16)
-    out, total, returned = lax.optimization_barrier((out, total, returned))
     for bit in bits_of("graph"):
+        early, late = (1, 2) if bit == 0 else (2, ranks)
+        if bit < 2:
+            tied = (out, total, returned[early:late])
+            out, total, returned[early:late] = lax.optimization_barrier(tied)
         got, out = doubled(out, total, "graph", bit)
         total = (total.astype(F32) + got.astype(F32)).astype(BF16)
     (grad_edge,) = call(

time: 93.1 us -> 89.1 us (0.957)
  local copies, waits for them, and re-layouts: 3.06 us -> 0.1 us
  waiting for transfers between devices: 28.5 us -> 26.1 us
  Pallas kernels: 23.1 us -> 25.3 us
  other arithmetic: 4.1 us -> 2.24 us
  starting transfers between devices: 32.4 us -> 33.4 us
    ppermute x8 -> x6, waiting for transfers between devices: 21.2 us -> 12.2 us  [swap(): lax.ppermute(value, axis, [(k, k ^ mask) for k in range(lax.axis_size(axi...]
    ppermute x15, waiting for transfers between devices: 7.3 us -> 12.9 us  [shift(): lax.ppermute(value, axis, [(k, (k + by) % count) for k in range(count)])]
    unnamed x20 -> x12, local copies, waits for them, and re-layouts: 2.97 us -> 0.04 us
    pallas_call x7 -> x8, Pallas kernels: 23.1 us -> 25.3 us  [call(): pl.pallas_call(inner if order else body, out_shape=tuple(outs), in_specs=...]
    all_to_all x1, starting transfers between devices: 4.33 us -> 6 us  [per_device(): lax.all_to_all(sent, ('graph', 'dp'), split_axis=0, concat_axis=0, tiled=...]
    reduce_sum x1, other arithmetic: 1.15 us -> 0.08 us  [per_device(): out_part = jnp.sum(out_parts.astype(F32), axis=0)]
    all_to_all x1, waiting for transfers between devices: 0.01 us -> 0.99 us  [per_device(): lax.all_to_all(sent, ('graph', 'dp'), split_axis=0, concat_axis=0, tiled=...]
    ppermute x8 -> x6, starting transfers between devices: 5.01 us -> 4.6 us  [swap(): lax.ppermute(value, axis, [(k, k ^ mask) for k in range(lax.axis_size(axi...]
  transfers between devices with their start and end apart: 24 -> 22, of which waited for: 12 -> 15; matrix products, arithmetic and copies ran while one was open for 1% -> 0% of each run, Pallas kernels for 18% -> 19%
where the time goes in v7:
time: 89.1 us; the launch traced here: 88.7 us
  starting transfers between devices  33.4 us (37%)
  waiting for transfers between devices  26.1 us (29%)
  Pallas kernels  25.3 us (28%)
  other arithmetic  2.24 us (3%)
  between operations  1.59 us (2%)
    pallas_call x8, Pallas kernels, call(): pl.pallas_call(inner if order else body, out_shape=tuple(outs), in_specs=...  25.3 us
    ppermute x15, starting transfers between devices, shift(): lax.ppermute(value, axis, [(k, (k + by) % count) for k in range(count)])  22.8 us
    ppermute x15, waiting for transfers between devices, shift(): lax.ppermute(value, axis, [(k, (k + by) % count) for k in range(count)])  12.9 us
    ppermute x6, waiting for transfers between devices, swap(): lax.ppermute(value, axis, [(k, k ^ mask) for k in range(lax.axis_size(axi...  12.2 us
    all_to_all x1, starting transfers between devices, per_device(): lax.all_to_all(sent, ('graph', 'dp'), split_axis=0, concat_axis=0, tiled=...  6 us
    ppermute x6, starting transfers between devices, swap(): lax.ppermute(value, axis, [(k, k ^ mask) for k in range(lax.axis_size(axi...  4.6 us
  transfers between devices with their start and end apart: 22, of which 15 were waited for; matrix products, arithmetic and copies ran while one was open for 0% of the time, Pallas kernels for 19%

profile of v7, /device:TPU:0, one launch (start us, length us, event | category | flops | bytes accessed | tf_op | source)
XLA Modules:
  0.0 88.7 jit_solution(2808828126893739665)
XLA Ops:
  0.6 0.8 shard_map.129.refs_0_.refs_1_
  1.4 5.1 %collective-permute-start.2 = (s32[4,128]{1,0:T(4,128)S(1)}, s32[4,128]{1,0:T(4,128)S(1)}, u32[]{:S(2)}, u32[]{:S(2)}) collective-permute-start(s32[4,128]{1,0:T(4,128)S(1)} %shard_map.129.refs_0_.refs_1_), channel_id=1, source_target_pairs={{0,12},{4,0},{8,4},{12,8},{1,13},{5,1},{9,5},{13,9},{2,14},{6,2},{... | collective-permute-start | bytes 6152 | tf_op jit(solution)/shard_map/ppermute | solution.py:272
  6.5 1.0 %collective-permute-start = (s32[4,128]{1,0:T(4,128)S(1)}, s32[4,128]{1,0:T(4,128)S(1)}, u32[]{:S(2)}, u32[]{:S(2)}) collective-permute-start(s32[4,128]{1,0:T(4,128)S(1)} %shard_map.129.refs_0_.refs_1_), channel_id=1, source_target_pairs={{0,4},{4,8},{8,12},{12,0},{1,5},{5,9},{9,13},{13,1},{2,6},{6,10},{... | collective-permute-start | bytes 6152 | tf_op jit(solution)/shard_map/ppermute | solution.py:272
  7.8 3.2 %collective-permute-done.1.refs_2_.refs_3_ = s32[4,128]{1,0:T(4,128)S(1)} collective-permute-done((s32[4,128]{1,0:T(4,128)S(1)}, s32[4,128]{1,0:T(4,128)S(1)}, u32[]{:S(2)}, u32[]{:S(2)}) %collective-permute-start.1) | collective-permute-done | bytes 2080 | tf_op jit(solution)/shard_map/ppermute | solution.py:272
  11.0 0.9 %collective-permute-done.refs_1_.refs_2_ = s32[4,128]{1,0:T(4,128)S(1)} collective-permute-done((s32[4,128]{1,0:T(4,128)S(1)}, s32[4,128]{1,0:T(4,128)S(1)}, u32[]{:S(2)}, u32[]{:S(2)}) %collective-permute-start) | collective-permute-done | bytes 2080 | tf_op jit(solution)/shard_map/ppermute | solution.py:272
  11.9 2.2 %shard_map.130 = (bf16[64,512]{1,0:T(8,128)(2,1)S(1)}, bf16[64,512]{1,0:T(8,128)(2,1)S(1)}, bf16[64,512]{1,0:T(8,128)(2,1)S(1)}, bf16[64,512]{1,0:T(8,128)(2,1)S(1)}) custom-call(s32[2]{0:T(128)S(1)} %pad_add_fusion.me.refs_0_, s32[4,128]{1,0:T(4,128)S(1)} %shard_map.129.refs_0_.refs_1_, s32[4,128]{1,0:T(4,128)S(1)} %collective-permute-done.refs_1_.refs_2_, ...), custom_call_target="tpu_custom_call" | custom-call | flops 268435456 | bytes 1318920 | tf_op jit(solution)/shard_map/pallas_call | solution.py:48
  15.4 1.9 %collective-permute-start.5 = (bf16[64,512]{1,0:T(8,128)(2,1)S(1)}, bf16[64,512]{1,0:T(8,128)(2,1)S(1)}, u32[]{:S(2)}, u32[]{:S(2)}) collective-permute-start(bf16[64,512]{1,0:T(8,128)(2,1)S(1)} %get-tuple-element.39), channel_id=1, source_target_pairs={{0,4},{4,8},{8,12},{12,0},{1,5},{5,9},{9,13},{13,1},{2,6},{6,10},{... | collective-permute-start | bytes 196616 | tf_op jit(solution)/shard_map/ppermute | solution.py:272
  18.0 2.9 %shard_map.131 = (bf16[256,256]{1,0:T(8,128)(2,1)S(1)}, f32[256,512]{1,0:T(8,128)S(1)}) custom-call(s32[2]{0:T(128)S(1)} %pad_add_fusion.me.refs_0_, s32[4,128]{1,0:T(4,128)S(1)} %shard_map.129.refs_0_.refs_1_, s32[4,128]{1,0:T(4,128)S(1)} %collective-permute-done.refs_1_.refs_2_, s32[4,128]{1,0:T(4,128)S(1)} %collective-permute-done.1.refs_2_.refs_3_, ...), custom_call_target="tpu_custom_call" | custom-call | flops 536870912 | bytes 2301960 | tf_op jit(solution)/shard_map/pallas_call | solution.py:48
  21.6 5.3 %shard_map.132 = (bf16[64,512]{1,0:T(8,128)(2,1)S(1)}, bf16[64,512]{1,0:T(8,128)(2,1)S(1)}, bf16[64,512]{1,0:T(8,128)(2,1)S(1)}, bf16[64,512]{1,0:T(8,128)(2,1)S(1)}) custom-call(s32[2]{0:T(128)S(1)} %pad_add_fusion.me.refs_0_, s32[1,1]{1,0:T(1,128)S(6)} %copy.14.refs_1_, bf16[64,512]{1,0:T(8,128)(2,1)S(1)} %get-tuple-element.36.refs_7_.refs_2_, ...), custom_call_target="tpu_custom_call" | custom-call | flops 2684354560 | bytes 1867788 | tf_op jit(solution)/shard_map/pallas_call | solution.py:48
  27.2 2.0 %collective-permute-start.7 = (bf16[64,512]{1,0:T(8,128)(2,1)S(1)}, bf16[64,512]{1,0:T(8,128)(2,1)S(1)}, u32[]{:S(2)}, u32[]{:S(2)}) collective-permute-start(bf16[64,512]{1,0:T(8,128)(2,1)S(1)} %get-tuple-element.43), channel_id=1, source_target_pairs={{0,8},{4,12},{8,0},{12,4},{1,9},{5,13},{9,1},{13,5},{2,10},{6,14},... | collective-permute-start | bytes 196616 | tf_op jit(solution)/shard_map/ppermute | solution.py:272
  29.3 1.8 %collective-permute-start.8 = (bf16[64,512]{1,0:T(8,128)(2,1)S(1)}, bf16[64,512]{1,0:T(8,128)(2,1)S(1)}, u32[]{:S(2)}, u32[]{:S(2)}) collective-permute-start(bf16[64,512]{1,0:T(8,128)(2,1)S(1)} %get-tuple-element.44), channel_id=1, source_target_pairs={{0,12},{4,0},{8,4},{12,8},{1,13},{5,1},{9,5},{13,9},{2,14},{6,2},{... | collective-permute-start | bytes 196616 | tf_op jit(solution)/shard_map/ppermute | solution.py:272
  31.1 2.1 %collective-permute-done.6.refs_1_.refs_6_ = bf16[64,512]{1,0:T(8,128)(2,1)S(1)} collective-permute-done((bf16[64,512]{1,0:T(8,128)(2,1)S(1)}, bf16[64,512]{1,0:T(8,128)(2,1)S(1)}, u32[]{:S(2)}, u32[]{:S(2)}) %collective-permute-start.6) | collective-permute-done | bytes 65568 | tf_op jit(solution)/shard_map/ppermute | solution.py:272
  33.1 1.2 %collective-permute-done.8.refs_3_.refs_8_ = bf16[64,512]{1,0:T(8,128)(2,1)S(1)} collective-permute-done((bf16[64,512]{1,0:T(8,128)(2,1)S(1)}, bf16[64,512]{1,0:T(8,128)(2,1)S(1)}, u32[]{:S(2)}, u32[]{:S(2)}) %collective-permute-start.8) | collective-permute-done | bytes 65568 | tf_op jit(solution)/shard_map/ppermute | solution.py:272
  34.7 2.8 %collective-permute-start.9 = (bf16[64,512]{1,0:T(8,128)(2,1)S(1)}, bf16[64,512]{1,0:T(8,128)(2,1)S(1)}, u32[]{:S(2)}, u32[]{:S(2)}) collective-permute-start(bf16[64,512]{1,0:T(8,128)(2,1)S(1)} %get-tuple-element.49), channel_id=1, source_target_pairs={{0,12},{4,0},{8,4},{12,8},{1,13},{5,1},{9,5},{13,9},{2,14},{6,2},{... | collective-permute-start | bytes 196616 | tf_op jit(solution)/shard_map/ppermute | solution.py:272
  38.2 3.8 %shard_map.134 = (bf16[1024,512]{1,0:T(8,128)(2,1)}, bf16[16,32,512]{2,1,0:T(8,128)(2,1)}) custom-call(s32[2]{0:T(128)S(1)} %pad_add_fusion.me.refs_0_, s32[4,128]{1,0:T(4,128)S(1)} %shard_map.129.refs_0_.refs_1_, s32[4,128]{1,0:T(4,128)S(1)} %collective-permute-done.refs_1_.refs_2_, s32[4,128]{1,0:T(4,128)S(1)} %collective-permute-done.1.refs_2_.refs_3_, ...), custom_call_target="tpu_custom_call" | custom-call | flops 1342177280 | bytes 4530184 | tf_op jit(solution)/shard_map/pallas_call | solution.py:48
  42.0 6.0 %all-to-all-start = ((bf16[16,32,512]{2,1,0:T(8,128)(2,1)}), bf16[16,32,512]{2,1,0:T(8,128)(2,1)S(1)}, u32[]{:S(2)}, u32[]{:S(2)}) async-start(bf16[16,32,512]{2,1,0:T(8,128)(2,1)} %get-tuple-element.48.refs_14_), calls=%async_computation | async-start | bytes 1048576 | tf_op jit(solution)/shard_map/all_to_all | solution.py:405
  48.0 7.8 %shard_map.135 = (f32[64,512]{1,0:T(8,128)S(1)}, bf16[64,512]{1,0:T(8,128)(2,1)S(1)}, bf16[64,512]{1,0:T(8,128)(2,1)S(1)}, bf16[64,512]{1,0:T(8,128)(2,1)S(1)}, ...) custom-call(s32[2]{0:T(128)S(1)} %pad_add_fusion.me.refs_0_, s32[1,1]{1,0:T(1,128)S(6)} %copy.14.refs_1_, ...), custom_call_target="tpu_custom_call" | custom-call | flops 4294967296 | bytes 2719756 | tf_op jit(solution)/shard_map/pallas_call | solution.py:48
  56.3 0.9 %collective-permute-done.12 = bf16[64,512]{1,0:T(8,128)(2,1)S(1)} collective-permute-done((bf16[64,512]{1,0:T(8,128)(2,1)S(1)}, bf16[64,512]{1,0:T(8,128)(2,1)S(1)}, u32[]{:S(2)}, u32[]{:S(2)}) %collective-permute-start.12) | collective-permute-done | bytes 65568 | tf_op jit(solution)/shard_map/ppermute | solution.py:267
  57.3 1.9 %collective-permute-start.13 = (bf16[32,512]{1,0:T(8,128)(2,1)S(1)}, bf16[32,512]{1,0:T(8,128)(2,1)S(1)}, u32[]{:S(2)}, u32[]{:S(2)}) collective-permute-start(bf16[32,512]{1,0:T(8,128)(2,1)S(1)} %fusion.2), channel_id=1, source_target_pairs={{0,2},{1,3},{2,0},{3,1},{4,6},{5,7},{6,4},{7,5},{8,10},{9,11},{10,... | collective-permute-start | bytes 98312 | tf_op jit(solution)/shard_map/ppermute | solution.py:267
  59.2 1.5 %collective-permute-start.14 = (bf16[64,512]{1,0:T(8,128)(2,1)S(1)}, bf16[64,512]{1,0:T(8,128)(2,1)S(1)}, u32[]{:S(2)}, u32[]{:S(2)}) collective-permute-start(bf16[64,512]{1,0:T(8,128)(2,1)S(1)} %get-tuple-element.54), channel_id=1, source_target_pairs={{0,4},{4,8},{8,12},{12,0},{1,5},{5,9},{9,13},{13,1},{2,6},{6,10},{... | collective-permute-start | bytes 196616 | tf_op jit(solution)/shard_map/ppermute | solution.py:272
  61.5 1.0 %all-to-all-done = bf16[16,32,512]{2,1,0:T(8,128)(2,1)S(1)} async-done(((bf16[16,32,512]{2,1,0:T(8,128)(2,1)}), bf16[16,32,512]{2,1,0:T(8,128)(2,1)S(1)}, u32[]{:S(2)}, u32[]{:S(2)}) %all-to-all-start) | async-done | bytes 524320 | tf_op jit(solution)/shard_map/all_to_all | solution.py:405
  62.5 2.8 %collective-permute-done.14.refs_5_ = bf16[64,512]{1,0:T(8,128)(2,1)S(1)} collective-permute-done((bf16[64,512]{1,0:T(8,128)(2,1)S(1)}, bf16[64,512]{1,0:T(8,128)(2,1)S(1)}, u32[]{:S(2)}, u32[]{:S(2)}) %collective-permute-start.14) | collective-permute-done | bytes 65568 | tf_op jit(solution)/shard_map/ppermute | solution.py:272
  65.3 2.0 %collective-permute-start.16 = (bf16[64,512]{1,0:T(8,128)(2,1)S(1)}, bf16[64,512]{1,0:T(8,128)(2,1)S(1)}, u32[]{:S(2)}, u32[]{:S(2)}) collective-permute-start(bf16[64,512]{1,0:T(8,128)(2,1)S(1)} %get-tuple-element.57), channel_id=1, source_target_pairs={{0,8},{4,12},{8,0},{12,4},{1,9},{5,13},{9,1},{13,5},{2,10},{6,14},... | collective-permute-start | bytes 196616 | tf_op jit(solution)/shard_map/ppermute | solution.py:272
  67.3 2.4 %collective-permute-start.17 = (bf16[64,512]{1,0:T(8,128)(2,1)S(1)}, bf16[64,512]{1,0:T(8,128)(2,1)S(1)}, u32[]{:S(2)}, u32[]{:S(2)}) collective-permute-start(bf16[64,512]{1,0:T(8,128)(2,1)S(1)} %get-tuple-element.58), channel_id=1, source_target_pairs={{0,12},{4,0},{8,4},{12,8},{1,13},{5,1},{9,5},{13,9},{2,14},{6,2},{... | collective-permute-start | bytes 196616 | tf_op jit(solution)/shard_map/ppermute | solution.py:272
  70.2 1.9 %collective-permute-done.16.refs_6_ = bf16[64,512]{1,0:T(8,128)(2,1)S(1)} collective-permute-done((bf16[64,512]{1,0:T(8,128)(2,1)S(1)}, bf16[64,512]{1,0:T(8,128)(2,1)S(1)}, u32[]{:S(2)}, u32[]{:S(2)}) %collective-permute-start.16) | collective-permute-done | bytes 65568 | tf_op jit(solution)/shard_map/ppermute | solution.py:272
  72.1 1.2 %collective-permute-start.18 = (bf16[96,512]{1,0:T(8,128)(2,1)S(1)}, bf16[96,512]{1,0:T(8,128)(2,1)S(1)}, u32[]{:S(2)}, u32[]{:S(2)}) collective-permute-start(bf16[96,512]{1,0:T(8,128)(2,1)S(1)} %pad_maximum_fusion.2), channel_id=1, source_target_pairs={{0,8},{4,12},{8,0},{12,4},{1,9},{5,13},{9,1},{13,5},{2,10},{6,14},... | collective-permute-start | bytes 294920 | tf_op jit(solution)/shard_map/ppermute | solution.py:267
  73.3 2.2 %shard_map.136 = bf16[1024,512]{1,0:T(8,128)(2,1)} custom-call(s32[2]{0:T(128)S(1)} %pad_add_fusion.me.refs_0_, s32[4,128]{1,0:T(4,128)S(1)} %shard_map.129.refs_0_.refs_1_, s32[4,128]{1,0:T(4,128)S(1)} %collective-permute-done.refs_1_.refs_2_, s32[4,128]{1,0:T(4,128)S(1)} %collective-permute-done.1.refs_2_.refs_3_, ...), custom_call_target="tpu_custom_call" | custom-call | flops 268435456 | bytes 2367496 | tf_op jit(solution)/shard_map/pallas_call | solution.py:48
  75.5 4.0 %collective-permute-done.18 = bf16[96,512]{1,0:T(8,128)(2,1)S(1)} collective-permute-done((bf16[96,512]{1,0:T(8,128)(2,1)S(1)}, bf16[96,512]{1,0:T(8,128)(2,1)S(1)}, u32[]{:S(2)}, u32[]{:S(2)}) %collective-permute-start.18) | collective-permute-done | bytes 98336 | tf_op jit(solution)/shard_map/ppermute | solution.py:267
  79.6 0.9 %collective-permute-start.19 = (bf16[160,512]{1,0:T(8,128)(2,1)S(1)}, bf16[160,512]{1,0:T(8,128)(2,1)S(1)}, u32[]{:S(2)}, u32[]{:S(2)}) collective-permute-start(bf16[160,512]{1,0:T(8,128)(2,1)S(1)} %pad_maximum_fusion.1), channel_id=1, source_target_pairs={{0,2},{1,3},{2,0},{3,1},{4,6},{5,7},{6,4},{7,5},{8,10},{9,11},{10,... | collective-permute-start | bytes 491528 | tf_op jit(solution)/shard_map/ppermute | solution.py:267
  80.5 4.4 %collective-permute-done.19 = bf16[160,512]{1,0:T(8,128)(2,1)S(1)} collective-permute-done((bf16[160,512]{1,0:T(8,128)(2,1)S(1)}, bf16[160,512]{1,0:T(8,128)(2,1)S(1)}, u32[]{:S(2)}, u32[]{:S(2)}) %collective-permute-start.19) | collective-permute-done | bytes 163872 | tf_op jit(solution)/shard_map/ppermute | solution.py:267
  85.2 1.6 %collective-permute-done.20 = bf16[320,512]{1,0:T(8,128)(2,1)S(1)} collective-permute-done((bf16[320,512]{1,0:T(8,128)(2,1)S(1)}, bf16[320,512]{1,0:T(8,128)(2,1)S(1)}, u32[]{:S(2)}, u32[]{:S(2)}) %collective-permute-start.20) | collective-permute-done | bytes 327712 | tf_op jit(solution)/shard_map/ppermute | solution.py:267
  87.6 1.1 %convert_multiply_fusion = f32[512,512]{1,0:T(8,128)} fusion(bf16[256,512]{1,0:T(8,128)(2,1)S(1)} %slice.38, bf16[256,512]{1,0:T(8,128)(2,1)S(1)} %maximum_select_fusion.1, pred[]{:T(512)S(6)} %eq.16), kind=kLoop, calls=%fused_computation | loop fusion | flops 2883584 | bytes 1572865 | tf_op jit(solution)/shard_map/div | solution.py:449
  (55 shorter events, 6.4 us)
Async XLA Ops:
  1.4 6.4 %collective-permute-start.2 = (s32[4,128]{1,0:T(4,128)S(1)}, s32[4,128]{1,0:T(4,128)S(1)}, u32[]{:S(2)}, u32[]{:S(2)}) collective-permute-start(s32[4,128]{1,0:T(4,128)S(1)} %shard_map.129.refs_0_.refs_1_), channel_id=1, source_target_pairs={{0,12},{4,0},{8,4},{12,8},{1,13},{5,1},{9,5},{13,9},{2,14},{6,2},{... | collective-permute-start | bytes 6152 | tf_op jit(solution)/shard_map/ppermute | solution.py:272
  6.5 4.5 %collective-permute-start.1 = (s32[4,128]{1,0:T(4,128)S(1)}, s32[4,128]{1,0:T(4,128)S(1)}, u32[]{:S(2)}, u32[]{:S(2)}) collective-permute-start(s32[4,128]{1,0:T(4,128)S(1)} %shard_map.129.refs_0_.refs_1_), channel_id=1, source_target_pairs={{0,8},{4,12},{8,0},{12,4},{1,9},{5,13},{9,1},{13,5},{2,10},{6,14},... | collective-permute-start | bytes 6152 | tf_op jit(solution)/shard_map/ppermute | solution.py:272
  6.5 5.4 %collective-permute-start = (s32[4,128]{1,0:T(4,128)S(1)}, s32[4,128]{1,0:T(4,128)S(1)}, u32[]{:S(2)}, u32[]{:S(2)}) collective-permute-start(s32[4,128]{1,0:T(4,128)S(1)} %shard_map.129.refs_0_.refs_1_), channel_id=1, source_target_pairs={{0,4},{4,8},{8,12},{12,0},{1,5},{5,9},{9,13},{13,1},{2,6},{6,10},{... | collective-permute-start | bytes 6152 | tf_op jit(solution)/shard_map/ppermute | solution.py:272
  14.1 6.8 %collective-permute-start.3 = (bf16[64,512]{1,0:T(8,128)(2,1)S(1)}, bf16[64,512]{1,0:T(8,128)(2,1)S(1)}, u32[]{:S(2)}, u32[]{:S(2)}) collective-permute-start(bf16[64,512]{1,0:T(8,128)(2,1)S(1)} %get-tuple-element.37), channel_id=1, source_target_pairs={{0,12},{4,0},{8,4},{12,8},{1,13},{5,1},{9,5},{13,9},{2,14},{6,2},{... | collective-permute-start | bytes 196616 | tf_op jit(solution)/shard_map/ppermute | solution.py:272
  14.8 6.2 %collective-permute-start.4 = (bf16[64,512]{1,0:T(8,128)(2,1)S(1)}, bf16[64,512]{1,0:T(8,128)(2,1)S(1)}, u32[]{:S(2)}, u32[]{:S(2)}) collective-permute-start(bf16[64,512]{1,0:T(8,128)(2,1)S(1)} %get-tuple-element.38), channel_id=1, source_target_pairs={{0,8},{4,12},{8,0},{12,4},{1,9},{5,13},{9,1},{13,5},{2,10},{6,14},... | collective-permute-start | bytes 196616 | tf_op jit(solution)/shard_map/ppermute | solution.py:272
  15.4 6.2 %collective-permute-start.5 = (bf16[64,512]{1,0:T(8,128)(2,1)S(1)}, bf16[64,512]{1,0:T(8,128)(2,1)S(1)}, u32[]{:S(2)}, u32[]{:S(2)}) collective-permute-start(bf16[64,512]{1,0:T(8,128)(2,1)S(1)} %get-tuple-element.39), channel_id=1, source_target_pairs={{0,4},{4,8},{8,12},{12,0},{1,5},{5,9},{9,13},{13,1},{2,6},{6,10},{... | collective-permute-start | bytes 196616 | tf_op jit(solution)/shard_map/ppermute | solution.py:272
  18.0 3.6 %copy-start.3 = (bf16[128,512]{1,0:T(8,128)(2,1)S(1)}, bf16[128,512]{1,0:T(8,128)(2,1)}, u32[]{:S(2)}) copy-start(bf16[128,512]{1,0:T(8,128)(2,1)} %refs_12_.1) | copy-start | bytes 393220
  18.0 3.6 %copy-start.4 = (s32[1,32,128]{2,1,0:T(8,128)S(1)}, s32[1,32,128]{2,1,0:T(8,128)}, u32[]{:S(2)}) copy-start(s32[1,32,128]{2,1,0:T(8,128)} %param.14) | copy-start | bytes 49156
  18.0 3.6 %copy-start.5 = (s32[1,32,128]{2,1,0:T(8,128)S(1)}, s32[1,32,128]{2,1,0:T(8,128)}, u32[]{:S(2)}) copy-start(s32[1,32,128]{2,1,0:T(8,128)} %param.15) | copy-start | bytes 49156
  21.6 16.6 %copy-start = (bf16[1,1024,512]{2,1,0:T(8,128)(2,1)S(1)}, bf16[1,1024,512]{2,1,0:T(8,128)(2,1)}, u32[]{:S(2)}) copy-start(bf16[1,1024,512]{2,1,0:T(8,128)(2,1)} %param.10) | copy-start | bytes 3145732
  21.6 16.6 %copy-start.1 = (bf16[1,1024,512]{2,1,0:T(8,128)(2,1)S(1)}, bf16[1,1024,512]{2,1,0:T(8,128)(2,1)}, u32[]{:S(2)}) copy-start(bf16[1,1024,512]{2,1,0:T(8,128)(2,1)} %param.11) | copy-start | bytes 3145732
  26.9 11.3 %copy-start.2 = (bf16[512,512]{1,0:T(8,128)(2,1)S(1)}, bf16[512,512]{1,0:T(8,128)(2,1)}, u32[]{:S(2)}) copy-start(bf16[512,512]{1,0:T(8,128)(2,1)} %refs_11_.1) | copy-start | bytes 1572868
  26.9 6.2 %collective-permute-start.6 = (bf16[64,512]{1,0:T(8,128)(2,1)S(1)}, bf16[64,512]{1,0:T(8,128)(2,1)S(1)}, u32[]{:S(2)}, u32[]{:S(2)}) collective-permute-start(bf16[64,512]{1,0:T(8,128)(2,1)S(1)} %get-tuple-element.42), channel_id=1, source_target_pairs={{0,4},{4,8},{8,12},{12,0},{1,5},{5,9},{9,13},{13,1},{2,6},{6,10},{... | collective-permute-start | bytes 196616 | tf_op jit(solution)/shard_map/ppermute | solution.py:272
  27.2 5.9 %collective-permute-start.7 = (bf16[64,512]{1,0:T(8,128)(2,1)S(1)}, bf16[64,512]{1,0:T(8,128)(2,1)S(1)}, u32[]{:S(2)}, u32[]{:S(2)}) collective-permute-start(bf16[64,512]{1,0:T(8,128)(2,1)S(1)} %get-tuple-element.43), channel_id=1, source_target_pairs={{0,8},{4,12},{8,0},{12,4},{1,9},{5,13},{9,1},{13,5},{2,10},{6,14},... | collective-permute-start | bytes 196616 | tf_op jit(solution)/shard_map/ppermute | solution.py:272
  29.3 5.1 %collective-permute-start.8 = (bf16[64,512]{1,0:T(8,128)(2,1)S(1)}, bf16[64,512]{1,0:T(8,128)(2,1)S(1)}, u32[]{:S(2)}, u32[]{:S(2)}) collective-permute-start(bf16[64,512]{1,0:T(8,128)(2,1)S(1)} %get-tuple-element.44), channel_id=1, source_target_pairs={{0,12},{4,0},{8,4},{12,8},{1,13},{5,1},{9,5},{13,9},{2,14},{6,2},{... | collective-permute-start | bytes 196616 | tf_op jit(solution)/shard_map/ppermute | solution.py:272
  34.7 13.3 %collective-permute-start.9 = (bf16[64,512]{1,0:T(8,128)(2,1)S(1)}, bf16[64,512]{1,0:T(8,128)(2,1)S(1)}, u32[]{:S(2)}, u32[]{:S(2)}) collective-permute-start(bf16[64,512]{1,0:T(8,128)(2,1)S(1)} %get-tuple-element.49), channel_id=1, source_target_pairs={{0,12},{4,0},{8,4},{12,8},{1,13},{5,1},{9,5},{13,9},{2,14},{6,2},{... | collective-permute-start | bytes 196616 | tf_op jit(solution)/shard_map/ppermute | solution.py:272
  37.5 10.5 %collective-permute-start.10 = (bf16[64,512]{1,0:T(8,128)(2,1)S(1)}, bf16[64,512]{1,0:T(8,128)(2,1)S(1)}, u32[]{:S(2)}, u32[]{:S(2)}) collective-permute-start(bf16[64,512]{1,0:T(8,128)(2,1)S(1)} %get-tuple-element.50), channel_id=1, source_target_pairs={{0,8},{4,12},{8,0},{12,4},{1,9},{5,13},{9,1},{13,5},{2,10},{6,14},... | collective-permute-start | bytes 196616 | tf_op jit(solution)/shard_map/ppermute | solution.py:272
  38.0 10.0 %collective-permute-start.11 = (bf16[64,512]{1,0:T(8,128)(2,1)S(1)}, bf16[64,512]{1,0:T(8,128)(2,1)S(1)}, u32[]{:S(2)}, u32[]{:S(2)}) collective-permute-start(bf16[64,512]{1,0:T(8,128)(2,1)S(1)} %get-tuple-element.51), channel_id=1, source_target_pairs={{0,4},{4,8},{8,12},{12,0},{1,5},{5,9},{9,13},{13,1},{2,6},{6,10},{... | collective-permute-start | bytes 196616 | tf_op jit(solution)/shard_map/ppermute | solution.py:272
  42.0 20.5 %all-to-all-start = ((bf16[16,32,512]{2,1,0:T(8,128)(2,1)}), bf16[16,32,512]{2,1,0:T(8,128)(2,1)S(1)}, u32[]{:S(2)}, u32[]{:S(2)}) async-start(bf16[16,32,512]{2,1,0:T(8,128)(2,1)} %get-tuple-element.48.refs_14_), calls=%async_computation | async-start | bytes 1048576 | tf_op jit(solution)/shard_map/all_to_all | solution.py:405
  55.9 1.4 %collective-permute-start.12 = (bf16[64,512]{1,0:T(8,128)(2,1)S(1)}, bf16[64,512]{1,0:T(8,128)(2,1)S(1)}, u32[]{:S(2)}, u32[]{:S(2)}) collective-permute-start(bf16[64,512]{1,0:T(8,128)(2,1)S(1)} %get-tuple-element.53), channel_id=1, source_target_pairs={{0,1},{1,0},{2,3},{3,2},{4,5},{5,4},{6,7},{7,6},{8,9},{9,8},{10,11... | collective-permute-start | bytes 196616 | tf_op jit(solution)/shard_map/ppermute | solution.py:267
  57.3 4.2 %collective-permute-start.13 = (bf16[32,512]{1,0:T(8,128)(2,1)S(1)}, bf16[32,512]{1,0:T(8,128)(2,1)S(1)}, u32[]{:S(2)}, u32[]{:S(2)}) collective-permute-start(bf16[32,512]{1,0:T(8,128)(2,1)S(1)} %fusion.2), channel_id=1, source_target_pairs={{0,2},{1,3},{2,0},{3,1},{4,6},{5,7},{6,4},{7,5},{8,10},{9,11},{10,... | collective-permute-start | bytes 98312 | tf_op jit(solution)/shard_map/ppermute | solution.py:267
  59.2 6.1 %collective-permute-start.14 = (bf16[64,512]{1,0:T(8,128)(2,1)S(1)}, bf16[64,512]{1,0:T(8,128)(2,1)S(1)}, u32[]{:S(2)}, u32[]{:S(2)}) collective-permute-start(bf16[64,512]{1,0:T(8,128)(2,1)S(1)} %get-tuple-element.54), channel_id=1, source_target_pairs={{0,4},{4,8},{8,12},{12,0},{1,5},{5,9},{9,13},{13,1},{2,6},{6,10},{... | collective-permute-start | bytes 196616 | tf_op jit(solution)/shard_map/ppermute | solution.py:272
  65.3 4.8 %collective-permute-start.15 = (bf16[64,512]{1,0:T(8,128)(2,1)S(1)}, bf16[64,512]{1,0:T(8,128)(2,1)S(1)}, u32[]{:S(2)}, u32[]{:S(2)}) collective-permute-start(bf16[64,512]{1,0:T(8,128)(2,1)S(1)} %pad_maximum_fusion.4), channel_id=1, source_target_pairs={{0,4},{4,0},{8,12},{12,8},{1,5},{5,1},{9,13},{13,9},{2,6},{6,2},{1... | collective-permute-start | bytes 196616 | tf_op jit(solution)/shard_map/ppermute | solution.py:267
  65.3 6.8 %collective-permute-start.16 = (bf16[64,512]{1,0:T(8,128)(2,1)S(1)}, bf16[64,512]{1,0:T(8,128)(2,1)S(1)}, u32[]{:S(2)}, u32[]{:S(2)}) collective-permute-start(bf16[64,512]{1,0:T(8,128)(2,1)S(1)} %get-tuple-element.57), channel_id=1, source_target_pairs={{0,8},{4,12},{8,0},{12,4},{1,9},{5,13},{9,1},{13,5},{2,10},{6,14},... | collective-permute-start | bytes 196616 | tf_op jit(solution)/shard_map/ppermute | solution.py:272
  67.3 4.7 %collective-permute-start.17 = (bf16[64,512]{1,0:T(8,128)(2,1)S(1)}, bf16[64,512]{1,0:T(8,128)(2,1)S(1)}, u32[]{:S(2)}, u32[]{:S(2)}) collective-permute-start(bf16[64,512]{1,0:T(8,128)(2,1)S(1)} %get-tuple-element.58), channel_id=1, source_target_pairs={{0,12},{4,0},{8,4},{12,8},{1,13},{5,1},{9,5},{13,9},{2,14},{6,2},{... | collective-permute-start | bytes 196616 | tf_op jit(solution)/shard_map/ppermute | solution.py:272
  72.1 7.4 %collective-permute-start.18 = (bf16[96,512]{1,0:T(8,128)(2,1)S(1)}, bf16[96,512]{1,0:T(8,128)(2,1)S(1)}, u32[]{:S(2)}, u32[]{:S(2)}) collective-permute-start(bf16[96,512]{1,0:T(8,128)(2,1)S(1)} %pad_maximum_fusion.2), channel_id=1, source_target_pairs={{0,8},{4,12},{8,0},{12,4},{1,9},{5,13},{9,1},{13,5},{2,10},{6,14},... | collective-permute-start | bytes 294920 | tf_op jit(solution)/shard_map/ppermute | solution.py:267
  79.6 5.4 %collective-permute-start.19 = (bf16[160,512]{1,0:T(8,128)(2,1)S(1)}, bf16[160,512]{1,0:T(8,128)(2,1)S(1)}, u32[]{:S(2)}, u32[]{:S(2)}) collective-permute-start(bf16[160,512]{1,0:T(8,128)(2,1)S(1)} %pad_maximum_fusion.1), channel_id=1, source_target_pairs={{0,2},{1,3},{2,0},{3,1},{4,6},{5,7},{6,4},{7,5},{8,10},{9,11},{10,... | collective-permute-start | bytes 491528 | tf_op jit(solution)/shard_map/ppermute | solution.py:267
  85.1 1.7 %collective-permute-start.20 = (bf16[320,512]{1,0:T(8,128)(2,1)S(1)}, bf16[320,512]{1,0:T(8,128)(2,1)S(1)}, u32[]{:S(2)}, u32[]{:S(2)}) collective-permute-start(bf16[320,512]{1,0:T(8,128)(2,1)S(1)} %pad_maximum_fusion), channel_id=1, source_target_pairs={{0,1},{1,0},{2,3},{3,2},{4,5},{5,4},{6,7},{7,6},{8,9},{9,8},{10,11... | collective-permute-start | bytes 983048 | tf_op jit(solution)/shard_map/ppermute | solution.py:267

commit v8 on v7

--- a/solution.py
+++ b/solution.py
@@ -1,4 +1,5 @@
 import functools
+import math
 
 import jax
 import jax.numpy as jnp
@@ -127,13 +128,14 @@
     out[...] = jnp.concatenate([fetch_v[...], store_v[...]], axis=1)
 
 
+def near_kernel(edges, out, sems):
+    waited(loads([edges], [out], sems))
+
+
 def lend_kernel(ranks, me, *refs):
-    lists, edges, outs = refs[:ranks], refs[ranks], refs[ranks + 1 : 2 * ranks + 1]
-    edges_v, sems = refs[2 * ranks + 1 :]
-    arrive = loads([edges], [edges_v], sems)
+    lists, edges, outs = refs[:ranks], refs[ranks], refs[ranks + 1 :]
     hot = hot_rows(columns_of(lists, me[0], False, outs[0].shape[0]), edges.shape[0])
-    waited(arrive)
-    scattered(dot(hot, edges_v[...]).astype(BF16), outs)
+    scattered(dot(hot, edges[...]).astype(BF16), outs)
 
 
 def owner_kernel(ranks, me, *refs):
@@ -210,7 +212,7 @@
         parts, part = term.shape[0], term.shape[1]
         copies = parts // ranks
         for k in range(parts):
-            block = reverse(k % copies, copies) * ranks + k // copies
+            block = reverse(k % copies, copies) * ranks + reverse(k // copies, ranks)
             term[k] = total[block * part : (block + 1) * part]
     waited(leave)
 
@@ -263,6 +265,18 @@
     waited(leave)
 
 
+def finish_kernel(scales, low, out, out_got, basis, basis_got, out_full, basis_full):
+    for own, got, full, scale in (
+        (out, out_got, out_full, scales[0]),
+        (basis, basis_got, basis_full, scales[1]),
+    ):
+        rows = own.shape[0]
+        mine = pl.multiple_of(low[1] * rows, rows)
+        other = pl.multiple_of((1 - low[1]) * rows, rows)
+        full[pl.ds(mine, rows), :] = own[...].astype(F32) * scale
+        full[pl.ds(other, rows), :] = got[...].astype(F32) * scale
+
+
 def swap(value, axis, mask):
     return lax.ppermute(value, axis, [(k, k ^ mask) for k in range(lax.axis_size(axis))])
 
@@ -340,15 +354,22 @@
         pin=True,
     )
     lists = exchange([both] * ranks, 1)
+    (near,) = call(
+        near_kernel,
+        [shape(edges.shape)],
+        [edges],
+        far=(0,),
+        flops=wide,
+        scratch=[dma((1,))],
+        order=[both],
+        pin=True,
+    )
     lend = call(
         functools.partial(lend_kernel, ranks),
         pieces,
-        [place] + lists + [edges],
+        [place] + lists + [near],
         smem=(0,),
-        far=(ranks + 1,),
         flops=2 * slots * edge_dev * width,
-        scratch=[held(edges), dma((1,))],
-        pin=True,
     )
     fetched = exchange(lend, -1)
     same, dhidden = call(
@@ -399,7 +420,9 @@
     )
     sent = out_term
     if part % 16:
-        blocks_of = [reverse(k % copies, copies) * ranks + k // copies for k in range(parts)]
+        blocks_of = [
+            reverse(k % copies, copies) * ranks + reverse(k // copies, ranks) for k in range(parts)
+        ]
         split = out_term.reshape(parts, part, width)
         sent = jnp.stack([split[block] for block in blocks_of])
     out_parts = lax.all_to_all(sent, ("graph", "dp"), split_axis=0, concat_axis=0, tiled=True)
@@ -423,11 +446,9 @@
         basis_part = halve(basis_part, "dp", bit)
     out_part = jnp.sum(out_parts.astype(F32), axis=0)
     out, total = out_part.astype(BF16), basis_part.astype(BF16)
-    for bit in bits_of("graph"):
-        early, late = (1, 2) if bit == 0 else (2, ranks)
-        if bit < 2:
-            tied = (out, total, returned[early:late])
-            out, total, returned[early:late] = lax.optimization_barrier(tied)
+    for bit in reversed(bits_of("graph")):
+        if bit == 0:
+            out, total, returned = lax.optimization_barrier((out, total, returned))
         got, out = doubled(out, total, "graph", bit)
         total = (total.astype(F32) + got.astype(F32)).astype(BF16)
     (grad_edge,) = call(
@@ -441,12 +462,20 @@
         scratch=[held(upstream), held(upstream), dma((1,)), dma((edge_dev // 256,))],
     )
     out, total, grad_edge = lax.optimization_barrier((out, total, grad_edge))
-    for bit in reversed(bits_of("dp")):
+    for bit in reversed(bits_of("dp")[1:]):
         got, out = doubled(out, total, "dp", bit)
         total = double(total, got, "dp", bit)
-    out_scale = jnp.sqrt(F32(copies * ranks * edge_dev))
-    basis_scale = 2.0 * jnp.sqrt(F32(copies * ranks * blocks * block_rows))
-    return (updated[None], grad_edge[None], out.astype(F32) / out_scale, total.astype(F32) / basis_scale)
+    rows = total.shape[0]
+    got = swap(jnp.concatenate([total, out]), "dp", 1)
+    out_scale = 1.0 / math.sqrt(copies * ranks * edge_dev)
+    basis_scale = 0.5 / math.sqrt(copies * ranks * blocks * block_rows)
+    grad_w_out, grad_w_basis = call(
+        functools.partial(finish_kernel, (out_scale, basis_scale)),
+        [shape((width, width), F32), shape((basis_width, width), F32)],
+        [place, out, got[rows:], total, got[:rows]],
+        smem=(0,),
+    )
+    return (updated[None], grad_edge[None], grad_w_out, grad_w_basis)
 
 
 def solution(mesh):

time: 89.1 us -> 86.8 us (0.974)
  waiting for transfers between devices: 26.1 us -> 23 us
  Pallas kernels: 25.3 us -> 27.2 us
  other arithmetic: 2.24 us -> 0.36 us
    ppermute x15, waiting for transfers between devices: 12.9 us -> 8.37 us  [shift(): lax.ppermute(value, axis, [(k, (k + by) % count) for k in range(count)])]
    ppermute x6, starting transfers between devices: 4.6 us -> 7.38 us  [swap(): lax.ppermute(value, axis, [(k, k ^ mask) for k in range(lax.axis_size(axi...]
    ppermute x15, starting transfers between devices: 22.8 us -> 20.7 us  [shift(): lax.ppermute(value, axis, [(k, (k + by) % count) for k in range(count)])]
    div x2 -> x0, other arithmetic: 1.87 us -> none  [the longest x1 1.13 us: per_device(): out.astype(F32) / out_scale]
    pallas_call x8 -> x10, Pallas kernels: 25.3 us -> 27.2 us  [call(): pl.pallas_call(inner if order else body, out_shape=tuple(outs), in_specs=...]
    ppermute x6, waiting for transfers between devices: 12.2 us -> 13.7 us  [swap(): lax.ppermute(value, axis, [(k, k ^ mask) for k in range(lax.axis_size(axi...]
  transfers between devices with their start and end apart: 22 -> 22, of which waited for: 15 -> 13; matrix products, arithmetic and copies ran while one was open for 0% -> 0% of each run, Pallas kernels for 19% -> 21%
where the time goes in v8:
time: 86.8 us; the launch traced here: 86.4 us
  starting transfers between devices  34.1 us (39%)
  Pallas kernels  27.2 us (31%)
  waiting for transfers between devices  23 us (26%)
  between operations  1.6 us (2%)
    pallas_call x10, Pallas kernels, call(): pl.pallas_call(inner if order else body, out_shape=tuple(outs), in_specs=...  27.2 us
    ppermute x15, starting transfers between devices, shift(): lax.ppermute(value, axis, [(k, (k + by) % count) for k in range(count)])  20.7 us
    ppermute x6, waiting for transfers between devices, swap(): lax.ppermute(value, axis, [(k, k ^ mask) for k in range(lax.axis_size(axi...  13.7 us
    ppermute x15, waiting for transfers between devices, shift(): lax.ppermute(value, axis, [(k, (k + by) % count) for k in range(count)])  8.37 us
    ppermute x6, starting transfers between devices, swap(): lax.ppermute(value, axis, [(k, k ^ mask) for k in range(lax.axis_size(axi...  7.38 us
    all_to_all x1, starting transfers between devices, per_device(): lax.all_to_all(sent, ('graph', 'dp'), split_axis=0, concat_axis=0, tiled=...  6 us
  transfers between devices with their start and end apart: 22, of which 13 were waited for; matrix products, arithmetic and copies ran while one was open for 0% of the time, Pallas kernels for 21%

profile of v8, /device:TPU:0, one launch (start us, length us, event | category | flops | bytes accessed | tf_op | source)
XLA Modules:
  0.0 86.4 jit_solution(1333208155783043482)
XLA Ops:
  1.4 5.1 %collective-permute-start.2 = (s32[4,128]{1,0:T(4,128)S(1)}, s32[4,128]{1,0:T(4,128)S(1)}, u32[]{:S(2)}, u32[]{:S(2)}) collective-permute-start(s32[4,128]{1,0:T(4,128)S(1)} %shard_map.129.refs_1_.refs_0_), channel_id=1, source_target_pairs={{0,12},{4,0},{8,4},{12,8},{1,13},{5,1},{9,5},{13,9},{2,14},{6,2},{... | collective-permute-start | bytes 6152 | tf_op jit(solution)/shard_map/ppermute | solution.py:286
  6.5 1.0 %collective-permute-start = (s32[4,128]{1,0:T(4,128)S(1)}, s32[4,128]{1,0:T(4,128)S(1)}, u32[]{:S(2)}, u32[]{:S(2)}) collective-permute-start(s32[4,128]{1,0:T(4,128)S(1)} %shard_map.129.refs_1_.refs_0_), channel_id=1, source_target_pairs={{0,4},{4,8},{8,12},{12,0},{1,5},{5,9},{9,13},{13,1},{2,6},{6,10},{... | collective-permute-start | bytes 6152 | tf_op jit(solution)/shard_map/ppermute | solution.py:286
  7.6 1.2 %shard_map.130.refs_4_ = bf16[1024,512]{1,0:T(8,128)(2,1)S(1)} custom-call(bf16[1024,512]{1,0:T(8,128)(2,1)} %bitcast.21, s32[4,128]{1,0:T(4,128)S(1)} %shard_map.129.refs_1_.refs_0_), custom_call_target="tpu_custom_call" | custom-call | flops 1073741824 | bytes 2099200 | tf_op jit(solution)/shard_map/pallas_call | solution.py:49
  8.9 2.1 %collective-permute-done.1.refs_2_.refs_3_ = s32[4,128]{1,0:T(4,128)S(1)} collective-permute-done((s32[4,128]{1,0:T(4,128)S(1)}, s32[4,128]{1,0:T(4,128)S(1)}, u32[]{:S(2)}, u32[]{:S(2)}) %collective-permute-start.1) | collective-permute-done | bytes 2080 | tf_op jit(solution)/shard_map/ppermute | solution.py:286
  11.0 0.9 %collective-permute-done.refs_1_.refs_2_ = s32[4,128]{1,0:T(4,128)S(1)} collective-permute-done((s32[4,128]{1,0:T(4,128)S(1)}, s32[4,128]{1,0:T(4,128)S(1)}, u32[]{:S(2)}, u32[]{:S(2)}) %collective-permute-start) | collective-permute-done | bytes 2080 | tf_op jit(solution)/shard_map/ppermute | solution.py:286
  11.9 1.2 %shard_map.131 = (bf16[64,512]{1,0:T(8,128)(2,1)S(1)}, bf16[64,512]{1,0:T(8,128)(2,1)S(1)}, bf16[64,512]{1,0:T(8,128)(2,1)S(1)}, bf16[64,512]{1,0:T(8,128)(2,1)S(1)}) custom-call(s32[2]{0:T(128)S(1)} %pad_add_fusion.me.refs_0_.low, s32[4,128]{1,0:T(4,128)S(1)} %shard_map.129.refs_1_.refs_0_, s32[4,128]{1,0:T(4,128)S(1)} %collective-permute-done.refs_1_.refs_2_, ...), custom_call_target="tpu_custom_call" | custom-call | flops 268435456 | bytes 1318920 | tf_op jit(solution)/shard_map/pallas_call | solution.py:49
  14.3 1.9 %collective-permute-start.5 = (bf16[64,512]{1,0:T(8,128)(2,1)S(1)}, bf16[64,512]{1,0:T(8,128)(2,1)S(1)}, u32[]{:S(2)}, u32[]{:S(2)}) collective-permute-start(bf16[64,512]{1,0:T(8,128)(2,1)S(1)} %get-tuple-element.40), channel_id=1, source_target_pairs={{0,4},{4,8},{8,12},{12,0},{1,5},{5,9},{9,13},{13,1},{2,6},{6,10},{... | collective-permute-start | bytes 196616 | tf_op jit(solution)/shard_map/ppermute | solution.py:286
  17.0 2.9 %shard_map.132 = (bf16[256,256]{1,0:T(8,128)(2,1)S(1)}, f32[256,512]{1,0:T(8,128)S(1)}) custom-call(s32[2]{0:T(128)S(1)} %pad_add_fusion.me.refs_0_.low, s32[4,128]{1,0:T(4,128)S(1)} %shard_map.129.refs_1_.refs_0_, s32[4,128]{1,0:T(4,128)S(1)} %collective-permute-done.refs_1_.refs_2_, s32[4,128]{1,0:T(4,128)S(1)} %collective-permute-done.1.refs_2_.refs_3_, ...), custom_call_target="tpu_custom_call" | custom-call | flops 536870912 | bytes 2301960 | tf_op jit(solution)/shard_map/pallas_call | solution.py:49
  20.6 5.3 %shard_map.133 = (bf16[64,512]{1,0:T(8,128)(2,1)S(1)}, bf16[64,512]{1,0:T(8,128)(2,1)S(1)}, bf16[64,512]{1,0:T(8,128)(2,1)S(1)}, bf16[64,512]{1,0:T(8,128)(2,1)S(1)}) custom-call(s32[2]{0:T(128)S(1)} %pad_add_fusion.me.refs_0_.low, s32[1,1]{1,0:T(1,128)S(6)} %copy.14.refs_1_, bf16[64,512]{1,0:T(8,128)(2,1)S(1)} %get-tuple-element.37.refs_7_.refs_2_, ...), custom_call_target="tpu_custom_call" | custom-call | flops 2684354560 | bytes 1867788 | tf_op jit(solution)/shard_map/pallas_call | solution.py:49
  26.2 2.0 %collective-permute-start.7 = (bf16[64,512]{1,0:T(8,128)(2,1)S(1)}, bf16[64,512]{1,0:T(8,128)(2,1)S(1)}, u32[]{:S(2)}, u32[]{:S(2)}) collective-permute-start(bf16[64,512]{1,0:T(8,128)(2,1)S(1)} %get-tuple-element.44), channel_id=1, source_target_pairs={{0,8},{4,12},{8,0},{12,4},{1,9},{5,13},{9,1},{13,5},{2,10},{6,14},... | collective-permute-start | bytes 196616 | tf_op jit(solution)/shard_map/ppermute | solution.py:286
  28.2 1.8 %collective-permute-start.8 = (bf16[64,512]{1,0:T(8,128)(2,1)S(1)}, bf16[64,512]{1,0:T(8,128)(2,1)S(1)}, u32[]{:S(2)}, u32[]{:S(2)}) collective-permute-start(bf16[64,512]{1,0:T(8,128)(2,1)S(1)} %get-tuple-element.45), channel_id=1, source_target_pairs={{0,12},{4,0},{8,4},{12,8},{1,13},{5,1},{9,5},{13,9},{2,14},{6,2},{... | collective-permute-start | bytes 196616 | tf_op jit(solution)/shard_map/ppermute | solution.py:286
  30.0 2.1 %collective-permute-done.6.refs_1_.refs_6_ = bf16[64,512]{1,0:T(8,128)(2,1)S(1)} collective-permute-done((bf16[64,512]{1,0:T(8,128)(2,1)S(1)}, bf16[64,512]{1,0:T(8,128)(2,1)S(1)}, u32[]{:S(2)}, u32[]{:S(2)}) %collective-permute-start.6) | collective-permute-done | bytes 65568 | tf_op jit(solution)/shard_map/ppermute | solution.py:286
  32.1 1.2 %collective-permute-done.8.refs_3_.refs_8_ = bf16[64,512]{1,0:T(8,128)(2,1)S(1)} collective-permute-done((bf16[64,512]{1,0:T(8,128)(2,1)S(1)}, bf16[64,512]{1,0:T(8,128)(2,1)S(1)}, u32[]{:S(2)}, u32[]{:S(2)}) %collective-permute-start.8) | collective-permute-done | bytes 65568 | tf_op jit(solution)/shard_map/ppermute | solution.py:286
  33.7 2.8 %collective-permute-start.9 = (bf16[64,512]{1,0:T(8,128)(2,1)S(1)}, bf16[64,512]{1,0:T(8,128)(2,1)S(1)}, u32[]{:S(2)}, u32[]{:S(2)}) collective-permute-start(bf16[64,512]{1,0:T(8,128)(2,1)S(1)} %get-tuple-element.50), channel_id=1, source_target_pairs={{0,12},{4,0},{8,4},{12,8},{1,13},{5,1},{9,5},{13,9},{2,14},{6,2},{... | collective-permute-start | bytes 196616 | tf_op jit(solution)/shard_map/ppermute | solution.py:286
  37.1 3.8 %shard_map.135 = (bf16[1024,512]{1,0:T(8,128)(2,1)}, bf16[16,32,512]{2,1,0:T(8,128)(2,1)}) custom-call(s32[2]{0:T(128)S(1)} %pad_add_fusion.me.refs_0_.low, s32[4,128]{1,0:T(4,128)S(1)} %shard_map.129.refs_1_.refs_0_, s32[4,128]{1,0:T(4,128)S(1)} %collective-permute-done.refs_1_.refs_2_, s32[4,128]{1,0:T(4,128)S(1)} %collective-permute-done.1.refs_2_.refs_3_, ...), custom_call_target="tpu_custom_call" | custom-call | flops 1342177280 | bytes 4530184 | tf_op jit(solution)/shard_map/pallas_call | solution.py:49
  40.9 6.0 %all-to-all-start = ((bf16[16,32,512]{2,1,0:T(8,128)(2,1)}), bf16[16,32,512]{2,1,0:T(8,128)(2,1)S(1)}, u32[]{:S(2)}, u32[]{:S(2)}) async-start(bf16[16,32,512]{2,1,0:T(8,128)(2,1)} %get-tuple-element.49.refs_14_), calls=%async_computation | async-start | bytes 1048576 | tf_op jit(solution)/shard_map/all_to_all | solution.py:428
  47.0 7.8 %shard_map.136 = (f32[64,512]{1,0:T(8,128)S(1)}, bf16[64,512]{1,0:T(8,128)(2,1)S(1)}, bf16[64,512]{1,0:T(8,128)(2,1)S(1)}, bf16[64,512]{1,0:T(8,128)(2,1)S(1)}, ...) custom-call(s32[2]{0:T(128)S(1)} %pad_add_fusion.me.refs_0_.low, s32[1,1]{1,0:T(1,128)S(6)} %copy.14.refs_1_, ...), custom_call_target="tpu_custom_call" | custom-call | flops 4294967296 | bytes 2719756 | tf_op jit(solution)/shard_map/pallas_call | solution.py:49
  55.3 0.9 %collective-permute-done.12 = bf16[64,512]{1,0:T(8,128)(2,1)S(1)} collective-permute-done((bf16[64,512]{1,0:T(8,128)(2,1)S(1)}, bf16[64,512]{1,0:T(8,128)(2,1)S(1)}, u32[]{:S(2)}, u32[]{:S(2)}) %collective-permute-start.12) | collective-permute-done | bytes 65568 | tf_op jit(solution)/shard_map/ppermute | solution.py:281
  56.2 1.9 %collective-permute-start.13 = (bf16[32,512]{1,0:T(8,128)(2,1)S(1)}, bf16[32,512]{1,0:T(8,128)(2,1)S(1)}, u32[]{:S(2)}, u32[]{:S(2)}) collective-permute-start(bf16[32,512]{1,0:T(8,128)(2,1)S(1)} %fusion.2), channel_id=1, source_target_pairs={{0,2},{1,3},{2,0},{3,1},{4,6},{5,7},{6,4},{7,5},{8,10},{9,11},{10,... | collective-permute-start | bytes 98312 | tf_op jit(solution)/shard_map/ppermute | solution.py:281
  58.2 2.2 %collective-permute-done.13 = bf16[32,512]{1,0:T(8,128)(2,1)S(1)} collective-permute-done((bf16[32,512]{1,0:T(8,128)(2,1)S(1)}, bf16[32,512]{1,0:T(8,128)(2,1)S(1)}, u32[]{:S(2)}, u32[]{:S(2)}) %collective-permute-start.13) | collective-permute-done | bytes 32800 | tf_op jit(solution)/shard_map/ppermute | solution.py:281
  60.4 1.0 %all-to-all-done = bf16[16,32,512]{2,1,0:T(8,128)(2,1)S(1)} async-done(((bf16[16,32,512]{2,1,0:T(8,128)(2,1)}), bf16[16,32,512]{2,1,0:T(8,128)(2,1)S(1)}, u32[]{:S(2)}, u32[]{:S(2)}) %all-to-all-start) | async-done | bytes 524320 | tf_op jit(solution)/shard_map/all_to_all | solution.py:428
  61.5 2.3 %collective-permute-start.14 = (bf16[64,512]{1,0:T(8,128)(2,1)S(1)}, bf16[64,512]{1,0:T(8,128)(2,1)S(1)}, u32[]{:S(2)}, u32[]{:S(2)}) collective-permute-start(bf16[64,512]{1,0:T(8,128)(2,1)S(1)} %pad_maximum_fusion.4), channel_id=1, source_target_pairs={{0,8},{4,12},{8,0},{12,4},{1,9},{5,13},{9,1},{13,5},{2,10},{6,14},... | collective-permute-start | bytes 196616 | tf_op jit(solution)/shard_map/ppermute | solution.py:281
  64.6 1.0 %collective-permute-start.16 = (bf16[64,512]{1,0:T(8,128)(2,1)S(1)}, bf16[64,512]{1,0:T(8,128)(2,1)S(1)}, u32[]{:S(2)}, u32[]{:S(2)}) collective-permute-start(bf16[64,512]{1,0:T(8,128)(2,1)S(1)} %get-tuple-element.57), channel_id=1, source_target_pairs={{0,8},{4,12},{8,0},{12,4},{1,9},{5,13},{9,1},{13,5},{2,10},{6,14},... | collective-permute-start | bytes 196616 | tf_op jit(solution)/shard_map/ppermute | solution.py:286
  65.6 2.0 %collective-permute-start.17 = (bf16[64,512]{1,0:T(8,128)(2,1)S(1)}, bf16[64,512]{1,0:T(8,128)(2,1)S(1)}, u32[]{:S(2)}, u32[]{:S(2)}) collective-permute-start(bf16[64,512]{1,0:T(8,128)(2,1)S(1)} %get-tuple-element.58), channel_id=1, source_target_pairs={{0,12},{4,0},{8,4},{12,8},{1,13},{5,1},{9,5},{13,9},{2,14},{6,2},{... | collective-permute-start | bytes 196616 | tf_op jit(solution)/shard_map/ppermute | solution.py:286
  67.7 3.7 %collective-permute-done.14 = bf16[64,512]{1,0:T(8,128)(2,1)S(1)} collective-permute-done((bf16[64,512]{1,0:T(8,128)(2,1)S(1)}, bf16[64,512]{1,0:T(8,128)(2,1)S(1)}, u32[]{:S(2)}, u32[]{:S(2)}) %collective-permute-start.14) | collective-permute-done | bytes 65568 | tf_op jit(solution)/shard_map/ppermute | solution.py:281
  71.4 1.3 %collective-permute-done.16.refs_6_ = bf16[64,512]{1,0:T(8,128)(2,1)S(1)} collective-permute-done((bf16[64,512]{1,0:T(8,128)(2,1)S(1)}, bf16[64,512]{1,0:T(8,128)(2,1)S(1)}, u32[]{:S(2)}, u32[]{:S(2)}) %collective-permute-start.16) | collective-permute-done | bytes 65568 | tf_op jit(solution)/shard_map/ppermute | solution.py:286
  72.8 1.6 %collective-permute-start.18 = (bf16[96,512]{1,0:T(8,128)(2,1)S(1)}, bf16[96,512]{1,0:T(8,128)(2,1)S(1)}, u32[]{:S(2)}, u32[]{:S(2)}) collective-permute-start(bf16[96,512]{1,0:T(8,128)(2,1)S(1)} %pad_maximum_fusion.2), channel_id=1, source_target_pairs={{0,4},{4,0},{8,12},{12,8},{1,5},{5,1},{9,13},{13,9},{2,6},{6,2},{1... | collective-permute-start | bytes 294920 | tf_op jit(solution)/shard_map/ppermute | solution.py:281
  74.4 2.2 %shard_map.137 = bf16[1024,512]{1,0:T(8,128)(2,1)} custom-call(s32[2]{0:T(128)S(1)} %pad_add_fusion.me.refs_0_.low, s32[4,128]{1,0:T(4,128)S(1)} %shard_map.129.refs_1_.refs_0_, s32[4,128]{1,0:T(4,128)S(1)} %collective-permute-done.refs_1_.refs_2_, s32[4,128]{1,0:T(4,128)S(1)} %collective-permute-done.1.refs_2_.refs_3_, ...), custom_call_target="tpu_custom_call" | custom-call | flops 268435456 | bytes 2367496 | tf_op jit(solution)/shard_map/pallas_call | solution.py:49
  77.5 0.9 %collective-permute-start.19 = (bf16[160,512]{1,0:T(8,128)(2,1)S(1)}, bf16[160,512]{1,0:T(8,128)(2,1)S(1)}, u32[]{:S(2)}, u32[]{:S(2)}) collective-permute-start(bf16[160,512]{1,0:T(8,128)(2,1)S(1)} %pad_maximum_fusion.1), channel_id=1, source_target_pairs={{0,2},{1,3},{2,0},{3,1},{4,6},{5,7},{6,4},{7,5},{8,10},{9,11},{10,... | collective-permute-start | bytes 491528 | tf_op jit(solution)/shard_map/ppermute | solution.py:281
  78.5 4.4 %collective-permute-done.19 = bf16[160,512]{1,0:T(8,128)(2,1)S(1)} collective-permute-done((bf16[160,512]{1,0:T(8,128)(2,1)S(1)}, bf16[160,512]{1,0:T(8,128)(2,1)S(1)}, u32[]{:S(2)}, u32[]{:S(2)}) %collective-permute-start.19) | collective-permute-done | bytes 163872 | tf_op jit(solution)/shard_map/ppermute | solution.py:281
  83.1 1.6 %collective-permute-done.20 = bf16[320,512]{1,0:T(8,128)(2,1)S(1)} collective-permute-done((bf16[320,512]{1,0:T(8,128)(2,1)S(1)}, bf16[320,512]{1,0:T(8,128)(2,1)S(1)}, u32[]{:S(2)}, u32[]{:S(2)}) %collective-permute-start.20) | collective-permute-done | bytes 327712 | tf_op jit(solution)/shard_map/ppermute | solution.py:281
  84.8 1.7 %shard_map.138 = (f32[512,512]{1,0:T(8,128)}, f32[128,512]{1,0:T(8,128)}) custom-call(s32[2]{0:T(128)S(1)} %pad_add_fusion.me.refs_0_.low, bf16[256,512]{1,0:T(8,128)(2,1)S(1)} %maximum_select_fusion.out, bf16[256,512]{1,0:T(8,128)(2,1)S(1)} %slice.38.out_got, bf16[64,512]{1,0:T(8,128)(2,1)S(1)} %maximum_select_fusion.2.basis, ...), custom_call_target="tpu_custom_call" | custom-call | bytes 1966088 | tf_op jit(solution)/shard_map/pallas_call | solution.py:49
  (55 shorter events, 6.7 us)
Async XLA Ops:
  1.4 7.4 %collective-permute-start.2 = (s32[4,128]{1,0:T(4,128)S(1)}, s32[4,128]{1,0:T(4,128)S(1)}, u32[]{:S(2)}, u32[]{:S(2)}) collective-permute-start(s32[4,128]{1,0:T(4,128)S(1)} %shard_map.129.refs_1_.refs_0_), channel_id=1, source_target_pairs={{0,12},{4,0},{8,4},{12,8},{1,13},{5,1},{9,5},{13,9},{2,14},{6,2},{... | collective-permute-start | bytes 6152 | tf_op jit(solution)/shard_map/ppermute | solution.py:286
  6.5 4.5 %collective-permute-start.1 = (s32[4,128]{1,0:T(4,128)S(1)}, s32[4,128]{1,0:T(4,128)S(1)}, u32[]{:S(2)}, u32[]{:S(2)}) collective-permute-start(s32[4,128]{1,0:T(4,128)S(1)} %shard_map.129.refs_1_.refs_0_), channel_id=1, source_target_pairs={{0,8},{4,12},{8,0},{12,4},{1,9},{5,13},{9,1},{13,5},{2,10},{6,14},... | collective-permute-start | bytes 6152 | tf_op jit(solution)/shard_map/ppermute | solution.py:286
  6.5 5.4 %collective-permute-start = (s32[4,128]{1,0:T(4,128)S(1)}, s32[4,128]{1,0:T(4,128)S(1)}, u32[]{:S(2)}, u32[]{:S(2)}) collective-permute-start(s32[4,128]{1,0:T(4,128)S(1)} %shard_map.129.refs_1_.refs_0_), channel_id=1, source_target_pairs={{0,4},{4,8},{8,12},{12,0},{1,5},{5,9},{9,13},{13,1},{2,6},{6,10},{... | collective-permute-start | bytes 6152 | tf_op jit(solution)/shard_map/ppermute | solution.py:286
  13.1 6.8 %collective-permute-start.3 = (bf16[64,512]{1,0:T(8,128)(2,1)S(1)}, bf16[64,512]{1,0:T(8,128)(2,1)S(1)}, u32[]{:S(2)}, u32[]{:S(2)}) collective-permute-start(bf16[64,512]{1,0:T(8,128)(2,1)S(1)} %get-tuple-element.38), channel_id=1, source_target_pairs={{0,12},{4,0},{8,4},{12,8},{1,13},{5,1},{9,5},{13,9},{2,14},{6,2},{... | collective-permute-start | bytes 196616 | tf_op jit(solution)/shard_map/ppermute | solution.py:286
  13.7 6.2 %collective-permute-start.4 = (bf16[64,512]{1,0:T(8,128)(2,1)S(1)}, bf16[64,512]{1,0:T(8,128)(2,1)S(1)}, u32[]{:S(2)}, u32[]{:S(2)}) collective-permute-start(bf16[64,512]{1,0:T(8,128)(2,1)S(1)} %get-tuple-element.39), channel_id=1, source_target_pairs={{0,8},{4,12},{8,0},{12,4},{1,9},{5,13},{9,1},{13,5},{2,10},{6,14},... | collective-permute-start | bytes 196616 | tf_op jit(solution)/shard_map/ppermute | solution.py:286
  14.3 6.2 %collective-permute-start.5 = (bf16[64,512]{1,0:T(8,128)(2,1)S(1)}, bf16[64,512]{1,0:T(8,128)(2,1)S(1)}, u32[]{:S(2)}, u32[]{:S(2)}) collective-permute-start(bf16[64,512]{1,0:T(8,128)(2,1)S(1)} %get-tuple-element.40), channel_id=1, source_target_pairs={{0,4},{4,8},{8,12},{12,0},{1,5},{5,9},{9,13},{13,1},{2,6},{6,10},{... | collective-permute-start | bytes 196616 | tf_op jit(solution)/shard_map/ppermute | solution.py:286
  16.9 3.6 %copy-start.3 = (bf16[128,512]{1,0:T(8,128)(2,1)S(1)}, bf16[128,512]{1,0:T(8,128)(2,1)}, u32[]{:S(2)}) copy-start(bf16[128,512]{1,0:T(8,128)(2,1)} %refs_12_.1) | copy-start | bytes 393220
  17.0 3.6 %copy-start.4 = (s32[1,32,128]{2,1,0:T(8,128)S(1)}, s32[1,32,128]{2,1,0:T(8,128)}, u32[]{:S(2)}) copy-start(s32[1,32,128]{2,1,0:T(8,128)} %param.14) | copy-start | bytes 49156
  17.0 3.6 %copy-start.5 = (s32[1,32,128]{2,1,0:T(8,128)S(1)}, s32[1,32,128]{2,1,0:T(8,128)}, u32[]{:S(2)}) copy-start(s32[1,32,128]{2,1,0:T(8,128)} %param.15) | copy-start | bytes 49156
  20.5 16.6 %copy-start = (bf16[1,1024,512]{2,1,0:T(8,128)(2,1)S(1)}, bf16[1,1024,512]{2,1,0:T(8,128)(2,1)}, u32[]{:S(2)}) copy-start(bf16[1,1024,512]{2,1,0:T(8,128)(2,1)} %param.11) | copy-start | bytes 3145732
  20.6 16.6 %copy-start.1 = (bf16[1,1024,512]{2,1,0:T(8,128)(2,1)S(1)}, bf16[1,1024,512]{2,1,0:T(8,128)(2,1)}, u32[]{:S(2)}) copy-start(bf16[1,1024,512]{2,1,0:T(8,128)(2,1)} %param.10) | copy-start | bytes 3145732
  25.9 11.3 %copy-start.2 = (bf16[512,512]{1,0:T(8,128)(2,1)S(1)}, bf16[512,512]{1,0:T(8,128)(2,1)}, u32[]{:S(2)}) copy-start(bf16[512,512]{1,0:T(8,128)(2,1)} %refs_11_.1) | copy-start | bytes 1572868
  25.9 6.2 %collective-permute-start.6 = (bf16[64,512]{1,0:T(8,128)(2,1)S(1)}, bf16[64,512]{1,0:T(8,128)(2,1)S(1)}, u32[]{:S(2)}, u32[]{:S(2)}) collective-permute-start(bf16[64,512]{1,0:T(8,128)(2,1)S(1)} %get-tuple-element.43), channel_id=1, source_target_pairs={{0,4},{4,8},{8,12},{12,0},{1,5},{5,9},{9,13},{13,1},{2,6},{6,10},{... | collective-permute-start | bytes 196616 | tf_op jit(solution)/shard_map/ppermute | solution.py:286
  26.2 5.9 %collective-permute-start.7 = (bf16[64,512]{1,0:T(8,128)(2,1)S(1)}, bf16[64,512]{1,0:T(8,128)(2,1)S(1)}, u32[]{:S(2)}, u32[]{:S(2)}) collective-permute-start(bf16[64,512]{1,0:T(8,128)(2,1)S(1)} %get-tuple-element.44), channel_id=1, source_target_pairs={{0,8},{4,12},{8,0},{12,4},{1,9},{5,13},{9,1},{13,5},{2,10},{6,14},... | collective-permute-start | bytes 196616 | tf_op jit(solution)/shard_map/ppermute | solution.py:286
  28.2 5.1 %collective-permute-start.8 = (bf16[64,512]{1,0:T(8,128)(2,1)S(1)}, bf16[64,512]{1,0:T(8,128)(2,1)S(1)}, u32[]{:S(2)}, u32[]{:S(2)}) collective-permute-start(bf16[64,512]{1,0:T(8,128)(2,1)S(1)} %get-tuple-element.45), channel_id=1, source_target_pairs={{0,12},{4,0},{8,4},{12,8},{1,13},{5,1},{9,5},{13,9},{2,14},{6,2},{... | collective-permute-start | bytes 196616 | tf_op jit(solution)/shard_map/ppermute | solution.py:286
  33.7 13.3 %collective-permute-start.9 = (bf16[64,512]{1,0:T(8,128)(2,1)S(1)}, bf16[64,512]{1,0:T(8,128)(2,1)S(1)}, u32[]{:S(2)}, u32[]{:S(2)}) collective-permute-start(bf16[64,512]{1,0:T(8,128)(2,1)S(1)} %get-tuple-element.50), channel_id=1, source_target_pairs={{0,12},{4,0},{8,4},{12,8},{1,13},{5,1},{9,5},{13,9},{2,14},{6,2},{... | collective-permute-start | bytes 196616 | tf_op jit(solution)/shard_map/ppermute | solution.py:286
  36.5 10.5 %collective-permute-start.10 = (bf16[64,512]{1,0:T(8,128)(2,1)S(1)}, bf16[64,512]{1,0:T(8,128)(2,1)S(1)}, u32[]{:S(2)}, u32[]{:S(2)}) collective-permute-start(bf16[64,512]{1,0:T(8,128)(2,1)S(1)} %get-tuple-element.51), channel_id=1, source_target_pairs={{0,8},{4,12},{8,0},{12,4},{1,9},{5,13},{9,1},{13,5},{2,10},{6,14},... | collective-permute-start | bytes 196616 | tf_op jit(solution)/shard_map/ppermute | solution.py:286
  37.0 10.0 %collective-permute-start.11 = (bf16[64,512]{1,0:T(8,128)(2,1)S(1)}, bf16[64,512]{1,0:T(8,128)(2,1)S(1)}, u32[]{:S(2)}, u32[]{:S(2)}) collective-permute-start(bf16[64,512]{1,0:T(8,128)(2,1)S(1)} %get-tuple-element.52), channel_id=1, source_target_pairs={{0,4},{4,8},{8,12},{12,0},{1,5},{5,9},{9,13},{13,1},{2,6},{6,10},{... | collective-permute-start | bytes 196616 | tf_op jit(solution)/shard_map/ppermute | solution.py:286
  40.9 20.5 %all-to-all-start = ((bf16[16,32,512]{2,1,0:T(8,128)(2,1)}), bf16[16,32,512]{2,1,0:T(8,128)(2,1)S(1)}, u32[]{:S(2)}, u32[]{:S(2)}) async-start(bf16[16,32,512]{2,1,0:T(8,128)(2,1)} %get-tuple-element.49.refs_14_), calls=%async_computation | async-start | bytes 1048576 | tf_op jit(solution)/shard_map/all_to_all | solution.py:428
  54.8 1.4 %collective-permute-start.12 = (bf16[64,512]{1,0:T(8,128)(2,1)S(1)}, bf16[64,512]{1,0:T(8,128)(2,1)S(1)}, u32[]{:S(2)}, u32[]{:S(2)}) collective-permute-start(bf16[64,512]{1,0:T(8,128)(2,1)S(1)} %get-tuple-element.54), channel_id=1, source_target_pairs={{0,1},{1,0},{2,3},{3,2},{4,5},{5,4},{6,7},{7,6},{8,9},{9,8},{10,11... | collective-permute-start | bytes 196616 | tf_op jit(solution)/shard_map/ppermute | solution.py:281
  56.2 4.2 %collective-permute-start.13 = (bf16[32,512]{1,0:T(8,128)(2,1)S(1)}, bf16[32,512]{1,0:T(8,128)(2,1)S(1)}, u32[]{:S(2)}, u32[]{:S(2)}) collective-permute-start(bf16[32,512]{1,0:T(8,128)(2,1)S(1)} %fusion.2), channel_id=1, source_target_pairs={{0,2},{1,3},{2,0},{3,1},{4,6},{5,7},{6,4},{7,5},{8,10},{9,11},{10,... | collective-permute-start | bytes 98312 | tf_op jit(solution)/shard_map/ppermute | solution.py:281
  61.5 9.8 %collective-permute-start.14 = (bf16[64,512]{1,0:T(8,128)(2,1)S(1)}, bf16[64,512]{1,0:T(8,128)(2,1)S(1)}, u32[]{:S(2)}, u32[]{:S(2)}) collective-permute-start(bf16[64,512]{1,0:T(8,128)(2,1)S(1)} %pad_maximum_fusion.4), channel_id=1, source_target_pairs={{0,8},{4,12},{8,0},{12,4},{1,9},{5,13},{9,1},{13,5},{2,10},{6,14},... | collective-permute-start | bytes 196616 | tf_op jit(solution)/shard_map/ppermute | solution.py:281
  63.8 7.6 %collective-permute-start.15 = (bf16[64,512]{1,0:T(8,128)(2,1)S(1)}, bf16[64,512]{1,0:T(8,128)(2,1)S(1)}, u32[]{:S(2)}, u32[]{:S(2)}) collective-permute-start(bf16[64,512]{1,0:T(8,128)(2,1)S(1)} %get-tuple-element.56), channel_id=1, source_target_pairs={{0,4},{4,8},{8,12},{12,0},{1,5},{5,9},{9,13},{13,1},{2,6},{6,10},{... | collective-permute-start | bytes 196616 | tf_op jit(solution)/shard_map/ppermute | solution.py:286
  64.6 8.1 %collective-permute-start.16 = (bf16[64,512]{1,0:T(8,128)(2,1)S(1)}, bf16[64,512]{1,0:T(8,128)(2,1)S(1)}, u32[]{:S(2)}, u32[]{:S(2)}) collective-permute-start(bf16[64,512]{1,0:T(8,128)(2,1)S(1)} %get-tuple-element.57), channel_id=1, source_target_pairs={{0,8},{4,12},{8,0},{12,4},{1,9},{5,13},{9,1},{13,5},{2,10},{6,14},... | collective-permute-start | bytes 196616 | tf_op jit(solution)/shard_map/ppermute | solution.py:286
  65.6 7.1 %collective-permute-start.17 = (bf16[64,512]{1,0:T(8,128)(2,1)S(1)}, bf16[64,512]{1,0:T(8,128)(2,1)S(1)}, u32[]{:S(2)}, u32[]{:S(2)}) collective-permute-start(bf16[64,512]{1,0:T(8,128)(2,1)S(1)} %get-tuple-element.58), channel_id=1, source_target_pairs={{0,12},{4,0},{8,4},{12,8},{1,13},{5,1},{9,5},{13,9},{2,14},{6,2},{... | collective-permute-start | bytes 196616 | tf_op jit(solution)/shard_map/ppermute | solution.py:286
  72.8 4.7 %collective-permute-start.18 = (bf16[96,512]{1,0:T(8,128)(2,1)S(1)}, bf16[96,512]{1,0:T(8,128)(2,1)S(1)}, u32[]{:S(2)}, u32[]{:S(2)}) collective-permute-start(bf16[96,512]{1,0:T(8,128)(2,1)S(1)} %pad_maximum_fusion.2), channel_id=1, source_target_pairs={{0,4},{4,0},{8,12},{12,8},{1,5},{5,1},{9,13},{13,9},{2,6},{6,2},{1... | collective-permute-start | bytes 294920 | tf_op jit(solution)/shard_map/ppermute | solution.py:281
  77.5 5.4 %collective-permute-start.19 = (bf16[160,512]{1,0:T(8,128)(2,1)S(1)}, bf16[160,512]{1,0:T(8,128)(2,1)S(1)}, u32[]{:S(2)}, u32[]{:S(2)}) collective-permute-start(bf16[160,512]{1,0:T(8,128)(2,1)S(1)} %pad_maximum_fusion.1), channel_id=1, source_target_pairs={{0,2},{1,3},{2,0},{3,1},{4,6},{5,7},{6,4},{7,5},{8,10},{9,11},{10,... | collective-permute-start | bytes 491528 | tf_op jit(solution)/shard_map/ppermute | solution.py:281
  83.0 1.7 %collective-permute-start.20 = (bf16[320,512]{1,0:T(8,128)(2,1)S(1)}, bf16[320,512]{1,0:T(8,128)(2,1)S(1)}, u32[]{:S(2)}, u32[]{:S(2)}) collective-permute-start(bf16[320,512]{1,0:T(8,128)(2,1)S(1)} %pad_maximum_fusion), channel_id=1, source_target_pairs={{0,1},{1,0},{2,3},{3,2},{4,5},{5,4},{6,7},{7,6},{8,9},{9,8},{10,11... | collective-permute-start | bytes 983048 | tf_op jit(solution)/shard_map/ppermute | solution.py:281

commit v9 on v8

--- a/solution.py
+++ b/solution.py
@@ -116,6 +116,15 @@
         column = jnp.broadcast_to(row, (8, row.shape[1])).T[:, :1]
         parts.append(column[per_owner : 2 * per_owner] if kept else column[:per_owner])
     return jnp.concatenate(parts, axis=0)
+
+
+def hot_edges(lists, me, kept, per_owner, edge_dev):
+    first = per_owner if kept else 0
+    row = jnp.concatenate(
+        [ref[pl.ds(me, 1), :][:, first : first + per_owner] for ref in lists], axis=1
+    )
+    edges = lax.broadcasted_iota(jnp.int32, (edge_dev, row.shape[1]), 0)
+    return jnp.where(edges == row, 1.0, 0.0).astype(BF16)
 
 
 def hot_rows(column, edge_dev):
@@ -188,7 +197,7 @@
     arrive = loads([w_out, edges, upstream], [w_out_v, edges_v, upstream_v], sems)
     home = gathered(pieces)
     rows = edges.shape[0]
-    hot_t = hot_rows(columns_of(lists, me[0], True, pieces[0].shape[0]), rows).T
+    hot_t = hot_edges(lists, me[0], True, pieces[0].shape[0], rows)
     turns = rows // step
     spans = [pl.ds(i * step, step) for i in range(turns)]
     leave = [
@@ -253,7 +262,7 @@
     arrive = loads([upstream], [upstream_v], sems)
     back = gathered(pieces)
     rows = upstream.shape[0]
-    hot_t = hot_rows(columns_of(lists, me[0], False, pieces[0].shape[0]), rows).T
+    hot_t = hot_edges(lists, me[0], False, pieces[0].shape[0], rows)
     waited(arrive)
     leave = []
     for i in range(rows // step):

time: 86.8 us -> 86.6 us (level)
  transfers between devices with their start and end apart: 22 -> 22, of which waited for: 13 -> 13; matrix products, arithmetic and copies ran while one was open for 0% -> 0% of each run, Pallas kernels for 21% -> 20%
where the time goes in v9:
time: 86.6 us; the launch traced here: 86.3 us
  starting transfers between devices  34.1 us (39%)
  Pallas kernels  26.9 us (31%)
  waiting for transfers between devices  23.2 us (27%)
  between operations  1.6 us (2%)
    pallas_call x10, Pallas kernels, call(): pl.pallas_call(inner if order else body, out_shape=tuple(outs), in_specs=...  26.9 us
    ppermute x15, starting transfers between devices, shift(): lax.ppermute(value, axis, [(k, (k + by) % count) for k in range(count)])  20.7 us
    ppermute x6, waiting for transfers between devices, swap(): lax.ppermute(value, axis, [(k, k ^ mask) for k in range(lax.axis_size(axi...  13.8 us
    ppermute x15, waiting for transfers between devices, shift(): lax.ppermute(value, axis, [(k, (k + by) % count) for k in range(count)])  8.37 us
    ppermute x6, starting transfers between devices, swap(): lax.ppermute(value, axis, [(k, k ^ mask) for k in range(lax.axis_size(axi...  7.39 us
    all_to_all x1, starting transfers between devices, per_device(): lax.all_to_all(sent, ('graph', 'dp'), split_axis=0, concat_axis=0, tiled=...  6 us
  transfers between devices with their start and end apart: 22, of which 13 were waited for; matrix products, arithmetic and copies ran while one was open for 0% of the time, Pallas kernels for 20%

profile of v9, /device:TPU:0, one launch (start us, length us, event | category | flops | bytes accessed | tf_op | source)
XLA Modules:
  0.0 86.3 jit_solution(10043786137714335610)
XLA Ops:
  1.4 5.1 %collective-permute-start.2 = (s32[4,128]{1,0:T(4,128)S(1)}, s32[4,128]{1,0:T(4,128)S(1)}, u32[]{:S(2)}, u32[]{:S(2)}) collective-permute-start(s32[4,128]{1,0:T(4,128)S(1)} %shard_map.129.refs_1_.refs_0_), channel_id=1, source_target_pairs={{0,12},{4,0},{8,4},{12,8},{1,13},{5,1},{9,5},{13,9},{2,14},{6,2},{... | collective-permute-start | bytes 6152 | tf_op jit(solution)/shard_map/ppermute | solution.py:295
  6.5 1.0 %collective-permute-start = (s32[4,128]{1,0:T(4,128)S(1)}, s32[4,128]{1,0:T(4,128)S(1)}, u32[]{:S(2)}, u32[]{:S(2)}) collective-permute-start(s32[4,128]{1,0:T(4,128)S(1)} %shard_map.129.refs_1_.refs_0_), channel_id=1, source_target_pairs={{0,4},{4,8},{8,12},{12,0},{1,5},{5,9},{9,13},{13,1},{2,6},{6,10},{... | collective-permute-start | bytes 6152 | tf_op jit(solution)/shard_map/ppermute | solution.py:295
  7.6 1.2 %shard_map.130.refs_4_ = bf16[1024,512]{1,0:T(8,128)(2,1)S(1)} custom-call(bf16[1024,512]{1,0:T(8,128)(2,1)} %bitcast.21, s32[4,128]{1,0:T(4,128)S(1)} %shard_map.129.refs_1_.refs_0_), custom_call_target="tpu_custom_call" | custom-call | flops 1073741824 | bytes 2099200 | tf_op jit(solution)/shard_map/pallas_call | solution.py:49
  8.9 2.1 %collective-permute-done.1.refs_2_.refs_3_ = s32[4,128]{1,0:T(4,128)S(1)} collective-permute-done((s32[4,128]{1,0:T(4,128)S(1)}, s32[4,128]{1,0:T(4,128)S(1)}, u32[]{:S(2)}, u32[]{:S(2)}) %collective-permute-start.1) | collective-permute-done | bytes 2080 | tf_op jit(solution)/shard_map/ppermute | solution.py:295
  11.9 1.2 %shard_map.131 = (bf16[64,512]{1,0:T(8,128)(2,1)S(1)}, bf16[64,512]{1,0:T(8,128)(2,1)S(1)}, bf16[64,512]{1,0:T(8,128)(2,1)S(1)}, bf16[64,512]{1,0:T(8,128)(2,1)S(1)}) custom-call(s32[2]{0:T(128)S(1)} %pad_add_fusion.me.refs_0_.low, s32[4,128]{1,0:T(4,128)S(1)} %shard_map.129.refs_1_.refs_0_, s32[4,128]{1,0:T(4,128)S(1)} %collective-permute-done.refs_1_.refs_2_, ...), custom_call_target="tpu_custom_call" | custom-call | flops 268435456 | bytes 1318920 | tf_op jit(solution)/shard_map/pallas_call | solution.py:49
  14.3 1.9 %collective-permute-start.5 = (bf16[64,512]{1,0:T(8,128)(2,1)S(1)}, bf16[64,512]{1,0:T(8,128)(2,1)S(1)}, u32[]{:S(2)}, u32[]{:S(2)}) collective-permute-start(bf16[64,512]{1,0:T(8,128)(2,1)S(1)} %get-tuple-element.40), channel_id=1, source_target_pairs={{0,4},{4,8},{8,12},{12,0},{1,5},{5,9},{9,13},{13,1},{2,6},{6,10},{... | collective-permute-start | bytes 196616 | tf_op jit(solution)/shard_map/ppermute | solution.py:295
  17.0 2.9 %shard_map.132 = (bf16[256,256]{1,0:T(8,128)(2,1)S(1)}, f32[256,512]{1,0:T(8,128)S(1)}) custom-call(s32[2]{0:T(128)S(1)} %pad_add_fusion.me.refs_0_.low, s32[4,128]{1,0:T(4,128)S(1)} %shard_map.129.refs_1_.refs_0_, s32[4,128]{1,0:T(4,128)S(1)} %collective-permute-done.refs_1_.refs_2_, s32[4,128]{1,0:T(4,128)S(1)} %collective-permute-done.1.refs_2_.refs_3_, ...), custom_call_target="tpu_custom_call" | custom-call | flops 536870912 | bytes 2301960 | tf_op jit(solution)/shard_map/pallas_call | solution.py:49
  20.6 5.3 %shard_map.133 = (bf16[64,512]{1,0:T(8,128)(2,1)S(1)}, bf16[64,512]{1,0:T(8,128)(2,1)S(1)}, bf16[64,512]{1,0:T(8,128)(2,1)S(1)}, bf16[64,512]{1,0:T(8,128)(2,1)S(1)}) custom-call(s32[2]{0:T(128)S(1)} %pad_add_fusion.me.refs_0_.low, s32[1,1]{1,0:T(1,128)S(6)} %copy.14.refs_1_, bf16[64,512]{1,0:T(8,128)(2,1)S(1)} %get-tuple-element.37.refs_7_.refs_2_, ...), custom_call_target="tpu_custom_call" | custom-call | flops 2684354560 | bytes 1867788 | tf_op jit(solution)/shard_map/pallas_call | solution.py:49
  26.2 2.0 %collective-permute-start.7 = (bf16[64,512]{1,0:T(8,128)(2,1)S(1)}, bf16[64,512]{1,0:T(8,128)(2,1)S(1)}, u32[]{:S(2)}, u32[]{:S(2)}) collective-permute-start(bf16[64,512]{1,0:T(8,128)(2,1)S(1)} %get-tuple-element.44), channel_id=1, source_target_pairs={{0,8},{4,12},{8,0},{12,4},{1,9},{5,13},{9,1},{13,5},{2,10},{6,14},... | collective-permute-start | bytes 196616 | tf_op jit(solution)/shard_map/ppermute | solution.py:295
  28.2 1.8 %collective-permute-start.8 = (bf16[64,512]{1,0:T(8,128)(2,1)S(1)}, bf16[64,512]{1,0:T(8,128)(2,1)S(1)}, u32[]{:S(2)}, u32[]{:S(2)}) collective-permute-start(bf16[64,512]{1,0:T(8,128)(2,1)S(1)} %get-tuple-element.45), channel_id=1, source_target_pairs={{0,12},{4,0},{8,4},{12,8},{1,13},{5,1},{9,5},{13,9},{2,14},{6,2},{... | collective-permute-start | bytes 196616 | tf_op jit(solution)/shard_map/ppermute | solution.py:295
  30.0 2.1 %collective-permute-done.6.refs_1_.refs_6_ = bf16[64,512]{1,0:T(8,128)(2,1)S(1)} collective-permute-done((bf16[64,512]{1,0:T(8,128)(2,1)S(1)}, bf16[64,512]{1,0:T(8,128)(2,1)S(1)}, u32[]{:S(2)}, u32[]{:S(2)}) %collective-permute-start.6) | collective-permute-done | bytes 65568 | tf_op jit(solution)/shard_map/ppermute | solution.py:295
  32.1 1.2 %collective-permute-done.8.refs_3_.refs_8_ = bf16[64,512]{1,0:T(8,128)(2,1)S(1)} collective-permute-done((bf16[64,512]{1,0:T(8,128)(2,1)S(1)}, bf16[64,512]{1,0:T(8,128)(2,1)S(1)}, u32[]{:S(2)}, u32[]{:S(2)}) %collective-permute-start.8) | collective-permute-done | bytes 65568 | tf_op jit(solution)/shard_map/ppermute | solution.py:295
  33.7 2.8 %collective-permute-start.9 = (bf16[64,512]{1,0:T(8,128)(2,1)S(1)}, bf16[64,512]{1,0:T(8,128)(2,1)S(1)}, u32[]{:S(2)}, u32[]{:S(2)}) collective-permute-start(bf16[64,512]{1,0:T(8,128)(2,1)S(1)} %get-tuple-element.50), channel_id=1, source_target_pairs={{0,12},{4,0},{8,4},{12,8},{1,13},{5,1},{9,5},{13,9},{2,14},{6,2},{... | collective-permute-start | bytes 196616 | tf_op jit(solution)/shard_map/ppermute | solution.py:295
  37.1 3.6 %shard_map.135 = (bf16[1024,512]{1,0:T(8,128)(2,1)}, bf16[16,32,512]{2,1,0:T(8,128)(2,1)}) custom-call(s32[2]{0:T(128)S(1)} %pad_add_fusion.me.refs_0_.low, s32[4,128]{1,0:T(4,128)S(1)} %shard_map.129.refs_1_.refs_0_, s32[4,128]{1,0:T(4,128)S(1)} %collective-permute-done.refs_1_.refs_2_, s32[4,128]{1,0:T(4,128)S(1)} %collective-permute-done.1.refs_2_.refs_3_, ...), custom_call_target="tpu_custom_call" | custom-call | flops 1342177280 | bytes 4530184 | tf_op jit(solution)/shard_map/pallas_call | solution.py:49
  40.8 6.0 %all-to-all-start = ((bf16[16,32,512]{2,1,0:T(8,128)(2,1)}), bf16[16,32,512]{2,1,0:T(8,128)(2,1)S(1)}, u32[]{:S(2)}, u32[]{:S(2)}) async-start(bf16[16,32,512]{2,1,0:T(8,128)(2,1)} %get-tuple-element.49.refs_14_), calls=%async_computation | async-start | bytes 1048576 | tf_op jit(solution)/shard_map/all_to_all | solution.py:437
  46.8 7.8 %shard_map.136 = (f32[64,512]{1,0:T(8,128)S(1)}, bf16[64,512]{1,0:T(8,128)(2,1)S(1)}, bf16[64,512]{1,0:T(8,128)(2,1)S(1)}, bf16[64,512]{1,0:T(8,128)(2,1)S(1)}, ...) custom-call(s32[2]{0:T(128)S(1)} %pad_add_fusion.me.refs_0_.low, s32[1,1]{1,0:T(1,128)S(6)} %copy.14.refs_1_, ...), custom_call_target="tpu_custom_call" | custom-call | flops 4294967296 | bytes 2719756 | tf_op jit(solution)/shard_map/pallas_call | solution.py:49
  55.1 0.9 %collective-permute-done.12 = bf16[64,512]{1,0:T(8,128)(2,1)S(1)} collective-permute-done((bf16[64,512]{1,0:T(8,128)(2,1)S(1)}, bf16[64,512]{1,0:T(8,128)(2,1)S(1)}, u32[]{:S(2)}, u32[]{:S(2)}) %collective-permute-start.12) | collective-permute-done | bytes 65568 | tf_op jit(solution)/shard_map/ppermute | solution.py:290
  56.1 1.9 %collective-permute-start.13 = (bf16[32,512]{1,0:T(8,128)(2,1)S(1)}, bf16[32,512]{1,0:T(8,128)(2,1)S(1)}, u32[]{:S(2)}, u32[]{:S(2)}) collective-permute-start(bf16[32,512]{1,0:T(8,128)(2,1)S(1)} %fusion.2), channel_id=1, source_target_pairs={{0,2},{1,3},{2,0},{3,1},{4,6},{5,7},{6,4},{7,5},{8,10},{9,11},{10,... | collective-permute-start | bytes 98312 | tf_op jit(solution)/shard_map/ppermute | solution.py:290
  58.0 2.2 %collective-permute-done.13 = bf16[32,512]{1,0:T(8,128)(2,1)S(1)} collective-permute-done((bf16[32,512]{1,0:T(8,128)(2,1)S(1)}, bf16[32,512]{1,0:T(8,128)(2,1)S(1)}, u32[]{:S(2)}, u32[]{:S(2)}) %collective-permute-start.13) | collective-permute-done | bytes 32800 | tf_op jit(solution)/shard_map/ppermute | solution.py:290
  60.2 1.0 %all-to-all-done = bf16[16,32,512]{2,1,0:T(8,128)(2,1)S(1)} async-done(((bf16[16,32,512]{2,1,0:T(8,128)(2,1)}), bf16[16,32,512]{2,1,0:T(8,128)(2,1)S(1)}, u32[]{:S(2)}, u32[]{:S(2)}) %all-to-all-start) | async-done | bytes 524320 | tf_op jit(solution)/shard_map/all_to_all | solution.py:437
  61.3 2.3 %collective-permute-start.14 = (bf16[64,512]{1,0:T(8,128)(2,1)S(1)}, bf16[64,512]{1,0:T(8,128)(2,1)S(1)}, u32[]{:S(2)}, u32[]{:S(2)}) collective-permute-start(bf16[64,512]{1,0:T(8,128)(2,1)S(1)} %pad_maximum_fusion.4), channel_id=1, source_target_pairs={{0,8},{4,12},{8,0},{12,4},{1,9},{5,13},{9,1},{13,5},{2,10},{6,14},... | collective-permute-start | bytes 196616 | tf_op jit(solution)/shard_map/ppermute | solution.py:290
  64.5 1.0 %collective-permute-start.16 = (bf16[64,512]{1,0:T(8,128)(2,1)S(1)}, bf16[64,512]{1,0:T(8,128)(2,1)S(1)}, u32[]{:S(2)}, u32[]{:S(2)}) collective-permute-start(bf16[64,512]{1,0:T(8,128)(2,1)S(1)} %get-tuple-element.57), channel_id=1, source_target_pairs={{0,8},{4,12},{8,0},{12,4},{1,9},{5,13},{9,1},{13,5},{2,10},{6,14},... | collective-permute-start | bytes 196616 | tf_op jit(solution)/shard_map/ppermute | solution.py:295
  65.4 2.0 %collective-permute-start.17 = (bf16[64,512]{1,0:T(8,128)(2,1)S(1)}, bf16[64,512]{1,0:T(8,128)(2,1)S(1)}, u32[]{:S(2)}, u32[]{:S(2)}) collective-permute-start(bf16[64,512]{1,0:T(8,128)(2,1)S(1)} %get-tuple-element.58), channel_id=1, source_target_pairs={{0,12},{4,0},{8,4},{12,8},{1,13},{5,1},{9,5},{13,9},{2,14},{6,2},{... | collective-permute-start | bytes 196616 | tf_op jit(solution)/shard_map/ppermute | solution.py:295
  67.5 3.7 %collective-permute-done.14 = bf16[64,512]{1,0:T(8,128)(2,1)S(1)} collective-permute-done((bf16[64,512]{1,0:T(8,128)(2,1)S(1)}, bf16[64,512]{1,0:T(8,128)(2,1)S(1)}, u32[]{:S(2)}, u32[]{:S(2)}) %collective-permute-start.14) | collective-permute-done | bytes 65568 | tf_op jit(solution)/shard_map/ppermute | solution.py:290
  71.2 1.3 %collective-permute-done.16.refs_6_ = bf16[64,512]{1,0:T(8,128)(2,1)S(1)} collective-permute-done((bf16[64,512]{1,0:T(8,128)(2,1)S(1)}, bf16[64,512]{1,0:T(8,128)(2,1)S(1)}, u32[]{:S(2)}, u32[]{:S(2)}) %collective-permute-start.16) | collective-permute-done | bytes 65568 | tf_op jit(solution)/shard_map/ppermute | solution.py:295
  72.6 1.6 %collective-permute-start.18 = (bf16[96,512]{1,0:T(8,128)(2,1)S(1)}, bf16[96,512]{1,0:T(8,128)(2,1)S(1)}, u32[]{:S(2)}, u32[]{:S(2)}) collective-permute-start(bf16[96,512]{1,0:T(8,128)(2,1)S(1)} %pad_maximum_fusion.2), channel_id=1, source_target_pairs={{0,4},{4,0},{8,12},{12,8},{1,5},{5,1},{9,13},{13,9},{2,6},{6,2},{1... | collective-permute-start | bytes 294920 | tf_op jit(solution)/shard_map/ppermute | solution.py:290
  74.2 2.0 %shard_map.137 = bf16[1024,512]{1,0:T(8,128)(2,1)} custom-call(s32[2]{0:T(128)S(1)} %pad_add_fusion.me.refs_0_.low, s32[4,128]{1,0:T(4,128)S(1)} %shard_map.129.refs_1_.refs_0_, s32[4,128]{1,0:T(4,128)S(1)} %collective-permute-done.refs_1_.refs_2_, s32[4,128]{1,0:T(4,128)S(1)} %collective-permute-done.1.refs_2_.refs_3_, ...), custom_call_target="tpu_custom_call" | custom-call | flops 268435456 | bytes 2367496 | tf_op jit(solution)/shard_map/pallas_call | solution.py:49
  76.3 1.0 %collective-permute-done.18 = bf16[96,512]{1,0:T(8,128)(2,1)S(1)} collective-permute-done((bf16[96,512]{1,0:T(8,128)(2,1)S(1)}, bf16[96,512]{1,0:T(8,128)(2,1)S(1)}, u32[]{:S(2)}, u32[]{:S(2)}) %collective-permute-start.18) | collective-permute-done | bytes 98336 | tf_op jit(solution)/shard_map/ppermute | solution.py:290
  77.3 0.9 %collective-permute-start.19 = (bf16[160,512]{1,0:T(8,128)(2,1)S(1)}, bf16[160,512]{1,0:T(8,128)(2,1)S(1)}, u32[]{:S(2)}, u32[]{:S(2)}) collective-permute-start(bf16[160,512]{1,0:T(8,128)(2,1)S(1)} %pad_maximum_fusion.1), channel_id=1, source_target_pairs={{0,2},{1,3},{2,0},{3,1},{4,6},{5,7},{6,4},{7,5},{8,10},{9,11},{10,... | collective-permute-start | bytes 491528 | tf_op jit(solution)/shard_map/ppermute | solution.py:290
  78.3 4.4 %collective-permute-done.19 = bf16[160,512]{1,0:T(8,128)(2,1)S(1)} collective-permute-done((bf16[160,512]{1,0:T(8,128)(2,1)S(1)}, bf16[160,512]{1,0:T(8,128)(2,1)S(1)}, u32[]{:S(2)}, u32[]{:S(2)}) %collective-permute-start.19) | collective-permute-done | bytes 163872 | tf_op jit(solution)/shard_map/ppermute | solution.py:290
  82.9 1.6 %collective-permute-done.20 = bf16[320,512]{1,0:T(8,128)(2,1)S(1)} collective-permute-done((bf16[320,512]{1,0:T(8,128)(2,1)S(1)}, bf16[320,512]{1,0:T(8,128)(2,1)S(1)}, u32[]{:S(2)}, u32[]{:S(2)}) %collective-permute-start.20) | collective-permute-done | bytes 327712 | tf_op jit(solution)/shard_map/ppermute | solution.py:290
  84.6 1.7 %shard_map.138 = (f32[512,512]{1,0:T(8,128)}, f32[128,512]{1,0:T(8,128)}) custom-call(s32[2]{0:T(128)S(1)} %pad_add_fusion.me.refs_0_.low, bf16[256,512]{1,0:T(8,128)(2,1)S(1)} %maximum_select_fusion.out, bf16[256,512]{1,0:T(8,128)(2,1)S(1)} %slice.38.out_got, bf16[64,512]{1,0:T(8,128)(2,1)S(1)} %maximum_select_fusion.2.basis, ...), custom_call_target="tpu_custom_call" | custom-call | bytes 1966088 | tf_op jit(solution)/shard_map/pallas_call | solution.py:49
  (55 shorter events, 6.8 us)
Async XLA Ops:
  1.4 7.4 %collective-permute-start.2 = (s32[4,128]{1,0:T(4,128)S(1)}, s32[4,128]{1,0:T(4,128)S(1)}, u32[]{:S(2)}, u32[]{:S(2)}) collective-permute-start(s32[4,128]{1,0:T(4,128)S(1)} %shard_map.129.refs_1_.refs_0_), channel_id=1, source_target_pairs={{0,12},{4,0},{8,4},{12,8},{1,13},{5,1},{9,5},{13,9},{2,14},{6,2},{... | collective-permute-start | bytes 6152 | tf_op jit(solution)/shard_map/ppermute | solution.py:295
  6.5 4.5 %collective-permute-start.1 = (s32[4,128]{1,0:T(4,128)S(1)}, s32[4,128]{1,0:T(4,128)S(1)}, u32[]{:S(2)}, u32[]{:S(2)}) collective-permute-start(s32[4,128]{1,0:T(4,128)S(1)} %shard_map.129.refs_1_.refs_0_), channel_id=1, source_target_pairs={{0,8},{4,12},{8,0},{12,4},{1,9},{5,13},{9,1},{13,5},{2,10},{6,14},... | collective-permute-start | bytes 6152 | tf_op jit(solution)/shard_map/ppermute | solution.py:295
  6.5 5.4 %collective-permute-start = (s32[4,128]{1,0:T(4,128)S(1)}, s32[4,128]{1,0:T(4,128)S(1)}, u32[]{:S(2)}, u32[]{:S(2)}) collective-permute-start(s32[4,128]{1,0:T(4,128)S(1)} %shard_map.129.refs_1_.refs_0_), channel_id=1, source_target_pairs={{0,4},{4,8},{8,12},{12,0},{1,5},{5,9},{9,13},{13,1},{2,6},{6,10},{... | collective-permute-start | bytes 6152 | tf_op jit(solution)/shard_map/ppermute | solution.py:295
  13.1 6.8 %collective-permute-start.3 = (bf16[64,512]{1,0:T(8,128)(2,1)S(1)}, bf16[64,512]{1,0:T(8,128)(2,1)S(1)}, u32[]{:S(2)}, u32[]{:S(2)}) collective-permute-start(bf16[64,512]{1,0:T(8,128)(2,1)S(1)} %get-tuple-element.38), channel_id=1, source_target_pairs={{0,12},{4,0},{8,4},{12,8},{1,13},{5,1},{9,5},{13,9},{2,14},{6,2},{... | collective-permute-start | bytes 196616 | tf_op jit(solution)/shard_map/ppermute | solution.py:295
  13.7 6.2 %collective-permute-start.4 = (bf16[64,512]{1,0:T(8,128)(2,1)S(1)}, bf16[64,512]{1,0:T(8,128)(2,1)S(1)}, u32[]{:S(2)}, u32[]{:S(2)}) collective-permute-start(bf16[64,512]{1,0:T(8,128)(2,1)S(1)} %get-tuple-element.39), channel_id=1, source_target_pairs={{0,8},{4,12},{8,0},{12,4},{1,9},{5,13},{9,1},{13,5},{2,10},{6,14},... | collective-permute-start | bytes 196616 | tf_op jit(solution)/shard_map/ppermute | solution.py:295
  14.3 6.2 %collective-permute-start.5 = (bf16[64,512]{1,0:T(8,128)(2,1)S(1)}, bf16[64,512]{1,0:T(8,128)(2,1)S(1)}, u32[]{:S(2)}, u32[]{:S(2)}) collective-permute-start(bf16[64,512]{1,0:T(8,128)(2,1)S(1)} %get-tuple-element.40), channel_id=1, source_target_pairs={{0,4},{4,8},{8,12},{12,0},{1,5},{5,9},{9,13},{13,1},{2,6},{6,10},{... | collective-permute-start | bytes 196616 | tf_op jit(solution)/shard_map/ppermute | solution.py:295
  16.9 3.6 %copy-start.3 = (bf16[128,512]{1,0:T(8,128)(2,1)S(1)}, bf16[128,512]{1,0:T(8,128)(2,1)}, u32[]{:S(2)}) copy-start(bf16[128,512]{1,0:T(8,128)(2,1)} %refs_12_.1) | copy-start | bytes 393220
  17.0 3.6 %copy-start.4 = (s32[1,32,128]{2,1,0:T(8,128)S(1)}, s32[1,32,128]{2,1,0:T(8,128)}, u32[]{:S(2)}) copy-start(s32[1,32,128]{2,1,0:T(8,128)} %param.14) | copy-start | bytes 49156
  17.0 3.6 %copy-start.5 = (s32[1,32,128]{2,1,0:T(8,128)S(1)}, s32[1,32,128]{2,1,0:T(8,128)}, u32[]{:S(2)}) copy-start(s32[1,32,128]{2,1,0:T(8,128)} %param.15) | copy-start | bytes 49156
  20.5 16.6 %copy-start = (bf16[1,1024,512]{2,1,0:T(8,128)(2,1)S(1)}, bf16[1,1024,512]{2,1,0:T(8,128)(2,1)}, u32[]{:S(2)}) copy-start(bf16[1,1024,512]{2,1,0:T(8,128)(2,1)} %param.11) | copy-start | bytes 3145732
  20.6 16.6 %copy-start.1 = (bf16[1,1024,512]{2,1,0:T(8,128)(2,1)S(1)}, bf16[1,1024,512]{2,1,0:T(8,128)(2,1)}, u32[]{:S(2)}) copy-start(bf16[1,1024,512]{2,1,0:T(8,128)(2,1)} %param.10) | copy-start | bytes 3145732
  25.9 11.3 %copy-start.2 = (bf16[512,512]{1,0:T(8,128)(2,1)S(1)}, bf16[512,512]{1,0:T(8,128)(2,1)}, u32[]{:S(2)}) copy-start(bf16[512,512]{1,0:T(8,128)(2,1)} %refs_11_.1) | copy-start | bytes 1572868
  25.9 6.2 %collective-permute-start.6 = (bf16[64,512]{1,0:T(8,128)(2,1)S(1)}, bf16[64,512]{1,0:T(8,128)(2,1)S(1)}, u32[]{:S(2)}, u32[]{:S(2)}) collective-permute-start(bf16[64,512]{1,0:T(8,128)(2,1)S(1)} %get-tuple-element.43), channel_id=1, source_target_pairs={{0,4},{4,8},{8,12},{12,0},{1,5},{5,9},{9,13},{13,1},{2,6},{6,10},{... | collective-permute-start | bytes 196616 | tf_op jit(solution)/shard_map/ppermute | solution.py:295
  26.2 5.9 %collective-permute-start.7 = (bf16[64,512]{1,0:T(8,128)(2,1)S(1)}, bf16[64,512]{1,0:T(8,128)(2,1)S(1)}, u32[]{:S(2)}, u32[]{:S(2)}) collective-permute-start(bf16[64,512]{1,0:T(8,128)(2,1)S(1)} %get-tuple-element.44), channel_id=1, source_target_pairs={{0,8},{4,12},{8,0},{12,4},{1,9},{5,13},{9,1},{13,5},{2,10},{6,14},... | collective-permute-start | bytes 196616 | tf_op jit(solution)/shard_map/ppermute | solution.py:295
  28.2 5.1 %collective-permute-start.8 = (bf16[64,512]{1,0:T(8,128)(2,1)S(1)}, bf16[64,512]{1,0:T(8,128)(2,1)S(1)}, u32[]{:S(2)}, u32[]{:S(2)}) collective-permute-start(bf16[64,512]{1,0:T(8,128)(2,1)S(1)} %get-tuple-element.45), channel_id=1, source_target_pairs={{0,12},{4,0},{8,4},{12,8},{1,13},{5,1},{9,5},{13,9},{2,14},{6,2},{... | collective-permute-start | bytes 196616 | tf_op jit(solution)/shard_map/ppermute | solution.py:295
  33.7 13.1 %collective-permute-start.9 = (bf16[64,512]{1,0:T(8,128)(2,1)S(1)}, bf16[64,512]{1,0:T(8,128)(2,1)S(1)}, u32[]{:S(2)}, u32[]{:S(2)}) collective-permute-start(bf16[64,512]{1,0:T(8,128)(2,1)S(1)} %get-tuple-element.50), channel_id=1, source_target_pairs={{0,12},{4,0},{8,4},{12,8},{1,13},{5,1},{9,5},{13,9},{2,14},{6,2},{... | collective-permute-start | bytes 196616 | tf_op jit(solution)/shard_map/ppermute | solution.py:295
  36.5 10.3 %collective-permute-start.10 = (bf16[64,512]{1,0:T(8,128)(2,1)S(1)}, bf16[64,512]{1,0:T(8,128)(2,1)S(1)}, u32[]{:S(2)}, u32[]{:S(2)}) collective-permute-start(bf16[64,512]{1,0:T(8,128)(2,1)S(1)} %get-tuple-element.51), channel_id=1, source_target_pairs={{0,8},{4,12},{8,0},{12,4},{1,9},{5,13},{9,1},{13,5},{2,10},{6,14},... | collective-permute-start | bytes 196616 | tf_op jit(solution)/shard_map/ppermute | solution.py:295
  37.0 9.8 %collective-permute-start.11 = (bf16[64,512]{1,0:T(8,128)(2,1)S(1)}, bf16[64,512]{1,0:T(8,128)(2,1)S(1)}, u32[]{:S(2)}, u32[]{:S(2)}) collective-permute-start(bf16[64,512]{1,0:T(8,128)(2,1)S(1)} %get-tuple-element.52), channel_id=1, source_target_pairs={{0,4},{4,8},{8,12},{12,0},{1,5},{5,9},{9,13},{13,1},{2,6},{6,10},{... | collective-permute-start | bytes 196616 | tf_op jit(solution)/shard_map/ppermute | solution.py:295
  40.8 20.5 %all-to-all-start = ((bf16[16,32,512]{2,1,0:T(8,128)(2,1)}), bf16[16,32,512]{2,1,0:T(8,128)(2,1)S(1)}, u32[]{:S(2)}, u32[]{:S(2)}) async-start(bf16[16,32,512]{2,1,0:T(8,128)(2,1)} %get-tuple-element.49.refs_14_), calls=%async_computation | async-start | bytes 1048576 | tf_op jit(solution)/shard_map/all_to_all | solution.py:437
  54.7 1.4 %collective-permute-start.12 = (bf16[64,512]{1,0:T(8,128)(2,1)S(1)}, bf16[64,512]{1,0:T(8,128)(2,1)S(1)}, u32[]{:S(2)}, u32[]{:S(2)}) collective-permute-start(bf16[64,512]{1,0:T(8,128)(2,1)S(1)} %get-tuple-element.54), channel_id=1, source_target_pairs={{0,1},{1,0},{2,3},{3,2},{4,5},{5,4},{6,7},{7,6},{8,9},{9,8},{10,11... | collective-permute-start | bytes 196616 | tf_op jit(solution)/shard_map/ppermute | solution.py:290
  56.1 4.2 %collective-permute-start.13 = (bf16[32,512]{1,0:T(8,128)(2,1)S(1)}, bf16[32,512]{1,0:T(8,128)(2,1)S(1)}, u32[]{:S(2)}, u32[]{:S(2)}) collective-permute-start(bf16[32,512]{1,0:T(8,128)(2,1)S(1)} %fusion.2), channel_id=1, source_target_pairs={{0,2},{1,3},{2,0},{3,1},{4,6},{5,7},{6,4},{7,5},{8,10},{9,11},{10,... | collective-permute-start | bytes 98312 | tf_op jit(solution)/shard_map/ppermute | solution.py:290
  61.3 9.8 %collective-permute-start.14 = (bf16[64,512]{1,0:T(8,128)(2,1)S(1)}, bf16[64,512]{1,0:T(8,128)(2,1)S(1)}, u32[]{:S(2)}, u32[]{:S(2)}) collective-permute-start(bf16[64,512]{1,0:T(8,128)(2,1)S(1)} %pad_maximum_fusion.4), channel_id=1, source_target_pairs={{0,8},{4,12},{8,0},{12,4},{1,9},{5,13},{9,1},{13,5},{2,10},{6,14},... | collective-permute-start | bytes 196616 | tf_op jit(solution)/shard_map/ppermute | solution.py:290
  63.6 7.6 %collective-permute-start.15 = (bf16[64,512]{1,0:T(8,128)(2,1)S(1)}, bf16[64,512]{1,0:T(8,128)(2,1)S(1)}, u32[]{:S(2)}, u32[]{:S(2)}) collective-permute-start(bf16[64,512]{1,0:T(8,128)(2,1)S(1)} %get-tuple-element.56), channel_id=1, source_target_pairs={{0,4},{4,8},{8,12},{12,0},{1,5},{5,9},{9,13},{13,1},{2,6},{6,10},{... | collective-permute-start | bytes 196616 | tf_op jit(solution)/shard_map/ppermute | solution.py:295
  64.5 8.1 %collective-permute-start.16 = (bf16[64,512]{1,0:T(8,128)(2,1)S(1)}, bf16[64,512]{1,0:T(8,128)(2,1)S(1)}, u32[]{:S(2)}, u32[]{:S(2)}) collective-permute-start(bf16[64,512]{1,0:T(8,128)(2,1)S(1)} %get-tuple-element.57), channel_id=1, source_target_pairs={{0,8},{4,12},{8,0},{12,4},{1,9},{5,13},{9,1},{13,5},{2,10},{6,14},... | collective-permute-start | bytes 196616 | tf_op jit(solution)/shard_map/ppermute | solution.py:295
  65.4 7.1 %collective-permute-start.17 = (bf16[64,512]{1,0:T(8,128)(2,1)S(1)}, bf16[64,512]{1,0:T(8,128)(2,1)S(1)}, u32[]{:S(2)}, u32[]{:S(2)}) collective-permute-start(bf16[64,512]{1,0:T(8,128)(2,1)S(1)} %get-tuple-element.58), channel_id=1, source_target_pairs={{0,12},{4,0},{8,4},{12,8},{1,13},{5,1},{9,5},{13,9},{2,14},{6,2},{... | collective-permute-start | bytes 196616 | tf_op jit(solution)/shard_map/ppermute | solution.py:295
  72.6 4.7 %collective-permute-start.18 = (bf16[96,512]{1,0:T(8,128)(2,1)S(1)}, bf16[96,512]{1,0:T(8,128)(2,1)S(1)}, u32[]{:S(2)}, u32[]{:S(2)}) collective-permute-start(bf16[96,512]{1,0:T(8,128)(2,1)S(1)} %pad_maximum_fusion.2), channel_id=1, source_target_pairs={{0,4},{4,0},{8,12},{12,8},{1,5},{5,1},{9,13},{13,9},{2,6},{6,2},{1... | collective-permute-start | bytes 294920 | tf_op jit(solution)/shard_map/ppermute | solution.py:290
  77.3 5.4 %collective-permute-start.19 = (bf16[160,512]{1,0:T(8,128)(2,1)S(1)}, bf16[160,512]{1,0:T(8,128)(2,1)S(1)}, u32[]{:S(2)}, u32[]{:S(2)}) collective-permute-start(bf16[160,512]{1,0:T(8,128)(2,1)S(1)} %pad_maximum_fusion.1), channel_id=1, source_target_pairs={{0,2},{1,3},{2,0},{3,1},{4,6},{5,7},{6,4},{7,5},{8,10},{9,11},{10,... | collective-permute-start | bytes 491528 | tf_op jit(solution)/shard_map/ppermute | solution.py:290
  82.9 1.7 %collective-permute-start.20 = (bf16[320,512]{1,0:T(8,128)(2,1)S(1)}, bf16[320,512]{1,0:T(8,128)(2,1)S(1)}, u32[]{:S(2)}, u32[]{:S(2)}) collective-permute-start(bf16[320,512]{1,0:T(8,128)(2,1)S(1)} %pad_maximum_fusion), channel_id=1, source_target_pairs={{0,1},{1,0},{2,3},{3,2},{4,5},{5,4},{6,7},{7,6},{8,9},{9,8},{10,11... | collective-permute-start | bytes 983048 | tf_op jit(solution)/shard_map/ppermute | solution.py:290

commit v10 on v9

--- a/solution.py
+++ b/solution.py
@@ -229,10 +229,10 @@
 def backward_kernel(ranks, step, place, count, *refs):
     fetched, pieces = refs[:ranks], refs[ranks : 2 * ranks]
     src, dst, weight, basis, kept, away = refs[2 * ranks : 2 * ranks + 6]
-    outs = refs[2 * ranks + 6 : 3 * ranks + 6]
-    basis_v, message, dpre, hot, back_hot, total, sems = refs[3 * ranks + 6 :]
+    out = refs[2 * ranks + 6]
+    basis_v, message, dpre, hot, back_hot, total, sems = refs[2 * ranks + 7 :]
     arrive = loads([basis], [basis_v], sems)
-    per_owner = outs[0].shape[0]
+    per_owner = out.shape[1]
     slots, block = ranks * per_owner, src.shape[1]
     src_t = turned(src, per_owner, ranks, place[0])
     dst_t = turned(dst, per_owner, ranks, place[0])
@@ -253,16 +253,21 @@
     half = kept.shape[0]
     kept[...] = total[pl.ds(pl.multiple_of(place[1] * half, half), half), :]
     away[...] = total[pl.ds(pl.multiple_of((1 - place[1]) * half, half), half), :].astype(BF16)
-    scattered(dot(hot[...], message[...], NT).astype(BF16), outs)
+    result = dot(hot[...], message[...], NT).astype(BF16)
+    for s in range(ranks):
+        piece = result[s * per_owner : (s + 1) * per_owner]
+        out[(place[0] + s) % ranks] = piece
 
 
 def final_kernel(ranks, step, me, *refs):
-    lists, pieces = refs[:ranks], refs[ranks : 2 * ranks]
-    upstream, out, upstream_v, out_v, sems, out_sems = refs[2 * ranks :]
+    lists, pieces = refs[:ranks], refs[ranks]
+    upstream, out, upstream_v, out_v, sems, out_sems = refs[ranks + 1 :]
     arrive = loads([upstream], [upstream_v], sems)
-    back = gathered(pieces)
+    back = jnp.concatenate(
+        [pieces[(me[0] - s + ranks) % ranks] for s in range(ranks)], axis=0
+    )
     rows = upstream.shape[0]
-    hot_t = hot_edges(lists, me[0], False, pieces[0].shape[0], rows)
+    hot_t = hot_edges(lists, me[0], False, pieces.shape[1], rows)
     waited(arrive)
     leave = []
     for i in range(rows // step):
@@ -436,9 +441,10 @@
         sent = jnp.stack([split[block] for block in blocks_of])
     out_parts = lax.all_to_all(sent, ("graph", "dp"), split_axis=0, concat_axis=0, tiled=True)
     basis_half = basis_width // 2
-    basis_kept, basis_away, *dfetch = call(
+    basis_kept, basis_away, dfetch = call(
         functools.partial(backward_kernel, ranks, step),
-        [shape((basis_half, width), F32), shape((basis_half, width))] + pieces,
+        [shape((basis_half, width), F32), shape((basis_half, width))]
+        + [shape((ranks, per_owner, width))],
         [place, block_count] + fetched + dpartial + [src, dst, w_basis, basis],
         smem=(0, 1),
         far=(2 * ranks + 5,),
@@ -449,31 +455,29 @@
         vmem=36,
         pin=True,
     )
-    returned = exchange(dfetch, 1)
+    returned = lax.all_to_all(dfetch, "graph", split_axis=0, concat_axis=0, tiled=True)
     basis_part = joined(basis_kept, basis_away)
     for bit in bits_of("dp")[1:]:
         basis_part = halve(basis_part, "dp", bit)
     out_part = jnp.sum(out_parts.astype(F32), axis=0)
     out, total = out_part.astype(BF16), basis_part.astype(BF16)
     for bit in reversed(bits_of("graph")):
-        if bit == 0:
-            out, total, returned = lax.optimization_barrier((out, total, returned))
         got, out = doubled(out, total, "graph", bit)
         total = (total.astype(F32) + got.astype(F32)).astype(BF16)
     (grad_edge,) = call(
         functools.partial(final_kernel, ranks, 256),
         [shape((edge_dev, width))],
-        [place] + lists + returned + [upstream],
+        [place] + lists + [returned, upstream],
         smem=(0,),
-        far=(2 * ranks + 1,),
+        far=(ranks + 2,),
         far_out=(0,),
         flops=2 * slots * edge_dev * width,
         scratch=[held(upstream), held(upstream), dma((1,)), dma((edge_dev // 256,))],
     )
-    out, total, grad_edge = lax.optimization_barrier((out, total, grad_edge))
     for bit in reversed(bits_of("dp")[1:]):
         got, out = doubled(out, total, "dp", bit)
         total = double(total, got, "dp", bit)
+    out, total, grad_edge = lax.optimization_barrier((out, total, grad_edge))
     rows = total.shape[0]
     got = swap(jnp.concatenate([total, out]), "dp", 1)
     out_scale = 1.0 / math.sqrt(copies * ranks * edge_dev)

time: 86.6 us -> 86.3 us (level)
  starting transfers between devices: 34.1 us -> 33.2 us
    all_to_all x0 -> x1, waiting for transfers between devices: none -> 6 us  [per_device(): lax.all_to_all(dfetch, 'graph', split_axis=0, concat_axis=0, tiled=True)]
    all_to_all x0 -> x1, starting transfers between devices: none -> 4.04 us  [per_device(): lax.all_to_all(dfetch, 'graph', split_axis=0, concat_axis=0, tiled=True)]
    ppermute x15 -> x12, starting transfers between devices: 20.7 us -> 16.9 us  [shift(): lax.ppermute(value, axis, [(k, (k + by) % count) for k in range(count)])]
    ppermute x6, waiting for transfers between devices: 13.8 us -> 10.1 us  [swap(): lax.ppermute(value, axis, [(k, k ^ mask) for k in range(lax.axis_size(axi...]
    ppermute x15 -> x12, waiting for transfers between devices: 8.37 us -> 7.02 us  [shift(): lax.ppermute(value, axis, [(k, (k + by) % count) for k in range(count)])]
    ppermute x6, starting transfers between devices: 7.39 us -> 6.22 us  [swap(): lax.ppermute(value, axis, [(k, k ^ mask) for k in range(lax.axis_size(axi...]
    all_to_all x1, waiting for transfers between devices: 0.99 us -> 0.01 us  [per_device(): lax.all_to_all(sent, ('graph', 'dp'), split_axis=0, concat_axis=0, tiled=...]
  transfers between devices with their start and end apart: 22 -> 20, of which waited for: 13 -> 11; matrix products, arithmetic and copies ran while one was open for 0% -> 0% of each run, Pallas kernels for 20% -> 21%
where the time goes in v10:
time: 86.3 us; the launch traced here: 85.9 us
  starting transfers between devices  33.2 us (38%)
  Pallas kernels  27.5 us (32%)
  waiting for transfers between devices  23.1 us (27%)
  between operations  1.62 us (2%)
    pallas_call x10, Pallas kernels, call(): pl.pallas_call(inner if order else body, out_shape=tuple(outs), in_specs=...  27.5 us
    ppermute x12, starting transfers between devices, shift(): lax.ppermute(value, axis, [(k, (k + by) % count) for k in range(count)])  16.9 us
    ppermute x6, waiting for transfers between devices, swap(): lax.ppermute(value, axis, [(k, k ^ mask) for k in range(lax.axis_size(axi...  10.1 us
    ppermute x12, waiting for transfers between devices, shift(): lax.ppermute(value, axis, [(k, (k + by) % count) for k in range(count)])  7.02 us
    ppermute x6, starting transfers between devices, swap(): lax.ppermute(value, axis, [(k, k ^ mask) for k in range(lax.axis_size(axi...  6.22 us
    all_to_all x1, starting transfers between devices, per_device(): lax.all_to_all(sent, ('graph', 'dp'), split_axis=0, concat_axis=0, tiled=...  6 us
    all_to_all x1, waiting for transfers between devices, per_device(): lax.all_to_all(dfetch, 'graph', split_axis=0, concat_axis=0, tiled=True)  6 us
    all_to_all x1, starting transfers between devices, per_device(): lax.all_to_all(dfetch, 'graph', split_axis=0, concat_axis=0, tiled=True)  4.04 us
  transfers between devices with their start and end apart: 20, of which 11 were waited for; matrix products, arithmetic and copies ran while one was open for 0% of the time, Pallas kernels for 21%

profile of v10, /device:TPU:0, one launch (start us, length us, event | category | flops | bytes accessed | tf_op | source)
XLA Modules:
  0.0 85.9 jit_solution(13500907387871923862)
XLA Ops:
  0.6 0.8 shard_map.129.refs_1_.refs_0_
  1.4 5.1 %collective-permute-start.2 = (s32[4,128]{1,0:T(4,128)S(1)}, s32[4,128]{1,0:T(4,128)S(1)}, u32[]{:S(2)}, u32[]{:S(2)}) collective-permute-start(s32[4,128]{1,0:T(4,128)S(1)} %shard_map.129.refs_1_.refs_0_), channel_id=1, source_target_pairs={{0,12},{4,0},{8,4},{12,8},{1,13},{5,1},{9,5},{13,9},{2,14},{6,2},{... | collective-permute-start | bytes 6152 | tf_op jit(solution)/shard_map/ppermute | solution.py:300
  6.5 1.0 %collective-permute-start = (s32[4,128]{1,0:T(4,128)S(1)}, s32[4,128]{1,0:T(4,128)S(1)}, u32[]{:S(2)}, u32[]{:S(2)}) collective-permute-start(s32[4,128]{1,0:T(4,128)S(1)} %shard_map.129.refs_1_.refs_0_), channel_id=1, source_target_pairs={{0,4},{4,8},{8,12},{12,0},{1,5},{5,9},{9,13},{13,1},{2,6},{6,10},{... | collective-permute-start | bytes 6152 | tf_op jit(solution)/shard_map/ppermute | solution.py:300
  7.6 1.2 %shard_map.130.refs_4_ = bf16[1024,512]{1,0:T(8,128)(2,1)S(1)} custom-call(bf16[1024,512]{1,0:T(8,128)(2,1)} %bitcast.21, s32[4,128]{1,0:T(4,128)S(1)} %shard_map.129.refs_1_.refs_0_), custom_call_target="tpu_custom_call" | custom-call | flops 1073741824 | bytes 2099200 | tf_op jit(solution)/shard_map/pallas_call | solution.py:49
  8.9 2.1 %collective-permute-done.1.refs_2_.refs_3_ = s32[4,128]{1,0:T(4,128)S(1)} collective-permute-done((s32[4,128]{1,0:T(4,128)S(1)}, s32[4,128]{1,0:T(4,128)S(1)}, u32[]{:S(2)}, u32[]{:S(2)}) %collective-permute-start.1) | collective-permute-done | bytes 2080 | tf_op jit(solution)/shard_map/ppermute | solution.py:300
  11.0 0.9 %collective-permute-done.refs_1_.refs_2_ = s32[4,128]{1,0:T(4,128)S(1)} collective-permute-done((s32[4,128]{1,0:T(4,128)S(1)}, s32[4,128]{1,0:T(4,128)S(1)}, u32[]{:S(2)}, u32[]{:S(2)}) %collective-permute-start) | collective-permute-done | bytes 2080 | tf_op jit(solution)/shard_map/ppermute | solution.py:300
  11.9 1.2 %shard_map.131 = (bf16[64,512]{1,0:T(8,128)(2,1)S(1)}, bf16[64,512]{1,0:T(8,128)(2,1)S(1)}, bf16[64,512]{1,0:T(8,128)(2,1)S(1)}, bf16[64,512]{1,0:T(8,128)(2,1)S(1)}) custom-call(s32[2]{0:T(128)S(1)} %pad_add_fusion.me.refs_0_.low, s32[4,128]{1,0:T(4,128)S(1)} %shard_map.129.refs_1_.refs_0_, s32[4,128]{1,0:T(4,128)S(1)} %collective-permute-done.refs_1_.refs_2_, ...), custom_call_target="tpu_custom_call" | custom-call | flops 268435456 | bytes 1318920 | tf_op jit(solution)/shard_map/pallas_call | solution.py:49
  13.1 0.6 collective-permute-start.3
  13.7 0.6 collective-permute-start.4
  14.3 1.9 %collective-permute-start.5 = (bf16[64,512]{1,0:T(8,128)(2,1)S(1)}, bf16[64,512]{1,0:T(8,128)(2,1)S(1)}, u32[]{:S(2)}, u32[]{:S(2)}) collective-permute-start(bf16[64,512]{1,0:T(8,128)(2,1)S(1)} %get-tuple-element.31), channel_id=1, source_target_pairs={{0,4},{4,8},{8,12},{12,0},{1,5},{5,9},{9,13},{13,1},{2,6},{6,10},{... | collective-permute-start | bytes 196616 | tf_op jit(solution)/shard_map/ppermute | solution.py:300
  17.0 2.9 %shard_map.132 = (bf16[256,256]{1,0:T(8,128)(2,1)S(1)}, f32[256,512]{1,0:T(8,128)S(1)}) custom-call(s32[2]{0:T(128)S(1)} %pad_add_fusion.me.refs_0_.low, s32[4,128]{1,0:T(4,128)S(1)} %shard_map.129.refs_1_.refs_0_, s32[4,128]{1,0:T(4,128)S(1)} %collective-permute-done.refs_1_.refs_2_, s32[4,128]{1,0:T(4,128)S(1)} %collective-permute-done.1.refs_2_.refs_3_, ...), custom_call_target="tpu_custom_call" | custom-call | flops 536870912 | bytes 2301960 | tf_op jit(solution)/shard_map/pallas_call | solution.py:49
  19.9 0.7 collective-permute-done.5.refs_5_
  20.6 5.3 %shard_map.133 = (bf16[64,512]{1,0:T(8,128)(2,1)S(1)}, bf16[64,512]{1,0:T(8,128)(2,1)S(1)}, bf16[64,512]{1,0:T(8,128)(2,1)S(1)}, bf16[64,512]{1,0:T(8,128)(2,1)S(1)}) custom-call(s32[2]{0:T(128)S(1)} %pad_add_fusion.me.refs_0_.low, s32[1,1]{1,0:T(1,128)S(6)} %copy.14.refs_1_, bf16[64,512]{1,0:T(8,128)(2,1)S(1)} %get-tuple-element.28.refs_7_.refs_2_, ...), custom_call_target="tpu_custom_call" | custom-call | flops 2684354560 | bytes 1867788 | tf_op jit(solution)/shard_map/pallas_call | solution.py:49
  26.2 2.0 %collective-permute-start.7 = (bf16[64,512]{1,0:T(8,128)(2,1)S(1)}, bf16[64,512]{1,0:T(8,128)(2,1)S(1)}, u32[]{:S(2)}, u32[]{:S(2)}) collective-permute-start(bf16[64,512]{1,0:T(8,128)(2,1)S(1)} %get-tuple-element.35), channel_id=1, source_target_pairs={{0,8},{4,12},{8,0},{12,4},{1,9},{5,13},{9,1},{13,5},{2,10},{6,14},... | collective-permute-start | bytes 196616 | tf_op jit(solution)/shard_map/ppermute | solution.py:300
  28.2 1.8 %collective-permute-start.8 = (bf16[64,512]{1,0:T(8,128)(2,1)S(1)}, bf16[64,512]{1,0:T(8,128)(2,1)S(1)}, u32[]{:S(2)}, u32[]{:S(2)}) collective-permute-start(bf16[64,512]{1,0:T(8,128)(2,1)S(1)} %get-tuple-element.36), channel_id=1, source_target_pairs={{0,12},{4,0},{8,4},{12,8},{1,13},{5,1},{9,5},{13,9},{2,14},{6,2},{... | collective-permute-start | bytes 196616 | tf_op jit(solution)/shard_map/ppermute | solution.py:300
  30.0 2.1 %collective-permute-done.6.refs_1_.refs_6_ = bf16[64,512]{1,0:T(8,128)(2,1)S(1)} collective-permute-done((bf16[64,512]{1,0:T(8,128)(2,1)S(1)}, bf16[64,512]{1,0:T(8,128)(2,1)S(1)}, u32[]{:S(2)}, u32[]{:S(2)}) %collective-permute-start.6) | collective-permute-done | bytes 65568 | tf_op jit(solution)/shard_map/ppermute | solution.py:300
  32.1 1.2 %collective-permute-done.8.refs_3_.refs_8_ = bf16[64,512]{1,0:T(8,128)(2,1)S(1)} collective-permute-done((bf16[64,512]{1,0:T(8,128)(2,1)S(1)}, bf16[64,512]{1,0:T(8,128)(2,1)S(1)}, u32[]{:S(2)}, u32[]{:S(2)}) %collective-permute-start.8) | collective-permute-done | bytes 65568 | tf_op jit(solution)/shard_map/ppermute | solution.py:300
  33.7 2.8 %collective-permute-start.9 = (bf16[64,512]{1,0:T(8,128)(2,1)S(1)}, bf16[64,512]{1,0:T(8,128)(2,1)S(1)}, u32[]{:S(2)}, u32[]{:S(2)}) collective-permute-start(bf16[64,512]{1,0:T(8,128)(2,1)S(1)} %get-tuple-element.41), channel_id=1, source_target_pairs={{0,12},{4,0},{8,4},{12,8},{1,13},{5,1},{9,5},{13,9},{2,14},{6,2},{... | collective-permute-start | bytes 196616 | tf_op jit(solution)/shard_map/ppermute | solution.py:300
  37.1 3.6 %shard_map.135 = (bf16[1024,512]{1,0:T(8,128)(2,1)}, bf16[16,32,512]{2,1,0:T(8,128)(2,1)}) custom-call(s32[2]{0:T(128)S(1)} %pad_add_fusion.me.refs_0_.low, s32[4,128]{1,0:T(4,128)S(1)} %shard_map.129.refs_1_.refs_0_, s32[4,128]{1,0:T(4,128)S(1)} %collective-permute-done.refs_1_.refs_2_, s32[4,128]{1,0:T(4,128)S(1)} %collective-permute-done.1.refs_2_.refs_3_, ...), custom_call_target="tpu_custom_call" | custom-call | flops 1342177280 | bytes 4530184 | tf_op jit(solution)/shard_map/pallas_call | solution.py:49
  40.8 6.0 %all-to-all-start = ((bf16[16,32,512]{2,1,0:T(8,128)(2,1)}), bf16[16,32,512]{2,1,0:T(8,128)(2,1)S(1)}, u32[]{:S(2)}, u32[]{:S(2)}) async-start(bf16[16,32,512]{2,1,0:T(8,128)(2,1)} %get-tuple-element.40.refs_14_), calls=%async_computation | async-start | bytes 1048576 | tf_op jit(solution)/shard_map/all_to_all | solution.py:442
  46.8 8.5 %shard_map.136 = (f32[64,512]{1,0:T(8,128)S(1)}, bf16[64,512]{1,0:T(8,128)(2,1)S(1)}, bf16[4,64,512]{2,1,0:T(8,128)(2,1)}) custom-call(s32[2]{0:T(128)S(1)} %pad_add_fusion.me.refs_0_.low, s32[1,1]{1,0:T(1,128)S(6)} %copy.14.refs_1_, bf16[64,512]{1,0:T(8,128)(2,1)S(1)} %get-tuple-element.28.refs_7_.refs_2_, ...), custom_call_target="tpu_custom_call" | custom-call | flops 4294967296 | bytes 2719756 | tf_op jit(solution)/shard_map/pallas_call | solution.py:49
  55.8 0.9 %collective-permute-done.12 = bf16[64,512]{1,0:T(8,128)(2,1)S(1)} collective-permute-done((bf16[64,512]{1,0:T(8,128)(2,1)S(1)}, bf16[64,512]{1,0:T(8,128)(2,1)S(1)}, u32[]{:S(2)}, u32[]{:S(2)}) %collective-permute-start.12) | collective-permute-done | bytes 65568 | tf_op jit(solution)/shard_map/ppermute | solution.py:295
  56.7 1.9 %collective-permute-start.13 = (bf16[32,512]{1,0:T(8,128)(2,1)S(1)}, bf16[32,512]{1,0:T(8,128)(2,1)S(1)}, u32[]{:S(2)}, u32[]{:S(2)}) collective-permute-start(bf16[32,512]{1,0:T(8,128)(2,1)S(1)} %fusion.2), channel_id=1, source_target_pairs={{0,2},{1,3},{2,0},{3,1},{4,6},{5,7},{6,4},{7,5},{8,10},{9,11},{10,... | collective-permute-start | bytes 98312 | tf_op jit(solution)/shard_map/ppermute | solution.py:295
  58.6 2.8 %collective-permute-done.13 = bf16[32,512]{1,0:T(8,128)(2,1)S(1)} collective-permute-done((bf16[32,512]{1,0:T(8,128)(2,1)S(1)}, bf16[32,512]{1,0:T(8,128)(2,1)S(1)}, u32[]{:S(2)}, u32[]{:S(2)}) %collective-permute-start.13) | collective-permute-done | bytes 32800 | tf_op jit(solution)/shard_map/ppermute | solution.py:295
  61.6 2.4 %collective-permute-start.14 = (bf16[64,512]{1,0:T(8,128)(2,1)S(1)}, bf16[64,512]{1,0:T(8,128)(2,1)S(1)}, u32[]{:S(2)}, u32[]{:S(2)}) collective-permute-start(bf16[64,512]{1,0:T(8,128)(2,1)S(1)} %pad_maximum_fusion.4), channel_id=1, source_target_pairs={{0,8},{4,12},{8,0},{12,4},{1,9},{5,13},{9,1},{13,5},{2,10},{6,14},... | collective-permute-start | bytes 196616 | tf_op jit(solution)/shard_map/ppermute | solution.py:295
  64.0 4.2 %collective-permute-done.14 = bf16[64,512]{1,0:T(8,128)(2,1)S(1)} collective-permute-done((bf16[64,512]{1,0:T(8,128)(2,1)S(1)}, bf16[64,512]{1,0:T(8,128)(2,1)S(1)}, u32[]{:S(2)}, u32[]{:S(2)}) %collective-permute-start.14) | collective-permute-done | bytes 65568 | tf_op jit(solution)/shard_map/ppermute | solution.py:295
  68.3 4.0 %all-to-all-start.1 = ((bf16[4,64,512]{2,1,0:T(8,128)(2,1)}), bf16[4,64,512]{2,1,0:T(8,128)(2,1)S(1)}, u32[]{:S(2)}, u32[]{:S(2)}) async-start(bf16[4,64,512]{2,1,0:T(8,128)(2,1)} %get-tuple-element.46), calls=%async_computation.1 | async-start | bytes 524288 | tf_op jit(solution)/shard_map/all_to_all | solution.py:458
  73.0 1.3 %collective-permute-start.16 = (bf16[160,512]{1,0:T(8,128)(2,1)S(1)}, bf16[160,512]{1,0:T(8,128)(2,1)S(1)}, u32[]{:S(2)}, u32[]{:S(2)}) collective-permute-start(bf16[160,512]{1,0:T(8,128)(2,1)S(1)} %pad_maximum_fusion.1), channel_id=1, source_target_pairs={{0,2},{1,3},{2,0},{3,1},{4,6},{5,7},{6,4},{7,5},{8,10},{9,11},{10,... | collective-permute-start | bytes 491528 | tf_op jit(solution)/shard_map/ppermute | solution.py:295
  74.3 6.0 %all-to-all-done.1.refs_4_ = bf16[4,64,512]{2,1,0:T(8,128)(2,1)S(1)} async-done(((bf16[4,64,512]{2,1,0:T(8,128)(2,1)}), bf16[4,64,512]{2,1,0:T(8,128)(2,1)S(1)}, u32[]{:S(2)}, u32[]{:S(2)}) %all-to-all-start.1) | async-done | bytes 262176 | tf_op jit(solution)/shard_map/all_to_all | solution.py:458
  80.3 2.0 %shard_map.137 = bf16[1024,512]{1,0:T(8,128)(2,1)} custom-call(s32[2]{0:T(128)S(1)} %pad_add_fusion.me.refs_0_.low, s32[4,128]{1,0:T(4,128)S(1)} %shard_map.129.refs_1_.refs_0_, s32[4,128]{1,0:T(4,128)S(1)} %collective-permute-done.refs_1_.refs_2_, s32[4,128]{1,0:T(4,128)S(1)} %collective-permute-done.1.refs_2_.refs_3_, ...), custom_call_target="tpu_custom_call" | custom-call | flops 268435456 | bytes 2367496 | tf_op jit(solution)/shard_map/pallas_call | solution.py:49
  82.6 1.6 %collective-permute-done.17 = bf16[320,512]{1,0:T(8,128)(2,1)S(1)} collective-permute-done((bf16[320,512]{1,0:T(8,128)(2,1)S(1)}, bf16[320,512]{1,0:T(8,128)(2,1)S(1)}, u32[]{:S(2)}, u32[]{:S(2)}) %collective-permute-start.17) | collective-permute-done | bytes 327712 | tf_op jit(solution)/shard_map/ppermute | solution.py:295
  84.2 1.7 %shard_map.138 = (f32[512,512]{1,0:T(8,128)}, f32[128,512]{1,0:T(8,128)}) custom-call(s32[2]{0:T(128)S(1)} %pad_add_fusion.me.refs_0_.low, bf16[256,512]{1,0:T(8,128)(2,1)S(1)} %maximum_select_fusion.out, bf16[256,512]{1,0:T(8,128)(2,1)S(1)} %slice.38.out_got, bf16[64,512]{1,0:T(8,128)(2,1)S(1)} %maximum_select_fusion.2.basis, ...), custom_call_target="tpu_custom_call" | custom-call | bytes 1966088 | tf_op jit(solution)/shard_map/pallas_call | solution.py:49
  (51 shorter events, 3.0 us)
Async XLA Ops:
  1.4 7.4 %collective-permute-start.2 = (s32[4,128]{1,0:T(4,128)S(1)}, s32[4,128]{1,0:T(4,128)S(1)}, u32[]{:S(2)}, u32[]{:S(2)}) collective-permute-start(s32[4,128]{1,0:T(4,128)S(1)} %shard_map.129.refs_1_.refs_0_), channel_id=1, source_target_pairs={{0,12},{4,0},{8,4},{12,8},{1,13},{5,1},{9,5},{13,9},{2,14},{6,2},{... | collective-permute-start | bytes 6152 | tf_op jit(solution)/shard_map/ppermute | solution.py:300
  6.5 4.5 %collective-permute-start.1 = (s32[4,128]{1,0:T(4,128)S(1)}, s32[4,128]{1,0:T(4,128)S(1)}, u32[]{:S(2)}, u32[]{:S(2)}) collective-permute-start(s32[4,128]{1,0:T(4,128)S(1)} %shard_map.129.refs_1_.refs_0_), channel_id=1, source_target_pairs={{0,8},{4,12},{8,0},{12,4},{1,9},{5,13},{9,1},{13,5},{2,10},{6,14},... | collective-permute-start | bytes 6152 | tf_op jit(solution)/shard_map/ppermute | solution.py:300
  6.5 5.4 %collective-permute-start = (s32[4,128]{1,0:T(4,128)S(1)}, s32[4,128]{1,0:T(4,128)S(1)}, u32[]{:S(2)}, u32[]{:S(2)}) collective-permute-start(s32[4,128]{1,0:T(4,128)S(1)} %shard_map.129.refs_1_.refs_0_), channel_id=1, source_target_pairs={{0,4},{4,8},{8,12},{12,0},{1,5},{5,9},{9,13},{13,1},{2,6},{6,10},{... | collective-permute-start | bytes 6152 | tf_op jit(solution)/shard_map/ppermute | solution.py:300
  13.1 6.8 %collective-permute-start.3 = (bf16[64,512]{1,0:T(8,128)(2,1)S(1)}, bf16[64,512]{1,0:T(8,128)(2,1)S(1)}, u32[]{:S(2)}, u32[]{:S(2)}) collective-permute-start(bf16[64,512]{1,0:T(8,128)(2,1)S(1)} %get-tuple-element.29), channel_id=1, source_target_pairs={{0,12},{4,0},{8,4},{12,8},{1,13},{5,1},{9,5},{13,9},{2,14},{6,2},{... | collective-permute-start | bytes 196616 | tf_op jit(solution)/shard_map/ppermute | solution.py:300
  13.7 6.2 %collective-permute-start.4 = (bf16[64,512]{1,0:T(8,128)(2,1)S(1)}, bf16[64,512]{1,0:T(8,128)(2,1)S(1)}, u32[]{:S(2)}, u32[]{:S(2)}) collective-permute-start(bf16[64,512]{1,0:T(8,128)(2,1)S(1)} %get-tuple-element.30), channel_id=1, source_target_pairs={{0,8},{4,12},{8,0},{12,4},{1,9},{5,13},{9,1},{13,5},{2,10},{6,14},... | collective-permute-start | bytes 196616 | tf_op jit(solution)/shard_map/ppermute | solution.py:300
  14.3 6.2 %collective-permute-start.5 = (bf16[64,512]{1,0:T(8,128)(2,1)S(1)}, bf16[64,512]{1,0:T(8,128)(2,1)S(1)}, u32[]{:S(2)}, u32[]{:S(2)}) collective-permute-start(bf16[64,512]{1,0:T(8,128)(2,1)S(1)} %get-tuple-element.31), channel_id=1, source_target_pairs={{0,4},{4,8},{8,12},{12,0},{1,5},{5,9},{9,13},{13,1},{2,6},{6,10},{... | collective-permute-start | bytes 196616 | tf_op jit(solution)/shard_map/ppermute | solution.py:300
  16.9 3.6 %copy-start.3 = (bf16[128,512]{1,0:T(8,128)(2,1)S(1)}, bf16[128,512]{1,0:T(8,128)(2,1)}, u32[]{:S(2)}) copy-start(bf16[128,512]{1,0:T(8,128)(2,1)} %refs_12_.1) | copy-start | bytes 393220
  17.0 3.6 %copy-start.4 = (s32[1,32,128]{2,1,0:T(8,128)S(1)}, s32[1,32,128]{2,1,0:T(8,128)}, u32[]{:S(2)}) copy-start(s32[1,32,128]{2,1,0:T(8,128)} %param.14) | copy-start | bytes 49156
  17.0 3.6 %copy-start.5 = (s32[1,32,128]{2,1,0:T(8,128)S(1)}, s32[1,32,128]{2,1,0:T(8,128)}, u32[]{:S(2)}) copy-start(s32[1,32,128]{2,1,0:T(8,128)} %param.15) | copy-start | bytes 49156
  20.5 16.6 %copy-start = (bf16[1,1024,512]{2,1,0:T(8,128)(2,1)S(1)}, bf16[1,1024,512]{2,1,0:T(8,128)(2,1)}, u32[]{:S(2)}) copy-start(bf16[1,1024,512]{2,1,0:T(8,128)(2,1)} %param.11) | copy-start | bytes 3145732
  20.6 16.6 %copy-start.1 = (bf16[1,1024,512]{2,1,0:T(8,128)(2,1)S(1)}, bf16[1,1024,512]{2,1,0:T(8,128)(2,1)}, u32[]{:S(2)}) copy-start(bf16[1,1024,512]{2,1,0:T(8,128)(2,1)} %param.10) | copy-start | bytes 3145732
  25.9 11.3 %copy-start.2 = (bf16[512,512]{1,0:T(8,128)(2,1)S(1)}, bf16[512,512]{1,0:T(8,128)(2,1)}, u32[]{:S(2)}) copy-start(bf16[512,512]{1,0:T(8,128)(2,1)} %refs_11_.1) | copy-start | bytes 1572868
  25.9 6.2 %collective-permute-start.6 = (bf16[64,512]{1,0:T(8,128)(2,1)S(1)}, bf16[64,512]{1,0:T(8,128)(2,1)S(1)}, u32[]{:S(2)}, u32[]{:S(2)}) collective-permute-start(bf16[64,512]{1,0:T(8,128)(2,1)S(1)} %get-tuple-element.34), channel_id=1, source_target_pairs={{0,4},{4,8},{8,12},{12,0},{1,5},{5,9},{9,13},{13,1},{2,6},{6,10},{... | collective-permute-start | bytes 196616 | tf_op jit(solution)/shard_map/ppermute | solution.py:300
  26.2 5.9 %collective-permute-start.7 = (bf16[64,512]{1,0:T(8,128)(2,1)S(1)}, bf16[64,512]{1,0:T(8,128)(2,1)S(1)}, u32[]{:S(2)}, u32[]{:S(2)}) collective-permute-start(bf16[64,512]{1,0:T(8,128)(2,1)S(1)} %get-tuple-element.35), channel_id=1, source_target_pairs={{0,8},{4,12},{8,0},{12,4},{1,9},{5,13},{9,1},{13,5},{2,10},{6,14},... | collective-permute-start | bytes 196616 | tf_op jit(solution)/shard_map/ppermute | solution.py:300
  28.2 5.1 %collective-permute-start.8 = (bf16[64,512]{1,0:T(8,128)(2,1)S(1)}, bf16[64,512]{1,0:T(8,128)(2,1)S(1)}, u32[]{:S(2)}, u32[]{:S(2)}) collective-permute-start(bf16[64,512]{1,0:T(8,128)(2,1)S(1)} %get-tuple-element.36), channel_id=1, source_target_pairs={{0,12},{4,0},{8,4},{12,8},{1,13},{5,1},{9,5},{13,9},{2,14},{6,2},{... | collective-permute-start | bytes 196616 | tf_op jit(solution)/shard_map/ppermute | solution.py:300
  33.7 13.1 %collective-permute-start.9 = (bf16[64,512]{1,0:T(8,128)(2,1)S(1)}, bf16[64,512]{1,0:T(8,128)(2,1)S(1)}, u32[]{:S(2)}, u32[]{:S(2)}) collective-permute-start(bf16[64,512]{1,0:T(8,128)(2,1)S(1)} %get-tuple-element.41), channel_id=1, source_target_pairs={{0,12},{4,0},{8,4},{12,8},{1,13},{5,1},{9,5},{13,9},{2,14},{6,2},{... | collective-permute-start | bytes 196616 | tf_op jit(solution)/shard_map/ppermute | solution.py:300
  36.5 10.3 %collective-permute-start.10 = (bf16[64,512]{1,0:T(8,128)(2,1)S(1)}, bf16[64,512]{1,0:T(8,128)(2,1)S(1)}, u32[]{:S(2)}, u32[]{:S(2)}) collective-permute-start(bf16[64,512]{1,0:T(8,128)(2,1)S(1)} %get-tuple-element.42), channel_id=1, source_target_pairs={{0,8},{4,12},{8,0},{12,4},{1,9},{5,13},{9,1},{13,5},{2,10},{6,14},... | collective-permute-start | bytes 196616 | tf_op jit(solution)/shard_map/ppermute | solution.py:300
  37.0 9.8 %collective-permute-start.11 = (bf16[64,512]{1,0:T(8,128)(2,1)S(1)}, bf16[64,512]{1,0:T(8,128)(2,1)S(1)}, u32[]{:S(2)}, u32[]{:S(2)}) collective-permute-start(bf16[64,512]{1,0:T(8,128)(2,1)S(1)} %get-tuple-element.43), channel_id=1, source_target_pairs={{0,4},{4,8},{8,12},{12,0},{1,5},{5,9},{9,13},{13,1},{2,6},{6,10},{... | collective-permute-start | bytes 196616 | tf_op jit(solution)/shard_map/ppermute | solution.py:300
  40.8 20.7 %all-to-all-start = ((bf16[16,32,512]{2,1,0:T(8,128)(2,1)}), bf16[16,32,512]{2,1,0:T(8,128)(2,1)S(1)}, u32[]{:S(2)}, u32[]{:S(2)}) async-start(bf16[16,32,512]{2,1,0:T(8,128)(2,1)} %get-tuple-element.40.refs_14_), calls=%async_computation | async-start | bytes 1048576 | tf_op jit(solution)/shard_map/all_to_all | solution.py:442
  55.3 1.4 %collective-permute-start.12 = (bf16[64,512]{1,0:T(8,128)(2,1)S(1)}, bf16[64,512]{1,0:T(8,128)(2,1)S(1)}, u32[]{:S(2)}, u32[]{:S(2)}) collective-permute-start(bf16[64,512]{1,0:T(8,128)(2,1)S(1)} %get-tuple-element.45), channel_id=1, source_target_pairs={{0,1},{1,0},{2,3},{3,2},{4,5},{5,4},{6,7},{7,6},{8,9},{9,8},{10,11... | collective-permute-start | bytes 196616 | tf_op jit(solution)/shard_map/ppermute | solution.py:295
  56.7 4.8 %collective-permute-start.13 = (bf16[32,512]{1,0:T(8,128)(2,1)S(1)}, bf16[32,512]{1,0:T(8,128)(2,1)S(1)}, u32[]{:S(2)}, u32[]{:S(2)}) collective-permute-start(bf16[32,512]{1,0:T(8,128)(2,1)S(1)} %fusion.2), channel_id=1, source_target_pairs={{0,2},{1,3},{2,0},{3,1},{4,6},{5,7},{6,4},{7,5},{8,10},{9,11},{10,... | collective-permute-start | bytes 98312 | tf_op jit(solution)/shard_map/ppermute | solution.py:295
  61.6 6.6 %collective-permute-start.14 = (bf16[64,512]{1,0:T(8,128)(2,1)S(1)}, bf16[64,512]{1,0:T(8,128)(2,1)S(1)}, u32[]{:S(2)}, u32[]{:S(2)}) collective-permute-start(bf16[64,512]{1,0:T(8,128)(2,1)S(1)} %pad_maximum_fusion.4), channel_id=1, source_target_pairs={{0,8},{4,12},{8,0},{12,4},{1,9},{5,13},{9,1},{13,5},{2,10},{6,14},... | collective-permute-start | bytes 196616 | tf_op jit(solution)/shard_map/ppermute | solution.py:295
  68.2 4.7 %collective-permute-start.15 = (bf16[96,512]{1,0:T(8,128)(2,1)S(1)}, bf16[96,512]{1,0:T(8,128)(2,1)S(1)}, u32[]{:S(2)}, u32[]{:S(2)}) collective-permute-start(bf16[96,512]{1,0:T(8,128)(2,1)S(1)} %pad_maximum_fusion.2), channel_id=1, source_target_pairs={{0,4},{4,0},{8,12},{12,8},{1,5},{5,1},{9,13},{13,9},{2,6},{6,2},{1... | collective-permute-start | bytes 294920 | tf_op jit(solution)/shard_map/ppermute | solution.py:295
  68.3 12.0 %all-to-all-start.1 = ((bf16[4,64,512]{2,1,0:T(8,128)(2,1)}), bf16[4,64,512]{2,1,0:T(8,128)(2,1)S(1)}, u32[]{:S(2)}, u32[]{:S(2)}) async-start(bf16[4,64,512]{2,1,0:T(8,128)(2,1)} %get-tuple-element.46), calls=%async_computation.1 | async-start | bytes 524288 | tf_op jit(solution)/shard_map/all_to_all | solution.py:458
  73.0 9.3 %collective-permute-start.16 = (bf16[160,512]{1,0:T(8,128)(2,1)S(1)}, bf16[160,512]{1,0:T(8,128)(2,1)S(1)}, u32[]{:S(2)}, u32[]{:S(2)}) collective-permute-start(bf16[160,512]{1,0:T(8,128)(2,1)S(1)} %pad_maximum_fusion.1), channel_id=1, source_target_pairs={{0,2},{1,3},{2,0},{3,1},{4,6},{5,7},{6,4},{7,5},{8,10},{9,11},{10,... | collective-permute-start | bytes 491528 | tf_op jit(solution)/shard_map/ppermute | solution.py:295
  82.5 1.7 %collective-permute-start.17 = (bf16[320,512]{1,0:T(8,128)(2,1)S(1)}, bf16[320,512]{1,0:T(8,128)(2,1)S(1)}, u32[]{:S(2)}, u32[]{:S(2)}) collective-permute-start(bf16[320,512]{1,0:T(8,128)(2,1)S(1)} %pad_maximum_fusion), channel_id=1, source_target_pairs={{0,1},{1,0},{2,3},{3,2},{4,5},{5,4},{6,7},{7,6},{8,9},{9,8},{10,11... | collective-permute-start | bytes 983048 | tf_op jit(solution)/shard_map/ppermute | solution.py:295

commit v11 on v10

--- a/solution.py
+++ b/solution.py
@@ -175,7 +175,7 @@
     waited(arrive)
     for at in spans:
         act = silu_parts(dot(weight_t, basis_v[at, :], NT))[0]
-        message[:, at] = (dot(table, near_hot[:, at]) * act).astype(BF16)
+        message[:, at] = dot(table, near_hot[:, at]).astype(BF16) * act.astype(BF16)
     scattered(dot(hot[...], message[...], NT).astype(BF16), outs)
 
 

time: 86.3 us -> 86.3 us (level)
  no operation moved by 1% of the time
where the time goes in v11:
time: 86.3 us; the launch traced here: 85.9 us
  starting transfers between devices  33.2 us (38%)
  Pallas kernels  27.5 us (32%)
  waiting for transfers between devices  23.1 us (27%)
  between operations  1.62 us (2%)
    pallas_call x10, Pallas kernels, call(): pl.pallas_call(inner if order else body, out_shape=tuple(outs), in_specs=...  27.5 us
    ppermute x12, starting transfers between devices, shift(): lax.ppermute(value, axis, [(k, (k + by) % count) for k in range(count)])  16.9 us
    ppermute x6, waiting for transfers between devices, swap(): lax.ppermute(value, axis, [(k, k ^ mask) for k in range(lax.axis_size(axi...  10.1 us
    ppermute x12, waiting for transfers between devices, shift(): lax.ppermute(value, axis, [(k, (k + by) % count) for k in range(count)])  7.02 us
    ppermute x6, starting transfers between devices, swap(): lax.ppermute(value, axis, [(k, k ^ mask) for k in range(lax.axis_size(axi...  6.22 us
    all_to_all x1, starting transfers between devices, per_device(): lax.all_to_all(sent, ('graph', 'dp'), split_axis=0, concat_axis=0, tiled=...  6 us
    all_to_all x1, waiting for transfers between devices, per_device(): lax.all_to_all(dfetch, 'graph', split_axis=0, concat_axis=0, tiled=True)  6 us
    all_to_all x1, starting transfers between devices, per_device(): lax.all_to_all(dfetch, 'graph', split_axis=0, concat_axis=0, tiled=True)  4.04 us
  transfers between devices with their start and end apart: 20, of which 11 were waited for; matrix products, arithmetic and copies ran while one was open for 0% of the time, Pallas kernels for 21%

profile of v11, /device:TPU:0, one launch (start us, length us, event | category | flops | bytes accessed | tf_op | source)
XLA Modules:
  0.0 85.9 jit_solution(6367921642446214432)
XLA Ops:
  0.6 0.8 shard_map.129.refs_1_.refs_0_
  1.4 5.1 %collective-permute-start.2 = (s32[4,128]{1,0:T(4,128)S(1)}, s32[4,128]{1,0:T(4,128)S(1)}, u32[]{:S(2)}, u32[]{:S(2)}) collective-permute-start(s32[4,128]{1,0:T(4,128)S(1)} %shard_map.129.refs_1_.refs_0_), channel_id=1, source_target_pairs={{0,12},{4,0},{8,4},{12,8},{1,13},{5,1},{9,5},{13,9},{2,14},{6,2},{... | collective-permute-start | bytes 6152 | tf_op jit(solution)/shard_map/ppermute | solution.py:300
  6.5 1.0 %collective-permute-start = (s32[4,128]{1,0:T(4,128)S(1)}, s32[4,128]{1,0:T(4,128)S(1)}, u32[]{:S(2)}, u32[]{:S(2)}) collective-permute-start(s32[4,128]{1,0:T(4,128)S(1)} %shard_map.129.refs_1_.refs_0_), channel_id=1, source_target_pairs={{0,4},{4,8},{8,12},{12,0},{1,5},{5,9},{9,13},{13,1},{2,6},{6,10},{... | collective-permute-start | bytes 6152 | tf_op jit(solution)/shard_map/ppermute | solution.py:300
  7.6 1.2 %shard_map.130.refs_4_ = bf16[1024,512]{1,0:T(8,128)(2,1)S(1)} custom-call(bf16[1024,512]{1,0:T(8,128)(2,1)} %bitcast.21, s32[4,128]{1,0:T(4,128)S(1)} %shard_map.129.refs_1_.refs_0_), custom_call_target="tpu_custom_call" | custom-call | flops 1073741824 | bytes 2099200 | tf_op jit(solution)/shard_map/pallas_call | solution.py:49
  8.9 2.1 %collective-permute-done.1.refs_2_.refs_3_ = s32[4,128]{1,0:T(4,128)S(1)} collective-permute-done((s32[4,128]{1,0:T(4,128)S(1)}, s32[4,128]{1,0:T(4,128)S(1)}, u32[]{:S(2)}, u32[]{:S(2)}) %collective-permute-start.1) | collective-permute-done | bytes 2080 | tf_op jit(solution)/shard_map/ppermute | solution.py:300
  11.0 0.9 %collective-permute-done.refs_1_.refs_2_ = s32[4,128]{1,0:T(4,128)S(1)} collective-permute-done((s32[4,128]{1,0:T(4,128)S(1)}, s32[4,128]{1,0:T(4,128)S(1)}, u32[]{:S(2)}, u32[]{:S(2)}) %collective-permute-start) | collective-permute-done | bytes 2080 | tf_op jit(solution)/shard_map/ppermute | solution.py:300
  11.9 1.2 %shard_map.131 = (bf16[64,512]{1,0:T(8,128)(2,1)S(1)}, bf16[64,512]{1,0:T(8,128)(2,1)S(1)}, bf16[64,512]{1,0:T(8,128)(2,1)S(1)}, bf16[64,512]{1,0:T(8,128)(2,1)S(1)}) custom-call(s32[2]{0:T(128)S(1)} %pad_add_fusion.me.refs_0_.low, s32[4,128]{1,0:T(4,128)S(1)} %shard_map.129.refs_1_.refs_0_, s32[4,128]{1,0:T(4,128)S(1)} %collective-permute-done.refs_1_.refs_2_, ...), custom_call_target="tpu_custom_call" | custom-call | flops 268435456 | bytes 1318920 | tf_op jit(solution)/shard_map/pallas_call | solution.py:49
  13.1 0.6 collective-permute-start.3
  13.7 0.6 collective-permute-start.4
  14.3 1.9 %collective-permute-start.5 = (bf16[64,512]{1,0:T(8,128)(2,1)S(1)}, bf16[64,512]{1,0:T(8,128)(2,1)S(1)}, u32[]{:S(2)}, u32[]{:S(2)}) collective-permute-start(bf16[64,512]{1,0:T(8,128)(2,1)S(1)} %get-tuple-element.31), channel_id=1, source_target_pairs={{0,4},{4,8},{8,12},{12,0},{1,5},{5,9},{9,13},{13,1},{2,6},{6,10},{... | collective-permute-start | bytes 196616 | tf_op jit(solution)/shard_map/ppermute | solution.py:300
  17.0 2.9 %shard_map.132 = (bf16[256,256]{1,0:T(8,128)(2,1)S(1)}, f32[256,512]{1,0:T(8,128)S(1)}) custom-call(s32[2]{0:T(128)S(1)} %pad_add_fusion.me.refs_0_.low, s32[4,128]{1,0:T(4,128)S(1)} %shard_map.129.refs_1_.refs_0_, s32[4,128]{1,0:T(4,128)S(1)} %collective-permute-done.refs_1_.refs_2_, s32[4,128]{1,0:T(4,128)S(1)} %collective-permute-done.1.refs_2_.refs_3_, ...), custom_call_target="tpu_custom_call" | custom-call | flops 536870912 | bytes 2301960 | tf_op jit(solution)/shard_map/pallas_call | solution.py:49
  19.9 0.7 collective-permute-done.5.refs_5_
  20.6 5.3 %shard_map.133 = (bf16[64,512]{1,0:T(8,128)(2,1)S(1)}, bf16[64,512]{1,0:T(8,128)(2,1)S(1)}, bf16[64,512]{1,0:T(8,128)(2,1)S(1)}, bf16[64,512]{1,0:T(8,128)(2,1)S(1)}) custom-call(s32[2]{0:T(128)S(1)} %pad_add_fusion.me.refs_0_.low, s32[1,1]{1,0:T(1,128)S(6)} %copy.14.refs_1_, bf16[64,512]{1,0:T(8,128)(2,1)S(1)} %get-tuple-element.28.refs_7_.refs_2_, ...), custom_call_target="tpu_custom_call" | custom-call | flops 2684354560 | bytes 1867788 | tf_op jit(solution)/shard_map/pallas_call | solution.py:49
  26.2 2.0 %collective-permute-start.7 = (bf16[64,512]{1,0:T(8,128)(2,1)S(1)}, bf16[64,512]{1,0:T(8,128)(2,1)S(1)}, u32[]{:S(2)}, u32[]{:S(2)}) collective-permute-start(bf16[64,512]{1,0:T(8,128)(2,1)S(1)} %get-tuple-element.35), channel_id=1, source_target_pairs={{0,8},{4,12},{8,0},{12,4},{1,9},{5,13},{9,1},{13,5},{2,10},{6,14},... | collective-permute-start | bytes 196616 | tf_op jit(solution)/shard_map/ppermute | solution.py:300
  28.2 1.8 %collective-permute-start.8 = (bf16[64,512]{1,0:T(8,128)(2,1)S(1)}, bf16[64,512]{1,0:T(8,128)(2,1)S(1)}, u32[]{:S(2)}, u32[]{:S(2)}) collective-permute-start(bf16[64,512]{1,0:T(8,128)(2,1)S(1)} %get-tuple-element.36), channel_id=1, source_target_pairs={{0,12},{4,0},{8,4},{12,8},{1,13},{5,1},{9,5},{13,9},{2,14},{6,2},{... | collective-permute-start | bytes 196616 | tf_op jit(solution)/shard_map/ppermute | solution.py:300
  30.0 2.1 %collective-permute-done.6.refs_1_.refs_6_ = bf16[64,512]{1,0:T(8,128)(2,1)S(1)} collective-permute-done((bf16[64,512]{1,0:T(8,128)(2,1)S(1)}, bf16[64,512]{1,0:T(8,128)(2,1)S(1)}, u32[]{:S(2)}, u32[]{:S(2)}) %collective-permute-start.6) | collective-permute-done | bytes 65568 | tf_op jit(solution)/shard_map/ppermute | solution.py:300
  32.1 1.2 %collective-permute-done.8.refs_3_.refs_8_ = bf16[64,512]{1,0:T(8,128)(2,1)S(1)} collective-permute-done((bf16[64,512]{1,0:T(8,128)(2,1)S(1)}, bf16[64,512]{1,0:T(8,128)(2,1)S(1)}, u32[]{:S(2)}, u32[]{:S(2)}) %collective-permute-start.8) | collective-permute-done | bytes 65568 | tf_op jit(solution)/shard_map/ppermute | solution.py:300
  33.7 2.8 %collective-permute-start.9 = (bf16[64,512]{1,0:T(8,128)(2,1)S(1)}, bf16[64,512]{1,0:T(8,128)(2,1)S(1)}, u32[]{:S(2)}, u32[]{:S(2)}) collective-permute-start(bf16[64,512]{1,0:T(8,128)(2,1)S(1)} %get-tuple-element.41), channel_id=1, source_target_pairs={{0,12},{4,0},{8,4},{12,8},{1,13},{5,1},{9,5},{13,9},{2,14},{6,2},{... | collective-permute-start | bytes 196616 | tf_op jit(solution)/shard_map/ppermute | solution.py:300
  37.1 3.6 %shard_map.135 = (bf16[1024,512]{1,0:T(8,128)(2,1)}, bf16[16,32,512]{2,1,0:T(8,128)(2,1)}) custom-call(s32[2]{0:T(128)S(1)} %pad_add_fusion.me.refs_0_.low, s32[4,128]{1,0:T(4,128)S(1)} %shard_map.129.refs_1_.refs_0_, s32[4,128]{1,0:T(4,128)S(1)} %collective-permute-done.refs_1_.refs_2_, s32[4,128]{1,0:T(4,128)S(1)} %collective-permute-done.1.refs_2_.refs_3_, ...), custom_call_target="tpu_custom_call" | custom-call | flops 1342177280 | bytes 4530184 | tf_op jit(solution)/shard_map/pallas_call | solution.py:49
  40.8 6.0 %all-to-all-start = ((bf16[16,32,512]{2,1,0:T(8,128)(2,1)}), bf16[16,32,512]{2,1,0:T(8,128)(2,1)S(1)}, u32[]{:S(2)}, u32[]{:S(2)}) async-start(bf16[16,32,512]{2,1,0:T(8,128)(2,1)} %get-tuple-element.40.refs_14_), calls=%async_computation | async-start | bytes 1048576 | tf_op jit(solution)/shard_map/all_to_all | solution.py:442
  46.8 8.5 %shard_map.136 = (f32[64,512]{1,0:T(8,128)S(1)}, bf16[64,512]{1,0:T(8,128)(2,1)S(1)}, bf16[4,64,512]{2,1,0:T(8,128)(2,1)}) custom-call(s32[2]{0:T(128)S(1)} %pad_add_fusion.me.refs_0_.low, s32[1,1]{1,0:T(1,128)S(6)} %copy.14.refs_1_, bf16[64,512]{1,0:T(8,128)(2,1)S(1)} %get-tuple-element.28.refs_7_.refs_2_, ...), custom_call_target="tpu_custom_call" | custom-call | flops 4294967296 | bytes 2719756 | tf_op jit(solution)/shard_map/pallas_call | solution.py:49
  55.7 0.9 %collective-permute-done.12 = bf16[64,512]{1,0:T(8,128)(2,1)S(1)} collective-permute-done((bf16[64,512]{1,0:T(8,128)(2,1)S(1)}, bf16[64,512]{1,0:T(8,128)(2,1)S(1)}, u32[]{:S(2)}, u32[]{:S(2)}) %collective-permute-start.12) | collective-permute-done | bytes 65568 | tf_op jit(solution)/shard_map/ppermute | solution.py:295
  56.7 1.9 %collective-permute-start.13 = (bf16[32,512]{1,0:T(8,128)(2,1)S(1)}, bf16[32,512]{1,0:T(8,128)(2,1)S(1)}, u32[]{:S(2)}, u32[]{:S(2)}) collective-permute-start(bf16[32,512]{1,0:T(8,128)(2,1)S(1)} %fusion.2), channel_id=1, source_target_pairs={{0,2},{1,3},{2,0},{3,1},{4,6},{5,7},{6,4},{7,5},{8,10},{9,11},{10,... | collective-permute-start | bytes 98312 | tf_op jit(solution)/shard_map/ppermute | solution.py:295
  58.6 2.8 %collective-permute-done.13 = bf16[32,512]{1,0:T(8,128)(2,1)S(1)} collective-permute-done((bf16[32,512]{1,0:T(8,128)(2,1)S(1)}, bf16[32,512]{1,0:T(8,128)(2,1)S(1)}, u32[]{:S(2)}, u32[]{:S(2)}) %collective-permute-start.13) | collective-permute-done | bytes 32800 | tf_op jit(solution)/shard_map/ppermute | solution.py:295
  61.6 2.4 %collective-permute-start.14 = (bf16[64,512]{1,0:T(8,128)(2,1)S(1)}, bf16[64,512]{1,0:T(8,128)(2,1)S(1)}, u32[]{:S(2)}, u32[]{:S(2)}) collective-permute-start(bf16[64,512]{1,0:T(8,128)(2,1)S(1)} %pad_maximum_fusion.4), channel_id=1, source_target_pairs={{0,8},{4,12},{8,0},{12,4},{1,9},{5,13},{9,1},{13,5},{2,10},{6,14},... | collective-permute-start | bytes 196616 | tf_op jit(solution)/shard_map/ppermute | solution.py:295
  64.0 4.2 %collective-permute-done.14 = bf16[64,512]{1,0:T(8,128)(2,1)S(1)} collective-permute-done((bf16[64,512]{1,0:T(8,128)(2,1)S(1)}, bf16[64,512]{1,0:T(8,128)(2,1)S(1)}, u32[]{:S(2)}, u32[]{:S(2)}) %collective-permute-start.14) | collective-permute-done | bytes 65568 | tf_op jit(solution)/shard_map/ppermute | solution.py:295
  68.3 4.0 %all-to-all-start.1 = ((bf16[4,64,512]{2,1,0:T(8,128)(2,1)}), bf16[4,64,512]{2,1,0:T(8,128)(2,1)S(1)}, u32[]{:S(2)}, u32[]{:S(2)}) async-start(bf16[4,64,512]{2,1,0:T(8,128)(2,1)} %get-tuple-element.46), calls=%async_computation.1 | async-start | bytes 524288 | tf_op jit(solution)/shard_map/all_to_all | solution.py:458
  73.0 1.3 %collective-permute-start.16 = (bf16[160,512]{1,0:T(8,128)(2,1)S(1)}, bf16[160,512]{1,0:T(8,128)(2,1)S(1)}, u32[]{:S(2)}, u32[]{:S(2)}) collective-permute-start(bf16[160,512]{1,0:T(8,128)(2,1)S(1)} %pad_maximum_fusion.1), channel_id=1, source_target_pairs={{0,2},{1,3},{2,0},{3,1},{4,6},{5,7},{6,4},{7,5},{8,10},{9,11},{10,... | collective-permute-start | bytes 491528 | tf_op jit(solution)/shard_map/ppermute | solution.py:295
  74.3 6.0 %all-to-all-done.1.refs_4_ = bf16[4,64,512]{2,1,0:T(8,128)(2,1)S(1)} async-done(((bf16[4,64,512]{2,1,0:T(8,128)(2,1)}), bf16[4,64,512]{2,1,0:T(8,128)(2,1)S(1)}, u32[]{:S(2)}, u32[]{:S(2)}) %all-to-all-start.1) | async-done | bytes 262176 | tf_op jit(solution)/shard_map/all_to_all | solution.py:458
  80.3 2.0 %shard_map.137 = bf16[1024,512]{1,0:T(8,128)(2,1)} custom-call(s32[2]{0:T(128)S(1)} %pad_add_fusion.me.refs_0_.low, s32[4,128]{1,0:T(4,128)S(1)} %shard_map.129.refs_1_.refs_0_, s32[4,128]{1,0:T(4,128)S(1)} %collective-permute-done.refs_1_.refs_2_, s32[4,128]{1,0:T(4,128)S(1)} %collective-permute-done.1.refs_2_.refs_3_, ...), custom_call_target="tpu_custom_call" | custom-call | flops 268435456 | bytes 2367496 | tf_op jit(solution)/shard_map/pallas_call | solution.py:49
  82.6 1.6 %collective-permute-done.17 = bf16[320,512]{1,0:T(8,128)(2,1)S(1)} collective-permute-done((bf16[320,512]{1,0:T(8,128)(2,1)S(1)}, bf16[320,512]{1,0:T(8,128)(2,1)S(1)}, u32[]{:S(2)}, u32[]{:S(2)}) %collective-permute-start.17) | collective-permute-done | bytes 327712 | tf_op jit(solution)/shard_map/ppermute | solution.py:295
  84.2 1.7 %shard_map.138 = (f32[512,512]{1,0:T(8,128)}, f32[128,512]{1,0:T(8,128)}) custom-call(s32[2]{0:T(128)S(1)} %pad_add_fusion.me.refs_0_.low, bf16[256,512]{1,0:T(8,128)(2,1)S(1)} %maximum_select_fusion.out, bf16[256,512]{1,0:T(8,128)(2,1)S(1)} %slice.38.out_got, bf16[64,512]{1,0:T(8,128)(2,1)S(1)} %maximum_select_fusion.2.basis, ...), custom_call_target="tpu_custom_call" | custom-call | bytes 1966088 | tf_op jit(solution)/shard_map/pallas_call | solution.py:49
  (51 shorter events, 3.0 us)
Async XLA Ops:
  1.4 7.4 %collective-permute-start.2 = (s32[4,128]{1,0:T(4,128)S(1)}, s32[4,128]{1,0:T(4,128)S(1)}, u32[]{:S(2)}, u32[]{:S(2)}) collective-permute-start(s32[4,128]{1,0:T(4,128)S(1)} %shard_map.129.refs_1_.refs_0_), channel_id=1, source_target_pairs={{0,12},{4,0},{8,4},{12,8},{1,13},{5,1},{9,5},{13,9},{2,14},{6,2},{... | collective-permute-start | bytes 6152 | tf_op jit(solution)/shard_map/ppermute | solution.py:300
  6.5 4.5 %collective-permute-start.1 = (s32[4,128]{1,0:T(4,128)S(1)}, s32[4,128]{1,0:T(4,128)S(1)}, u32[]{:S(2)}, u32[]{:S(2)}) collective-permute-start(s32[4,128]{1,0:T(4,128)S(1)} %shard_map.129.refs_1_.refs_0_), channel_id=1, source_target_pairs={{0,8},{4,12},{8,0},{12,4},{1,9},{5,13},{9,1},{13,5},{2,10},{6,14},... | collective-permute-start | bytes 6152 | tf_op jit(solution)/shard_map/ppermute | solution.py:300
  6.5 5.4 %collective-permute-start = (s32[4,128]{1,0:T(4,128)S(1)}, s32[4,128]{1,0:T(4,128)S(1)}, u32[]{:S(2)}, u32[]{:S(2)}) collective-permute-start(s32[4,128]{1,0:T(4,128)S(1)} %shard_map.129.refs_1_.refs_0_), channel_id=1, source_target_pairs={{0,4},{4,8},{8,12},{12,0},{1,5},{5,9},{9,13},{13,1},{2,6},{6,10},{... | collective-permute-start | bytes 6152 | tf_op jit(solution)/shard_map/ppermute | solution.py:300
  13.1 6.8 %collective-permute-start.3 = (bf16[64,512]{1,0:T(8,128)(2,1)S(1)}, bf16[64,512]{1,0:T(8,128)(2,1)S(1)}, u32[]{:S(2)}, u32[]{:S(2)}) collective-permute-start(bf16[64,512]{1,0:T(8,128)(2,1)S(1)} %get-tuple-element.29), channel_id=1, source_target_pairs={{0,12},{4,0},{8,4},{12,8},{1,13},{5,1},{9,5},{13,9},{2,14},{6,2},{... | collective-permute-start | bytes 196616 | tf_op jit(solution)/shard_map/ppermute | solution.py:300
  13.7 6.2 %collective-permute-start.4 = (bf16[64,512]{1,0:T(8,128)(2,1)S(1)}, bf16[64,512]{1,0:T(8,128)(2,1)S(1)}, u32[]{:S(2)}, u32[]{:S(2)}) collective-permute-start(bf16[64,512]{1,0:T(8,128)(2,1)S(1)} %get-tuple-element.30), channel_id=1, source_target_pairs={{0,8},{4,12},{8,0},{12,4},{1,9},{5,13},{9,1},{13,5},{2,10},{6,14},... | collective-permute-start | bytes 196616 | tf_op jit(solution)/shard_map/ppermute | solution.py:300
  14.3 6.2 %collective-permute-start.5 = (bf16[64,512]{1,0:T(8,128)(2,1)S(1)}, bf16[64,512]{1,0:T(8,128)(2,1)S(1)}, u32[]{:S(2)}, u32[]{:S(2)}) collective-permute-start(bf16[64,512]{1,0:T(8,128)(2,1)S(1)} %get-tuple-element.31), channel_id=1, source_target_pairs={{0,4},{4,8},{8,12},{12,0},{1,5},{5,9},{9,13},{13,1},{2,6},{6,10},{... | collective-permute-start | bytes 196616 | tf_op jit(solution)/shard_map/ppermute | solution.py:300
  16.9 3.6 %copy-start.3 = (bf16[128,512]{1,0:T(8,128)(2,1)S(1)}, bf16[128,512]{1,0:T(8,128)(2,1)}, u32[]{:S(2)}) copy-start(bf16[128,512]{1,0:T(8,128)(2,1)} %refs_12_.1) | copy-start | bytes 393220
  17.0 3.6 %copy-start.4 = (s32[1,32,128]{2,1,0:T(8,128)S(1)}, s32[1,32,128]{2,1,0:T(8,128)}, u32[]{:S(2)}) copy-start(s32[1,32,128]{2,1,0:T(8,128)} %param.14) | copy-start | bytes 49156
  17.0 3.6 %copy-start.5 = (s32[1,32,128]{2,1,0:T(8,128)S(1)}, s32[1,32,128]{2,1,0:T(8,128)}, u32[]{:S(2)}) copy-start(s32[1,32,128]{2,1,0:T(8,128)} %param.15) | copy-start | bytes 49156
  20.5 16.6 %copy-start = (bf16[1,1024,512]{2,1,0:T(8,128)(2,1)S(1)}, bf16[1,1024,512]{2,1,0:T(8,128)(2,1)}, u32[]{:S(2)}) copy-start(bf16[1,1024,512]{2,1,0:T(8,128)(2,1)} %param.11) | copy-start | bytes 3145732
  20.6 16.6 %copy-start.1 = (bf16[1,1024,512]{2,1,0:T(8,128)(2,1)S(1)}, bf16[1,1024,512]{2,1,0:T(8,128)(2,1)}, u32[]{:S(2)}) copy-start(bf16[1,1024,512]{2,1,0:T(8,128)(2,1)} %param.10) | copy-start | bytes 3145732
  25.9 11.3 %copy-start.2 = (bf16[512,512]{1,0:T(8,128)(2,1)S(1)}, bf16[512,512]{1,0:T(8,128)(2,1)}, u32[]{:S(2)}) copy-start(bf16[512,512]{1,0:T(8,128)(2,1)} %refs_11_.1) | copy-start | bytes 1572868
  25.9 6.2 %collective-permute-start.6 = (bf16[64,512]{1,0:T(8,128)(2,1)S(1)}, bf16[64,512]{1,0:T(8,128)(2,1)S(1)}, u32[]{:S(2)}, u32[]{:S(2)}) collective-permute-start(bf16[64,512]{1,0:T(8,128)(2,1)S(1)} %get-tuple-element.34), channel_id=1, source_target_pairs={{0,4},{4,8},{8,12},{12,0},{1,5},{5,9},{9,13},{13,1},{2,6},{6,10},{... | collective-permute-start | bytes 196616 | tf_op jit(solution)/shard_map/ppermute | solution.py:300
  26.2 5.9 %collective-permute-start.7 = (bf16[64,512]{1,0:T(8,128)(2,1)S(1)}, bf16[64,512]{1,0:T(8,128)(2,1)S(1)}, u32[]{:S(2)}, u32[]{:S(2)}) collective-permute-start(bf16[64,512]{1,0:T(8,128)(2,1)S(1)} %get-tuple-element.35), channel_id=1, source_target_pairs={{0,8},{4,12},{8,0},{12,4},{1,9},{5,13},{9,1},{13,5},{2,10},{6,14},... | collective-permute-start | bytes 196616 | tf_op jit(solution)/shard_map/ppermute | solution.py:300
  28.2 5.1 %collective-permute-start.8 = (bf16[64,512]{1,0:T(8,128)(2,1)S(1)}, bf16[64,512]{1,0:T(8,128)(2,1)S(1)}, u32[]{:S(2)}, u32[]{:S(2)}) collective-permute-start(bf16[64,512]{1,0:T(8,128)(2,1)S(1)} %get-tuple-element.36), channel_id=1, source_target_pairs={{0,12},{4,0},{8,4},{12,8},{1,13},{5,1},{9,5},{13,9},{2,14},{6,2},{... | collective-permute-start | bytes 196616 | tf_op jit(solution)/shard_map/ppermute | solution.py:300
  33.7 13.1 %collective-permute-start.9 = (bf16[64,512]{1,0:T(8,128)(2,1)S(1)}, bf16[64,512]{1,0:T(8,128)(2,1)S(1)}, u32[]{:S(2)}, u32[]{:S(2)}) collective-permute-start(bf16[64,512]{1,0:T(8,128)(2,1)S(1)} %get-tuple-element.41), channel_id=1, source_target_pairs={{0,12},{4,0},{8,4},{12,8},{1,13},{5,1},{9,5},{13,9},{2,14},{6,2},{... | collective-permute-start | bytes 196616 | tf_op jit(solution)/shard_map/ppermute | solution.py:300
  36.5 10.3 %collective-permute-start.10 = (bf16[64,512]{1,0:T(8,128)(2,1)S(1)}, bf16[64,512]{1,0:T(8,128)(2,1)S(1)}, u32[]{:S(2)}, u32[]{:S(2)}) collective-permute-start(bf16[64,512]{1,0:T(8,128)(2,1)S(1)} %get-tuple-element.42), channel_id=1, source_target_pairs={{0,8},{4,12},{8,0},{12,4},{1,9},{5,13},{9,1},{13,5},{2,10},{6,14},... | collective-permute-start | bytes 196616 | tf_op jit(solution)/shard_map/ppermute | solution.py:300
  37.0 9.8 %collective-permute-start.11 = (bf16[64,512]{1,0:T(8,128)(2,1)S(1)}, bf16[64,512]{1,0:T(8,128)(2,1)S(1)}, u32[]{:S(2)}, u32[]{:S(2)}) collective-permute-start(bf16[64,512]{1,0:T(8,128)(2,1)S(1)} %get-tuple-element.43), channel_id=1, source_target_pairs={{0,4},{4,8},{8,12},{12,0},{1,5},{5,9},{9,13},{13,1},{2,6},{6,10},{... | collective-permute-start | bytes 196616 | tf_op jit(solution)/shard_map/ppermute | solution.py:300
  40.8 20.7 %all-to-all-start = ((bf16[16,32,512]{2,1,0:T(8,128)(2,1)}), bf16[16,32,512]{2,1,0:T(8,128)(2,1)S(1)}, u32[]{:S(2)}, u32[]{:S(2)}) async-start(bf16[16,32,512]{2,1,0:T(8,128)(2,1)} %get-tuple-element.40.refs_14_), calls=%async_computation | async-start | bytes 1048576 | tf_op jit(solution)/shard_map/all_to_all | solution.py:442
  55.3 1.4 %collective-permute-start.12 = (bf16[64,512]{1,0:T(8,128)(2,1)S(1)}, bf16[64,512]{1,0:T(8,128)(2,1)S(1)}, u32[]{:S(2)}, u32[]{:S(2)}) collective-permute-start(bf16[64,512]{1,0:T(8,128)(2,1)S(1)} %get-tuple-element.45), channel_id=1, source_target_pairs={{0,1},{1,0},{2,3},{3,2},{4,5},{5,4},{6,7},{7,6},{8,9},{9,8},{10,11... | collective-permute-start | bytes 196616 | tf_op jit(solution)/shard_map/ppermute | solution.py:295
  56.7 4.8 %collective-permute-start.13 = (bf16[32,512]{1,0:T(8,128)(2,1)S(1)}, bf16[32,512]{1,0:T(8,128)(2,1)S(1)}, u32[]{:S(2)}, u32[]{:S(2)}) collective-permute-start(bf16[32,512]{1,0:T(8,128)(2,1)S(1)} %fusion.2), channel_id=1, source_target_pairs={{0,2},{1,3},{2,0},{3,1},{4,6},{5,7},{6,4},{7,5},{8,10},{9,11},{10,... | collective-permute-start | bytes 98312 | tf_op jit(solution)/shard_map/ppermute | solution.py:295
  61.6 6.6 %collective-permute-start.14 = (bf16[64,512]{1,0:T(8,128)(2,1)S(1)}, bf16[64,512]{1,0:T(8,128)(2,1)S(1)}, u32[]{:S(2)}, u32[]{:S(2)}) collective-permute-start(bf16[64,512]{1,0:T(8,128)(2,1)S(1)} %pad_maximum_fusion.4), channel_id=1, source_target_pairs={{0,8},{4,12},{8,0},{12,4},{1,9},{5,13},{9,1},{13,5},{2,10},{6,14},... | collective-permute-start | bytes 196616 | tf_op jit(solution)/shard_map/ppermute | solution.py:295
  68.2 4.7 %collective-permute-start.15 = (bf16[96,512]{1,0:T(8,128)(2,1)S(1)}, bf16[96,512]{1,0:T(8,128)(2,1)S(1)}, u32[]{:S(2)}, u32[]{:S(2)}) collective-permute-start(bf16[96,512]{1,0:T(8,128)(2,1)S(1)} %pad_maximum_fusion.2), channel_id=1, source_target_pairs={{0,4},{4,0},{8,12},{12,8},{1,5},{5,1},{9,13},{13,9},{2,6},{6,2},{1... | collective-permute-start | bytes 294920 | tf_op jit(solution)/shard_map/ppermute | solution.py:295
  68.3 12.0 %all-to-all-start.1 = ((bf16[4,64,512]{2,1,0:T(8,128)(2,1)}), bf16[4,64,512]{2,1,0:T(8,128)(2,1)S(1)}, u32[]{:S(2)}, u32[]{:S(2)}) async-start(bf16[4,64,512]{2,1,0:T(8,128)(2,1)} %get-tuple-element.46), calls=%async_computation.1 | async-start | bytes 524288 | tf_op jit(solution)/shard_map/all_to_all | solution.py:458
  73.0 9.3 %collective-permute-start.16 = (bf16[160,512]{1,0:T(8,128)(2,1)S(1)}, bf16[160,512]{1,0:T(8,128)(2,1)S(1)}, u32[]{:S(2)}, u32[]{:S(2)}) collective-permute-start(bf16[160,512]{1,0:T(8,128)(2,1)S(1)} %pad_maximum_fusion.1), channel_id=1, source_target_pairs={{0,2},{1,3},{2,0},{3,1},{4,6},{5,7},{6,4},{7,5},{8,10},{9,11},{10,... | collective-permute-start | bytes 491528 | tf_op jit(solution)/shard_map/ppermute | solution.py:295
  82.5 1.7 %collective-permute-start.17 = (bf16[320,512]{1,0:T(8,128)(2,1)S(1)}, bf16[320,512]{1,0:T(8,128)(2,1)S(1)}, u32[]{:S(2)}, u32[]{:S(2)}) collective-permute-start(bf16[320,512]{1,0:T(8,128)(2,1)S(1)} %pad_maximum_fusion), channel_id=1, source_target_pairs={{0,1},{1,0},{2,3},{3,2},{4,5},{5,4},{6,7},{7,6},{8,9},{9,8},{10,11... | collective-permute-start | bytes 983048 | tf_op jit(solution)/shard_map/ppermute | solution.py:295
